TPU v7x, 32 devices: a whole 2x2x4 slice. The times are simulated.
32 devices in a mesh: dp: 4 (over z), fsdp: 8 (over y, x, core).
Axes of the slice: x: 2, y: 2, z: 4, core: 2. Of those that a mesh axis runs over, the one named last changes fastest.
Arguments:
- tokens: bfloat16 [4, 4096, 2048], P('dp', 'fsdp'), may hold values from -6 to 6
- summaries: bfloat16 [4, 150, 2048], P('dp', None, 'fsdp'), may hold values from -6 to 6
- segment_lengths: int32 [4, 4], P('dp'), may hold values from 0 to 2048, as said below
- pad_lengths: int32 [4], P('dp'), may hold values from 0 to 511
- output_grad: bfloat16 [4, 4096, 2048], P('dp', 'fsdp'), may hold values from -6 to 6
- norm1_gain: bfloat16 [2048], P(('dp', 'fsdp')), may hold values from 0.5 to 1.5
- norm1_bias: bfloat16 [2048], P(('dp', 'fsdp')), may hold values from -1.5 to 1.5
- query_weight: bfloat16 [2048, 2048], P(('dp', 'fsdp')), may hold values from -0.125 to 0.125
- query_bias: bfloat16 [2048], P(('dp', 'fsdp')), may hold values from -1.5 to 1.5
- key_weight: bfloat16 [2048, 2048], P(('dp', 'fsdp')), may hold values from -0.125 to 0.125
- value_weight: bfloat16 [2048, 2048], P(('dp', 'fsdp')), may hold values from -0.125 to 0.125
- value_bias: bfloat16 [2048], P(('dp', 'fsdp')), may hold values from -1.5 to 1.5
- out_weight: bfloat16 [2048, 2048], P(('dp', 'fsdp')), may hold values from -1 to 1
- out_bias: bfloat16 [2048], P(('dp', 'fsdp')), may hold values from -1.5 to 1.5
- norm2_gain: bfloat16 [2048], P(('dp', 'fsdp')), may hold values from 0.5 to 1.5
- norm2_bias: bfloat16 [2048], P(('dp', 'fsdp')), may hold values from -1.5 to 1.5
- up_weight: bfloat16 [2048, 8192], P(('dp', 'fsdp')), may hold values from -0.125 to 0.125
- up_bias: bfloat16 [8192], P(('dp', 'fsdp')), may hold values from -1.5 to 1.5
- down_weight: bfloat16 [8192, 2048], P(('dp', 'fsdp')), may hold values from -0.0625 to 0.0625
- down_bias: bfloat16 [2048], P(('dp', 'fsdp')), may hold values from -1.5 to 1.5
Outputs:
- output: bfloat16 [4, 4096, 2048], P('dp', 'fsdp')
- tokens_grad: float32 [4, 4096, 2048], P('dp', 'fsdp')
- summaries_grad: float32 [4, 150, 2048], P('dp', None, 'fsdp')
- norm1_gain_grad: float32 [2048], P(('dp', 'fsdp'))
- norm1_bias_grad: float32 [2048], P(('dp', 'fsdp'))
- query_weight_grad: float32 [2048, 2048], P(('dp', 'fsdp'))
- query_bias_grad: float32 [2048], P(('dp', 'fsdp'))
- key_weight_grad: float32 [2048, 2048], P(('dp', 'fsdp'))
- value_weight_grad: float32 [2048, 2048], P(('dp', 'fsdp'))
- value_bias_grad: float32 [2048], P(('dp', 'fsdp'))
- out_weight_grad: float32 [2048, 2048], P(('dp', 'fsdp'))
- out_bias_grad: float32 [2048], P(('dp', 'fsdp'))
- norm2_gain_grad: float32 [2048], P(('dp', 'fsdp'))
- norm2_bias_grad: float32 [2048], P(('dp', 'fsdp'))
- up_weight_grad: float32 [2048, 8192], P(('dp', 'fsdp'))
- up_bias_grad: float32 [8192], P(('dp', 'fsdp'))
- down_weight_grad: float32 [8192, 2048], P(('dp', 'fsdp'))
- down_bias_grad: float32 [2048], P(('dp', 'fsdp'))
Inputs may be any that keep to these rules, and one draw needn't show every extreme that they name: `segment_lengths`: each row lists its item's segment lengths in order, each from 1024 to 2048, summing to 4096, followed by zeros; every row has two or more segments, one of them of exactly 2048 tokens. Summary rows of segments past an item's last but one are read by no query. `pad_lengths`: an item's last tokens, as many as its entry, are padding; they lie in its last segment.
All inputs are finite; a program needn't handle non-finite values.
Results may differ from a plain program's by a relative error of at most 0.012.
Values may be sent and summed in bfloat16 or wider, within the bound.
No kernel may reach another device: no remote copies, remote signals or barrier semaphores. Data moves between devices by JAX's collectives and lax.ppermute only.
A program may use at most 512 MiB of HBM per device.

v0:
```python
import math

import jax
import jax.numpy as jnp
from jax import lax
from jax.sharding import PartitionSpec as P

HEAD = 64
SUMM = 50
SEG_MAX = 2048


epsilon = 1e-05
masked_score = -1e30


def passed_along(x, axis, by):
    devices = lax.axis_size(axis)
    pairs = [(i, i + by) for i in range(devices) if 0 <= i + by < devices]
    return lax.ppermute(x, axis, pairs)


def layer_norm(values, gains, shifts):
    centre = jnp.mean(values, axis=-1, keepdims=True)
    centred = values - centre
    spread = jnp.mean(centred * centred, axis=-1, keepdims=True)
    return centred * lax.rsqrt(spread + epsilon) * gains + shifts


def gelu_tanh(values):
    return jax.nn.gelu(values, approximate=True)


def product(left, right):
    return jnp.dot(left, right, preferred_element_type=jnp.float32)


def inner_rows(left, right):
    return lax.dot_general(
        left, right, (((0,), (0,)), ((), ())), preferred_element_type=jnp.float32
    )


def inner_cols(left, right):
    return lax.dot_general(
        left, right, (((1,), (1,)), ((), ())), preferred_element_type=jnp.float32
    )


def segment_of(lengths, places):
    bounds = jnp.cumsum(lengths)
    return jnp.sum((places[:, None] >= bounds[None, :]).astype(jnp.int32), axis=1)


def visibility(query_places, key_places, lengths, padding, summary_rows, item_length):
    query_segment = segment_of(lengths, query_places)
    key_segment = segment_of(lengths, key_places)
    same = (key_segment[None, :] == query_segment[:, None]) & (
        key_places[None, :] <= query_places[:, None]
    )
    living = (key_places[None, :] < item_length - padding) | (
        key_places[None, :] == query_places[:, None]
    )
    inside = key_places[None, :] >= 0
    summary_segment = jnp.arange(summary_rows, dtype=jnp.int32) // SUMM
    earlier = summary_segment[None, :] < query_segment[:, None]
    return jnp.concatenate([earlier, same & living & inside], axis=1)


def per_device(
    tokens,
    summaries,
    segment_lengths,
    pad_lengths,
    output_grad,
    norm1_gain,
    norm1_bias,
    query_weight,
    query_bias,
    key_weight,
    value_weight,
    value_bias,
    out_weight,
    out_bias,
    norm2_gain,
    norm2_bias,
    up_weight,
    up_bias,
    down_weight,
    down_bias,
):
    shards = lax.axis_size("fsdp")
    position = lax.axis_index("fsdp")
    tok_rows = tokens.shape[1]
    width = tokens.shape[2]
    item_length = tok_rows * shards
    summary_rows = summaries.shape[1]
    summary_cols = summaries.shape[2]
    heads = width // HEAD
    group = math.gcd(heads, 4)
    group_width = group * HEAD
    scale = 1.0 / math.sqrt(HEAD)
    reach = min(shards - 1, (SEG_MAX + tok_rows - 2) // tok_rows)
    window = (reach + 1) * tok_rows
    key_count = summary_rows + window
    attn_small = jnp.stack([norm1_gain, norm1_bias, query_bias, value_bias, out_bias], axis=1)
    ffn_small = jnp.stack([norm2_gain, norm2_bias, down_bias], axis=1)
    attn_full = (
        lax.all_gather(query_weight, ("dp", "fsdp"), axis=0, tiled=True),
        lax.all_gather(key_weight, ("dp", "fsdp"), axis=0, tiled=True),
        lax.all_gather(value_weight, ("dp", "fsdp"), axis=0, tiled=True),
        lax.all_gather(out_weight, ("dp", "fsdp"), axis=0, tiled=True),
        lax.all_gather(attn_small, ("dp", "fsdp"), axis=0, tiled=True),
    )
    query_full, key_full, value_full, out_full, attn_vectors = attn_full
    attn_floats = attn_vectors.astype(jnp.float32)
    gain_one = attn_floats[:, 0]
    shift_one = attn_floats[:, 1]
    query_shift = attn_floats[:, 2]
    value_shift = attn_floats[:, 3]
    out_shift = attn_floats[:, 4]
    summ_full = lax.all_gather(summaries[0], "fsdp", axis=1, tiled=True)
    inputs = tokens[0].astype(jnp.float32)
    summ_inputs = summ_full.astype(jnp.float32)
    normed = layer_norm(inputs, gain_one, shift_one).astype(jnp.bfloat16)
    normed_summ = layer_norm(summ_inputs, gain_one, shift_one).astype(jnp.bfloat16)
    queries = (product(normed, query_full) + query_shift).astype(jnp.bfloat16)
    keys = product(normed, key_full).astype(jnp.bfloat16)
    values = (product(normed, value_full) + value_shift).astype(jnp.bfloat16)
    summ_keys = product(normed_summ, key_full).astype(jnp.bfloat16)
    summ_values = (product(normed_summ, value_full) + value_shift).astype(jnp.bfloat16)
    key_parts = [keys]
    value_parts = [values]
    for distance in range(1, reach + 1):
        earlier_keys, earlier_values = passed_along((keys, values), "fsdp", distance)
        key_parts.insert(0, earlier_keys)
        value_parts.insert(0, earlier_values)
    first_row = position * tok_rows
    window_start = first_row - reach * tok_rows
    all_keys = jnp.concatenate([summ_keys] + key_parts, axis=0)
    all_values = jnp.concatenate([summ_values] + value_parts, axis=0)
    query_places = first_row + jnp.arange(tok_rows, dtype=jnp.int32)
    key_places = window_start + jnp.arange(window, dtype=jnp.int32)
    mask = visibility(
        query_places, key_places, segment_lengths[0], pad_lengths[0], summary_rows, item_length
    )

    def head_block(source, index, count):
        return lax.dynamic_slice_in_dim(source, index * group_width, group_width, 1).reshape(
            count, group, HEAD
        )

    def head_scores(index):
        query_block = head_block(queries, index, tok_rows)
        key_block = head_block(all_keys, index, key_count)
        scores = (
            jnp.einsum("qgd,kgd->gqk", query_block, key_block, preferred_element_type=jnp.float32)
            * scale
        )
        return jnp.where(mask[None], scores, masked_score)

    def forward_group(index, carry):
        mixed_all, log_totals = carry
        scores = head_scores(index)
        highest = jnp.max(scores, axis=-1, keepdims=True)
        weights = jnp.exp(scores - highest)
        totals = jnp.sum(weights, axis=-1, keepdims=True)
        probs_low = (weights / totals).astype(jnp.bfloat16)
        value_block = head_block(all_values, index, key_count)
        mixed = jnp.einsum(
            "gqk,kgd->qgd", probs_low, value_block, preferred_element_type=jnp.float32
        )
        mixed_all = lax.dynamic_update_slice_in_dim(
            mixed_all, mixed.reshape(tok_rows, group_width), index * group_width, 1
        )
        log_totals = lax.dynamic_update_slice_in_dim(
            log_totals, (highest + jnp.log(totals))[:, :, 0], index * group, 0
        )
        return (mixed_all, log_totals)

    attn_mixed, log_totals = lax.fori_loop(
        0,
        heads // group,
        forward_group,
        (jnp.zeros((tok_rows, width), jnp.float32), jnp.zeros((heads, tok_rows), jnp.float32)),
    )
    attn_low = attn_mixed.astype(jnp.bfloat16)
    resid = inputs + product(attn_low, out_full) + out_shift
    ffn_full = (
        lax.all_gather(up_weight, ("dp", "fsdp"), axis=0, tiled=True),
        lax.all_gather(down_weight, ("dp", "fsdp"), axis=0, tiled=True),
        lax.all_gather(up_bias, ("dp", "fsdp"), axis=0, tiled=True),
        lax.all_gather(ffn_small, ("dp", "fsdp"), axis=0, tiled=True),
    )
    up_full, down_full, up_shift_low, ffn_vectors = ffn_full
    ffn_floats = ffn_vectors.astype(jnp.float32)
    gain_two = ffn_floats[:, 0]
    shift_two = ffn_floats[:, 1]
    down_shift = ffn_floats[:, 2]
    normed_two = layer_norm(resid, gain_two, shift_two).astype(jnp.bfloat16)
    upper = product(normed_two, up_full) + up_shift_low.astype(jnp.float32)
    active = gelu_tanh(upper).astype(jnp.bfloat16)
    result = (resid + product(active, down_full) + down_shift).astype(jnp.bfloat16)
    ffn_back = (
        lax.all_gather(up_weight, ("dp", "fsdp"), axis=0, tiled=True),
        lax.all_gather(down_weight, ("dp", "fsdp"), axis=0, tiled=True),
        lax.all_gather(up_bias, ("dp", "fsdp"), axis=0, tiled=True),
        lax.all_gather(ffn_small, ("dp", "fsdp"), axis=0, tiled=True),
    )
    up_back = ffn_back[0]
    down_back = ffn_back[1]
    grad_output = output_grad[0]
    grad_floats = grad_output.astype(jnp.float32)
    down_grad = inner_rows(active, grad_output)
    down_shift_grad = jnp.sum(grad_floats, axis=0)
    grad_active = inner_cols(grad_output, down_back)
    _, gelu_pull = jax.vjp(gelu_tanh, upper)
    grad_upper = gelu_pull(grad_active)[0].astype(jnp.bfloat16)
    up_grad = inner_rows(normed_two, grad_upper)
    up_shift_grad = jnp.sum(grad_upper.astype(jnp.float32), axis=0)
    grad_normed_two = inner_cols(grad_upper, up_back)
    _, norm_two_pull = jax.vjp(layer_norm, resid, gain_two, shift_two)
    grad_resid, gain_two_grad, shift_two_grad = norm_two_pull(grad_normed_two)
    grad_resid = grad_resid + grad_floats
    ffn_sums = (
        lax.psum_scatter(up_grad, ("dp", "fsdp"), scatter_dimension=0, tiled=True),
        lax.psum_scatter(down_grad, ("dp", "fsdp"), scatter_dimension=0, tiled=True),
        lax.psum_scatter(up_shift_grad, ("dp", "fsdp"), scatter_dimension=0, tiled=True),
        lax.psum_scatter(
            jnp.stack([gain_two_grad, shift_two_grad, down_shift_grad], axis=1),
            ("dp", "fsdp"),
            scatter_dimension=0,
            tiled=True,
        ),
    )
    attn_back = (
        lax.all_gather(query_weight, ("dp", "fsdp"), axis=0, tiled=True),
        lax.all_gather(key_weight, ("dp", "fsdp"), axis=0, tiled=True),
        lax.all_gather(value_weight, ("dp", "fsdp"), axis=0, tiled=True),
        lax.all_gather(out_weight, ("dp", "fsdp"), axis=0, tiled=True),
        lax.all_gather(attn_small, ("dp", "fsdp"), axis=0, tiled=True),
    )
    query_back, key_back, value_back, out_back = (
        attn_back[0],
        attn_back[1],
        attn_back[2],
        attn_back[3],
    )
    grad_proj = grad_resid.astype(jnp.bfloat16)
    out_shift_grad = jnp.sum(grad_proj.astype(jnp.float32), axis=0)
    out_grad_full = inner_rows(attn_low, grad_proj)
    grad_attn = inner_cols(grad_proj, out_back).astype(jnp.bfloat16)

    def backward_group(index, carry):
        grad_queries, grad_summ_keys, grad_summ_values, grad_window_keys, grad_window_values = carry
        scores = head_scores(index)
        log_block = lax.dynamic_slice_in_dim(log_totals, index * group, group, 0)
        probs = jnp.exp(scores - log_block[:, :, None])
        probs_low = probs.astype(jnp.bfloat16)
        value_block = head_block(all_values, index, key_count)
        key_block = head_block(all_keys, index, key_count)
        query_block = head_block(queries, index, tok_rows)
        grad_block = head_block(grad_attn, index, tok_rows)
        grad_probs = jnp.einsum(
            "qgd,kgd->gqk", grad_block, value_block, preferred_element_type=jnp.float32
        )
        row_terms = jnp.sum(grad_probs * probs, axis=-1, keepdims=True)
        grad_scores = (probs * (grad_probs - row_terms)).astype(jnp.bfloat16)
        grad_query_block = (
            jnp.einsum("gqk,kgd->qgd", grad_scores, key_block, preferred_element_type=jnp.float32)
            * scale
        )
        grad_key_block = (
            jnp.einsum("gqk,qgd->kgd", grad_scores, query_block, preferred_element_type=jnp.float32)
            * scale
        )
        grad_value_block = jnp.einsum(
            "gqk,qgd->kgd", probs_low, grad_block, preferred_element_type=jnp.float32
        )
        grad_key_block = grad_key_block.reshape(key_count, group_width)
        grad_value_block = grad_value_block.reshape(key_count, group_width)
        column = index * group_width
        grad_queries = lax.dynamic_update_slice_in_dim(
            grad_queries, grad_query_block.reshape(tok_rows, group_width), column, 1
        )
        grad_summ_keys = lax.dynamic_update_slice_in_dim(
            grad_summ_keys, grad_key_block[:summary_rows], column, 1
        )
        grad_summ_values = lax.dynamic_update_slice_in_dim(
            grad_summ_values, grad_value_block[:summary_rows], column, 1
        )
        grad_window_keys = lax.dynamic_update_slice_in_dim(
            grad_window_keys, grad_key_block[summary_rows:], column, 1
        )
        grad_window_values = lax.dynamic_update_slice_in_dim(
            grad_window_values, grad_value_block[summary_rows:], column, 1
        )
        return (
            grad_queries,
            grad_summ_keys,
            grad_summ_values,
            grad_window_keys,
            grad_window_values,
        )

    grad_queries, grad_summ_keys, grad_summ_values, grad_window_keys, grad_window_values = (
        lax.fori_loop(
            0,
            heads // group,
            backward_group,
            (
                jnp.zeros((tok_rows, width), jnp.float32),
                jnp.zeros((summary_rows, width), jnp.float32),
                jnp.zeros((summary_rows, width), jnp.float32),
                jnp.zeros((window, width), jnp.float32),
                jnp.zeros((window, width), jnp.float32),
            ),
        )
    )
    own_grad_keys = grad_window_keys[reach * tok_rows :]
    own_grad_values = grad_window_values[reach * tok_rows :]
    for distance in range(1, reach + 1):
        begin = (reach - distance) * tok_rows
        later_keys, later_values = passed_along(
            (
                grad_window_keys[begin : begin + tok_rows],
                grad_window_values[begin : begin + tok_rows],
            ),
            "fsdp",
            -distance,
        )
        own_grad_keys = own_grad_keys + later_keys
        own_grad_values = own_grad_values + later_values
    part_summ_keys, part_summ_values = (
        lax.psum_scatter(grad_summ_keys, "fsdp", scatter_dimension=1, tiled=True),
        lax.psum_scatter(grad_summ_values, "fsdp", scatter_dimension=1, tiled=True),
    )
    queries_low = grad_queries.astype(jnp.bfloat16)
    keys_low = own_grad_keys.astype(jnp.bfloat16)
    values_low = own_grad_values.astype(jnp.bfloat16)
    summ_keys_low = part_summ_keys.astype(jnp.bfloat16)
    summ_values_low = part_summ_values.astype(jnp.bfloat16)
    column_start = position * summary_cols
    query_grad_full = inner_rows(normed, queries_low)
    query_shift_grad = jnp.sum(queries_low.astype(jnp.float32), axis=0)
    key_grad_full = inner_rows(normed, keys_low)
    value_grad_full = inner_rows(normed, values_low)
    key_grad_full = lax.dynamic_update_slice_in_dim(
        key_grad_full,
        lax.dynamic_slice_in_dim(key_grad_full, column_start, summary_cols, 1)
        + inner_rows(normed_summ, summ_keys_low),
        column_start,
        1,
    )
    value_grad_full = lax.dynamic_update_slice_in_dim(
        value_grad_full,
        lax.dynamic_slice_in_dim(value_grad_full, column_start, summary_cols, 1)
        + inner_rows(normed_summ, summ_values_low),
        column_start,
        1,
    )
    value_shift_grad = jnp.sum(values_low.astype(jnp.float32), axis=0)
    value_shift_grad = lax.dynamic_update_slice_in_dim(
        value_shift_grad,
        lax.dynamic_slice_in_dim(value_shift_grad, column_start, summary_cols, 0)
        + jnp.sum(summ_values_low.astype(jnp.float32), axis=0),
        column_start,
        0,
    )
    grad_normed = (
        inner_cols(queries_low, query_back)
        + inner_cols(keys_low, key_back)
        + inner_cols(values_low, value_back)
    )
    key_columns = lax.dynamic_slice_in_dim(key_back, column_start, summary_cols, 1)
    value_columns = lax.dynamic_slice_in_dim(value_back, column_start, summary_cols, 1)
    grad_normed_summ_part = inner_cols(summ_keys_low, key_columns) + inner_cols(
        summ_values_low, value_columns
    )
    grad_normed_summ = lax.psum(grad_normed_summ_part, "fsdp")
    _, norm_one_pull = jax.vjp(layer_norm, inputs, gain_one, shift_one)
    grad_inputs, gain_one_grad, shift_one_grad = norm_one_pull(grad_normed)
    grad_inputs = grad_inputs + grad_resid
    _, norm_summ_pull = jax.vjp(layer_norm, summ_inputs, gain_one, shift_one)
    grad_summ, gain_summ_grad, shift_summ_grad = norm_summ_pull(grad_normed_summ)
    column_keep = jnp.arange(width, dtype=jnp.int32) // summary_cols == position
    gain_one_grad = gain_one_grad + jnp.where(column_keep, gain_summ_grad, 0.0)
    shift_one_grad = shift_one_grad + jnp.where(column_keep, shift_summ_grad, 0.0)
    summary_grad = lax.dynamic_slice_in_dim(grad_summ, column_start, summary_cols, 1)
    attn_sums = (
        lax.psum_scatter(query_grad_full, ("dp", "fsdp"), scatter_dimension=0, tiled=True),
        lax.psum_scatter(key_grad_full, ("dp", "fsdp"), scatter_dimension=0, tiled=True),
        lax.psum_scatter(value_grad_full, ("dp", "fsdp"), scatter_dimension=0, tiled=True),
        lax.psum_scatter(out_grad_full, ("dp", "fsdp"), scatter_dimension=0, tiled=True),
        lax.psum_scatter(
            jnp.stack(
                [gain_one_grad, shift_one_grad, query_shift_grad, value_shift_grad, out_shift_grad],
                axis=1,
            ),
            ("dp", "fsdp"),
            scatter_dimension=0,
            tiled=True,
        ),
    )
    attn_vector_grads = attn_sums[4]
    ffn_vector_grads = ffn_sums[3]
    return (
        result[None],
        grad_inputs[None],
        summary_grad[None],
        attn_vector_grads[:, 0],
        attn_vector_grads[:, 1],
        attn_sums[0],
        attn_vector_grads[:, 2],
        attn_sums[1],
        attn_sums[2],
        attn_vector_grads[:, 3],
        attn_sums[3],
        attn_vector_grads[:, 4],
        ffn_vector_grads[:, 0],
        ffn_vector_grads[:, 1],
        ffn_sums[0],
        ffn_sums[2],
        ffn_sums[1],
        ffn_vector_grads[:, 2],
    )


def solution(mesh):
    return jax.shard_map(
        per_device,
        mesh=mesh,
        in_specs=(
            P("dp", "fsdp", None),
            P("dp", None, "fsdp"),
            P("dp", None),
            P("dp"),
            P("dp", "fsdp", None),
            P(("dp", "fsdp")),
            P(("dp", "fsdp")),
            P(("dp", "fsdp"), None),
            P(("dp", "fsdp")),
            P(("dp", "fsdp"), None),
            P(("dp", "fsdp"), None),
            P(("dp", "fsdp")),
            P(("dp", "fsdp"), None),
            P(("dp", "fsdp")),
            P(("dp", "fsdp")),
            P(("dp", "fsdp")),
            P(("dp", "fsdp"), None),
            P(("dp", "fsdp")),
            P(("dp", "fsdp"), None),
            P(("dp", "fsdp")),
        ),
        out_specs=(
            P("dp", "fsdp", None),
            P("dp", "fsdp", None),
            P("dp", None, "fsdp"),
            P(("dp", "fsdp")),
            P(("dp", "fsdp")),
            P(("dp", "fsdp"), None),
            P(("dp", "fsdp")),
            P(("dp", "fsdp"), None),
            P(("dp", "fsdp"), None),
            P(("dp", "fsdp")),
            P(("dp", "fsdp"), None),
            P(("dp", "fsdp")),
            P(("dp", "fsdp")),
            P(("dp", "fsdp")),
            P(("dp", "fsdp"), None),
            P(("dp", "fsdp")),
            P(("dp", "fsdp"), None),
            P(("dp", "fsdp")),
        ),
        check_vma=False,
    )
```

profile of v0, /device:TPU:0, one launch (start us, length us, event | category | flops | bytes accessed | tf_op | source)
XLA Modules:
  0.0 4616.0 jit_solution(2343111599140271161)
XLA Ops:
  14.8 43.5 all-gather.3
  59.0 36.9 all-gather.2
  96.1 38.9 all-gather.1
  135.6 13.6 all-gather
  193.9 25.6 collective-permute-start.2
  219.6 44.3 collective-permute-start.1
  264.5 154.5 %collective-permute-start = (bf16[512,2048]{1,0:T(8,128)(2,1)}, bf16[512,2048]{1,0:T(8,128)(2,1)}, u32[]{:S(2)}, u32[]{:S(2)}) collective-permute-start(bf16[512,2048]{1,0:T(8,128)(2,1)} %add_convert_fusion.5), channel_id=1, source_target_pairs={{0,4},{1,5},{2,6},{3,7},{8,12},{9,13},{10,14},{11,15},{16,20},{17,... | collective-permute-start | bytes 6291464 | tf_op jit(solution)/shard_map/ppermute | solution.py:20
  442.4 62.1 %concatenate.11 = bf16[2710,2048]{1,0:T(8,128)(2,1)} concatenate(bf16[150,2048]{1,0:T(8,128)(2,1)S(1)} %convolution_convert_fusion.2, bf16[512,2048]{1,0:T(8,128)(2,1)} %collective-permute-done.4, bf16[512,2048]{1,0:T(8,128)(2,1)} %collective-permute-done.5, bf16[512,2048]{1,0:T(8,128)(2,1)} %collective-permute-done.6, bf16[512,2048]{1,0:T(8,128)(2,1)} %collective-permute-done.7, ...), dimensions={0} | concatenate | bytes 22200320 | tf_op jit(solution)/shard_map/concatenate | solution.py:140
  504.5 16.0 copy.75
  520.5 62.2 %concatenate.9 = bf16[2710,2048]{1,0:T(8,128)(2,1)} concatenate(bf16[150,2048]{1,0:T(8,128)(2,1)S(1)} %fusion.38, bf16[512,2048]{1,0:T(8,128)(2,1)} %collective-permute-done, bf16[512,2048]{1,0:T(8,128)(2,1)} %collective-permute-done.1, bf16[512,2048]{1,0:T(8,128)(2,1)} %collective-permute-done.2, bf16[512,2048]{1,0:T(8,128)(2,1)} %collective-permute-done.3, ...), dimensions={0} | concatenate | bytes 22200320 | tf_op jit(solution)/shard_map/concatenate | solution.py:141
  582.7 15.3 copy.73
  599.5 297.8 %while.36 = (s32[]{:T(128)}, bf16[512,2048]{0,1:T(8,128)(2,1)}, f32[32,512]{1,0:T(8,128)S(1)}, bf16[2710,2048]{0,1:T(8,128)(2,1)}, pred[512,2710]{0,1:T(8,128)(4...) while((s32[]{:T(128)}, bf16[512,2048]{0,1:T(8,128)(2,1)}, ...), condition=%wide.region_10.11_spmd, body=%wide.region_7.10_spmd.sunk | while | flops 1487419392 | bytes 169528592 | solution.py:181
  610.4 12.0 copy-done
  628.3 11.4 fusion.178
  664.0 11.1 fusion.178
  700.4 11.7 fusion.178
  736.8 11.2 fusion.178
  772.6 11.2 fusion.178
  808.1 15.8 fusion.178
  848.5 11.1 fusion.178
  884.8 11.7 fusion.178
  910.3 28.5 fusion.88
  938.9 34.3 convert_reduce_fusion
  973.2 27.2 multiply_reduce_fusion.1
  1039.7 563.0 %while.37 = (s32[]{:T(128)}, bf16[512,2048]{0,1:T(8,128)(2,1)}, f32[150,2048]{0,1:T(8,128)}, f32[150,2048]{0,1:T(8,128)}, f32[2560,2048]{0,1:T(8,128)}, /*index=...) while((s32[]{:T(128)}, bf16[512,2048]{0,1:T(8,128)(2,1)}, ...), condition=%wide.region_17.18_spmd, body=%wide.region_15.17_spmd.sunk | while | flops 3636256256 | bytes 222910816 | solution.py:307
  1055.2 10.6 fusion.190
  1068.8 15.6 multiply_reduce_fusion.5
  1084.4 15.4 multiply_convert_fusion.5
  1125.6 10.6 fusion.190
  1139.2 15.5 multiply_reduce_fusion.5
  1154.7 15.4 multiply_convert_fusion.5
  1209.4 15.6 multiply_reduce_fusion.5
  1225.0 15.4 multiply_convert_fusion.5
  1266.0 10.6 fusion.190
  1279.7 15.5 multiply_reduce_fusion.5
  1295.2 15.4 multiply_convert_fusion.5
  1336.4 10.6 fusion.190
  1350.0 15.5 multiply_reduce_fusion.5
  1365.5 15.4 multiply_convert_fusion.5
  1406.6 10.6 fusion.190
  1420.2 15.6 multiply_reduce_fusion.5
  1435.8 15.4 multiply_convert_fusion.5
  1476.9 10.6 fusion.190
  1490.5 15.5 multiply_reduce_fusion.5
  1506.1 15.4 multiply_convert_fusion.5
  1560.9 15.6 multiply_reduce_fusion.5
  1576.4 15.4 multiply_convert_fusion.5
  1602.8 12.3 fusion.106
  1621.8 206.3 %reduce-scatter.15.cloned.1.call-done = f32[150,256]{0,1:T(8,128)} async-done(((f32[150,2048]{0,1:T(8,128)}), f32[150,256]{0,1:T(8,128)}) %reduce-scatter.15.cloned.1.call-update) | async-done | bytes 153616 | tf_op jit(solution)/shard_map/reduce_scatter | solution.py:335
  1829.9 51.7 %reduce-scatter.17.cloned.1.call-done = f32[150,256]{0,1:T(8,128)} async-done(((f32[150,2048]{0,1:T(8,128)}), f32[150,256]{0,1:T(8,128)}) %reduce-scatter.17.cloned.1.call-update) | async-done | bytes 153616 | tf_op jit(solution)/shard_map/reduce_scatter | solution.py:336
  1884.5 12.4 fusion.105
  1912.6 163.6 %all-reduce.3.cloned.1.call-done = f32[150,2048]{1,0:T(8,128)} async-done(((f32[150,2048]{1,0:T(8,128)}), f32[150,2048]{1,0:T(8,128)}) %all-reduce.3.cloned.1.call-update) | async-done | bytes 1228816 | tf_op jit(solution)/shard_map/psum | solution.py:380
  2108.0 11.7 fusion.101
  2125.8 12.5 fusion.114
  2179.1 32.5 fusion.39
  2212.3 32.0 fusion.87
  2245.0 225.5 %all-reduce = f32[8192]{0:T(1024)S(1)} all-reduce(f32[8192]{0:T(1024)S(1)} %copy-done.43), channel_id=12, replica_groups=mesh['dp'=4,'fsdp'=8] {'dp','fsdp'}, use_global_device_ids=true, to_apply=%region_44.45.clone | all-reduce | flops 8192 | bytes 65536
  2471.2 28.1 fusion.36
  2515.3 111.5 %reduce-scatter.25.cloned.1.call-done = f32[64,2048]{1,0:T(8,128)} async-done(((f32[2048,2048]{1,0:T(8,128)}), f32[64,2048]{1,0:T(8,128)}) %reduce-scatter.25.cloned.1.call-update) | async-done | bytes 524304 | tf_op jit(solution)/shard_map/reduce_scatter | solution.py:394
  2626.8 187.4 %reduce-scatter.19.cloned.1.call-done = f32[64,2048]{1,0:T(8,128)} async-done(((f32[2048,2048]{1,0:T(8,128)}), f32[64,2048]{1,0:T(8,128)}) %reduce-scatter.19.cloned.1.call-update) | async-done | bytes 524304 | tf_op jit(solution)/shard_map/reduce_scatter | solution.py:391
  2814.2 187.4 %reduce-scatter.23.cloned.1.call-done = f32[64,2048]{1,0:T(8,128)} async-done(((f32[2048,2048]{1,0:T(8,128)}), f32[64,2048]{1,0:T(8,128)}) %reduce-scatter.23.cloned.1.call-update) | async-done | bytes 524304 | tf_op jit(solution)/shard_map/reduce_scatter | solution.py:393
  3001.6 187.3 %reduce-scatter.21.cloned.1.call-done = f32[64,2048]{1,0:T(8,128)} async-done(((f32[2048,2048]{1,0:T(8,128)}), f32[64,2048]{1,0:T(8,128)}) %reduce-scatter.21.cloned.1.call-update) | async-done | bytes 524304 | tf_op jit(solution)/shard_map/reduce_scatter | solution.py:392
  3188.9 707.2 %reduce-scatter.29.cloned.1.call-done = f32[256,2048]{1,0:T(8,128)} async-done(((f32[8192,2048]{1,0:T(8,128)}), f32[256,2048]{1,0:T(8,128)}) %reduce-scatter.29.cloned.1.call-update) | async-done | bytes 2097168 | tf_op jit(solution)/shard_map/reduce_scatter | solution.py:227
  3896.2 713.2 %reduce-scatter.27.cloned.1.call-done = f32[64,8192]{1,0:T(8,128)} async-done(((f32[2048,8192]{1,0:T(8,128)}), f32[64,8192]{1,0:T(8,128)}) %reduce-scatter.27.cloned.1.call-update) | async-done | bytes 2097168 | tf_op jit(solution)/shard_map/reduce_scatter | solution.py:226
  (532 shorter events, 693.8 us)
Async XLA Ops:
  7.2 51.7 %copy-start.67 = (bf16[64]{0:T(256)(128)(2,1)S(1)}, bf16[64]{0:T(256)(128)(2,1)}, u32[]{:S(2)}) copy-start(bf16[64]{0:T(256)(128)(2,1)} %param.43) | copy-start | bytes 388
  7.2 51.7 %copy-start.68 = (bf16[64]{0:T(256)(128)(2,1)S(1)}, bf16[64]{0:T(256)(128)(2,1)}, u32[]{:S(2)}) copy-start(bf16[64]{0:T(256)(128)(2,1)} %param.39) | copy-start | bytes 388
  7.2 51.7 %copy-start.69 = (bf16[64]{0:T(256)(128)(2,1)S(1)}, bf16[64]{0:T(256)(128)(2,1)}, u32[]{:S(2)}) copy-start(bf16[64]{0:T(256)(128)(2,1)} %param.38) | copy-start | bytes 388
  7.2 88.7 %copy-start.74 = (bf16[64]{0:T(256)(128)(2,1)S(1)}, bf16[64]{0:T(256)(128)(2,1)}, u32[]{:S(2)}) copy-start(bf16[64]{0:T(256)(128)(2,1)} %param.37) | copy-start | bytes 388
  7.2 88.7 %copy-start.73 = (bf16[64]{0:T(256)(128)(2,1)S(1)}, bf16[64]{0:T(256)(128)(2,1)}, u32[]{:S(2)}) copy-start(bf16[64]{0:T(256)(128)(2,1)} %param.35) | copy-start | bytes 388
  7.3 88.7 %copy-start.72 = (bf16[64]{0:T(256)(128)(2,1)S(1)}, bf16[64]{0:T(256)(128)(2,1)}, u32[]{:S(2)}) copy-start(bf16[64]{0:T(256)(128)(2,1)} %param.32) | copy-start | bytes 388
  7.3 88.7 %copy-start.71 = (bf16[64]{0:T(256)(128)(2,1)S(1)}, bf16[64]{0:T(256)(128)(2,1)}, u32[]{:S(2)}) copy-start(bf16[64]{0:T(256)(128)(2,1)} %param.30) | copy-start | bytes 388
  7.3 88.7 %copy-start.70 = (bf16[64]{0:T(256)(128)(2,1)S(1)}, bf16[64]{0:T(256)(128)(2,1)}, u32[]{:S(2)}) copy-start(bf16[64]{0:T(256)(128)(2,1)} %param.29) | copy-start | bytes 388
  7.3 128.4 %copy-start.33 = (bf16[1,150,256]{2,1,0:T(8,128)(2,1)S(1)}, bf16[1,150,256]{2,1,0:T(8,128)(2,1)}, u32[]{:S(2)}) copy-start(bf16[1,150,256]{2,1,0:T(8,128)(2,1)} %param.25) | copy-start | bytes 230404
  7.3 147.6 %all-gather.15.cloned.1.call-start = ((), (), s32[]{:S(2)}) async-start(), calls=%async_computation.12 | async-start | bytes 8650752 | tf_op jit(solution)/shard_map/all_gather | solution.py:110
  8.0 172.4 %all-gather.11.cloned.1.call-start = ((), (), s32[]{:S(2)}) async-start(), calls=%async_computation.10 | async-start | bytes 8650752 | tf_op jit(solution)/shard_map/all_gather | solution.py:111
  8.8 410.3 %all-gather.13.cloned.1.call-start = ((), (), s32[]{:S(2)}) async-start(), calls=%async_computation.11 | async-start | bytes 8650752 | tf_op jit(solution)/shard_map/all_gather | solution.py:109
  9.5 887.8 %all-gather.17.cloned.1.call-start = ((), (), s32[]{:S(2)}) async-start(), calls=%async_computation.13 | async-start | bytes 8650752 | tf_op jit(solution)/shard_map/all_gather | solution.py:112
  10.1 900.2 %all-gather.19.cloned.1.call-start = ((), (), s32[]{:S(2)}) async-start(), calls=%async_computation.14 | async-start | bytes 34603008 | tf_op jit(solution)/shard_map/all_gather | solution.py:190
  10.7 928.2 %all-gather.21.cloned.1.call-start = ((), (), s32[]{:S(2)}) async-start(), calls=%async_computation.15 | async-start | bytes 34603008 | tf_op jit(solution)/shard_map/all_gather | solution.py:191
  11.3 1816.9 %reduce-scatter.15.cloned.1.call-start = ((), (), s32[]{:S(2)}) async-start(), calls=%async_computation.16 | async-start | bytes 2359296 | tf_op jit(solution)/shard_map/reduce_scatter | solution.py:335
  13.9 405.2 %copy-start.44 = (f32[512]{0:T(512)}, f32[512]{0:T(512)S(1)}, u32[]{:S(2)}) copy-start(f32[512]{0:T(512)S(1)} %broadcast_multiply_fusion.1) | copy-start | bytes 6148
  14.6 134.9 %copy-start.57 = (f32[512]{0:T(512)}, f32[512]{0:T(512)S(1)}, u32[]{:S(2)}) copy-start(f32[512]{0:T(512)S(1)} %fusion.33) | copy-start | bytes 6148
  14.6 404.5 %copy-start.52 = (f32[512]{0:T(512)}, f32[512]{0:T(512)S(1)}, u32[]{:S(2)}) copy-start(f32[512]{0:T(512)S(1)} %fusion.74) | copy-start | bytes 6148
  135.6 301.6 %copy-start.30 = (f32[2048,1]{0,1:T(1,128)}, f32[2048,1]{0,1:T(1,128)S(1)}, u32[]{:S(2)}) copy-start(f32[2048,1]{0,1:T(1,128)S(1)} %get-tuple-element.527) | copy-start | bytes 24580
  135.6 301.6 %copy-start.34 = (f32[2048,1]{0,1:T(1,128)}, f32[2048,1]{0,1:T(1,128)S(1)}, u32[]{:S(2)}) copy-start(f32[2048,1]{0,1:T(1,128)S(1)} %get-tuple-element.526) | copy-start | bytes 24580
  149.2 288.0 %copy-start.9 = (bf16[1,150,2048]{2,1,0:T(8,128)(2,1)}, bf16[1,150,2048]{2,1,0:T(8,128)(2,1)S(1)}, u32[]{:S(2)}) copy-start(bf16[1,150,2048]{2,1,0:T(8,128)(2,1)S(1)} %all-gather) | copy-start | bytes 1843204
  149.4 287.8 %copy-start.36 = (f32[150]{0:T(256)}, f32[150]{0:T(256)S(1)}, u32[]{:S(2)}) copy-start(f32[150]{0:T(256)S(1)} %broadcast_multiply_fusion.2) | copy-start | bytes 1804
  150.3 286.9 %copy-start.47 = (f32[150]{0:T(256)}, f32[150]{0:T(256)S(1)}, u32[]{:S(2)}) copy-start(f32[150]{0:T(256)S(1)} %fusion.76) | copy-start | bytes 1804
  164.3 29.6 collective-permute-start.7
  167.9 51.7 %collective-permute-start.6 = (bf16[512,2048]{1,0:T(8,128)(2,1)}, bf16[512,2048]{1,0:T(8,128)(2,1)}, u32[]{:S(2)}, u32[]{:S(2)}) collective-permute-start(bf16[512,2048]{1,0:T(8,128)(2,1)} %convolution_convert_fusion.1), channel_id=1, source_target_pairs={{0,2},{1,3},{2,4},{3,5},{4,6},{5,7},{8,10},{9,11},{10,12},{11,13},... | collective-permute-start | bytes 6291464 | tf_op jit(solution)/shard_map/ppermute | solution.py:20
  172.6 91.9 %collective-permute-start.5 = (bf16[512,2048]{1,0:T(8,128)(2,1)}, bf16[512,2048]{1,0:T(8,128)(2,1)}, u32[]{:S(2)}, u32[]{:S(2)}) collective-permute-start(bf16[512,2048]{1,0:T(8,128)(2,1)} %convolution_convert_fusion.1), channel_id=1, source_target_pairs={{0,3},{1,4},{2,5},{3,6},{4,7},{8,11},{9,12},{10,13},{11,14},{12,15... | collective-permute-start | bytes 6291464 | tf_op jit(solution)/shard_map/ppermute | solution.py:20
  177.8 264.6 %collective-permute-start.4 = (bf16[512,2048]{1,0:T(8,128)(2,1)}, bf16[512,2048]{1,0:T(8,128)(2,1)}, u32[]{:S(2)}, u32[]{:S(2)}) collective-permute-start(bf16[512,2048]{1,0:T(8,128)(2,1)} %convolution_convert_fusion.1), channel_id=1, source_target_pairs={{0,4},{1,5},{2,6},{3,7},{8,12},{9,13},{10,14},{11,15},{16,20},{17,... | collective-permute-start | bytes 6291464 | tf_op jit(solution)/shard_map/ppermute | solution.py:20
  190.0 330.5 %collective-permute-start.3 = (bf16[512,2048]{1,0:T(8,128)(2,1)}, bf16[512,2048]{1,0:T(8,128)(2,1)}, u32[]{:S(2)}, u32[]{:S(2)}) collective-permute-start(bf16[512,2048]{1,0:T(8,128)(2,1)} %add_convert_fusion.5), channel_id=1, source_target_pairs={{0,1},{1,2},{2,3},{3,4},{4,5},{5,6},{6,7},{8,9},{9,10},{10,11},{11... | collective-permute-start | bytes 6291464 | tf_op jit(solution)/shard_map/ppermute | solution.py:20
  193.9 326.6 %collective-permute-start.2 = (bf16[512,2048]{1,0:T(8,128)(2,1)}, bf16[512,2048]{1,0:T(8,128)(2,1)}, u32[]{:S(2)}, u32[]{:S(2)}) collective-permute-start(bf16[512,2048]{1,0:T(8,128)(2,1)} %add_convert_fusion.5), channel_id=1, source_target_pairs={{0,2},{1,3},{2,4},{3,5},{4,6},{5,7},{8,10},{9,11},{10,12},{11,13},... | collective-permute-start | bytes 6291464 | tf_op jit(solution)/shard_map/ppermute | solution.py:20
  219.6 300.9 %collective-permute-start.1 = (bf16[512,2048]{1,0:T(8,128)(2,1)}, bf16[512,2048]{1,0:T(8,128)(2,1)}, u32[]{:S(2)}, u32[]{:S(2)}) collective-permute-start(bf16[512,2048]{1,0:T(8,128)(2,1)} %add_convert_fusion.5), channel_id=1, source_target_pairs={{0,3},{1,4},{2,5},{3,6},{4,7},{8,11},{9,12},{10,13},{11,14},{12,15... | collective-permute-start | bytes 6291464 | tf_op jit(solution)/shard_map/ppermute | solution.py:20
  264.5 256.0 %collective-permute-start = (bf16[512,2048]{1,0:T(8,128)(2,1)}, bf16[512,2048]{1,0:T(8,128)(2,1)}, u32[]{:S(2)}, u32[]{:S(2)}) collective-permute-start(bf16[512,2048]{1,0:T(8,128)(2,1)} %add_convert_fusion.5), channel_id=1, source_target_pairs={{0,4},{1,5},{2,6},{3,7},{8,12},{9,13},{10,14},{11,15},{16,20},{17,... | collective-permute-start | bytes 6291464 | tf_op jit(solution)/shard_map/ppermute | solution.py:20
  599.5 297.8 %copy-start.64 = (f32[2048,1]{0,1:T(1,128)S(1)}, f32[2048,1]{0,1:T(1,128)}, u32[]{:S(2)}) copy-start(f32[2048,1]{0,1:T(1,128)} %get-tuple-element.524) | copy-start | bytes 24580
  907.7 92.8 %copy-start.24 = (f32[512]{0:T(512)}, f32[512]{0:T(512)S(1)}, u32[]{:S(2)}) copy-start(f32[512]{0:T(512)S(1)} %broadcast_multiply_fusion) | copy-start | bytes 6148
  910.2 90.2 %copy-start.26 = (f32[512]{0:T(512)}, f32[512]{0:T(512)S(1)}, u32[]{:S(2)}) copy-start(f32[512]{0:T(512)S(1)} %fusion.75) | copy-start | bytes 6148
  1602.7 278.9 %reduce-scatter.17.cloned.1.call-start = ((), (), s32[]{:S(2)}) async-start(), calls=%async_computation.17 | async-start | bytes 2359296 | tf_op jit(solution)/shard_map/reduce_scatter | solution.py:336
  1615.1 283.6 %collective-permute-start.8 = (f32[512,2048]{0,1:T(8,128)}, f32[512,2048]{0,1:T(8,128)}, u32[]{:S(2)}, u32[]{:S(2)}) collective-permute-start(f32[512,2048]{0,1:T(8,128)} %get-tuple-element.518), channel_id=1, source_target_pairs={{1,0},{2,1},{3,2},{4,3},{5,4},{6,5},{7,6},{9,8},{10,9},{11,10},{12... | collective-permute-start | bytes 12582920 | tf_op jit(solution)/shard_map/ppermute | solution.py:20
  1616.4 283.6 %collective-permute-start.11 = (f32[512,2048]{0,1:T(8,128)}, f32[512,2048]{0,1:T(8,128)}, u32[]{:S(2)}, u32[]{:S(2)}) collective-permute-start(f32[512,2048]{0,1:T(8,128)} %get-tuple-element.519), channel_id=1, source_target_pairs={{4,0},{5,1},{6,2},{7,3},{12,8},{13,9},{14,10},{15,11},{20,16},{21,... | collective-permute-start | bytes 12582920 | tf_op jit(solution)/shard_map/ppermute | solution.py:20
  1617.7 283.6 %collective-permute-start.10 = (f32[512,2048]{0,1:T(8,128)}, f32[512,2048]{0,1:T(8,128)}, u32[]{:S(2)}, u32[]{:S(2)}) collective-permute-start(f32[512,2048]{0,1:T(8,128)} %get-tuple-element.520), channel_id=1, source_target_pairs={{3,0},{4,1},{5,2},{6,3},{7,4},{11,8},{12,9},{13,10},{14,11},{15,12... | collective-permute-start | bytes 12582920 | tf_op jit(solution)/shard_map/ppermute | solution.py:20
  1619.1 457.2 %all-reduce.3.cloned.1.call-start = ((), (), s32[]{:S(2)}) async-start(), calls=%async_computation.18 | async-start | bytes 2490368 | tf_op jit(solution)/shard_map/psum | solution.py:380
  1619.1 459.5 %collective-permute-start.9 = (f32[512,2048]{0,1:T(8,128)}, f32[512,2048]{0,1:T(8,128)}, u32[]{:S(2)}, u32[]{:S(2)}) collective-permute-start(f32[512,2048]{0,1:T(8,128)} %get-tuple-element.521), channel_id=1, source_target_pairs={{2,0},{3,1},{4,2},{5,3},{6,4},{7,5},{10,8},{11,9},{12,10},{13,11},... | collective-permute-start | bytes 12582920 | tf_op jit(solution)/shard_map/ppermute | solution.py:20
  1884.5 614.8 %reduce-scatter.33.cloned.1.call-start = ((), (), s32[]{:S(2)}) async-start(), calls=%async_computation.26 | async-start | bytes 1081344
  1897.0 201.5 %collective-permute-start.12 = (f32[512,2048]{0,1:T(8,128)}, f32[512,2048]{0,1:T(8,128)}, u32[]{:S(2)}, u32[]{:S(2)}) collective-permute-start(f32[512,2048]{0,1:T(8,128)} %get-tuple-element.514), channel_id=1, source_target_pairs={{1,0},{2,1},{3,2},{4,3},{5,4},{6,5},{7,6},{9,8},{10,9},{11,10},{12... | collective-permute-start | bytes 12582920 | tf_op jit(solution)/shard_map/ppermute | solution.py:20
  1898.3 613.0 %reduce-scatter.31.cloned.1.call-start = ((), (), s32[]{:S(2)}) async-start(), calls=%async_computation.25 | async-start | bytes 1081344
  1898.7 199.8 %collective-permute-start.15 = (f32[512,2048]{0,1:T(8,128)}, f32[512,2048]{0,1:T(8,128)}, u32[]{:S(2)}, u32[]{:S(2)}) collective-permute-start(f32[512,2048]{0,1:T(8,128)} %get-tuple-element.515), channel_id=1, source_target_pairs={{4,0},{5,1},{6,2},{7,3},{12,8},{13,9},{14,10},{15,11},{20,16},{21,... | collective-permute-start | bytes 12582920 | tf_op jit(solution)/shard_map/ppermute | solution.py:20
  1900.0 198.5 %collective-permute-start.14 = (f32[512,2048]{0,1:T(8,128)}, f32[512,2048]{0,1:T(8,128)}, u32[]{:S(2)}, u32[]{:S(2)}) collective-permute-start(f32[512,2048]{0,1:T(8,128)} %get-tuple-element.516), channel_id=1, source_target_pairs={{3,0},{4,1},{5,2},{6,3},{7,4},{11,8},{12,9},{13,10},{14,11},{15,12... | collective-permute-start | bytes 12582920 | tf_op jit(solution)/shard_map/ppermute | solution.py:20
  1901.3 174.9 %copy-start.10 = (bf16[1,150,2048]{2,1,0:T(8,128)(2,1)S(1)}, bf16[1,150,2048]{2,1,0:T(8,128)(2,1)}, u32[]{:S(2)}) copy-start(bf16[1,150,2048]{2,1,0:T(8,128)(2,1)} %copy-done.9) | copy-start | bytes 1843204
  1901.3 174.9 %copy-start.31 = (f32[2048,1]{0,1:T(1,128)S(1)}, f32[2048,1]{0,1:T(1,128)}, u32[]{:S(2)}) copy-start(f32[2048,1]{0,1:T(1,128)} %copy-done.30) | copy-start | bytes 24580
  1901.4 174.9 %copy-start.37 = (f32[150]{0:T(256)S(1)}, f32[150]{0:T(256)}, u32[]{:S(2)}) copy-start(f32[150]{0:T(256)} %copy-done.36) | copy-start | bytes 1804
  1901.4 174.9 %copy-start.48 = (f32[150]{0:T(256)S(1)}, f32[150]{0:T(256)}, u32[]{:S(2)}) copy-start(f32[150]{0:T(256)} %copy-done.47) | copy-start | bytes 1804
  1901.4 197.2 %collective-permute-start.13 = (f32[512,2048]{0,1:T(8,128)}, f32[512,2048]{0,1:T(8,128)}, u32[]{:S(2)}, u32[]{:S(2)}) collective-permute-start(f32[512,2048]{0,1:T(8,128)} %get-tuple-element.517), channel_id=1, source_target_pairs={{2,0},{3,1},{4,2},{5,3},{6,4},{7,5},{10,8},{11,9},{12,10},{13,11},... | collective-permute-start | bytes 12582920 | tf_op jit(solution)/shard_map/ppermute | solution.py:20
  2125.8 501.0 %reduce-scatter.25.cloned.1.call-start = ((), (), s32[]{:S(2)}) async-start(), calls=%async_computation.22 | async-start | bytes 17301504 | tf_op jit(solution)/shard_map/reduce_scatter | solution.py:394
  2138.3 675.9 %reduce-scatter.19.cloned.1.call-start = ((), (), s32[]{:S(2)}) async-start(), calls=%async_computation.19 | async-start | bytes 17301504 | tf_op jit(solution)/shard_map/reduce_scatter | solution.py:391
  2149.4 852.1 %reduce-scatter.23.cloned.1.call-start = ((), (), s32[]{:S(2)}) async-start(), calls=%async_computation.21 | async-start | bytes 17301504 | tf_op jit(solution)/shard_map/reduce_scatter | solution.py:393
  2163.4 1025.5 %reduce-scatter.21.cloned.1.call-start = ((), (), s32[]{:S(2)}) async-start(), calls=%async_computation.20 | async-start | bytes 17301504 | tf_op jit(solution)/shard_map/reduce_scatter | solution.py:392
  2177.5 1718.6 %reduce-scatter.29.cloned.1.call-start = ((), (), s32[]{:S(2)}) async-start(), calls=%async_computation.24 | async-start | bytes 69206016 | tf_op jit(solution)/shard_map/reduce_scatter | solution.py:227
  2211.6 2397.7 %reduce-scatter.27.cloned.1.call-start = ((), (), s32[]{:S(2)}) async-start(), calls=%async_computation.23 | async-start | bytes 69206016 | tf_op jit(solution)/shard_map/reduce_scatter | solution.py:226
  2244.2 226.9 %copy-start.65 = (f32[2048,1]{0,1:T(1,128)S(1)}, f32[2048,1]{0,1:T(1,128)}, u32[]{:S(2)}) copy-start(f32[2048,1]{0,1:T(1,128)} %get-tuple-element.537) | copy-start | bytes 24580
  2471.1 31.0 copy-start.32
  2471.1 33.6 copy-start.61
  2471.2 33.6 copy-start.46
  2471.2 33.6 copy-start.51
  2471.2 33.6 copy-start.54
  2471.2 33.6 copy-start.56
  (65 other events, 561.6 us)
Sparse Core Ops, SparseCore 0:
  11.0 80.3 all-gather.14
  94.3 77.9 all-gather.10
  175.1 242.7 all-gather.12
  420.7 89.1 all-gather.16
  512.6 200.1 all-gather.18
  715.5 192.9 all-gather.20
  1602.9 225.2 reduce-scatter.14
  1831.7 49.8 reduce-scatter.16
  1885.4 190.7 all-reduce.2
  2078.4 135.9 reduce-scatter.32
  2216.6 227.9 reduce-scatter.30
  2447.4 179.3 reduce-scatter.24
  2629.8 184.3 reduce-scatter.18
  2817.0 184.4 reduce-scatter.22
  3004.4 184.4 reduce-scatter.20
  3191.8 704.2 reduce-scatter.28
  3899.1 710.2 reduce-scatter.26
where the time goes:
time: 4640 us; the launch traced here: 4620 us
  waiting for transfers between devices  2520 us (54%)
  matrix products  795 us (17%)
  local copies, waits for them, and re-layouts  452 us (10%)
  blocking collectives  358 us (8%)
  starting transfers between devices  254 us (5%)
  other arithmetic  219 us (5%)
    reduce_scatter x1, waiting for transfers between devices, per_device(): lax.psum_scatter(up_grad, ('dp', 'fsdp'), scatter_dimension=0, tiled=True)  713 us
    reduce_scatter x1, waiting for transfers between devices, per_device(): lax.psum_scatter(down_grad, ('dp', 'fsdp'), scatter_dimension=0, tiled=True)  707 us
    ppermute x16, starting transfers between devices, passed_along(): return lax.ppermute(x, axis, pairs)  252 us
    unnamed x1, blocking collectives  225 us
    reduce_scatter x1, waiting for transfers between devices, per_device(): lax.psum_scatter(grad_summ_keys, 'fsdp', scatter_dimension=1, tiled=True)  206 us
    reduce_scatter x1, waiting for transfers between devices, per_device(): lax.psum_scatter(query_grad_full, ('dp', 'fsdp'), scatter_dimension=0, ti...  187 us
    reduce_scatter x1, waiting for transfers between devices, per_device(): lax.psum_scatter(value_grad_full, ('dp', 'fsdp'), scatter_dimension=0, ti...  187 us
    reduce_scatter x1, waiting for transfers between devices, per_device(): lax.psum_scatter(key_grad_full, ('dp', 'fsdp'), scatter_dimension=0, tile...  187 us
  transfers between devices with their start and end apart: 33, of which 11 were waited for; matrix products, arithmetic and copies ran while one was open for 16% of the time, Pallas kernels for 0%

commit v1 on v0

v1 whole, which is shorter than its diff:
```python
import functools
import math

import jax
import jax.numpy as jnp
from jax import lax
from jax.experimental import pallas as pl
from jax.experimental.pallas import tpu as pltpu
from jax.sharding import PartitionSpec as P

HEAD = 64
SUMM = 50

epsilon = 1e-05
masked_score = -1e30
bf16 = jnp.bfloat16
f32 = jnp.float32
BOTH = ("dp", "fsdp")
score_scale = 1.0 / math.sqrt(HEAD)

ROWS_BY_ROWS = (((1,), (0,)), ((), ()))
ROWS_BY_COLS = (((1,), (1,)), ((), ()))
COLS_BY_ROWS = (((0,), (0,)), ((), ()))


def dot(left, right, dims):
    return lax.dot_general(left, right, dims, preferred_element_type=f32)


def layer_norm(values, gains, shifts):
    centre = jnp.mean(values, axis=-1, keepdims=True)
    centred = values - centre
    spread = jnp.mean(centred * centred, axis=-1, keepdims=True)
    return centred * lax.rsqrt(spread + epsilon) * gains + shifts


def gelu_tanh(values):
    return jax.nn.gelu(values, approximate=True)


def swapped(x, bit):
    devices = lax.axis_size("fsdp")
    return lax.ppermute(x, "fsdp", [(i, i ^ bit) for i in range(devices)])


def gathered(own):
    devices = lax.axis_size("fsdp")
    if devices != 8:
        pieces = [own]
        bit = 1
        while bit < devices:
            pieces = pieces + [swapped(piece, bit) for piece in pieces]
            bit *= 2
        return pieces
    half = own.shape[0] // 2
    along_x = swapped(own, 2)
    along_y = swapped(own, 4)
    mate = swapped(own, 1)
    across = jnp.concatenate([swapped(along_x[:half], 4), swapped(along_y[half:], 2)], axis=0)
    return [
        own,
        mate,
        along_x,
        swapped(along_x, 1),
        along_y,
        swapped(along_y, 1),
        across,
        swapped(across, 1),
    ]


def summed_low(left, right):
    return (left.astype(f32) + right.astype(f32)).astype(bf16)


def scattered_sum(pieces):
    devices = len(pieces)
    if devices != 8:
        bit = devices // 2
        while bit > 1:
            pieces = [summed_low(pieces[m], swapped(pieces[m + bit], bit)) for m in range(bit)]
            bit //= 2
        return pieces[0].astype(f32) + swapped(pieces[1], 1).astype(f32)
    half = pieces[0].shape[0] // 2
    across = summed_low(pieces[6], swapped(pieces[7], 1))
    along_x = summed_low(pieces[2], swapped(pieces[3], 1))
    along_y = summed_low(pieces[4], swapped(pieces[5], 1))
    upper_part = swapped(across[:half], 4)
    lower_part = swapped(across[half:], 2)
    along_x = jnp.concatenate([summed_low(along_x[:half], upper_part), along_x[half:]], axis=0)
    along_y = jnp.concatenate([along_y[:half], summed_low(along_y[half:], lower_part)], axis=0)
    return (
        (pieces[0].astype(f32) + swapped(pieces[1], 1).astype(f32))
        + swapped(along_x, 2).astype(f32)
        + swapped(along_y, 4).astype(f32)
    )


def only_head(values, head):
    columns = lax.broadcasted_iota(jnp.int32, values.shape, 1) // HEAD
    return jnp.where(columns == head, values, jnp.zeros_like(values))


def attn_forward_kernel(
    block, heads, plan_ref, q_ref, k_ref, vt_ref, sk_ref, svt_ref, row_ref, o_ref, log_ref,
    q_heads, tops, sums, mixed,
):
    i = pl.program_id(0)
    blocks = pl.num_programs(0)
    q = q_ref[...].astype(f32) * score_scale
    for h in range(heads):
        q_heads[h] = only_head(q, h).astype(bf16)
    tops[...] = jnp.full_like(tops, masked_score)
    sums[...] = jnp.zeros_like(sums)
    mixed[...] = jnp.zeros_like(mixed)
    lowest = row_ref[0:1, :]
    highest = row_ref[1:2, :]
    summ_end = row_ref[2:3, :]
    me = row_ref[3:4, :]

    def step(keys, values_t, mask):
        each = range(heads)
        scores = [dot(keys, q_heads[h], ROWS_BY_COLS) for h in each]
        if mask is not None:
            scores = [jnp.where(mask, one, masked_score) for one in scores]
        before = [tops[h : h + 1, :] for h in each]
        top = [jnp.maximum(before[h], jnp.max(scores[h], axis=0, keepdims=True)) for h in each]
        weights = [jnp.exp(scores[h] - top[h]) for h in each]
        keep = [jnp.exp(before[h] - top[h]) for h in each]
        added = [jnp.sum(weights[h], axis=0, keepdims=True) for h in each]
        totals = [keep[h] * sums[h : h + 1, :] + added[h] for h in each]
        part_of = [slice(h * HEAD, (h + 1) * HEAD) for h in each]
        more = [dot(values_t[part_of[h], :], weights[h].astype(bf16), ROWS_BY_ROWS) for h in each]
        result = [keep[h] * mixed[part_of[h], :] + more[h] for h in each]
        for h in each:
            tops[h : h + 1, :] = top[h]
            sums[h : h + 1, :] = totals[h]
            mixed[part_of[h], :] = result[h]

    @pl.when(plan_ref[2 * blocks + i] > 0)
    def _():
        places = lax.broadcasted_iota(jnp.int32, (sk_ref.shape[0], block), 0)
        step(sk_ref[...], svt_ref[...], places < summ_end)

    def whole(j, carry):
        start = pl.multiple_of(j * block, block)
        step(k_ref[pl.ds(start, block), :], vt_ref[:, pl.ds(start, block)], None)
        return carry

    def part(j, carry):
        start = pl.multiple_of(j * block, block)
        places = start + lax.broadcasted_iota(jnp.int32, (block, block), 0)
        mask = ((places >= lowest) & (places <= highest)) | (places == me)
        step(k_ref[pl.ds(start, block), :], vt_ref[:, pl.ds(start, block)], mask)
        return carry

    lax.fori_loop(plan_ref[i], plan_ref[blocks + i], whole, 0)
    lax.fori_loop(plan_ref[blocks + i], i + 1, part, 0)
    for h in range(heads):
        r = slice(h * HEAD, (h + 1) * HEAD)
        mixed[r, :] = mixed[r, :] * (1.0 / sums[h : h + 1, :])
    log_ref[...] = tops[...] + jnp.log(jnp.maximum(sums[...], 1e-37))
    o_ref[...] = mixed[...].T.astype(bf16)


def attn_backward_kernel(
    block, heads, plan_ref, q_ref, k_ref, v_ref, kt_ref, sk_ref, sv_ref, skt_ref, row_ref, log_ref,
    o_ref, do_ref, dq_ref, dk_ref, dv_ref, dsk_ref, dsv_ref, q_heads, do_heads, dq_sum, dk_sum,
    dv_sum, dsk_sum, dsv_sum,
):
    i = pl.program_id(0)
    blocks = pl.num_programs(0)

    @pl.when(i == 0)
    def _():
        dk_sum[...] = jnp.zeros_like(dk_sum)
        dv_sum[...] = jnp.zeros_like(dv_sum)
        dsk_sum[...] = jnp.zeros_like(dsk_sum)
        dsv_sum[...] = jnp.zeros_like(dsv_sum)

    q = q_ref[...].astype(f32) * score_scale
    do = do_ref[...].astype(f32)
    for h in range(heads):
        q_heads[h] = only_head(q, h).astype(bf16)
        do_heads[h] = only_head(do, h).astype(bf16)
    both_t = (do * o_ref[...].astype(f32)).T
    row_terms = [
        jnp.sum(both_t[h * HEAD : (h + 1) * HEAD, :], axis=0, keepdims=True) for h in range(heads)
    ]
    dq_sum[...] = jnp.zeros_like(dq_sum)
    lowest = row_ref[0:1, :]
    highest = row_ref[1:2, :]
    summ_end = row_ref[2:3, :]
    me = row_ref[3:4, :]

    def step(keys, values, keys_t, mask, dk_at, dv_at):
        dk = dv = None
        for h in range(heads):
            scores = dot(keys, q_heads[h], ROWS_BY_COLS)
            if mask is not None:
                scores = jnp.where(mask, scores, masked_score)
            probs = jnp.exp(scores - log_ref[h : h + 1, :])
            grad_probs = dot(values, do_heads[h], ROWS_BY_COLS)
            grad_scores = (probs * (grad_probs - row_terms[h])).astype(bf16)
            r = slice(h * HEAD, (h + 1) * HEAD)
            dq_sum[r, :] += dot(keys_t[r, :], grad_scores, ROWS_BY_ROWS)
            dv_own = dot(probs.astype(bf16), do_heads[h], ROWS_BY_ROWS)
            dk_own = dot(grad_scores, q_heads[h], ROWS_BY_ROWS)
            dv = dv_own if dv is None else dv + dv_own
            dk = dk_own if dk is None else dk + dk_own
        dk_at[...] += dk
        dv_at[...] += dv

    @pl.when(plan_ref[2 * blocks + i] > 0)
    def _():
        places = lax.broadcasted_iota(jnp.int32, (sk_ref.shape[0], block), 0)
        step(sk_ref[...], sv_ref[...], skt_ref[...], places < summ_end, dsk_sum, dsv_sum)

    def whole(j, carry):
        d = pl.ds(pl.multiple_of(j * block, block), block)
        step(k_ref[d, :], v_ref[d, :], kt_ref[:, d], None, dk_sum.at[d, :], dv_sum.at[d, :])
        return carry

    def part(j, carry):
        start = pl.multiple_of(j * block, block)
        d = pl.ds(start, block)
        places = start + lax.broadcasted_iota(jnp.int32, (block, block), 0)
        mask = ((places >= lowest) & (places <= highest)) | (places == me)
        step(k_ref[d, :], v_ref[d, :], kt_ref[:, d], mask, dk_sum.at[d, :], dv_sum.at[d, :])
        return carry

    lax.fori_loop(plan_ref[i], plan_ref[blocks + i], whole, 0)
    lax.fori_loop(plan_ref[blocks + i], i + 1, part, 0)
    dq_ref[...] = (dq_sum[...] * score_scale).T.astype(bf16)

    @pl.when(i == blocks - 1)
    def _():
        dk_ref[...] = dk_sum[...].astype(bf16)
        dv_ref[...] = dv_sum[...].astype(bf16)
        dsk_ref[...] = dsk_sum[...].astype(bf16)
        dsv_ref[...] = dsv_sum[...].astype(bf16)


def held(shape):
    return pl.BlockSpec(shape, lambda i, *_: (0, 0))


def attn_forward(plan, rows, q, k, v_t, sk, sv_t, block):
    count, width = q.shape
    heads = width // HEAD
    by_rows = pl.BlockSpec((block, width), lambda i, *_: (i, 0))
    by_cols = pl.BlockSpec((8, block), lambda i, *_: (0, i))
    pairs = count * count // 4
    return pl.pallas_call(
        functools.partial(attn_forward_kernel, block, heads),
        grid_spec=pltpu.PrefetchScalarGridSpec(
            num_scalar_prefetch=1,
            grid=(count // block,),
            in_specs=[by_rows, held(k.shape), held(v_t.shape), held(sk.shape), held(sv_t.shape), by_cols],
            out_specs=[by_rows, by_cols],
            scratch_shapes=[
                pltpu.VMEM((heads, block, width), bf16),
                pltpu.VMEM((8, block), f32),
                pltpu.VMEM((8, block), f32),
                pltpu.VMEM((width, block), f32),
            ],
        ),
        out_shape=[
            jax.ShapeDtypeStruct((count, width), bf16),
            jax.ShapeDtypeStruct((8, count), f32),
        ],
        compiler_params=pltpu.CompilerParams(
            dimension_semantics=("arbitrary",), vmem_limit_bytes=32 * 2**20
        ),
        cost_estimate=pl.CostEstimate(
            flops=16 * pairs * width, bytes_accessed=8 * count * width, transcendentals=pairs * heads
        ),
        name="attn_forward",
    )(plan, q, k, v_t, sk, sv_t, rows)


def attn_backward(plan, rows, q, k, v, k_t, sk, sv, sk_t, logs, o, do, block):
    count, width = q.shape
    heads = width // HEAD
    by_rows = pl.BlockSpec((block, width), lambda i, *_: (i, 0))
    by_cols = pl.BlockSpec((8, block), lambda i, *_: (0, i))
    pairs = count * count // 4
    long = jax.ShapeDtypeStruct((count, width), bf16)
    short = jax.ShapeDtypeStruct(sk.shape, bf16)
    return pl.pallas_call(
        functools.partial(attn_backward_kernel, block, heads),
        grid_spec=pltpu.PrefetchScalarGridSpec(
            num_scalar_prefetch=1,
            grid=(count // block,),
            in_specs=[
                by_rows, held(k.shape), held(v.shape), held(k_t.shape), held(sk.shape),
                held(sv.shape), held(sk_t.shape), by_cols, by_cols, by_rows, by_rows,
            ],
            out_specs=[by_rows, held(k.shape), held(v.shape), held(sk.shape), held(sv.shape)],
            scratch_shapes=[
                pltpu.VMEM((heads, block, width), bf16),
                pltpu.VMEM((heads, block, width), bf16),
                pltpu.VMEM((width, block), f32),
                pltpu.VMEM((count, width), f32),
                pltpu.VMEM((count, width), f32),
                pltpu.VMEM(sk.shape, f32),
                pltpu.VMEM(sv.shape, f32),
            ],
        ),
        out_shape=[long, long, long, short, short],
        compiler_params=pltpu.CompilerParams(
            dimension_semantics=("arbitrary",), vmem_limit_bytes=48 * 2**20
        ),
        cost_estimate=pl.CostEstimate(
            flops=24 * pairs * width, bytes_accessed=20 * count * width, transcendentals=pairs * heads
        ),
        name="attn_backward",
    )(plan, q, k, v, k_t, sk, sv, sk_t, rows, logs, o, do)


def attention_plan(lengths, padding, count, block):
    places = jnp.arange(count, dtype=jnp.int32)
    ends = jnp.cumsum(lengths)
    passed = places[:, None] >= ends[None, :]
    segment = jnp.sum(passed.astype(jnp.int32), axis=1)
    lowest = jnp.max(jnp.where(passed, ends[None, :], 0), axis=1)
    living = count - padding
    highest = jnp.minimum(places, living - 1)
    nothing = jnp.zeros_like(places)
    rows = jnp.stack(
        [lowest, highest, segment * SUMM, places, nothing, nothing, nothing, nothing], axis=0
    )
    blocks = count // block
    starts = jnp.arange(blocks, dtype=jnp.int32) * block
    first = lowest.reshape(blocks, block)[:, 0] // block
    one_piece = lowest.reshape(blocks, block)[:, -1] <= first * block
    whole_end = jnp.maximum(jnp.minimum(starts, living) // block, first)
    split = jnp.where(one_piece, whole_end, first)
    summ_flag = (segment.reshape(blocks, block)[:, -1] > 0).astype(jnp.int32)
    return rows, jnp.concatenate([first, split, summ_flag]).astype(jnp.int32)


def per_device(
    tokens,
    summaries,
    segment_lengths,
    pad_lengths,
    output_grad,
    norm1_gain,
    norm1_bias,
    query_weight,
    query_bias,
    key_weight,
    value_weight,
    value_bias,
    out_weight,
    out_bias,
    norm2_gain,
    norm2_bias,
    up_weight,
    up_bias,
    down_weight,
    down_bias,
):
    shards = lax.axis_size("fsdp")
    items = lax.axis_size("dp")
    devices = shards * items
    position = lax.axis_index("fsdp")
    tok_rows = tokens.shape[1]
    width = tokens.shape[2]
    count = tok_rows * shards
    own_width = width // shards
    rows_held = query_weight.shape[0]
    units_held = up_bias.shape[0]
    own_units = units_held * items
    hidden = units_held * devices
    summary_rows = summaries.shape[1]
    padded_summ = -(-summary_rows // 32) * 32
    spread = rows_held % HEAD == 0
    block = math.gcd(count, 512)

    def for_shards(weight):
        if spread:
            split = weight.reshape(rows_held, items, shards, rows_held)
            return split.transpose(2, 0, 1, 3).reshape(shards, rows_held, own_width)
        return weight.reshape(rows_held, shards, own_width).transpose(1, 0, 2)

    def from_shards(parts):
        if spread:
            split = parts.reshape(shards, rows_held, items, rows_held)
            return split.transpose(1, 2, 0, 3).reshape(rows_held, width)
        return parts.transpose(1, 0, 2).reshape(rows_held, width)

    def own_columns(vector):
        if spread:
            split = vector.reshape(items, shards, rows_held)
            return lax.dynamic_index_in_dim(split, position, 1, keepdims=False).reshape(own_width)
        return lax.dynamic_slice_in_dim(vector, position * own_width, own_width, 0)

    def whole_columns(vector):
        if spread:
            split = jnp.zeros((items, shards, rows_held), f32)
            return lax.dynamic_update_index_in_dim(
                split, vector.reshape(items, 1, rows_held), position, 1
            ).reshape(width)
        return lax.dynamic_update_slice_in_dim(
            jnp.zeros((width,), f32), vector, position * own_width, 0
        )

    token_pieces = gathered(tokens[0])
    vectors = jnp.concatenate(
        [
            norm1_gain, norm1_bias, query_bias, value_bias, out_bias, norm2_gain, norm2_bias,
            down_bias, up_bias,
        ]
    ).astype(f32)
    vectors = lax.all_to_all(
        jnp.broadcast_to(vectors[None], (devices, vectors.shape[0])), BOTH, 0, 0, tiled=True
    )
    gain_one, shift_one, query_shift, value_shift, out_shift, gain_two, shift_two, down_shift = (
        vectors[:, n * rows_held : (n + 1) * rows_held].reshape(width) for n in range(8)
    )
    up_shift = lax.dynamic_index_in_dim(
        vectors[:, 8 * rows_held :].reshape(items, shards, units_held), position, 1, keepdims=False
    ).reshape(own_units)
    query_shift = own_columns(query_shift)
    value_shift = own_columns(value_shift)

    qkv_parts = jnp.concatenate(
        [for_shards(query_weight), for_shards(key_weight), for_shards(value_weight)], axis=2
    )
    qkv_parts = lax.all_to_all(qkv_parts, "fsdp", 0, 0, tiled=True)
    qkv_own = lax.all_gather(
        qkv_parts.reshape(shards * rows_held, 3 * own_width), "dp", axis=0, tiled=True
    )
    if spread:
        out_own = lax.all_gather(out_weight, "dp", axis=0, tiled=True)
    else:
        out_own = lax.dynamic_slice_in_dim(
            lax.all_gather(out_weight, BOTH, axis=0, tiled=True), position * own_width, own_width, 0
        )
    up_parts = up_weight.reshape(rows_held, items, shards, units_held).transpose(2, 0, 1, 3)
    up_parts = lax.all_to_all(
        up_parts.reshape(shards, rows_held, own_units), "fsdp", 0, 0, tiled=True
    )
    up_own = lax.all_gather(
        up_parts.reshape(shards * rows_held, own_units), "dp", axis=0, tiled=True
    )
    down_own = lax.all_gather(down_weight, "dp", axis=0, tiled=True)
    summ_full = lax.all_to_all(
        jnp.broadcast_to(summaries, (shards,) + summaries.shape[1:]), "fsdp", 0, 0, tiled=True
    )
    summ_full = summ_full.transpose(1, 0, 2).reshape(summary_rows, width)
    summ_inputs = jnp.pad(summ_full, ((0, padded_summ - summary_rows), (0, 0))).astype(f32)

    def start_of(m):
        return (position ^ m) * tok_rows

    def in_place(whole, piece, m):
        return lax.dynamic_update_slice(whole, piece, (start_of(m), 0))

    def in_order(whole):
        return [lax.dynamic_slice_in_dim(whole, start_of(m), tok_rows, 0) for m in range(shards)]

    normed = jnp.zeros((count, width), bf16)
    for m, piece in enumerate(token_pieces):
        normed = in_place(normed, layer_norm(piece.astype(f32), gain_one, shift_one).astype(bf16), m)
    normed_summ = layer_norm(summ_inputs, gain_one, shift_one).astype(bf16)
    query_own = qkv_own[:, :own_width]
    key_own = qkv_own[:, own_width : 2 * own_width]
    value_own = qkv_own[:, 2 * own_width :]
    queries = (dot(normed, query_own, ROWS_BY_ROWS) + query_shift).astype(bf16)
    keys = dot(normed, key_own, ROWS_BY_ROWS).astype(bf16)
    values = (dot(normed, value_own, ROWS_BY_ROWS) + value_shift).astype(bf16)
    summ_keys = dot(normed_summ, key_own, ROWS_BY_ROWS).astype(bf16)
    summ_values = (dot(normed_summ, value_own, ROWS_BY_ROWS) + value_shift).astype(bf16)
    rows, plan = attention_plan(segment_lengths[0], pad_lengths[0], count, block)
    attn, logs = attn_forward(
        plan, rows, queries, keys, values.T, summ_keys, summ_values.T, block
    )
    attn_pieces = in_order(attn)
    inputs = tokens[0].astype(f32)
    proj_sum = scattered_sum(
        [dot(piece, out_own, ROWS_BY_ROWS).astype(bf16) for piece in attn_pieces]
    )
    resid = inputs + proj_sum + out_shift

    normed_two_own = layer_norm(resid, gain_two, shift_two).astype(bf16)
    grad_pieces = gathered(output_grad[0])
    grad_rows = jnp.concatenate(grad_pieces, axis=0)
    normed_two = jnp.concatenate(gathered(normed_two_own), axis=0)
    upper = dot(normed_two, up_own, ROWS_BY_ROWS) + up_shift
    active = gelu_tanh(upper).astype(bf16)

    def cut(whole):
        return [whole[m * tok_rows : (m + 1) * tok_rows] for m in range(shards)]

    grad_active = dot(grad_rows, down_own, ROWS_BY_COLS)
    _, gelu_pull = jax.vjp(gelu_tanh, upper)
    grad_upper = gelu_pull(grad_active)[0].astype(bf16)
    grad_normed_two = scattered_sum(
        [dot(piece, up_own, ROWS_BY_COLS).astype(bf16) for piece in cut(grad_upper)]
    )
    result = scattered_sum(
        [dot(piece, down_own, ROWS_BY_ROWS).astype(bf16) for piece in cut(active)]
    )
    result = (resid + result + down_shift).astype(bf16)
    down_grad = dot(active, grad_rows, COLS_BY_ROWS).astype(bf16)
    down_grad = lax.psum_scatter(down_grad, "dp", scatter_dimension=0, tiled=True).astype(f32)
    up_grad = dot(normed_two, grad_upper, COLS_BY_ROWS).astype(bf16)
    up_grad = lax.psum_scatter(up_grad, "dp", scatter_dimension=0, tiled=True)
    up_grad = lax.all_to_all(
        up_grad.reshape(shards, rows_held, own_units), "fsdp", 0, 0, tiled=True
    )
    up_grad = up_grad.reshape(shards, rows_held, items, units_held).transpose(1, 2, 0, 3)
    up_grad = up_grad.reshape(rows_held, hidden).astype(f32)
    up_shift_grad = jnp.sum(grad_upper.astype(f32), axis=0)
    grad_floats = output_grad[0].astype(f32)
    down_shift_grad = jnp.sum(grad_floats, axis=0)
    _, norm_two_pull = jax.vjp(layer_norm, resid, gain_two, shift_two)
    grad_resid, gain_two_grad, shift_two_grad = norm_two_pull(grad_normed_two)
    grad_resid = grad_resid + grad_floats

    grad_proj = grad_resid.astype(bf16)
    out_shift_grad = jnp.sum(grad_proj.astype(f32), axis=0)
    proj_pieces = gathered(grad_proj)
    grad_attn = jnp.zeros((count, own_width), bf16)
    for m, piece in enumerate(proj_pieces):
        grad_attn = in_place(grad_attn, dot(piece, out_own, ROWS_BY_COLS).astype(bf16), m)
    out_grad = dot(
        jnp.concatenate(attn_pieces, axis=0), jnp.concatenate(proj_pieces, axis=0), COLS_BY_ROWS
    ).astype(bf16)
    if spread:
        out_grad = lax.psum_scatter(out_grad, "dp", scatter_dimension=0, tiled=True)
    else:
        out_grad = lax.psum_scatter(
            lax.dynamic_update_slice_in_dim(
                jnp.zeros((width, width), bf16), out_grad, position * own_width, 0
            ),
            BOTH,
            scatter_dimension=0,
            tiled=True,
        )
    out_grad = out_grad.astype(f32)
    grad_queries, grad_keys, grad_values, grad_summ_keys, grad_summ_values = attn_backward(
        plan, rows, queries, keys, values, keys.T, summ_keys, summ_values, summ_keys.T, logs, attn,
        grad_attn, block,
    )
    grad_qkv = jnp.concatenate([grad_queries, grad_keys, grad_values], axis=1)
    grad_summ_kv = jnp.concatenate([grad_summ_keys, grad_summ_values], axis=1)
    grad_normed = scattered_sum(
        [dot(piece, qkv_own, ROWS_BY_COLS).astype(bf16) for piece in in_order(grad_qkv)]
    )
    kv_own = qkv_own[:, own_width:]
    summ_share = -(-padded_summ // (shards * 16)) * 16
    grad_normed_summ = dot(grad_summ_kv, kv_own, ROWS_BY_COLS).astype(bf16)
    grad_normed_summ = jnp.pad(
        grad_normed_summ, ((0, summ_share * shards - padded_summ), (0, 0))
    ).reshape(shards, summ_share, width)
    grad_normed_summ = lax.all_to_all(grad_normed_summ, "fsdp", 0, 0, tiled=True)
    grad_normed_summ = jnp.sum(grad_normed_summ.astype(f32), axis=0)
    summ_own = lax.dynamic_slice_in_dim(
        jnp.pad(summ_inputs, ((0, summ_share * shards - padded_summ), (0, 0))),
        position * summ_share,
        summ_share,
        0,
    )
    qkv_grad = dot(normed, grad_qkv, COLS_BY_ROWS)
    summ_kv_grad = dot(normed_summ, grad_summ_kv, COLS_BY_ROWS)
    qkv_grad = qkv_grad + jnp.pad(summ_kv_grad, ((0, 0), (own_width, 0)))
    qkv_grad = lax.psum_scatter(qkv_grad.astype(bf16), "dp", scatter_dimension=0, tiled=True)
    qkv_grad = lax.all_to_all(
        qkv_grad.reshape(shards, rows_held, 3 * own_width), "fsdp", 0, 0, tiled=True
    )
    query_grad, key_grad, value_grad = (
        from_shards(qkv_grad[:, :, n * own_width : (n + 1) * own_width]).astype(f32)
        for n in range(3)
    )
    query_shift_grad = jnp.sum(grad_queries.astype(f32), axis=0)
    value_shift_grad = jnp.sum(grad_values.astype(f32), axis=0) + jnp.sum(
        grad_summ_values.astype(f32), axis=0
    )
    _, norm_one_pull = jax.vjp(layer_norm, inputs, gain_one, shift_one)
    grad_inputs, gain_one_grad, shift_one_grad = norm_one_pull(grad_normed)
    grad_inputs = grad_inputs + grad_resid
    _, norm_summ_pull = jax.vjp(layer_norm, summ_own, gain_one, shift_one)
    grad_summ, gain_summ_grad, shift_summ_grad = norm_summ_pull(grad_normed_summ)
    summary_cols = summaries.shape[2]
    grad_summ = lax.all_to_all(
        grad_summ.reshape(summ_share, shards, summary_cols).transpose(1, 0, 2),
        "fsdp",
        0,
        0,
        tiled=True,
    )
    summary_grad = grad_summ.reshape(shards * summ_share, summary_cols)[:summary_rows]

    vector_grads = jnp.stack(
        [
            gain_one_grad + gain_summ_grad,
            shift_one_grad + shift_summ_grad,
            whole_columns(query_shift_grad),
            whole_columns(value_shift_grad),
            out_shift_grad,
            gain_two_grad,
            shift_two_grad,
            down_shift_grad,
        ]
    )
    vector_grads = vector_grads.reshape(8, devices, rows_held).transpose(1, 0, 2)
    unit_grads = lax.dynamic_update_index_in_dim(
        jnp.zeros((items, shards, units_held), f32),
        up_shift_grad.reshape(items, 1, units_held),
        position,
        1,
    )
    all_grads = jnp.concatenate(
        [vector_grads.reshape(devices, 8 * rows_held), unit_grads.reshape(devices, units_held)],
        axis=1,
    )
    all_grads = jnp.sum(lax.all_to_all(all_grads, BOTH, 0, 0, tiled=True), axis=0)
    (
        gain_one_grad, shift_one_grad, query_shift_grad, value_shift_grad, out_shift_grad,
        gain_two_grad, shift_two_grad, down_shift_grad,
    ) = (all_grads[n * rows_held : (n + 1) * rows_held] for n in range(8))
    up_shift_grad = all_grads[8 * rows_held :]
    return (
        result[None],
        grad_inputs[None],
        summary_grad[None],
        gain_one_grad,
        shift_one_grad,
        query_grad,
        query_shift_grad,
        key_grad,
        value_grad,
        value_shift_grad,
        out_grad,
        out_shift_grad,
        gain_two_grad,
        shift_two_grad,
        up_grad,
        up_shift_grad,
        down_grad,
        down_shift_grad,
    )


def solution(mesh):
    vector = P(BOTH)
    matrix = P(BOTH, None)
    rows = P("dp", "fsdp", None)
    columns = P("dp", None, "fsdp")
    return jax.shard_map(
        per_device,
        mesh=mesh,
        in_specs=(
            rows, columns, P("dp", None), P("dp"), rows, vector, vector, matrix, vector, matrix,
            matrix, vector, matrix, vector, vector, vector, matrix, vector, matrix, vector,
        ),
        out_specs=(
            rows, rows, columns, vector, vector, matrix, vector, matrix, matrix, vector, matrix,
            vector, vector, vector, matrix, vector, matrix, vector,
        ),
        check_vma=False,
    )
```

time: 4640 us -> 1250 us (0.27)
  waiting for transfers between devices: 2520 us -> 437 us
  matrix products: 795 us -> 314 us
  blocking collectives: 358 us -> 30.6 us
  local copies, waits for them, and re-layouts: 452 us -> 137 us
  starting transfers between devices: 254 us -> 69 us
  Pallas kernels: 0 us -> 132 us
  other arithmetic: 219 us -> 108 us
    reduce_scatter x8 -> x4, waiting for transfers between devices: 2350 us -> 0.03 us  [the longest x1 0.02 us: per_device(): lax.psum_scatter(down_grad, 'dp', scatter_dimension=0, tiled=True)]
    dot_general x80 -> x53, matrix products: 795 us -> 314 us  [dot(): return lax.dot_general(left, right, dims, preferred_element_type=f32)]
    ppermute x16 -> x64, waiting for transfers between devices: 0.72 us -> 389 us  [swapped(): return lax.ppermute(x, 'fsdp', [(i, i ^ bit) for i in range(devices)])]
    unnamed x1 -> x0, blocking collectives: 225 us -> none
    ppermute x16 -> x64, starting transfers between devices: 252 us -> 36.9 us  [swapped(): return lax.ppermute(x, 'fsdp', [(i, i ^ bit) for i in range(devices)])]
    psum x1 -> x0, waiting for transfers between devices: 164 us -> none  [per_device(): grad_normed_summ = lax.psum(grad_normed_summ_part, 'fsdp')]
    all_gather x4 -> x0, blocking collectives: 133 us -> none  [the longest x1 43.5 us: per_device(): lax.all_gather(up_bias, ('dp', 'fsdp'), axis=0, tiled=True)]
    pallas_call x0 -> x2, Pallas kernels: none -> 132 us  [the longest x1 85.3 us: attn_backward(): pl.pallas_call(functools.partial(attn_backward_kernel, block, heads), gri...]
  transfers between devices with their start and end apart: 33 -> 79, of which waited for: 11 -> 26; matrix products, arithmetic and copies ran while one was open for 16% -> 39% of each run, Pallas kernels for 0% -> 11%
where the time goes in v1:
time: 1250 us; the launch traced here: 1240 us
  waiting for transfers between devices  437 us (35%)
  matrix products  314 us (25%)
  local copies, waits for them, and re-layouts  137 us (11%)
  Pallas kernels  132 us (11%)
  other arithmetic  108 us (9%)
  starting transfers between devices  69 us (6%)
  blocking collectives  30.6 us (2%)
  between operations  17.3 us (1%)
    ppermute x64, waiting for transfers between devices, swapped(): return lax.ppermute(x, 'fsdp', [(i, i ^ bit) for i in range(devices)])  389 us
    dot_general x53, matrix products, dot(): return lax.dot_general(left, right, dims, preferred_element_type=f32)  314 us
    pallas_call x1, Pallas kernels, attn_backward(): pl.pallas_call(functools.partial(attn_backward_kernel, block, heads), gri...  85.3 us
    unnamed x232, local copies, waits for them, and re-layouts  70.8 us
    pallas_call x1, Pallas kernels, attn_forward(): pl.pallas_call(functools.partial(attn_forward_kernel, block, heads), grid...  46.4 us
    all_to_all x1, waiting for transfers between devices, per_device(): lax.all_to_all(jnp.broadcast_to(vectors[None], (devices, vectors.shape[0]...  38 us
    ppermute x64, starting transfers between devices, swapped(): return lax.ppermute(x, 'fsdp', [(i, i ^ bit) for i in range(devices)])  36.9 us
  transfers between devices with their start and end apart: 79, of which 26 were waited for; matrix products, arithmetic and copies ran while one was open for 39% of the time, Pallas kernels for 11%

profile of v1, /device:TPU:0, one launch (start us, length us, event | category | flops | bytes accessed | tf_op | source)
XLA Modules:
  0.0 1244.9 jit_solution(7868579469465890720)
XLA Ops:
  15.2 17.8 %all_to_all.53 = bf16[8,64,768]{2,1,0:T(8,128)(2,1)} all-to-all(bf16[8,64,768]{2,1,0:T(8,128)(2,1)S(1)} %pad_maximum_fusion.10), channel_id=1, replica_groups=mesh['dp'=4,'fsdp'=8] {'fsdp'}, dimensions={0} | all-to-all | bytes 1572864 | tf_op jit(solution)/shard_map/all_to_all | solution.py:432
  35.1 5.8 all-to-all-start
  44.5 38.0 %all-to-all-done = f32[32,1,768]{2,1,0:T(1,128)S(1)} async-done(((f32[32,1,768]{2,1,0:T(1,128)}), f32[32,1,768]{2,1,0:T(1,128)S(1)}, u32[]{:S(2)}, u32[]{:S(2)}) %all-to-all-start) | async-done | bytes 98336 | tf_op jit(solution)/shard_map/all_to_all | solution.py:417
  87.9 6.3 broadcast_in_dim.41
  114.5 3.8 fusion.65
  124.4 8.3 collective-permute-done.5
  141.1 3.8 fusion.68
  153.0 10.6 fusion.11.v_ref
  166.6 11.9 convolution_convert_fusion
  178.5 4.1 copy.129.k_ref
  186.1 10.7 fusion.12.q_ref
  196.8 46.4 %attn_forward.1 = (bf16[4096,256]{1,0:T(8,128)(2,1)S(1)}, f32[8,4096]{1,0:T(8,128)S(1)}) custom-call(s32[24]{0:T(128)S(1)} %pad_add_fusion.plan_ref, bf16[4096,256]{1,0:T(8,128)(2,1)S(1)} %fusion.12.q_ref, bf16[4096,256]{1,0:T(8,128)(2,1)S(1)} %copy-done.4, bf16[256,4096]{1,0:T(8,128)(2,1)S(1)} %copy-done.5, ...), custom_call_target="tpu_custom_call" | custom-call | flops 17179869184 | bytes 8388608 | tf_op jit(solution)/shard_map/attn_forward/pallas_call | solution.py:254
  244.5 4.0 convolution_convert_fusion.21
  259.1 4.2 all-to-all-start.3
  271.1 8.1 all-to-all-done.3
  287.1 13.6 %collective-permute-done.11 = bf16[256,2048]{1,0:T(8,128)(2,1)} collective-permute-done((bf16[256,2048]{1,0:T(8,128)(2,1)}, bf16[256,2048]{1,0:T(8,128)(2,1)}, u32[]{:S(2)}, u32[]{:S(2)}) %collective-permute-start.11) | collective-permute-done | bytes 1048608 | tf_op jit(solution)/shard_map/ppermute | solution.py:43
  305.0 40.7 %collective-permute-done.14 = bf16[256,2048]{1,0:T(8,128)(2,1)S(1)} collective-permute-done((bf16[256,2048]{1,0:T(8,128)(2,1)S(1)}, bf16[256,2048]{1,0:T(8,128)(2,1)S(1)}, u32[]{:S(2)}, u32[]{:S(2)}) %collective-permute-start.14) | collective-permute-done | bytes 1048608 | tf_op jit(solution)/shard_map/ppermute | solution.py:43
  353.7 37.0 %collective-permute-done.12 = bf16[512,2048]{1,0:T(8,128)(2,1)} collective-permute-done((bf16[512,2048]{1,0:T(8,128)(2,1)}, bf16[512,2048]{1,0:T(8,128)(2,1)}, u32[]{:S(2)}, u32[]{:S(2)}) %collective-permute-start.12) | collective-permute-done | bytes 2097184 | tf_op jit(solution)/shard_map/ppermute | solution.py:43
  390.7 5.8 collective-permute-done.15
  396.5 4.4 fusion.149
  405.9 11.3 collective-permute-done.37
  428.8 28.8 %collective-permute-done.17 = bf16[512,2048]{1,0:T(8,128)(2,1)S(1)} collective-permute-done((bf16[512,2048]{1,0:T(8,128)(2,1)}, bf16[512,2048]{1,0:T(8,128)(2,1)S(1)}, u32[]{:S(2)}, u32[]{:S(2)}) %collective-permute-start.17) | collective-permute-done | bytes 2097184 | tf_op jit(solution)/shard_map/ppermute | solution.py:43
  474.5 11.3 collective-permute-done.21
  507.3 23.6 %fusion.157 = f32[4096,1024]{1,0:T(8,128)} fusion(bf16[4096,2048]{1,0:T(8,128)(2,1)} %constant_dynamic-update-slice_fusion.2, bf16[2048,1024]{1,0:T(8,128)(2,1)} %all-gather.9.cloned.1.call-done), kind=kOutput, calls=%fused_computation.394 | convolution fusion | flops 17179869184 | bytes 37748736 | tf_op jit(solution)/shard_map/dot_general | solution.py:27
  530.9 38.2 %convert_reduce_fusion = (f32[1024]{0:T(1024)}, bf16[4096,1024]{1,0:T(8,128)(2,1)}, bf16[4096,1024]{1,0:T(8,128)(2,1)}) fusion(f32[4096,1024]{1,0:T(8,128)} %fusion.157, f32[1024]{0:T(1024)S(1)} %bitcast.209, bf16[4096,2048]{1,0:T(8,128)(2,1)} %constant_dynamic-update-slice_fusion.11, bf16[1024,2048]{1,0:T(8,128)(2,1)} %all-gather.11.cloned.1.call-done), kind=kOutput, calls=%fused_computation.9 | convolution fusion | flops 17284726784 | bytes 54534144 | tf_op jit(solution)/shard_map/dot_general | solution.py:27
  569.0 5.0 convolution_convert_fusion.15
  578.3 5.1 convolution_convert_fusion.11
  591.8 4.9 convolution_convert_fusion.3
  596.8 4.0 convolution_convert_fusion.9
  600.8 4.9 convolution_convert_fusion.17
  623.5 3.8 add_convert_fusion.6
  627.9 4.3 add_convert_fusion.4
  632.7 33.1 %collective-permute-done.43 = bf16[256,2048]{1,0:T(8,128)(2,1)S(1)} collective-permute-done((bf16[256,2048]{1,0:T(8,128)(2,1)S(1)}, bf16[256,2048]{1,0:T(8,128)(2,1)S(1)}, u32[]{:S(2)}, u32[]{:S(2)}) %collective-permute-start.43) | collective-permute-done | bytes 1048608 | tf_op jit(solution)/shard_map/ppermute | solution.py:43
  670.5 21.4 %collective-permute-done.30 = bf16[256,2048]{1,0:T(8,128)(2,1)S(1)} collective-permute-done((bf16[256,2048]{1,0:T(8,128)(2,1)S(1)}, bf16[256,2048]{1,0:T(8,128)(2,1)S(1)}, u32[]{:S(2)}, u32[]{:S(2)}) %collective-permute-start.30) | collective-permute-done | bytes 1048608 | tf_op jit(solution)/shard_map/ppermute | solution.py:43
  693.5 4.9 convolution_convert_fusion.10
  698.4 5.0 convolution_convert_fusion.18
  703.4 33.4 %collective-permute-done.44 = bf16[512,2048]{1,0:T(8,128)(2,1)S(1)} collective-permute-done((bf16[512,2048]{1,0:T(8,128)(2,1)S(1)}, bf16[512,2048]{1,0:T(8,128)(2,1)S(1)}, u32[]{:S(2)}, u32[]{:S(2)}) %collective-permute-start.44) | collective-permute-done | bytes 2097184 | tf_op jit(solution)/shard_map/ppermute | solution.py:43
  740.4 40.1 %collective-permute-done.28 = bf16[512,2048]{1,0:T(8,128)(2,1)S(1)} collective-permute-done((bf16[512,2048]{1,0:T(8,128)(2,1)S(1)}, bf16[512,2048]{1,0:T(8,128)(2,1)S(1)}, u32[]{:S(2)}, u32[]{:S(2)}) %collective-permute-start.28) | collective-permute-done | bytes 2097184 | tf_op jit(solution)/shard_map/ppermute | solution.py:43
  780.5 3.8 fusion.148
  784.3 5.1 constant_dynamic-update-slice_fusion.35
  790.5 45.4 %collective-permute-done.49 = bf16[512,2048]{1,0:T(8,128)(2,1)} collective-permute-done((bf16[512,2048]{1,0:T(8,128)(2,1)S(1)}, bf16[512,2048]{1,0:T(8,128)(2,1)}, u32[]{:S(2)}, u32[]{:S(2)}) %collective-permute-start.49) | collective-permute-done | bytes 2097184 | tf_op jit(solution)/shard_map/ppermute | solution.py:43
  836.4 23.7 %convolution_convert_fusion.2 = bf16[2048,1024]{1,0:T(8,128)(2,1)} fusion(bf16[4096,2048]{1,0:T(8,128)(2,1)} %constant_dynamic-update-slice_fusion.2, bf16[4096,1024]{1,0:T(8,128)(2,1)} %get-tuple-element.122), kind=kOutput, calls=%fused_computation.116 | convolution fusion | flops 17181966336 | bytes 29360128 | tf_op jit(solution)/shard_map/dot_general | solution.py:27
  864.7 3.8 constant_dynamic-update-slice_fusion.34
  881.3 5.6 collective-permute-done.53
  905.2 85.3 %attn_backward.1 = (bf16[4096,256]{1,0:T(8,128)(2,1)S(1)}, bf16[4096,256]{1,0:T(8,128)(2,1)S(1)}, bf16[4096,256]{1,0:T(8,128)(2,1)}, bf16[160,256]{1,0:T(8,128)(2,1)S(1)}, bf16[160,256]{1,0:T(8,128)(2,1)S(1)}) custom-call(s32[24]{0:T(128)S(1)} %pad_add_fusion.plan_ref, bf16[4096,256]{1,0:T(8,128)(2,1)} %copy-done.12, bf16[4096,256]{1,0:T(8,128)(2,1)} %copy.129.k_ref, ...), custom_call_target="tpu_custom_call" | custom-call | flops 25769803776 | bytes 20971520 | tf_op jit(solution)/shard_map/attn_backward/pallas_call | solution.py:290
  996.2 20.4 %add_convert_fusion = bf16[2048,768]{1,0:T(8,128)(2,1)} fusion(f32[2048,512]{1,0:T(8,128)S(1)} %fusion.143, bf16[4096,2048]{1,0:T(8,128)(2,1)} %fusion.71, bf16[4096,768]{1,0:T(8,128)(2,1)} %constant_dynamic-update-slice_fusion.22), kind=kOutput, calls=%fused_computation.11 | convolution fusion | flops 12888047616 | bytes 30408704 | tf_op jit(solution)/shard_map/dot_general | solution.py:27
  1023.2 24.0 %convolution_convert_fusion.1 = bf16[1024,2048]{1,0:T(8,128)(2,1)} fusion(bf16[4096,1024]{1,0:T(8,128)(2,1)} %get-tuple-element.135, bf16[4096,2048]{1,0:T(8,128)(2,1)} %constant_dynamic-update-slice_fusion.11), kind=kOutput, calls=%fused_computation.115 | convolution fusion | flops 17181966336 | bytes 29360128 | tf_op jit(solution)/shard_map/dot_general | solution.py:27
  1059.4 3.9 all-to-all-start.4
  1063.6 5.6 convolution_convert_fusion.31
  1069.7 4.4 convolution_convert_fusion.29
  1074.2 4.4 convolution_convert_fusion.27
  1079.1 4.5 convolution_convert_fusion.33
  1083.8 7.1 convolution_convert_fusion.35
  1090.8 4.6 add_convert_fusion.2
  1103.0 4.1 add_convert_fusion.1
  1107.3 14.1 %collective-permute-done.59 = bf16[256,2048]{1,0:T(8,128)(2,1)S(1)} collective-permute-done((bf16[256,2048]{1,0:T(8,128)(2,1)S(1)}, bf16[256,2048]{1,0:T(8,128)(2,1)S(1)}, u32[]{:S(2)}, u32[]{:S(2)}) %collective-permute-start.59) | collective-permute-done | bytes 1048608 | tf_op jit(solution)/shard_map/ppermute | solution.py:43
  1131.0 5.4 convolution_convert_fusion.34
  1137.5 4.4 all-to-all-start.8
  1146.1 26.1 %collective-permute-done.60 = bf16[512,2048]{1,0:T(8,128)(2,1)} collective-permute-done((bf16[512,2048]{1,0:T(8,128)(2,1)}, bf16[512,2048]{1,0:T(8,128)(2,1)}, u32[]{:S(2)}, u32[]{:S(2)}) %collective-permute-start.60) | collective-permute-done | bytes 2097184 | tf_op jit(solution)/shard_map/ppermute | solution.py:43
  1172.2 6.0 collective-permute-done.63
  1178.2 5.7 fusion.144
  1187.6 5.6 all-to-all-start.5
  1193.2 6.4 convert_reduce_fusion.2
  1201.1 12.9 %all_to_all.54 = f32[32,1,768]{2,1,0:T(1,128)S(1)} all-to-all(f32[32,1,768]{2,1,0:T(1,128)S(1)} %copy.136), channel_id=1, replica_groups=mesh['dp'=4,'fsdp'=8] {'dp','fsdp'}, dimensions={0} | all-to-all | bytes 196608 | tf_op jit(solution)/shard_map/all_to_all | solution.py:621
  (599 shorter events, 317.1 us)
Async XLA Ops:
  7.2 145.8 %all-gather.5.cloned.1.call-start = ((), (), s32[]{:S(2)}) async-start(), calls=%async_computation.13 | async-start | bytes 3932160 | tf_op jit(solution)/shard_map/all_gather | solution.py:433
  33.0 65.5 %collective-permute-start = (bf16[512,2048]{1,0:T(8,128)(2,1)S(1)}, bf16[512,2048]{1,0:T(8,128)(2,1)}, u32[]{:S(2)}, u32[]{:S(2)}) collective-permute-start(bf16[512,2048]{1,0:T(8,128)(2,1)S(1)} %bitcast.168), channel_id=1, source_target_pairs={{0,1},{1,0},{2,3},{3,2},{4,5},{5,4},{6,7},{7,6},{8,9},{9,8},{10,11... | collective-permute-start | bytes 6291464 | tf_op jit(solution)/shard_map/ppermute | solution.py:43
  33.0 74.0 %collective-permute-start.1 = (bf16[512,2048]{1,0:T(8,128)(2,1)S(1)}, bf16[512,2048]{1,0:T(8,128)(2,1)}, u32[]{:S(2)}, u32[]{:S(2)}) collective-permute-start(bf16[512,2048]{1,0:T(8,128)(2,1)S(1)} %bitcast.169), channel_id=1, source_target_pairs={{0,2},{1,3},{2,0},{3,1},{4,6},{5,7},{6,4},{7,5},{8,10},{9,11},{10,... | collective-permute-start | bytes 6291464 | tf_op jit(solution)/shard_map/ppermute | solution.py:43
  33.7 66.7 %collective-permute-start.3 = (bf16[512,2048]{1,0:T(8,128)(2,1)S(1)}, bf16[512,2048]{1,0:T(8,128)(2,1)}, u32[]{:S(2)}, u32[]{:S(2)}) collective-permute-start(bf16[512,2048]{1,0:T(8,128)(2,1)S(1)} %bitcast.170), channel_id=1, source_target_pairs={{0,4},{1,5},{2,6},{3,7},{4,0},{5,1},{6,2},{7,3},{8,12},{9,13},{10,... | collective-permute-start | bytes 6291464 | tf_op jit(solution)/shard_map/ppermute | solution.py:43
  35.1 47.4 %all-to-all-start = ((f32[32,1,768]{2,1,0:T(1,128)}), f32[32,1,768]{2,1,0:T(1,128)S(1)}, u32[]{:S(2)}, u32[]{:S(2)}) async-start(f32[32,1,768]{2,1,0:T(1,128)} %broadcast_in_dim.42), calls=%async_computation | async-start | bytes 196608 | tf_op jit(solution)/shard_map/all_to_all | solution.py:417
  40.9 203.7 %all-gather.7.cloned.1.call-start = ((), (), s32[]{:S(2)}) async-start(), calls=%async_computation.14 | async-start | bytes 1310720 | tf_op jit(solution)/shard_map/all_gather | solution.py:437
  108.3 24.4 %collective-permute-start.5 = (bf16[256,2048]{1,0:T(8,128)(2,1)S(1)}, bf16[256,2048]{1,0:T(8,128)(2,1)S(1)}, u32[]{:S(2)}, u32[]{:S(2)}) collective-permute-start(bf16[256,2048]{1,0:T(8,128)(2,1)S(1)} %slice.313), channel_id=1, source_target_pairs={{0,4},{1,5},{2,6},{3,7},{4,0},{5,1},{6,2},{7,3},{8,12},{9,13},{10,... | collective-permute-start | bytes 3145736 | tf_op jit(solution)/shard_map/ppermute | solution.py:43
  110.5 25.0 %collective-permute-start.6 = (bf16[256,2048]{1,0:T(8,128)(2,1)S(1)}, bf16[256,2048]{1,0:T(8,128)(2,1)S(1)}, u32[]{:S(2)}, u32[]{:S(2)}) collective-permute-start(bf16[256,2048]{1,0:T(8,128)(2,1)S(1)} %slice.314), channel_id=1, source_target_pairs={{0,2},{1,3},{2,0},{3,1},{4,6},{5,7},{6,4},{7,5},{8,10},{9,11},{10,... | collective-permute-start | bytes 3145736 | tf_op jit(solution)/shard_map/ppermute | solution.py:43
  252.3 29.5 %collective-permute-start.9 = (bf16[512,2048]{1,0:T(8,128)(2,1)}, bf16[512,2048]{1,0:T(8,128)(2,1)}, u32[]{:S(2)}, u32[]{:S(2)}) collective-permute-start(bf16[512,2048]{1,0:T(8,128)(2,1)} %convolution_convert_fusion.23), channel_id=1, source_target_pairs={{0,1},{1,0},{2,3},{3,2},{4,5},{5,4},{6,7},{7,6},{8,9},{9,8},{10,11... | collective-permute-start | bytes 6291464 | tf_op jit(solution)/shard_map/ppermute | solution.py:43
  254.5 29.9 %collective-permute-start.13 = (bf16[512,2048]{1,0:T(8,128)(2,1)}, bf16[512,2048]{1,0:T(8,128)(2,1)}, u32[]{:S(2)}, u32[]{:S(2)}) collective-permute-start(bf16[512,2048]{1,0:T(8,128)(2,1)} %convolution_convert_fusion.19), channel_id=1, source_target_pairs={{0,1},{1,0},{2,3},{3,2},{4,5},{5,4},{6,7},{7,6},{8,9},{9,8},{10,11... | collective-permute-start | bytes 6291464 | tf_op jit(solution)/shard_map/ppermute | solution.py:43
  263.3 244.0 %all-gather.9.cloned.1.call-start = ((), (), s32[]{:S(2)}) async-start(), calls=%async_computation.15 | async-start | bytes 5242880 | tf_op jit(solution)/shard_map/all_gather | solution.py:446
  267.3 33.5 %collective-permute-start.11 = (bf16[256,2048]{1,0:T(8,128)(2,1)}, bf16[256,2048]{1,0:T(8,128)(2,1)}, u32[]{:S(2)}, u32[]{:S(2)}) collective-permute-start(bf16[256,2048]{1,0:T(8,128)(2,1)} %get-tuple-element.145), channel_id=1, source_target_pairs={{0,4},{1,5},{2,6},{3,7},{4,0},{5,1},{6,2},{7,3},{8,12},{9,13},{10,... | collective-permute-start | bytes 3145736 | tf_op jit(solution)/shard_map/ppermute | solution.py:43
  269.1 80.2 %collective-permute-start.33 = (bf16[512,2048]{1,0:T(8,128)(2,1)}, bf16[512,2048]{1,0:T(8,128)(2,1)}, u32[]{:S(2)}, u32[]{:S(2)}) collective-permute-start(bf16[512,2048]{1,0:T(8,128)(2,1)} %bitcast.24), channel_id=1, source_target_pairs={{0,2},{1,3},{2,0},{3,1},{4,6},{5,7},{6,4},{7,5},{8,10},{9,11},{10,... | collective-permute-start | bytes 6291464 | tf_op jit(solution)/shard_map/ppermute | solution.py:43
  270.6 80.3 %collective-permute-start.35 = (bf16[512,2048]{1,0:T(8,128)(2,1)}, bf16[512,2048]{1,0:T(8,128)(2,1)}, u32[]{:S(2)}, u32[]{:S(2)}) collective-permute-start(bf16[512,2048]{1,0:T(8,128)(2,1)} %bitcast.24), channel_id=1, source_target_pairs={{0,4},{1,5},{2,6},{3,7},{4,0},{5,1},{6,2},{7,3},{8,12},{9,13},{10,... | collective-permute-start | bytes 6291464 | tf_op jit(solution)/shard_map/ppermute | solution.py:43
  279.3 251.6 %all-gather.11.cloned.1.call-start = ((), (), s32[]{:S(2)}) async-start(), calls=%async_computation.16 | async-start | bytes 5242880 | tf_op jit(solution)/shard_map/all_gather | solution.py:449
  281.8 71.7 %collective-permute-start.8 = (bf16[512,2048]{1,0:T(8,128)(2,1)}, bf16[512,2048]{1,0:T(8,128)(2,1)}, u32[]{:S(2)}, u32[]{:S(2)}) collective-permute-start(bf16[512,2048]{1,0:T(8,128)(2,1)} %convolution_convert_fusion.25), channel_id=1, source_target_pairs={{0,1},{1,0},{2,3},{3,2},{4,5},{5,4},{6,7},{7,6},{8,9},{9,8},{10,11... | collective-permute-start | bytes 6291464 | tf_op jit(solution)/shard_map/ppermute | solution.py:43
  284.4 61.3 %collective-permute-start.14 = (bf16[256,2048]{1,0:T(8,128)(2,1)S(1)}, bf16[256,2048]{1,0:T(8,128)(2,1)S(1)}, u32[]{:S(2)}, u32[]{:S(2)}) collective-permute-start(bf16[256,2048]{1,0:T(8,128)(2,1)S(1)} %copy-done.36), channel_id=1, source_target_pairs={{0,2},{1,3},{2,0},{3,1},{4,6},{5,7},{6,4},{7,5},{8,10},{9,11},{10,... | collective-permute-start | bytes 3145736 | tf_op jit(solution)/shard_map/ppermute | solution.py:43
  303.9 86.8 %collective-permute-start.12 = (bf16[512,2048]{1,0:T(8,128)(2,1)}, bf16[512,2048]{1,0:T(8,128)(2,1)}, u32[]{:S(2)}, u32[]{:S(2)}) collective-permute-start(bf16[512,2048]{1,0:T(8,128)(2,1)} %pad_maximum_fusion), channel_id=1, source_target_pairs={{0,2},{1,3},{2,0},{3,1},{4,6},{5,7},{6,4},{7,5},{8,10},{9,11},{10,... | collective-permute-start | bytes 6291464 | tf_op jit(solution)/shard_map/ppermute | solution.py:43
  347.6 48.9 %collective-permute-start.15 = (bf16[512,2048]{1,0:T(8,128)(2,1)}, bf16[512,2048]{1,0:T(8,128)(2,1)}, u32[]{:S(2)}, u32[]{:S(2)}) collective-permute-start(bf16[512,2048]{1,0:T(8,128)(2,1)} %pad_maximum_fusion.1), channel_id=1, source_target_pairs={{0,4},{1,5},{2,6},{3,7},{4,0},{5,1},{6,2},{7,3},{8,12},{9,13},{10,... | collective-permute-start | bytes 6291464 | tf_op jit(solution)/shard_map/ppermute | solution.py:43
  349.3 75.6 %collective-permute-start.32 = (bf16[512,2048]{1,0:T(8,128)(2,1)}, bf16[512,2048]{1,0:T(8,128)(2,1)}, u32[]{:S(2)}, u32[]{:S(2)}) collective-permute-start(bf16[512,2048]{1,0:T(8,128)(2,1)} %bitcast.24), channel_id=1, source_target_pairs={{0,1},{1,0},{2,3},{3,2},{4,5},{5,4},{6,7},{7,6},{8,9},{9,8},{10,11... | collective-permute-start | bytes 6291464 | tf_op jit(solution)/shard_map/ppermute | solution.py:43
  350.9 66.4 %collective-permute-start.37 = (bf16[256,2048]{1,0:T(8,128)(2,1)S(1)}, bf16[256,2048]{1,0:T(8,128)(2,1)}, u32[]{:S(2)}, u32[]{:S(2)}) collective-permute-start(bf16[256,2048]{1,0:T(8,128)(2,1)S(1)} %slice.347), channel_id=1, source_target_pairs={{0,4},{1,5},{2,6},{3,7},{4,0},{5,1},{6,2},{7,3},{8,12},{9,13},{10,... | collective-permute-start | bytes 3145736 | tf_op jit(solution)/shard_map/ppermute | solution.py:43
  353.5 65.2 %collective-permute-start.38 = (bf16[256,2048]{1,0:T(8,128)(2,1)S(1)}, bf16[256,2048]{1,0:T(8,128)(2,1)S(1)}, u32[]{:S(2)}, u32[]{:S(2)}) collective-permute-start(bf16[256,2048]{1,0:T(8,128)(2,1)S(1)} %slice.348), channel_id=1, source_target_pairs={{0,2},{1,3},{2,0},{3,1},{4,6},{5,7},{6,4},{7,5},{8,10},{9,11},{10,... | collective-permute-start | bytes 3145736 | tf_op jit(solution)/shard_map/ppermute | solution.py:43
  405.8 51.8 %collective-permute-start.17 = (bf16[512,2048]{1,0:T(8,128)(2,1)}, bf16[512,2048]{1,0:T(8,128)(2,1)S(1)}, u32[]{:S(2)}, u32[]{:S(2)}) collective-permute-start(bf16[512,2048]{1,0:T(8,128)(2,1)} %get-tuple-element.130), channel_id=1, source_target_pairs={{0,2},{1,3},{2,0},{3,1},{4,6},{5,7},{6,4},{7,5},{8,10},{9,11},{10,... | collective-permute-start | bytes 6291464 | tf_op jit(solution)/shard_map/ppermute | solution.py:43
  405.9 51.7 %collective-permute-start.34 = (bf16[512,2048]{1,0:T(8,128)(2,1)}, bf16[512,2048]{1,0:T(8,128)(2,1)}, u32[]{:S(2)}, u32[]{:S(2)}) collective-permute-start(bf16[512,2048]{1,0:T(8,128)(2,1)} %collective-permute-done.33), channel_id=1, source_target_pairs={{0,1},{1,0},{2,3},{3,2},{4,5},{5,4},{6,7},{7,6},{8,9},{9,8},{10,11... | collective-permute-start | bytes 6291464 | tf_op jit(solution)/shard_map/ppermute | solution.py:43
  417.2 48.7 %collective-permute-start.19 = (bf16[512,2048]{1,0:T(8,128)(2,1)}, bf16[512,2048]{1,0:T(8,128)(2,1)}, u32[]{:S(2)}, u32[]{:S(2)}) collective-permute-start(bf16[512,2048]{1,0:T(8,128)(2,1)} %get-tuple-element.130), channel_id=1, source_target_pairs={{0,4},{1,5},{2,6},{3,7},{4,0},{5,1},{6,2},{7,3},{8,12},{9,13},{10,... | collective-permute-start | bytes 6291464 | tf_op jit(solution)/shard_map/ppermute | solution.py:43
  418.7 49.4 %collective-permute-start.36 = (bf16[512,2048]{1,0:T(8,128)(2,1)}, bf16[512,2048]{1,0:T(8,128)(2,1)}, u32[]{:S(2)}, u32[]{:S(2)}) collective-permute-start(bf16[512,2048]{1,0:T(8,128)(2,1)} %collective-permute-done.35), channel_id=1, source_target_pairs={{0,1},{1,0},{2,3},{3,2},{4,5},{5,4},{6,7},{7,6},{8,9},{9,8},{10,11... | collective-permute-start | bytes 6291464 | tf_op jit(solution)/shard_map/ppermute | solution.py:43
  418.7 717.7 %reduce-scatter.9.cloned.1.call-start = ((), (), s32[]{:S(2)}) async-start(), calls=%async_computation.19 | async-start | bytes 5242880 | tf_op jit(solution)/shard_map/reduce_scatter | solution.py:511
  424.9 67.6 %collective-permute-start.39 = (bf16[512,2048]{1,0:T(8,128)(2,1)S(1)}, bf16[512,2048]{1,0:T(8,128)(2,1)S(1)}, u32[]{:S(2)}, u32[]{:S(2)}) collective-permute-start(bf16[512,2048]{1,0:T(8,128)(2,1)S(1)} %pad_maximum_fusion.5), channel_id=1, source_target_pairs={{0,1},{1,0},{2,3},{3,2},{4,5},{5,4},{6,7},{7,6},{8,9},{9,8},{10,11... | collective-permute-start | bytes 6291464 | tf_op jit(solution)/shard_map/ppermute | solution.py:43
  457.5 36.6 %collective-permute-start.16 = (bf16[512,2048]{1,0:T(8,128)(2,1)}, bf16[512,2048]{1,0:T(8,128)(2,1)S(1)}, u32[]{:S(2)}, u32[]{:S(2)}) collective-permute-start(bf16[512,2048]{1,0:T(8,128)(2,1)} %get-tuple-element.130), channel_id=1, source_target_pairs={{0,1},{1,0},{2,3},{3,2},{4,5},{5,4},{6,7},{7,6},{8,9},{9,8},{10,11... | collective-permute-start | bytes 6291464 | tf_op jit(solution)/shard_map/ppermute | solution.py:43
  457.6 28.2 %collective-permute-start.21 = (bf16[256,2048]{1,0:T(8,128)(2,1)S(1)}, bf16[256,2048]{1,0:T(8,128)(2,1)S(1)}, u32[]{:S(2)}, u32[]{:S(2)}) collective-permute-start(bf16[256,2048]{1,0:T(8,128)(2,1)S(1)} %slice.329), channel_id=1, source_target_pairs={{0,4},{1,5},{2,6},{3,7},{4,0},{5,1},{6,2},{7,3},{8,12},{9,13},{10,... | collective-permute-start | bytes 3145736 | tf_op jit(solution)/shard_map/ppermute | solution.py:43
  467.2 25.0 %collective-permute-start.22 = (bf16[256,2048]{1,0:T(8,128)(2,1)S(1)}, bf16[256,2048]{1,0:T(8,128)(2,1)S(1)}, u32[]{:S(2)}, u32[]{:S(2)}) collective-permute-start(bf16[256,2048]{1,0:T(8,128)(2,1)S(1)} %slice.330), channel_id=1, source_target_pairs={{0,2},{1,3},{2,0},{3,1},{4,6},{5,7},{6,4},{7,5},{8,10},{9,11},{10,... | collective-permute-start | bytes 3145736 | tf_op jit(solution)/shard_map/ppermute | solution.py:43
  468.1 29.1 %collective-permute-start.18 = (bf16[512,2048]{1,0:T(8,128)(2,1)S(1)}, bf16[512,2048]{1,0:T(8,128)(2,1)S(1)}, u32[]{:S(2)}, u32[]{:S(2)}) collective-permute-start(bf16[512,2048]{1,0:T(8,128)(2,1)S(1)} %collective-permute-done.17), channel_id=1, source_target_pairs={{0,1},{1,0},{2,3},{3,2},{4,5},{5,4},{6,7},{7,6},{8,9},{9,8},{10,11... | collective-permute-start | bytes 6291464 | tf_op jit(solution)/shard_map/ppermute | solution.py:43
  574.0 40.0 %collective-permute-start.25 = (bf16[512,2048]{1,0:T(8,128)(2,1)S(1)}, bf16[512,2048]{1,0:T(8,128)(2,1)S(1)}, u32[]{:S(2)}, u32[]{:S(2)}) collective-permute-start(bf16[512,2048]{1,0:T(8,128)(2,1)S(1)} %convolution_convert_fusion.15), channel_id=1, source_target_pairs={{0,1},{1,0},{2,3},{3,2},{4,5},{5,4},{6,7},{7,6},{8,9},{9,8},{10,11... | collective-permute-start | bytes 6291464 | tf_op jit(solution)/shard_map/ppermute | solution.py:43
  578.2 27.5 %collective-permute-start.26 = (bf16[512,2048]{1,0:T(8,128)(2,1)S(1)}, bf16[512,2048]{1,0:T(8,128)(2,1)S(1)}, u32[]{:S(2)}, u32[]{:S(2)}) collective-permute-start(bf16[512,2048]{1,0:T(8,128)(2,1)S(1)} %convolution_convert_fusion.13), channel_id=1, source_target_pairs={{0,1},{1,0},{2,3},{3,2},{4,5},{5,4},{6,7},{7,6},{8,9},{9,8},{10,11... | collective-permute-start | bytes 6291464 | tf_op jit(solution)/shard_map/ppermute | solution.py:43
  583.4 34.4 %collective-permute-start.29 = (bf16[512,2048]{1,0:T(8,128)(2,1)}, bf16[512,2048]{1,0:T(8,128)(2,1)S(1)}, u32[]{:S(2)}, u32[]{:S(2)}) collective-permute-start(bf16[512,2048]{1,0:T(8,128)(2,1)} %convolution_convert_fusion.11), channel_id=1, source_target_pairs={{0,1},{1,0},{2,3},{3,2},{4,5},{5,4},{6,7},{7,6},{8,9},{9,8},{10,11... | collective-permute-start | bytes 6291464 | tf_op jit(solution)/shard_map/ppermute | solution.py:43
  587.6 34.4 %collective-permute-start.41 = (bf16[512,2048]{1,0:T(8,128)(2,1)S(1)}, bf16[512,2048]{1,0:T(8,128)(2,1)S(1)}, u32[]{:S(2)}, u32[]{:S(2)}) collective-permute-start(bf16[512,2048]{1,0:T(8,128)(2,1)S(1)} %convolution_convert_fusion.7), channel_id=1, source_target_pairs={{0,1},{1,0},{2,3},{3,2},{4,5},{5,4},{6,7},{7,6},{8,9},{9,8},{10,11... | collective-permute-start | bytes 6291464 | tf_op jit(solution)/shard_map/ppermute | solution.py:43
  609.4 83.7 %collective-permute-start.40 = (bf16[512,2048]{1,0:T(8,128)(2,1)S(1)}, bf16[512,2048]{1,0:T(8,128)(2,1)S(1)}, u32[]{:S(2)}, u32[]{:S(2)}) collective-permute-start(bf16[512,2048]{1,0:T(8,128)(2,1)S(1)} %convolution_convert_fusion.9), channel_id=1, source_target_pairs={{0,1},{1,0},{2,3},{3,2},{4,5},{5,4},{6,7},{7,6},{8,9},{9,8},{10,11... | collective-permute-start | bytes 6291464 | tf_op jit(solution)/shard_map/ppermute | solution.py:43
  614.0 126.4 %collective-permute-start.24 = (bf16[512,2048]{1,0:T(8,128)(2,1)}, bf16[512,2048]{1,0:T(8,128)(2,1)S(1)}, u32[]{:S(2)}, u32[]{:S(2)}) collective-permute-start(bf16[512,2048]{1,0:T(8,128)(2,1)} %convolution_convert_fusion.17), channel_id=1, source_target_pairs={{0,1},{1,0},{2,3},{3,2},{4,5},{5,4},{6,7},{7,6},{8,9},{9,8},{10,11... | collective-permute-start | bytes 6291464 | tf_op jit(solution)/shard_map/ppermute | solution.py:43
  617.7 51.5 %collective-permute-start.27 = (bf16[256,2048]{1,0:T(8,128)(2,1)S(1)}, bf16[256,2048]{1,0:T(8,128)(2,1)S(1)}, u32[]{:S(2)}, u32[]{:S(2)}) collective-permute-start(bf16[256,2048]{1,0:T(8,128)(2,1)S(1)} %get-tuple-element.143), channel_id=1, source_target_pairs={{0,4},{1,5},{2,6},{3,7},{4,0},{5,1},{6,2},{7,3},{8,12},{9,13},{10,... | collective-permute-start | bytes 3145736 | tf_op jit(solution)/shard_map/ppermute | solution.py:43
  622.0 43.9 %collective-permute-start.43 = (bf16[256,2048]{1,0:T(8,128)(2,1)S(1)}, bf16[256,2048]{1,0:T(8,128)(2,1)S(1)}, u32[]{:S(2)}, u32[]{:S(2)}) collective-permute-start(bf16[256,2048]{1,0:T(8,128)(2,1)S(1)} %get-tuple-element.141), channel_id=1, source_target_pairs={{0,4},{1,5},{2,6},{3,7},{4,0},{5,1},{6,2},{7,3},{8,12},{9,13},{10,... | collective-permute-start | bytes 3145736 | tf_op jit(solution)/shard_map/ppermute | solution.py:43
  627.3 39.7 %collective-permute-start.46 = (bf16[256,2048]{1,0:T(8,128)(2,1)S(1)}, bf16[256,2048]{1,0:T(8,128)(2,1)S(1)}, u32[]{:S(2)}, u32[]{:S(2)}) collective-permute-start(bf16[256,2048]{1,0:T(8,128)(2,1)S(1)} %get-tuple-element.142), channel_id=1, source_target_pairs={{0,2},{1,3},{2,0},{3,1},{4,6},{5,7},{6,4},{7,5},{8,10},{9,11},{10,... | collective-permute-start | bytes 3145736 | tf_op jit(solution)/shard_map/ppermute | solution.py:43
  665.8 26.1 %collective-permute-start.30 = (bf16[256,2048]{1,0:T(8,128)(2,1)S(1)}, bf16[256,2048]{1,0:T(8,128)(2,1)S(1)}, u32[]{:S(2)}, u32[]{:S(2)}) collective-permute-start(bf16[256,2048]{1,0:T(8,128)(2,1)S(1)} %get-tuple-element.144), channel_id=1, source_target_pairs={{0,2},{1,3},{2,0},{3,1},{4,6},{5,7},{6,4},{7,5},{8,10},{9,11},{10,... | collective-permute-start | bytes 3145736 | tf_op jit(solution)/shard_map/ppermute | solution.py:43
  667.0 69.8 %collective-permute-start.44 = (bf16[512,2048]{1,0:T(8,128)(2,1)S(1)}, bf16[512,2048]{1,0:T(8,128)(2,1)S(1)}, u32[]{:S(2)}, u32[]{:S(2)}) collective-permute-start(bf16[512,2048]{1,0:T(8,128)(2,1)S(1)} %pad_maximum_fusion.6), channel_id=1, source_target_pairs={{0,2},{1,3},{2,0},{3,1},{4,6},{5,7},{6,4},{7,5},{8,10},{9,11},{10,... | collective-permute-start | bytes 6291464 | tf_op jit(solution)/shard_map/ppermute | solution.py:43
  669.2 67.6 %collective-permute-start.47 = (bf16[512,2048]{1,0:T(8,128)(2,1)S(1)}, bf16[512,2048]{1,0:T(8,128)(2,1)S(1)}, u32[]{:S(2)}, u32[]{:S(2)}) collective-permute-start(bf16[512,2048]{1,0:T(8,128)(2,1)S(1)} %pad_maximum_fusion.7), channel_id=1, source_target_pairs={{0,4},{1,5},{2,6},{3,7},{4,0},{5,1},{6,2},{7,3},{8,12},{9,13},{10,... | collective-permute-start | bytes 6291464 | tf_op jit(solution)/shard_map/ppermute | solution.py:43
  691.9 88.6 %collective-permute-start.28 = (bf16[512,2048]{1,0:T(8,128)(2,1)S(1)}, bf16[512,2048]{1,0:T(8,128)(2,1)S(1)}, u32[]{:S(2)}, u32[]{:S(2)}) collective-permute-start(bf16[512,2048]{1,0:T(8,128)(2,1)S(1)} %pad_maximum_fusion.3), channel_id=1, source_target_pairs={{0,2},{1,3},{2,0},{3,1},{4,6},{5,7},{6,4},{7,5},{8,10},{9,11},{10,... | collective-permute-start | bytes 6291464 | tf_op jit(solution)/shard_map/ppermute | solution.py:43
  693.1 87.4 %collective-permute-start.31 = (bf16[512,2048]{1,0:T(8,128)(2,1)S(1)}, bf16[512,2048]{1,0:T(8,128)(2,1)S(1)}, u32[]{:S(2)}, u32[]{:S(2)}) collective-permute-start(bf16[512,2048]{1,0:T(8,128)(2,1)S(1)} %pad_maximum_fusion.4), channel_id=1, source_target_pairs={{0,4},{1,5},{2,6},{3,7},{4,0},{5,1},{6,2},{7,3},{8,12},{9,13},{10,... | collective-permute-start | bytes 6291464 | tf_op jit(solution)/shard_map/ppermute | solution.py:43
  789.4 46.5 %collective-permute-start.49 = (bf16[512,2048]{1,0:T(8,128)(2,1)S(1)}, bf16[512,2048]{1,0:T(8,128)(2,1)}, u32[]{:S(2)}, u32[]{:S(2)}) collective-permute-start(bf16[512,2048]{1,0:T(8,128)(2,1)S(1)} %get-tuple-element.120), channel_id=1, source_target_pairs={{0,2},{1,3},{2,0},{3,1},{4,6},{5,7},{6,4},{7,5},{8,10},{9,11},{10,... | collective-permute-start | bytes 6291464 | tf_op jit(solution)/shard_map/ppermute | solution.py:43
  790.0 46.2 %collective-permute-start.51 = (bf16[512,2048]{1,0:T(8,128)(2,1)S(1)}, bf16[512,2048]{1,0:T(8,128)(2,1)}, u32[]{:S(2)}, u32[]{:S(2)}) collective-permute-start(bf16[512,2048]{1,0:T(8,128)(2,1)S(1)} %get-tuple-element.120), channel_id=1, source_target_pairs={{0,4},{1,5},{2,6},{3,7},{4,0},{5,1},{6,2},{7,3},{8,12},{9,13},{10,... | collective-permute-start | bytes 6291464 | tf_op jit(solution)/shard_map/ppermute | solution.py:43
  790.4 74.3 %collective-permute-start.48 = (bf16[512,2048]{1,0:T(8,128)(2,1)S(1)}, bf16[512,2048]{1,0:T(8,128)(2,1)}, u32[]{:S(2)}, u32[]{:S(2)}) collective-permute-start(bf16[512,2048]{1,0:T(8,128)(2,1)S(1)} %get-tuple-element.120), channel_id=1, source_target_pairs={{0,1},{1,0},{2,3},{3,2},{4,5},{5,4},{6,7},{7,6},{8,9},{9,8},{10,11... | collective-permute-start | bytes 6291464 | tf_op jit(solution)/shard_map/ppermute | solution.py:43
  835.9 35.8 %collective-permute-start.50 = (bf16[512,2048]{1,0:T(8,128)(2,1)}, bf16[512,2048]{1,0:T(8,128)(2,1)}, u32[]{:S(2)}, u32[]{:S(2)}) collective-permute-start(bf16[512,2048]{1,0:T(8,128)(2,1)} %collective-permute-done.49), channel_id=1, source_target_pairs={{0,1},{1,0},{2,3},{3,2},{4,5},{5,4},{6,7},{7,6},{8,9},{9,8},{10,11... | collective-permute-start | bytes 6291464 | tf_op jit(solution)/shard_map/ppermute | solution.py:43
  836.1 41.9 %collective-permute-start.52 = (bf16[512,2048]{1,0:T(8,128)(2,1)}, bf16[512,2048]{1,0:T(8,128)(2,1)}, u32[]{:S(2)}, u32[]{:S(2)}) collective-permute-start(bf16[512,2048]{1,0:T(8,128)(2,1)} %collective-permute-done.51), channel_id=1, source_target_pairs={{0,1},{1,0},{2,3},{3,2},{4,5},{5,4},{6,7},{7,6},{8,9},{9,8},{10,11... | collective-permute-start | bytes 6291464 | tf_op jit(solution)/shard_map/ppermute | solution.py:43
  860.1 353.8 %reduce-scatter.5.cloned.1.call-start = ((), (), s32[]{:S(2)}) async-start(), calls=%async_computation.17 | async-start | bytes 3932160 | tf_op jit(solution)/shard_map/reduce_scatter | solution.py:571
  861.5 25.4 %collective-permute-start.53 = (bf16[256,2048]{1,0:T(8,128)(2,1)S(1)}, bf16[256,2048]{1,0:T(8,128)(2,1)S(1)}, u32[]{:S(2)}, u32[]{:S(2)}) collective-permute-start(bf16[256,2048]{1,0:T(8,128)(2,1)S(1)} %slice.363), channel_id=1, source_target_pairs={{0,4},{1,5},{2,6},{3,7},{4,0},{5,1},{6,2},{7,3},{8,12},{9,13},{10,... | collective-permute-start | bytes 3145736 | tf_op jit(solution)/shard_map/ppermute | solution.py:43
  863.4 24.9 %collective-permute-start.54 = (bf16[256,2048]{1,0:T(8,128)(2,1)S(1)}, bf16[256,2048]{1,0:T(8,128)(2,1)S(1)}, u32[]{:S(2)}, u32[]{:S(2)}) collective-permute-start(bf16[256,2048]{1,0:T(8,128)(2,1)S(1)} %slice.364), channel_id=1, source_target_pairs={{0,2},{1,3},{2,0},{3,1},{4,6},{5,7},{6,4},{7,5},{8,10},{9,11},{10,... | collective-permute-start | bytes 3145736 | tf_op jit(solution)/shard_map/ppermute | solution.py:43
  1016.6 201.1 %reduce-scatter.11.cloned.1.call-start = ((), (), s32[]{:S(2)}) async-start(), calls=%async_computation.20 | async-start | bytes 5242880 | tf_op jit(solution)/shard_map/reduce_scatter | solution.py:509
  1059.4 77.0 %all-to-all-start.4 = ((bf16[8,32,2048]{2,1,0:T(8,128)(2,1)}), bf16[8,32,2048]{2,1,0:T(8,128)(2,1)S(1)}, u32[]{:S(2)}, u32[]{:S(2)}) async-start(bf16[8,32,2048]{2,1,0:T(8,128)(2,1)} %bitcast.26), calls=%async_computation.4 | async-start | bytes 2097152 | tf_op jit(solution)/shard_map/all_to_all | solution.py:560
  1063.4 163.7 %reduce-scatter.7.cloned.1.call-start = ((), (), s32[]{:S(2)}) async-start(), calls=%async_computation.18 | async-start | bytes 1310720 | tf_op jit(solution)/shard_map/reduce_scatter | solution.py:534
  1069.2 30.0 %collective-permute-start.57 = (bf16[512,2048]{1,0:T(8,128)(2,1)}, bf16[512,2048]{1,0:T(8,128)(2,1)}, u32[]{:S(2)}, u32[]{:S(2)}) collective-permute-start(bf16[512,2048]{1,0:T(8,128)(2,1)} %convolution_convert_fusion.31), channel_id=1, source_target_pairs={{0,1},{1,0},{2,3},{3,2},{4,5},{5,4},{6,7},{7,6},{8,9},{9,8},{10,11... | collective-permute-start | bytes 6291464 | tf_op jit(solution)/shard_map/ppermute | solution.py:43
  1083.6 62.5 %collective-permute-start.56 = (bf16[512,2048]{1,0:T(8,128)(2,1)}, bf16[512,2048]{1,0:T(8,128)(2,1)}, u32[]{:S(2)}, u32[]{:S(2)}) collective-permute-start(bf16[512,2048]{1,0:T(8,128)(2,1)} %convolution_convert_fusion.33), channel_id=1, source_target_pairs={{0,1},{1,0},{2,3},{3,2},{4,5},{5,4},{6,7},{7,6},{8,9},{9,8},{10,11... | collective-permute-start | bytes 6291464 | tf_op jit(solution)/shard_map/ppermute | solution.py:43
  1095.7 25.6 %collective-permute-start.59 = (bf16[256,2048]{1,0:T(8,128)(2,1)S(1)}, bf16[256,2048]{1,0:T(8,128)(2,1)S(1)}, u32[]{:S(2)}, u32[]{:S(2)}) collective-permute-start(bf16[256,2048]{1,0:T(8,128)(2,1)S(1)} %get-tuple-element.139), channel_id=1, source_target_pairs={{0,4},{1,5},{2,6},{3,7},{4,0},{5,1},{6,2},{7,3},{8,12},{9,13},{10,... | collective-permute-start | bytes 3145736 | tf_op jit(solution)/shard_map/ppermute | solution.py:43
  1097.8 27.1 %collective-permute-start.62 = (bf16[256,2048]{1,0:T(8,128)(2,1)S(1)}, bf16[256,2048]{1,0:T(8,128)(2,1)S(1)}, u32[]{:S(2)}, u32[]{:S(2)}) collective-permute-start(bf16[256,2048]{1,0:T(8,128)(2,1)S(1)} %get-tuple-element.140), channel_id=1, source_target_pairs={{0,2},{1,3},{2,0},{3,1},{4,6},{5,7},{6,4},{7,5},{8,10},{9,11},{10,... | collective-permute-start | bytes 3145736 | tf_op jit(solution)/shard_map/ppermute | solution.py:43
  1123.3 48.8 %collective-permute-start.60 = (bf16[512,2048]{1,0:T(8,128)(2,1)}, bf16[512,2048]{1,0:T(8,128)(2,1)}, u32[]{:S(2)}, u32[]{:S(2)}) collective-permute-start(bf16[512,2048]{1,0:T(8,128)(2,1)} %pad_maximum_fusion.8), channel_id=1, source_target_pairs={{0,2},{1,3},{2,0},{3,1},{4,6},{5,7},{6,4},{7,5},{8,10},{9,11},{10,... | collective-permute-start | bytes 6291464 | tf_op jit(solution)/shard_map/ppermute | solution.py:43
  1126.9 51.3 %collective-permute-start.63 = (bf16[512,2048]{1,0:T(8,128)(2,1)}, bf16[512,2048]{1,0:T(8,128)(2,1)}, u32[]{:S(2)}, u32[]{:S(2)}) collective-permute-start(bf16[512,2048]{1,0:T(8,128)(2,1)} %pad_maximum_fusion.9), channel_id=1, source_target_pairs={{0,4},{1,5},{2,6},{3,7},{4,0},{5,1},{6,2},{7,3},{8,12},{9,13},{10,... | collective-permute-start | bytes 6291464 | tf_op jit(solution)/shard_map/ppermute | solution.py:43
  1137.5 50.1 %all-to-all-start.8 = ((bf16[8,64,1024]{2,1,0:T(8,128)(2,1)}), bf16[8,64,1024]{2,1,0:T(8,128)(2,1)}, u32[]{:S(2)}, u32[]{:S(2)}) async-start(bf16[8,64,1024]{2,1,0:T(8,128)(2,1)} %bitcast.196), calls=%async_computation.11 | async-start | bytes 2097152 | tf_op jit(solution)/shard_map/all_to_all | solution.py:512
  (111 other events, 2987.9 us)
Sparse Core Ops, SparseCore 0:
  33.1 64.9 all-gather.4
  99.6 26.4 all-gather.6
  279.4 79.0 all-gather.8
  418.9 79.2 all-gather.10
  860.2 75.9 reduce-scatter.8
  1016.7 60.7 reduce-scatter.4
  1080.0 76.7 reduce-scatter.10
  1159.1 27.6 reduce-scatter.6

commit v2 on v1

v2 whole, which is shorter than its diff:
```python
import functools
import math

import jax
import jax.numpy as jnp
from jax import lax
from jax.experimental import pallas as pl
from jax.experimental.pallas import tpu as pltpu
from jax.sharding import PartitionSpec as P

HEAD = 64
SUMM = 50

epsilon = 1e-05
masked_score = -1e30
bf16 = jnp.bfloat16
f32 = jnp.float32
BOTH = ("dp", "fsdp")
score_scale = 1.0 / math.sqrt(HEAD)

ROWS_BY_ROWS = (((1,), (0,)), ((), ()))
ROWS_BY_COLS = (((1,), (1,)), ((), ()))
COLS_BY_ROWS = (((0,), (0,)), ((), ()))


def dot(left, right, dims):
    return lax.dot_general(left, right, dims, preferred_element_type=f32)


def layer_norm(values, gains, shifts):
    centre = jnp.mean(values, axis=-1, keepdims=True)
    centred = values - centre
    spread = jnp.mean(centred * centred, axis=-1, keepdims=True)
    return centred * lax.rsqrt(spread + epsilon) * gains + shifts


def gelu_tanh(values):
    return jax.nn.gelu(values, approximate=True)


def slot_order(devices):
    if devices == 8:
        return [
            (0, 0), (0, 1), (1, 0), (1, 1),
            (2, 0), (3, 0), (4, 1), (5, 1),
            (2, 1), (3, 1), (4, 0), (5, 0),
            (6, 0), (6, 1), (7, 0), (7, 1),
        ]
    return [(m, h) for m in range(devices) for h in range(2)]


def slot_groups(devices):
    return len(slot_order(devices)) // 4


def in_groups(items):
    return [items[n : n + 4] for n in range(0, len(items), 4)]


def swapped(x, bit):
    devices = lax.axis_size("fsdp")
    return lax.ppermute(x, "fsdp", [(i, i ^ bit) for i in range(devices)])


def sent(own):
    if lax.axis_size("fsdp") != 8:
        return None
    x0 = swapped(own[0], 2)
    y1 = swapped(own[1], 4)
    x1 = swapped(own[1], 2)
    y0 = swapped(own[0], 4)
    return x0, y1, x1, y0


def passed_on(own, hops, earlier=()):
    devices = lax.axis_size("fsdp")
    if devices != 8:
        pieces = [own]
        bit = 1
        while bit < devices:
            pieces = pieces + [[swapped(half, bit) for half in piece] for piece in pieces]
            bit *= 2
        return in_groups([half for piece in pieces for half in piece])
    x0, y1, x1, y0 = hops
    if earlier:
        x0, y1 = after((x0, y1), *earlier)
    a0 = swapped(x0, 4)
    a1 = swapped(y1, 2)
    return [
        [own[0], own[1], swapped(own[0], 1), swapped(own[1], 1)],
        [x0, swapped(x0, 1), y1, swapped(y1, 1)],
        [x1, swapped(x1, 1), y0, swapped(y0, 1)],
        [a0, a1, swapped(a0, 1), swapped(a1, 1)],
    ]


def total(*terms):
    result = terms[0].astype(f32)
    for term in terms[1:]:
        result = result + term.astype(f32)
    return result


def paired(own, other):
    return total(own, swapped(other, 1)).astype(bf16)


def plain_scattered_sum(groups):
    flat = [half for group in groups for half in group]
    bit = len(flat) // 4
    while bit > 1:
        flat = [
            total(flat[n], swapped(flat[n + 2 * bit], bit)).astype(bf16) for n in range(2 * bit)
        ]
        bit //= 2
    return [total(flat[h], swapped(flat[h + 2], 1)) for h in range(2)]


def scattered_sum(make, groups, first=None, second=None):
    if groups != 4:
        made = [make(g, ()) for g in range(groups)]
        for extra in (first, second):
            if extra:
                done, use = extra(())
                use(done)
        return plain_scattered_sum(made)
    later = make(2, ())
    x1 = paired(later[0], later[1])
    y0 = paired(later[2], later[3])
    if first:
        done, use = first((x1, y0))
        x1, y0, done = after((swapped(x1, 2), swapped(y0, 4), done))
        use(done)
        far = make(3, (x1, y0))
    else:
        far = make(3, (x1, y0))
        far, x1, y0 = after((far, swapped(x1, 2), swapped(y0, 4)))
    a0 = paired(far[0], far[2])
    a1 = paired(far[1], far[3])
    near = make(1, (a0, a1))
    own = make(0, (a0, a1, near[0]))
    own, a0, a1 = after((own, swapped(a0, 4), swapped(a1, 2)))
    x0 = total(near[0], swapped(near[1], 1), a0).astype(bf16)
    y1 = total(near[2], swapped(near[3], 1), a1).astype(bf16)
    mine = [total(own[0], swapped(own[2], 1), y0), total(own[1], swapped(own[3], 1), x1)]
    done, use = second((x0, y1)) if second else ((), None)
    x0, y1, mine, done = after((swapped(x0, 2), swapped(y1, 4), mine, done))
    if use:
        use(done)
    return [total(mine[0], x0), total(mine[1], y1)]


def after(values, *earlier):
    flat, tree = jax.tree.flatten(values)
    flat = lax.optimization_barrier(tuple(flat) + earlier)[: len(flat)]
    return jax.tree.unflatten(tree, flat)


def held(shape, place=None):
    where = place or (0,) * len(shape)
    return pl.BlockSpec(shape, lambda *_: where, pipeline_mode=pl.Buffered(1))


anywhere = pl.BlockSpec(memory_space=pl.ANY)


def half_rows(chunk, width):
    return pl.BlockSpec((chunk, width), lambda s: (s, 0))


def group_rows(group, chunk, width):
    return pl.BlockSpec((4, chunk, width), lambda s: (group, s, 0))


def group_call(kernel, name, steps, ins, specs, outs, out_specs, earlier, scratch, flops, moved):
    aliases = {len(ins) + n: n for n in range(len(earlier))}
    made = pl.pallas_call(
        functools.partial(kernel, len(ins), len(earlier)),
        grid=(steps,),
        in_specs=specs + [anywhere] * len(earlier),
        out_specs=out_specs,
        out_shape=outs,
        scratch_shapes=scratch,
        input_output_aliases=aliases,
        compiler_params=pltpu.CompilerParams(
            dimension_semantics=("arbitrary",), vmem_limit_bytes=52 * 2**20
        ),
        cost_estimate=pl.CostEstimate(flops=flops, bytes_accessed=moved, transcendentals=0),
        name=name,
    )(*ins, *earlier)
    return list(made)


def split_refs(n_ins, n_earlier, refs):
    return refs[:n_ins], refs[n_ins + n_earlier :]


def norm_kernel(n_ins, n_earlier, *refs):
    ins, rest = split_refs(n_ins, n_earlier, refs)
    gain_ref, shift_ref = ins[4:]
    for n in range(4):
        rest[0][n] = layer_norm(
            ins[n][...].astype(f32), gain_ref[...], shift_ref[...]
        ).astype(bf16)


def norm_rows(group, halves, gain, shift, earlier, slots):
    half, wide = halves[0].shape
    chunk = half // 2
    return group_call(
        norm_kernel,
        "norm_rows",
        2,
        list(halves) + [gain, shift],
        [half_rows(chunk, wide)] * 4 + [held(gain.shape), held(shift.shape)],
        [jax.ShapeDtypeStruct((slots, half, wide), bf16)],
        [group_rows(group, chunk, wide)],
        earlier,
        [],
        80 * half * wide,
        16 * half * wide,
    )


def triple_kernel(n_ins, n_earlier, *refs):
    (rows_ref, weight_ref, bias_ref), outs = split_refs(n_ins, n_earlier, refs)
    width = outs[0].shape[1]
    made = (dot(rows_ref[...], weight_ref[...], ROWS_BY_ROWS) + bias_ref[...]).astype(bf16)
    for place in range(3):
        outs[place][...] = made[:, place * width : (place + 1) * width]


def triple(first, steps, rows, weight, bias, earlier, count):
    wide = rows.shape[1]
    size = count // slot_groups(lax.axis_size("fsdp"))
    width = weight.shape[1] // 3
    return group_call(
        triple_kernel,
        "triple",
        steps,
        [rows, weight, bias],
        [
            pl.BlockSpec((size, wide), lambda s: (s + first, 0)),
            held(weight.shape),
            held(bias.shape),
        ],
        [jax.ShapeDtypeStruct((count, width), bf16)] * 3,
        [pl.BlockSpec((size, width), lambda s: (s + first, 0))] * 3,
        earlier,
        [],
        6 * steps * size * wide * width,
        2 * steps * size * wide,
    )


def project_kernel(n_ins, n_earlier, *refs):
    ins, rest = split_refs(n_ins, n_earlier, refs)
    weight_ref, outs = ins[-1], rest[:4]
    chunk, wide = outs[0].shape
    parts = [ref[...].reshape(4 * chunk, ref.shape[2]) for ref in ins[:-1]]
    rows = parts[0] if len(parts) == 1 else jnp.concatenate(parts, axis=1)
    by_rows = weight_ref.shape[0] == rows.shape[1] and weight_ref.shape[1] == wide
    tile = min(wide, 512)
    for start in range(0, wide, tile):
        columns = slice(start, start + tile)
        if by_rows:
            made = dot(rows, weight_ref[:, columns], ROWS_BY_ROWS)
        else:
            made = dot(rows, weight_ref[columns, :], ROWS_BY_COLS)
        made = made.astype(bf16)
        for n in range(4):
            outs[n][:, columns] = made[n * chunk : (n + 1) * chunk, :]


def project(group, parts, weight, wide):
    half = parts[0].shape[1]
    chunk = half // 2
    return group_call(
        project_kernel,
        "project",
        2,
        list(parts) + [weight],
        [group_rows(group, chunk, part.shape[2]) for part in parts] + [held(weight.shape)],
        [jax.ShapeDtypeStruct((half, wide), bf16)] * 4,
        [half_rows(chunk, wide)] * 4,
        [],
        [],
        8 * half * weight.size,
        8 * half * wide + 2 * weight.size,
    )


def project_back_kernel(n_ins, n_earlier, *refs):
    ins, rest = split_refs(n_ins, n_earlier, refs)
    weight_ref = ins[4]
    made_ref, kept_ref, rows = rest
    chunk = ins[0].shape[0]
    for n in range(4):
        kept_ref[n] = ins[n][...]
        rows[n * chunk : (n + 1) * chunk, :] = ins[n][...]
    made = dot(rows[...], weight_ref[...], ROWS_BY_COLS).astype(bf16)
    for n in range(4):
        made_ref[n] = made[n * chunk : (n + 1) * chunk, :]


def project_back(group, halves, weight, earlier, slots):
    half, wide = halves[0].shape
    chunk = half // 2
    width = weight.shape[0]
    return group_call(
        project_back_kernel,
        "project_back",
        2,
        list(halves) + [weight],
        [half_rows(chunk, wide)] * 4 + [held(weight.shape)],
        [jax.ShapeDtypeStruct((slots, half, n), bf16) for n in (width, wide)],
        [group_rows(group, chunk, n) for n in (width, wide)],
        earlier,
        [pltpu.VMEM((4 * chunk, wide), bf16)],
        8 * half * weight.size,
        16 * half * wide,
    )


gelu_rate = math.sqrt(2.0 / math.pi)
gelu_cube = 0.044715


def feed_forward_kernel(n_ins, n_earlier, *refs):
    ins, rest = split_refs(n_ins, n_earlier, refs)
    up_ref, shift_ref, down_ref = ins[8:]
    active_ref, grad_ref, rows_ref, grad_rows_ref = rest[:4]
    back = rest[4:8]
    ahead = rest[8:12]
    shift_grad_ref, rows, grad_rows, active, grad_upper = rest[12:]
    chunk, wide = ins[0].shape
    units = up_ref.shape[1]
    for n in range(4):
        r = slice(n * chunk, (n + 1) * chunk)
        rows[r, :] = ins[n][...]
        grad_rows[r, :] = ins[4 + n][...]
        rows_ref[n] = ins[n][...]
        grad_rows_ref[n] = ins[4 + n][...]
    tile = min(units, 512)

    def hidden(t, carry):
        columns = pl.ds(pl.multiple_of(t * tile, tile), tile)
        upper = dot(rows[...], up_ref[:, columns], ROWS_BY_ROWS) + shift_ref[:, columns]
        grad_active = dot(grad_rows[...], down_ref[columns, :], ROWS_BY_COLS)
        square = upper * upper
        bend = jnp.tanh(gelu_rate * upper * (1.0 + gelu_cube * square))
        share = 0.5 * (1.0 + bend)
        slope = share + 0.5 * upper * (1.0 - bend * bend) * (
            gelu_rate * (1.0 + 3.0 * gelu_cube * square)
        )
        made = (upper * share).astype(bf16)
        grad = (grad_active * slope).astype(bf16)
        active[:, columns] = made
        grad_upper[:, columns] = grad
        shift_grad_ref[0, 0:1, columns] = jnp.sum(grad.astype(f32), axis=0, keepdims=True)
        for n in range(4):
            r = slice(n * chunk, (n + 1) * chunk)
            active_ref[n, :, columns] = made[r, :]
            grad_ref[n, :, columns] = grad[r, :]
        return carry

    lax.fori_loop(0, units // tile, hidden, 0)
    step = min(wide, 1024)

    def outer(t, carry):
        columns = pl.ds(pl.multiple_of(t * step, step), step)
        made_back = dot(grad_upper[...], up_ref[columns, :], ROWS_BY_COLS).astype(bf16)
        made_ahead = dot(active[...], down_ref[:, columns], ROWS_BY_ROWS).astype(bf16)
        for n in range(4):
            r = slice(n * chunk, (n + 1) * chunk)
            back[n][:, columns] = made_back[r, :]
            ahead[n][:, columns] = made_ahead[r, :]
        return carry

    lax.fori_loop(0, wide // step, outer, 0)


def feed_forward(group, halves, grad_halves, up, shift, down, earlier, slots):
    half, wide = halves[0].shape
    chunk = half // 2
    units = up.shape[1]
    sizes = (units, units, wide, wide)
    outs = [jax.ShapeDtypeStruct((slots, half, n), bf16) for n in sizes]
    outs += [jax.ShapeDtypeStruct((half, wide), bf16)] * 8
    outs += [jax.ShapeDtypeStruct((2, 8, units), f32)]
    made = group_call(
        feed_forward_kernel,
        "feed_forward",
        2,
        list(halves) + list(grad_halves) + [up, shift, down],
        [half_rows(chunk, wide)] * 8 + [held(up.shape), held(shift.shape), held(down.shape)],
        outs,
        [group_rows(group, chunk, n) for n in sizes]
        + [half_rows(chunk, wide)] * 8
        + [pl.BlockSpec((1, 8, units), lambda s: (s, 0, 0))],
        earlier,
        [pltpu.VMEM((4 * chunk, n), bf16) for n in (wide, wide, units, units)],
        32 * half * wide * units,
        48 * half * wide + 4 * wide * units,
    )
    return made[:4], made[4:8], made[8:12], jnp.sum(made[12][:, 0], axis=0)


def only_head(values, head):
    columns = lax.broadcasted_iota(jnp.int32, values.shape, 1) // HEAD
    return jnp.where(columns == head, values, jnp.zeros_like(values))


def transposed(values):
    return values.astype(f32).T.astype(bf16)


def places_of(plan_ref, blocks, subs, half, j):
    return [
        pl.ds(pl.multiple_of(plan_ref[3 * blocks + subs * j + n] * half, half), half)
        for n in range(subs)
    ]


def rows_of(ref, places):
    parts = [ref[place, :] for place in places]
    return parts[0] if len(parts) == 1 else jnp.concatenate(parts, axis=0)


def cols_of(ref, places):
    parts = [ref[:, place] for place in places]
    return parts[0] if len(parts) == 1 else jnp.concatenate(parts, axis=1)


def attn_forward_kernel(
    block, half, heads, plan_ref, q_ref, k_ref, v_ref, sk_ref, sv_ref, row_ref, o_ref, log_ref,
    q_heads, vt_all, svt, tops, sums, mixed,
):
    i = pl.program_id(0)
    blocks = pl.num_programs(0)
    subs = block // half

    @pl.when(i == 0)
    def _():
        for n in range(v_ref.shape[0] // half):
            r = slice(n * half, (n + 1) * half)
            vt_all[:, r] = transposed(v_ref[r, :])
        svt[...] = transposed(sv_ref[...])

    mine = places_of(plan_ref, blocks, subs, half, i)
    q = rows_of(q_ref, mine).astype(f32) * score_scale
    for h in range(heads):
        q_heads[h] = only_head(q, h).astype(bf16)
    tops[...] = jnp.full_like(tops, masked_score)
    sums[...] = jnp.zeros_like(sums)
    mixed[...] = jnp.zeros_like(mixed)
    lowest = row_ref[0:1, :]
    highest = row_ref[1:2, :]
    summ_end = row_ref[2:3, :]
    me = row_ref[3:4, :]

    def step(keys, values_t, mask):
        each = range(heads)
        scores = [dot(keys, q_heads[h], ROWS_BY_COLS) for h in each]
        if mask is not None:
            scores = [jnp.where(mask, one, masked_score) for one in scores]
        before = [tops[h : h + 1, :] for h in each]
        top = [jnp.maximum(before[h], jnp.max(scores[h], axis=0, keepdims=True)) for h in each]
        weights = [jnp.exp(scores[h] - top[h]) for h in each]
        keep = [jnp.exp(before[h] - top[h]) for h in each]
        added = [jnp.sum(weights[h], axis=0, keepdims=True) for h in each]
        totals = [keep[h] * sums[h : h + 1, :] + added[h] for h in each]
        part_of = [slice(h * HEAD, (h + 1) * HEAD) for h in each]
        more = [dot(values_t[part_of[h], :], weights[h].astype(bf16), ROWS_BY_ROWS) for h in each]
        result = [keep[h] * mixed[part_of[h], :] + more[h] for h in each]
        for h in each:
            tops[h : h + 1, :] = top[h]
            sums[h : h + 1, :] = totals[h]
            mixed[part_of[h], :] = result[h]

    @pl.when(plan_ref[2 * blocks + i] > 0)
    def _():
        places = lax.broadcasted_iota(jnp.int32, (sk_ref.shape[0], block), 0)
        step(sk_ref[...], svt[...], places < summ_end)

    def whole(j, carry):
        there = places_of(plan_ref, blocks, subs, half, j)
        step(rows_of(k_ref, there), cols_of(vt_all, there), None)
        return carry

    def part(j, carry):
        there = places_of(plan_ref, blocks, subs, half, j)
        places = j * block + lax.broadcasted_iota(jnp.int32, (block, block), 0)
        mask = ((places >= lowest) & (places <= highest)) | (places == me)
        step(rows_of(k_ref, there), cols_of(vt_all, there), mask)
        return carry

    lax.fori_loop(plan_ref[i], plan_ref[blocks + i], whole, 0)
    lax.fori_loop(plan_ref[blocks + i], i + 1, part, 0)
    for h in range(heads):
        r = slice(h * HEAD, (h + 1) * HEAD)
        mixed[r, :] = mixed[r, :] * (1.0 / sums[h : h + 1, :])
    log_ref[...] = tops[...] + jnp.log(jnp.maximum(sums[...], 1e-37))
    made = mixed[...].T.astype(bf16)
    for n, place in enumerate(mine):
        o_ref[place, :] = made[n * half : (n + 1) * half, :]


def attn_backward_kernel(
    block, half, heads, plan_ref, q_ref, k_ref, v_ref, sk_ref, sv_ref, row_ref, log_ref, o_ref, do_ref, dq_ref, dk_ref, dv_ref, dsk_ref, dsv_ref, shift_ref, q_heads, do_heads, kt_all, skt, dq_sum,
    dk_sum, dv_sum, dsk_sum, dsv_sum,
):
    i = pl.program_id(0)
    blocks = pl.num_programs(0)
    subs = block // half

    @pl.when(i == 0)
    def _():
        dk_sum[...] = jnp.zeros_like(dk_sum)
        dv_sum[...] = jnp.zeros_like(dv_sum)
        dsk_sum[...] = jnp.zeros_like(dsk_sum)
        dsv_sum[...] = jnp.zeros_like(dsv_sum)
        for n in range(k_ref.shape[0] // half):
            r = slice(n * half, (n + 1) * half)
            kt_all[:, r] = transposed(k_ref[r, :])
        skt[...] = transposed(sk_ref[...])

    mine = places_of(plan_ref, blocks, subs, half, i)
    q = rows_of(q_ref, mine).astype(f32) * score_scale
    do = rows_of(do_ref, mine).astype(f32)
    for h in range(heads):
        q_heads[h] = only_head(q, h).astype(bf16)
        do_heads[h] = only_head(do, h).astype(bf16)
    both_t = (do * rows_of(o_ref, mine).astype(f32)).T
    row_terms = [
        jnp.sum(both_t[h * HEAD : (h + 1) * HEAD, :], axis=0, keepdims=True) for h in range(heads)
    ]
    dq_sum[...] = jnp.zeros_like(dq_sum)
    lowest = row_ref[0:1, :]
    highest = row_ref[1:2, :]
    summ_end = row_ref[2:3, :]
    me = row_ref[3:4, :]

    def step(keys, values, keys_t, mask):
        dk = dv = None
        for h in range(heads):
            scores = dot(keys, q_heads[h], ROWS_BY_COLS)
            if mask is not None:
                scores = jnp.where(mask, scores, masked_score)
            probs = jnp.exp(scores - log_ref[h : h + 1, :])
            grad_probs = dot(values, do_heads[h], ROWS_BY_COLS)
            grad_scores = (probs * (grad_probs - row_terms[h])).astype(bf16)
            r = slice(h * HEAD, (h + 1) * HEAD)
            dq_sum[r, :] += dot(keys_t[r, :], grad_scores, ROWS_BY_ROWS)
            dv_own = dot(probs.astype(bf16), do_heads[h], ROWS_BY_ROWS)
            dk_own = dot(grad_scores, q_heads[h], ROWS_BY_ROWS)
            dv = dv_own if dv is None else dv + dv_own
            dk = dk_own if dk is None else dk + dk_own
        return dk, dv

    @pl.when(plan_ref[2 * blocks + i] > 0)
    def _():
        places = lax.broadcasted_iota(jnp.int32, (sk_ref.shape[0], block), 0)
        dk, dv = step(sk_ref[...], sv_ref[...], skt[...], places < summ_end)
        dsk_sum[...] += dk
        dsv_sum[...] += dv

    def whole(j, masked):
        there = places_of(plan_ref, blocks, subs, half, j)
        mask = None
        if masked:
            places = j * block + lax.broadcasted_iota(jnp.int32, (block, block), 0)
            mask = ((places >= lowest) & (places <= highest)) | (places == me)
        dk, dv = step(rows_of(k_ref, there), rows_of(v_ref, there), cols_of(kt_all, there), mask)
        for n, place in enumerate(there):
            dk_sum[place, :] += dk[n * half : (n + 1) * half, :]
            dv_sum[place, :] += dv[n * half : (n + 1) * half, :]

    def plain(j, carry):
        whole(j, False)
        return carry

    def part(j, carry):
        whole(j, True)
        return carry

    lax.fori_loop(plan_ref[i], plan_ref[blocks + i], plain, 0)
    lax.fori_loop(plan_ref[blocks + i], i + 1, part, 0)
    made = (dq_sum[...] * score_scale).T.astype(bf16)
    for n, place in enumerate(mine):
        dq_ref[place, :] = made[n * half : (n + 1) * half, :]

    @pl.when(i == blocks - 1)
    def _():
        dk_ref[...] = dk_sum[...].astype(bf16)
        dv_ref[...] = dv_sum[...].astype(bf16)
        dsk_ref[...] = dsk_sum[...].astype(bf16)
        dsv_ref[...] = dsv_sum[...].astype(bf16)

        def added(ref):
            return jnp.sum(ref[...].astype(f32), axis=0, keepdims=True)

        shift_ref[...] = jnp.zeros_like(shift_ref)
        shift_ref[0:1, :] = added(dq_ref)
        shift_ref[1:2, :] = added(dv_ref) + added(dsv_ref)


def attn_forward(part, parts, plan, rows, q, k, v, sk, sv, block, half):
    count = q.shape[0]
    width = q.shape[1] // parts
    heads = width // HEAD
    by_cols = pl.BlockSpec((8, block), lambda i, *_: (0, i))
    pairs = count * count // 4
    return pl.pallas_call(
        functools.partial(attn_forward_kernel, block, half, heads),
        grid_spec=pltpu.PrefetchScalarGridSpec(
            num_scalar_prefetch=1,
            grid=(count // block,),
            in_specs=[held((one.shape[0], width), (0, part)) for one in (q, k, v, sk, sv)] + [by_cols],
            out_specs=[held((count, width)), by_cols],
            scratch_shapes=[
                pltpu.VMEM((heads, block, width), bf16),
                pltpu.VMEM((width, count), bf16),
                pltpu.VMEM((width, sk.shape[0]), bf16),
                pltpu.VMEM((8, block), f32),
                pltpu.VMEM((8, block), f32),
                pltpu.VMEM((width, block), f32),
            ],
        ),
        out_shape=[
            jax.ShapeDtypeStruct((count, width), bf16),
            jax.ShapeDtypeStruct((8, count), f32),
        ],
        compiler_params=pltpu.CompilerParams(
            dimension_semantics=("arbitrary",), vmem_limit_bytes=40 * 2**20
        ),
        cost_estimate=pl.CostEstimate(
            flops=16 * pairs * width, bytes_accessed=8 * count * width, transcendentals=pairs * heads
        ),
        name="attn_forward",
    )(plan, q, k, v, sk, sv, rows)


def attn_backward(part, parts, plan, rows, q, k, v, sk, sv, logs, o, do, block, half):
    count = q.shape[0]
    width = q.shape[1] // parts
    heads = width // HEAD
    by_cols = pl.BlockSpec((8, block), lambda i, *_: (0, i))
    pairs = count * count // 4
    long = jax.ShapeDtypeStruct((count, width), bf16)
    short = jax.ShapeDtypeStruct((sk.shape[0], width), bf16)
    shift = jax.ShapeDtypeStruct((8, width), f32)
    long_in = held((count, width), (0, part))
    short_in = held((sk.shape[0], width), (0, part))
    return pl.pallas_call(
        functools.partial(attn_backward_kernel, block, half, heads),
        grid_spec=pltpu.PrefetchScalarGridSpec(
            num_scalar_prefetch=1,
            grid=(count // block,),
            in_specs=[long_in] * 3
            + [short_in] * 2
            + [by_cols] * 2
            + [held((count, width)), long_in],
            out_specs=[held(one.shape) for one in (long, long, long, short, short, shift)],
            scratch_shapes=[
                pltpu.VMEM((heads, block, width), bf16),
                pltpu.VMEM((heads, block, width), bf16),
                pltpu.VMEM((width, count), bf16),
                pltpu.VMEM((width, sk.shape[0]), bf16),
                pltpu.VMEM((width, block), f32),
                pltpu.VMEM((count, width), f32),
                pltpu.VMEM((count, width), f32),
                pltpu.VMEM((sk.shape[0], width), f32),
                pltpu.VMEM((sk.shape[0], width), f32),
            ],
        ),
        out_shape=[long, long, long, short, short, shift],
        compiler_params=pltpu.CompilerParams(
            dimension_semantics=("arbitrary",), vmem_limit_bytes=48 * 2**20
        ),
        cost_estimate=pl.CostEstimate(
            flops=24 * pairs * width, bytes_accessed=20 * count * width, transcendentals=pairs * heads
        ),
        name="attn_backward",
    )(plan, q, k, v, sk, sv, rows, logs, o, do)


def spread_columns_kernel(parts_ref, *outs):
    shards = parts_ref.shape[0]
    width = parts_ref.shape[2] // 3
    for n, ref in enumerate(outs):
        for d in range(width // HEAD):
            start = n * width + d * HEAD
            for f in range(0, shards, 2):
                pair = [parts_ref[f + m, :, start : start + HEAD].astype(f32) for m in range(2)]
                place = (d * shards + f) * HEAD
                ref[:, place : place + 2 * HEAD] = jnp.concatenate(pair, axis=1)


def spread_columns(parts):
    shards, count, width = parts.shape
    return pl.pallas_call(
        spread_columns_kernel,
        out_shape=[jax.ShapeDtypeStruct((count, shards * width // 3), f32)] * 3,
        name="spread_columns",
    )(parts)


def attention_plan(lengths, padding, count, block, slots):
    places = jnp.arange(count, dtype=jnp.int32)
    ends = jnp.cumsum(lengths)
    passed = places[:, None] >= ends[None, :]
    segment = jnp.sum(passed.astype(jnp.int32), axis=1)
    lowest = jnp.max(jnp.where(passed, ends[None, :], 0), axis=1)
    living = count - padding
    highest = jnp.minimum(places, living - 1)
    nothing = jnp.zeros_like(places)
    rows = jnp.stack(
        [lowest, highest, segment * SUMM, places, nothing, nothing, nothing, nothing], axis=0
    )
    blocks = count // block
    starts = jnp.arange(blocks, dtype=jnp.int32) * block
    first = lowest.reshape(blocks, block)[:, 0] // block
    one_piece = lowest.reshape(blocks, block)[:, -1] <= first * block
    whole_end = jnp.maximum(jnp.minimum(starts, living) // block, first)
    split = jnp.where(one_piece, whole_end, first)
    summ_flag = (segment.reshape(blocks, block)[:, -1] > 0).astype(jnp.int32)
    return rows, jnp.concatenate([first, split, summ_flag, slots]).astype(jnp.int32)


def per_device(
    tokens,
    summaries,
    segment_lengths,
    pad_lengths,
    output_grad,
    norm1_gain,
    norm1_bias,
    query_weight,
    query_bias,
    key_weight,
    value_weight,
    value_bias,
    out_weight,
    out_bias,
    norm2_gain,
    norm2_bias,
    up_weight,
    up_bias,
    down_weight,
    down_bias,
):
    shards = lax.axis_size("fsdp")
    items = lax.axis_size("dp")
    devices = shards * items
    position = lax.axis_index("fsdp")
    tok_rows = tokens.shape[1]
    width = tokens.shape[2]
    count = tok_rows * shards
    own_width = width // shards
    rows_held = query_weight.shape[0]
    units_held = up_bias.shape[0]
    own_units = units_held * items
    hidden = units_held * devices
    summary_rows = summaries.shape[1]
    padded_summ = -(-summary_rows // 32) * 32
    spread = rows_held % HEAD == 0
    block = math.gcd(count, 512)

    def for_shards(weight):
        if spread:
            split = weight.reshape(rows_held, items, shards, rows_held)
            return split.transpose(2, 0, 1, 3).reshape(shards, rows_held, own_width)
        return weight.reshape(rows_held, shards, own_width).transpose(1, 0, 2)

    def from_shards(parts):
        if spread:
            split = parts.reshape(shards, rows_held, items, rows_held)
            return split.transpose(1, 2, 0, 3).reshape(rows_held, width)
        return parts.transpose(1, 0, 2).reshape(rows_held, width)

    def own_columns(vector):
        if spread:
            split = vector.reshape(items, shards, rows_held)
            return lax.dynamic_index_in_dim(split, position, 1, keepdims=False).reshape(own_width)
        return lax.dynamic_slice_in_dim(vector, position * own_width, own_width, 0)

    def whole_columns(vector):
        if spread:
            split = jnp.zeros((items, shards, rows_held), f32)
            return lax.dynamic_update_index_in_dim(
                split, vector.reshape(items, 1, rows_held), position, 1
            ).reshape(width)
        return lax.dynamic_update_slice_in_dim(
            jnp.zeros((width,), f32), vector, position * own_width, 0
        )

    half = tok_rows // 2
    order = slot_order(shards)
    groups = len(order) // 4
    eight = shards == 8

    def halves(whole):
        return [whole[:half], whole[half:]]

    def flat(slotted):
        return slotted.reshape(count, slotted.shape[2])

    def slot_rows(slotted):
        return slotted.reshape(slotted.shape[0] * half, slotted.shape[2])

    qkv_parts = jnp.concatenate(
        [for_shards(query_weight), for_shards(key_weight), for_shards(value_weight)], axis=2
    )
    qkv_parts = lax.all_to_all(qkv_parts, "fsdp", 0, 0, tiled=True)
    qkv_own = lax.all_gather(
        qkv_parts.reshape(shards * rows_held, 3 * own_width), "dp", axis=0, tiled=True
    )
    vectors = jnp.concatenate(
        [
            norm1_gain, norm1_bias, query_bias, value_bias, out_bias, norm2_gain, norm2_bias,
            down_bias, up_bias,
        ]
    ).astype(f32)
    vectors = lax.all_to_all(
        jnp.broadcast_to(vectors[None], (devices, vectors.shape[0])), BOTH, 0, 0, tiled=True
    )
    gain_one, shift_one, query_shift, value_shift, out_shift, gain_two, shift_two, down_shift = (
        vectors[:, n * rows_held : (n + 1) * rows_held].reshape(width) for n in range(8)
    )
    token_halves = after(halves(tokens[0]), qkv_parts, vectors)
    token_hops = sent(token_halves)
    grad_own = halves(output_grad[0])
    up_parts = up_weight.reshape(rows_held, items, shards, units_held).transpose(2, 0, 1, 3)
    up_parts = up_parts.reshape(shards, rows_held, own_units)
    more_slots = -(-padded_summ // half)

    def normed_group(g, group, normed):
        return norm_rows(
            g, group, gain_one[None], shift_one[None], normed, 4 * groups + more_slots
        )

    if eight:
        mine = [*token_halves, *[swapped(one, 1) for one in token_halves]]
        normed = normed_group(0, mine, [])
        x0, y1, x1, y0 = token_hops
        x0, y1 = after((x0, y1), normed[0], up_parts, *grad_own)
        a0, a1 = swapped(x0, 4), swapped(y1, 2)
        normed = normed_group(1, [x0, swapped(x0, 1), y1, swapped(y1, 1)], normed)
        x1, y0, a0, a1 = after((x1, y0, a0, a1), normed[0])
        last_tokens = [a0, a1, swapped(a0, 1), swapped(a1, 1)]
        normed = normed_group(2, [x1, swapped(x1, 1), y0, swapped(y0, 1)], normed)
    else:
        normed = []
        token_groups = passed_on(token_halves, token_hops)
        last_tokens = token_groups[-1]
        for g in range(groups - 1):
            normed = normed_group(g, token_groups[g], normed)
    up_shift = lax.dynamic_index_in_dim(
        vectors[:, 8 * rows_held :].reshape(items, shards, units_held), position, 1, keepdims=False
    ).reshape(1, own_units)
    query_shift = own_columns(query_shift)
    value_shift = own_columns(value_shift)
    qkv_shift = jnp.concatenate([query_shift, jnp.zeros_like(query_shift), value_shift])[None]

    early = token_hops[:1] if eight else ()
    if spread:
        both = after(jnp.concatenate([out_weight, down_weight], axis=0), *early)
        both = lax.all_gather(both, "dp", axis=0)
        out_own = both[:, :rows_held].reshape(own_width, width)
        down_own = both[:, rows_held:].reshape(own_units, width)
    else:
        out_own = lax.dynamic_slice_in_dim(
            lax.all_gather(out_weight, BOTH, axis=0, tiled=True), position * own_width, own_width, 0
        )
        down_own = lax.all_gather(down_weight, "dp", axis=0, tiled=True)
    up_parts = after(up_parts, last_tokens[0])
    up_parts = lax.all_to_all(up_parts, "fsdp", 0, 0, tiled=True)
    grad_own = after(grad_own, *last_tokens)
    grad_hops = sent(grad_own)

    summ_full = after(
        jnp.broadcast_to(summaries, (shards,) + summaries.shape[1:]), last_tokens[0]
    )
    summ_full = lax.all_to_all(summ_full, "fsdp", 0, 0, tiled=True)
    made = triple(0, groups - 1, slot_rows(normed[0]), qkv_own, qkv_shift, [], count)
    last_tokens, made = after((last_tokens, made))
    normed = normed_group(groups - 1, last_tokens, normed)
    queries, keys, values = triple(
        groups - 1, 1, slot_rows(normed[0]), qkv_own, qkv_shift, made, count
    )
    queries, keys, values, summ_full, up_parts = after(
        (queries, keys, values, summ_full, up_parts)
    )
    up_own = lax.all_gather(
        up_parts.reshape(shards * rows_held, own_units), "dp", axis=0, tiled=True
    )
    summ_full = summ_full.transpose(1, 0, 2).reshape(summary_rows, width)
    summ_inputs = jnp.pad(summ_full, ((0, padded_summ - summary_rows), (0, 0))).astype(f32)
    normed_summ = layer_norm(summ_inputs, gain_one, shift_one).astype(bf16)
    extra_rows = ((0, more_slots * half - padded_summ), (0, 0))
    normed = lax.dynamic_update_slice(
        slot_rows(normed[0]), jnp.pad(normed_summ, extra_rows), (count, 0)
    )
    summ_qkv = dot(normed_summ, qkv_own, ROWS_BY_ROWS) + qkv_shift
    summ_keys = summ_qkv[:, own_width : 2 * own_width].astype(bf16)
    summ_values = summ_qkv[:, 2 * own_width :].astype(bf16)
    slot_of = [[order.index((m, h)) for h in range(2)] for m in range(shards)]
    slots = jnp.array(slot_of, jnp.int32)[jnp.arange(shards) ^ position].reshape(-1)
    rows, plan = attention_plan(segment_lengths[0], pad_lengths[0], count, block, slots)
    parts = 2 if own_width % 256 == 0 else 1
    attn = []
    logs = []
    for part in range(parts):
        one, log = attn_forward(
            part, parts, plan, rows, queries, keys, values, summ_keys, summ_values, block, half
        )
        if eight and part == 0:
            one, log, plan, *grad_hops = after((one, log, plan, *grad_hops))
            x0, y1, x1, y0 = grad_hops
            a0, a1 = swapped(x0, 4), swapped(y1, 2)
        elif eight:
            one, log, a0, a1 = after((one, log, a0, a1))
            grad_groups = [
                [*grad_own, swapped(grad_own[0], 1), swapped(grad_own[1], 1)],
                [x0, swapped(x0, 1), y1, swapped(y1, 1)],
                [x1, swapped(x1, 1), y0, swapped(y0, 1)],
                [a0, a1, swapped(a0, 1), swapped(a1, 1)],
            ]
        attn.append(one)
        logs.append(log)
    if not eight:
        grad_groups = passed_on(grad_own, grad_hops)
    attn_slots = [one.reshape(4 * groups, half, own_width // parts) for one in attn]
    inputs = [one.astype(f32) for one in halves(tokens[0])]
    proj_sums = scattered_sum(
        lambda g, earlier: project(g, attn_slots, after(out_own, *earlier), width), groups
    )
    resid = [inputs[h] + proj_sums[h] + out_shift for h in range(2)]

    normed_two_own = [layer_norm(one, gain_two, shift_two).astype(bf16) for one in resid]
    two_hops = sent(normed_two_own)
    two_groups = passed_on(normed_two_own, two_hops)
    made = []
    back = {}
    ahead = {}
    unit_sums = []

    def feed(g, earlier):
        nonlocal made
        for n in [1, 2, 3, 0] if eight else range(groups):
            if n not in back and g not in back:
                mine = two_groups[n]
                if n == 2 and eight:
                    x1, y0 = after((mine[0], mine[2]), back[1][0])
                    mine = [x1, swapped(x1, 1), y0, swapped(y0, 1)]
                made, back[n], ahead[n], unit_sum = feed_forward(
                    n, mine, grad_groups[n], up_own, up_shift, after(down_own, *earlier),
                    made, 4 * groups,
                )
                unit_sums.append(unit_sum)
        return back[g]

    kept = {}

    def down_grad_of(earlier):
        active, _, _, grad_rows = (flat(one) for one in made)
        grad = dot(after(active, *earlier), grad_rows, COLS_BY_ROWS).astype(bf16)
        return grad, functools.partial(kept.__setitem__, "down")

    def up_grad_of(earlier):
        _, grad_upper, normed_two, _ = (flat(one) for one in feed_made)
        return dot(after(normed_two, *earlier), grad_upper, COLS_BY_ROWS).astype(bf16)

    grad_normed_two = scattered_sum(feed, groups, None, down_grad_of)
    feed_made = made
    down_grad = lax.psum_scatter(kept["down"], "dp", scatter_dimension=0, tiled=True)
    grad_floats = [one.astype(f32) for one in halves(output_grad[0])]
    down_shift_grad = jnp.sum(output_grad[0].astype(f32), axis=0)

    def norm_back(values, gains, shifts, grads):
        pulled = [
            jax.vjp(layer_norm, value, gains, shifts)[1](grad) for value, grad in zip(values, grads)
        ]
        return (
            [one[0] for one in pulled],
            sum(one[1] for one in pulled),
            sum(one[2] for one in pulled),
        )

    grad_two, gain_two_grad, shift_two_grad = norm_back(resid, gain_two, shift_two, grad_normed_two)
    grad_resid = [grad_two[h] + grad_floats[h] for h in range(2)]

    grad_proj = [one.astype(bf16) for one in grad_resid]
    out_shift_grad = sum(jnp.sum(one.astype(f32), axis=0) for one in grad_proj)
    proj_hops = sent(grad_proj)
    if eight:
        mine = grad_proj + [swapped(one, 1) for one in grad_proj]
        made = project_back(0, mine, out_own, [], 4 * groups)
        up_grad = up_grad_of((made[0],))
        x0, y1, x1, y0 = proj_hops
        x0, y1, x1, y0, up_grad = after((x0, y1, x1, y0, up_grad))
        up_grad_dot = up_grad
        a0, a1 = swapped(x0, 4), swapped(y1, 2)
        made = project_back(
            1, [x0, swapped(x0, 1), y1, swapped(y1, 1)], out_own, made, 4 * groups
        )
        x1, y0, a0, a1 = after((x1, y0, a0, a1), made[0])
        made = project_back(
            2, [x1, swapped(x1, 1), y0, swapped(y0, 1)], out_own, made, 4 * groups
        )
        proj_groups = [None, None, None, [a0, a1, swapped(a0, 1), swapped(a1, 1)]]
    else:
        up_grad = up_grad_of(())
        made = []
        proj_groups = passed_on(grad_proj, proj_hops)
    up_grad = lax.psum_scatter(up_grad, "dp", scatter_dimension=0, tiled=True)
    up_grad = up_grad.reshape(shards, rows_held, own_units)
    if not eight:
        up_grad = lax.all_to_all(up_grad, "fsdp", 0, 0, tiled=True)
    ahead = [ahead[g] for g in range(groups)]
    if eight:
        own, near, later, far = after(ahead, up_grad_dot)
        x1, y0 = paired(later[0], later[1]), paired(later[2], later[3])
        a0, a1 = paired(far[0], far[2]), paired(far[1], far[3])
        near = [total(near[0], swapped(near[1], 1)), total(near[2], swapped(near[3], 1))]
        own = [total(own[0], swapped(own[2], 1)), total(own[1], swapped(own[3], 1))]
    for g in range(groups - 1 if eight else 0, groups):
        halves_now = proj_groups[g]
        if eight:
            halves_now, x1, y0, a0, a1, near, own = after(
                (halves_now, x1, y0, a0, a1, near, own)
            )
        made = project_back(g, halves_now, out_own, made, 4 * groups)
    grad_attn, proj_rows = (flat(one) for one in made)
    grad_attn, down_grad = after((grad_attn, down_grad))
    if eight:
        x1, y0, a0, a1 = after((x1, y0, a0, a1), *proj_groups[-1])
        travelling = [swapped(x1, 2), swapped(y0, 4), swapped(a0, 4), swapped(a1, 2)]
    else:
        result = plain_scattered_sum(ahead)
    pulled = []
    again = grad_attn
    for part in range(parts):
        one = list(attn_backward(
            part, parts, plan, rows, queries, keys, values, summ_keys, summ_values, logs[part],
            attn[part], again, block, half,
        ))
        if eight and part == 0:
            one, again, *travelling = after((one, again, *travelling))
            x1, y0, a0, a1 = travelling
            x0, y1 = total(near[0], a0).astype(bf16), total(near[1], a1).astype(bf16)
            travelling = [swapped(x0, 2), swapped(y1, 4)]
            up_grad = after(up_grad, x0, y1)
            up_grad = lax.all_to_all(up_grad, "fsdp", 0, 0, tiled=True)
        elif eight:
            one, up_grad, *travelling = after((one, up_grad, *travelling))
        pulled.append(one)
    grad_slots = [
        pulled[part][n].reshape(4 * groups, half, own_width // parts)
        for n in range(3)
        for part in range(parts)
    ]
    grad_summ_kv = jnp.concatenate(
        [pulled[part][n] for n in (3, 4) for part in range(parts)], axis=1
    )

    summ_share = -(-padded_summ // (shards * 16)) * 16
    more_rows = ((0, summ_share * shards - padded_summ), (0, 0))

    def qkv_grad_of(earlier):
        slots_now, summ_now = after((grad_slots, grad_summ_kv), *earlier)
        grad_qkv = jnp.concatenate([flat(one) for one in slots_now], axis=1)
        grad_qkv = jnp.concatenate(
            [grad_qkv, jnp.pad(summ_now, (extra_rows[0], (own_width, 0)))], axis=0
        )
        grad = dot(normed, grad_qkv, COLS_BY_ROWS).astype(bf16)
        return grad, functools.partial(kept.__setitem__, "qkv")

    def side_work(earlier):
        grad = lax.psum_scatter(kept["qkv"], "dp", scatter_dimension=0, tiled=True)
        up_now, down_now, result_parts = after((up_grad, down_grad, result_terms), *earlier)
        grad = after(grad, *earlier).reshape(shards, rows_held, 3 * own_width)
        kept["qkv_parts"] = lax.all_to_all(grad, "fsdp", 0, 0, tiled=True)
        made = jnp.concatenate(
            [(total(*result_parts[h]) + down_shift).astype(bf16) for h in range(2)], axis=0
        )
        up_now = up_now.reshape(shards, rows_held, items, units_held).transpose(1, 2, 0, 3)
        up_now = up_now.reshape(rows_held, hidden).astype(f32)

        def use(done):
            kept.update(zip(("qkv_parts", "result", "up", "down"), done))

        return (kept["qkv_parts"], made, up_now, down_now.astype(f32)), use

    if eight:
        x0, y1 = travelling
        result_terms = [(resid[0], own[0], y0, x0), (resid[1], own[1], x1, y1)]
    else:
        result_terms = [(resid[h], result[h]) for h in range(2)]

    def grad_rows_back(g, earlier):
        if g == 1 or not eight:
            back = dot(after(grad_summ_kv, *earlier), qkv_own[:, own_width:], ROWS_BY_COLS)
            kept["summ"] = jnp.pad(back.astype(bf16), more_rows).reshape(shards, summ_share, width)
            columns = jnp.concatenate(after(attn, *earlier), axis=1)
            kept["out"] = dot(columns, proj_rows, COLS_BY_ROWS).astype(bf16)
        made = project(g, grad_slots, after(qkv_own, *earlier), width)
        if g == 1:
            made, kept["out"] = after((made, kept["out"]))
        return made

    grad_normed = scattered_sum(
        grad_rows_back,
        groups,
        qkv_grad_of,
        side_work,
    )
    out_grad = kept["out"]
    result, up_grad, down_grad = kept["result"], kept["up"], kept["down"]
    if spread:
        out_grad = lax.psum_scatter(out_grad, "dp", scatter_dimension=0, tiled=True)
    else:
        out_grad = lax.psum_scatter(
            lax.dynamic_update_slice_in_dim(
                jnp.zeros((width, width), bf16), out_grad, position * own_width, 0
            ),
            BOTH,
            scatter_dimension=0,
            tiled=True,
        )
    out_grad = out_grad.astype(f32)
    grad_normed_summ = lax.all_to_all(kept["summ"], "fsdp", 0, 0, tiled=True)
    grad_normed_summ = jnp.sum(grad_normed_summ.astype(f32), axis=0)
    summ_own = lax.dynamic_slice_in_dim(
        jnp.pad(summ_inputs, more_rows),
        position * summ_share,
        summ_share,
        0,
    )
    qkv_grad = kept["qkv_parts"]
    if rows_held == HEAD and shards % 2 == 0:
        query_grad, key_grad, value_grad = spread_columns(qkv_grad)
    else:
        query_grad, key_grad, value_grad = (
            from_shards(qkv_grad[:, :, n * own_width : (n + 1) * own_width]).astype(f32)
            for n in range(3)
        )
    up_shift_grad = sum(unit_sums)
    query_shift_grad = jnp.concatenate([one[5][0] for one in pulled])
    value_shift_grad = jnp.concatenate([one[5][1] for one in pulled])
    grad_one, gain_one_grad, shift_one_grad = norm_back(inputs, gain_one, shift_one, grad_normed)
    grad_inputs = jnp.concatenate([grad_one[h] + grad_resid[h] for h in range(2)], axis=0)
    _, norm_summ_pull = jax.vjp(layer_norm, summ_own, gain_one, shift_one)
    grad_summ, gain_summ_grad, shift_summ_grad = norm_summ_pull(grad_normed_summ)
    summary_cols = summaries.shape[2]
    grad_summ = lax.all_to_all(
        grad_summ.reshape(summ_share, shards, summary_cols).transpose(1, 0, 2),
        "fsdp",
        0,
        0,
        tiled=True,
    )
    summary_grad = grad_summ.reshape(shards * summ_share, summary_cols)[:summary_rows]

    vector_grads = jnp.stack(
        [
            gain_one_grad + gain_summ_grad,
            shift_one_grad + shift_summ_grad,
            whole_columns(query_shift_grad),
            whole_columns(value_shift_grad),
            out_shift_grad,
            gain_two_grad,
            shift_two_grad,
            down_shift_grad,
        ]
    )
    vector_grads = vector_grads.reshape(8, devices, rows_held).transpose(1, 0, 2)
    unit_grads = lax.dynamic_update_index_in_dim(
        jnp.zeros((items, shards, units_held), f32),
        up_shift_grad.reshape(items, 1, units_held),
        position,
        1,
    )
    all_grads = jnp.concatenate(
        [vector_grads.reshape(devices, 8 * rows_held), unit_grads.reshape(devices, units_held)],
        axis=1,
    )
    all_grads = jnp.sum(lax.all_to_all(all_grads, BOTH, 0, 0, tiled=True), axis=0)
    (
        gain_one_grad, shift_one_grad, query_shift_grad, value_shift_grad, out_shift_grad,
        gain_two_grad, shift_two_grad, down_shift_grad,
    ) = (all_grads[n * rows_held : (n + 1) * rows_held] for n in range(8))
    up_shift_grad = all_grads[8 * rows_held :]
    return (
        result[None],
        grad_inputs[None],
        summary_grad[None],
        gain_one_grad,
        shift_one_grad,
        query_grad,
        query_shift_grad,
        key_grad,
        value_grad,
        value_shift_grad,
        out_grad,
        out_shift_grad,
        gain_two_grad,
        shift_two_grad,
        up_grad,
        up_shift_grad,
        down_grad,
        down_shift_grad,
    )


def solution(mesh):
    vector = P(BOTH)
    matrix = P(BOTH, None)
    rows = P("dp", "fsdp", None)
    columns = P("dp", None, "fsdp")
    return jax.shard_map(
        per_device,
        mesh=mesh,
        in_specs=(
            rows, columns, P("dp", None), P("dp"), rows, vector, vector, matrix, vector, matrix,
            matrix, vector, matrix, vector, vector, vector, matrix, vector, matrix, vector,
        ),
        out_specs=(
            rows, rows, columns, vector, vector, matrix, vector, matrix, matrix, vector, matrix,
            vector, vector, vector, matrix, vector, matrix, vector,
        ),
        check_vma=False,
    )
```

time: 1250 us -> 1010 us (0.81)
  matrix products: 314 us -> 74.8 us
  Pallas kernels: 132 us -> 364 us
  waiting for transfers between devices: 437 us -> 229 us
  local copies, waits for them, and re-layouts: 137 us -> 68.4 us
  starting transfers between devices: 69 us -> 108 us
  other arithmetic: 108 us -> 124 us
  blocking collectives: 30.6 us -> 17.8 us
    dot_general x53 -> x6, matrix products: 314 us -> 74.8 us  [dot(): return lax.dot_general(left, right, dims, preferred_element_type=f32)]
    pallas_call x2 -> x27, Pallas kernels: 132 us -> 364 us  [the longest x22 231 us: group_call(): pl.pallas_call(functools.partial(kernel, len(ins), len(earlier)), grid=(s...]
    ppermute x64 -> x112, waiting for transfers between devices: 389 us -> 188 us  [swapped(): return lax.ppermute(x, 'fsdp', [(i, i ^ bit) for i in range(devices)])]
    convert_element_type x10 -> x28, other arithmetic: 8.25 us -> 56.3 us  [the longest x16 26.3 us: paired(): return total(own, swapped(other, 1)).astype(bf16)]
    unnamed x232 -> x390, local copies, waits for them, and re-layouts: 70.8 us -> 34.1 us
    all_to_all x1, waiting for transfers between devices: 38 us -> 6.59 us  [per_device(): lax.all_to_all(jnp.broadcast_to(vectors[None], (devices, vectors.shape[0]...]
    add x1 -> x15, other arithmetic: 0.01 us -> 29.4 us  [the longest x10 24.6 us: total(): result = result + term.astype(f32)]
    ppermute x64 -> x112, starting transfers between devices: 36.9 us -> 63.8 us  [swapped(): return lax.ppermute(x, 'fsdp', [(i, i ^ bit) for i in range(devices)])]
  transfers between devices with their start and end apart: 79 -> 127, of which waited for: 26 -> 39; matrix products, arithmetic and copies ran while one was open for 39% -> 23% of each run, Pallas kernels for 11% -> 35%
where the time goes in v2:
time: 1010 us; the launch traced here: 1000 us
  Pallas kernels  364 us (36%)
  waiting for transfers between devices  229 us (23%)
  other arithmetic  124 us (12%)
  starting transfers between devices  108 us (11%)
  matrix products  74.8 us (7%)
  local copies, waits for them, and re-layouts  68.4 us (7%)
  blocking collectives  17.8 us (2%)
  between operations  17.5 us (2%)
    pallas_call x22, Pallas kernels, group_call(): pl.pallas_call(functools.partial(kernel, len(ins), len(earlier)), grid=(s...  231 us
    ppermute x112, waiting for transfers between devices, swapped(): return lax.ppermute(x, 'fsdp', [(i, i ^ bit) for i in range(devices)])  188 us
    pallas_call x2, Pallas kernels, attn_backward(): pl.pallas_call(functools.partial(attn_backward_kernel, block, half, heads...  80.2 us
    dot_general x6, matrix products, dot(): return lax.dot_general(left, right, dims, preferred_element_type=f32)  74.8 us
    ppermute x112, starting transfers between devices, swapped(): return lax.ppermute(x, 'fsdp', [(i, i ^ bit) for i in range(devices)])  63.8 us
    pallas_call x2, Pallas kernels, attn_forward(): pl.pallas_call(functools.partial(attn_forward_kernel, block, half, heads)...  49.6 us
    unnamed x390, local copies, waits for them, and re-layouts  34.1 us
    convert_element_type x16, other arithmetic, paired(): return total(own, swapped(other, 1)).astype(bf16)  26.3 us
  transfers between devices with their start and end apart: 127, of which 39 were waited for; matrix products, arithmetic and copies ran while one was open for 23% of the time, Pallas kernels for 35%

profile of v2, /device:TPU:0, one launch (start us, length us, event | category | flops | bytes accessed | tf_op | source)
XLA Modules:
  0.0 1002.8 jit_solution(6741805512124009805)
XLA Ops:
  11.7 17.8 %all_to_all.53 = bf16[8,64,768]{2,1,0:T(8,128)(2,1)} all-to-all(bf16[8,64,768]{2,1,0:T(8,128)(2,1)S(1)} %pad_maximum_fusion.2), channel_id=1, replica_groups=mesh['dp'=4,'fsdp'=8] {'fsdp'}, dimensions={0} | all-to-all | bytes 1572864 | tf_op jit(solution)/shard_map/all_to_all | solution.py:815
  30.3 4.0 all-to-all-start.1
  35.5 6.6 all-to-all-done.1
  46.5 20.9 %collective-permute-done.2.refs_0_ = bf16[256,2048]{1,0:T(8,128)(2,1)} collective-permute-done((bf16[256,2048]{1,0:T(8,128)(2,1)S(1)}, bf16[256,2048]{1,0:T(8,128)(2,1)}, u32[]{:S(2)}, u32[]{:S(2)}) %collective-permute-start.2) | collective-permute-done | bytes 1048608 | tf_op jit(solution)/shard_map/ppermute | solution.py:62
  72.3 5.8 norm_rows.4.refs_6_
  86.2 5.9 norm_rows.5.refs_6_
  92.2 12.6 %collective-permute-done.refs_0_ = bf16[256,2048]{1,0:T(8,128)(2,1)S(1)} collective-permute-done((bf16[256,2048]{1,0:T(8,128)(2,1)}, bf16[256,2048]{1,0:T(8,128)(2,1)S(1)}, u32[]{:S(2)}, u32[]{:S(2)}) %collective-permute-start) | collective-permute-done | bytes 1048608 | tf_op jit(solution)/shard_map/ppermute | solution.py:62
  105.1 21.2 %collective-permute-done.6.refs_0_ = bf16[256,2048]{1,0:T(8,128)(2,1)S(1)} collective-permute-done((bf16[256,2048]{1,0:T(8,128)(2,1)}, bf16[256,2048]{1,0:T(8,128)(2,1)S(1)}, u32[]{:S(2)}, u32[]{:S(2)}) %collective-permute-start.6) | collective-permute-done | bytes 1048608 | tf_op jit(solution)/shard_map/ppermute | solution.py:62
  130.3 3.5 all-to-all-start.2
  140.0 5.7 norm_rows.6.refs_6_
  145.8 4.1 all-to-all-start.3
  150.2 14.5 %triple.2 = (bf16[4096,256]{1,0:T(8,128)(2,1)}, bf16[4096,256]{1,0:T(8,128)(2,1)}, bf16[4096,256]{1,0:T(8,128)(2,1)}) custom-call(bf16[4352,2048]{1,0:T(8,128)(2,1)} %bitcast.176, bf16[2048,768]{1,0:T(8,128)(2,1)} %all-gather.5.cloned.1.call-done.refs_1_.refs_6_, f32[1,768]{1,0:T(1,128)S(1)} %broadcast_in_dim.94.refs_2_), custom_call_target="tpu_custom_call" | custom-call | flops 9663676416 | bytes 12582912 | tf_op jit(solution)/shard_map/triple/pallas_call | solution.py:177
  164.7 5.7 norm_rows.7
  170.4 7.5 triple.3
  178.0 22.8 %all-to-all-done.3 = bf16[8,64,1024]{2,1,0:T(8,128)(2,1)S(1)} async-done(((bf16[8,64,1024]{2,1,0:T(8,128)(2,1)}), bf16[8,64,1024]{2,1,0:T(8,128)(2,1)S(1)}, u32[]{:S(2)}, u32[]{:S(2)}) %all-to-all-start.3) | async-done | bytes 1048608 | tf_op jit(solution)/shard_map/all_to_all | solution.py:878
  205.7 24.6 %attn_forward.2 = (bf16[4096,128]{1,0:T(8,128)(2,1)S(1)}, f32[8,4096]{1,0:T(8,128)S(1)}) custom-call(s32[40]{0:T(128)S(1)} %pad_add_fusion.plan_ref, bf16[4096,256]{1,0:T(8,128)(2,1)S(1)} %copy-done, bf16[4096,256]{1,0:T(8,128)(2,1)S(1)} %copy-done.1, bf16[4096,256]{1,0:T(8,128)(2,1)S(1)} %copy-done.2, bf16[160,256]{1,0:T(8,128)(2,1)S(1)} %get-tuple-element.696.sk_ref, ...), custom_call_target="tpu_custom_call" | custom-call | flops 8589934592 | bytes 4194304 | tf_op jit(solution)/shard_map/attn_forward/pallas_call | solution.py:614
  232.6 25.0 %attn_forward.3 = (bf16[4096,128]{1,0:T(8,128)(2,1)S(1)}, f32[8,4096]{1,0:T(8,128)S(1)}) custom-call(s32[40]{0:T(128)S(1)} %pad_add_fusion.plan_ref, bf16[4096,256]{1,0:T(8,128)(2,1)S(1)} %copy-done, bf16[4096,256]{1,0:T(8,128)(2,1)S(1)} %copy-done.1, bf16[4096,256]{1,0:T(8,128)(2,1)S(1)} %copy-done.2, bf16[160,256]{1,0:T(8,128)(2,1)S(1)} %get-tuple-element.696.sk_ref, ...), custom_call_target="tpu_custom_call" | custom-call | flops 8589934592 | bytes 4194304 | tf_op jit(solution)/shard_map/attn_forward/pallas_call | solution.py:614
  262.9 3.9 project.8
  274.7 3.9 project.9
  278.7 17.9 %collective-permute-done.23 = bf16[256,2048]{1,0:T(8,128)(2,1)S(1)} collective-permute-done((bf16[256,2048]{1,0:T(8,128)(2,1)S(1)}, bf16[256,2048]{1,0:T(8,128)(2,1)S(1)}, u32[]{:S(2)}, u32[]{:S(2)}) %collective-permute-start.23) | collective-permute-done | bytes 1048608 | tf_op jit(solution)/shard_map/ppermute | solution.py:62
  307.1 4.0 project.10
  312.3 4.2 project.11
  316.5 12.6 %collective-permute-done.28 = bf16[256,2048]{1,0:T(8,128)(2,1)} collective-permute-done((bf16[256,2048]{1,0:T(8,128)(2,1)}, bf16[256,2048]{1,0:T(8,128)(2,1)}, u32[]{:S(2)}, u32[]{:S(2)}) %collective-permute-start.28) | collective-permute-done | bytes 1048608 | tf_op jit(solution)/shard_map/ppermute | solution.py:62
  338.8 20.7 %collective-permute-done.31 = bf16[256,2048]{1,0:T(8,128)(2,1)S(1)} collective-permute-done((bf16[256,2048]{1,0:T(8,128)(2,1)S(1)}, bf16[256,2048]{1,0:T(8,128)(2,1)S(1)}, u32[]{:S(2)}, u32[]{:S(2)}) %collective-permute-start.31) | collective-permute-done | bytes 1048608 | tf_op jit(solution)/shard_map/ppermute | solution.py:62
  370.0 21.8 %collective-permute-done.34.refs_0_ = bf16[256,2048]{1,0:T(8,128)(2,1)} collective-permute-done((bf16[256,2048]{1,0:T(8,128)(2,1)}, bf16[256,2048]{1,0:T(8,128)(2,1)}, u32[]{:S(2)}, u32[]{:S(2)}) %collective-permute-start.34) | collective-permute-done | bytes 1048608 | tf_op jit(solution)/shard_map/ppermute | solution.py:62
  400.8 29.8 %feed_forward.4 = (bf16[16,256,1024]{2,1,0:T(8,128)(2,1)}, bf16[16,256,1024]{2,1,0:T(8,128)(2,1)}, bf16[16,256,2048]{2,1,0:T(8,128)(2,1)}, bf16[16,256,2048]{2,1...) custom-call(bf16[256,2048]{1,0:T(8,128)(2,1)} %collective-permute-do, ...), custom_call_target="tpu_custom_call" | custom-call | flops 17179869184 | bytes 33554432 | tf_op jit(solution)/shard_map/feed_forward/pallas_call | solution.py:177
  436.1 29.9 %feed_forward.5 = (bf16[16,256,1024]{2,1,0:T(8,128)(2,1)}, bf16[16,256,1024]{2,1,0:T(8,128)(2,1)}, bf16[16,256,2048]{2,1,0:T(8,128)(2,1)}, bf16[16,256,2048]{2,1...) custom-call(bf16[256,2048]{1,0:T(8,128)(2,1)} %collective-permute-do, ...), custom_call_target="tpu_custom_call", output_to_operand_aliasing={{0}: (11, {}), {1}: (12, {}), {2}: (13, {}), {3}: (14, {})} | custom-call | flops 17179869184 | bytes 33554432 | tf_op jit(solution)/shard_map/feed_forward/pallas_call | solution.py:177
  477.2 30.3 %feed_forward.6 = (bf16[16,256,1024]{2,1,0:T(8,128)(2,1)}, bf16[16,256,1024]{2,1,0:T(8,128)(2,1)}, bf16[16,256,2048]{2,1,0:T(8,128)(2,1)}, bf16[16,256,2048]{2,1...) custom-call(bf16[256,2048]{1,0:T(8,128)(2,1)} %copy-done.69, ...), custom_call_target="tpu_custom_call", output_to_operand_aliasing={{0}: (11, {}), {1}: (12, {}), {2}: (13, {}), {3}: (14, {})} | custom-call | flops 17179869184 | bytes 33554432 | tf_op jit(solution)/shard_map/feed_forward/pallas_call | solution.py:177
  521.8 30.0 %feed_forward.7 = (bf16[16,256,1024]{2,1,0:T(8,128)(2,1)}, bf16[16,256,1024]{2,1,0:T(8,128)(2,1)}, bf16[16,256,2048]{2,1,0:T(8,128)(2,1)}, bf16[16,256,2048]{2,1...) custom-call(bf16[256,2048]{1,0:T(8,128)(2,1)} %get-tuple-element.706, ...), custom_call_target="tpu_custom_call", output_to_operand_aliasing={{0}: (11, {}), {1}: (12, {}), {2}: (13, {}), {3}: (14, {})} | custom-call | flops 17179869184 | bytes 33554432 | tf_op jit(solution)/shard_map/feed_forward/pallas_call | solution.py:177
  551.8 3.3 add_convert_fusion.14
  559.1 21.3 %convolution_convert_fusion.1 = bf16[1024,2048]{1,0:T(8,128)(2,1)} fusion(bf16[4096,1024]{1,0:T(8,128)(2,1)S(1)} %bitcast.182, bf16[4096,2048]{1,0:T(8,128)(2,1)} %bitcast.181), kind=kOutput, calls=%fused_computation.11 | convolution fusion | flops 17181966336 | bytes 29360128 | tf_op jit(solution)/shard_map/dot_general | solution.py:27
  580.4 3.7 convert_add_fusion.14
  584.1 3.4 convert_add_fusion.15
  588.3 5.3 multiply_reduce_fusion
  605.2 5.3 project_back.4
  610.6 21.3 %convolution_convert_fusion = bf16[2048,1024]{1,0:T(8,128)(2,1)} fusion(bf16[4096,2048]{1,0:T(8,128)(2,1)} %bitcast.180, bf16[4096,1024]{1,0:T(8,128)(2,1)S(1)} %bitcast.185), kind=kOutput, calls=%fused_computation.10 | convolution fusion | flops 17181966336 | bytes 29360128 | tf_op jit(solution)/shard_map/dot_general | solution.py:27
  631.9 15.9 %collective-permute-done.72.refs_0_ = bf16[256,2048]{1,0:T(8,128)(2,1)S(1)} collective-permute-done((bf16[256,2048]{1,0:T(8,128)(2,1)}, bf16[256,2048]{1,0:T(8,128)(2,1)S(1)}, u32[]{:S(2)}, u32[]{:S(2)}) %collective-permute-start.72) | collective-permute-done | bytes 1048608 | tf_op jit(solution)/shard_map/ppermute | solution.py:62
  653.8 5.5 project_back.5
  659.4 14.8 %collective-permute-done.76.refs_0_ = bf16[256,2048]{1,0:T(8,128)(2,1)S(1)} collective-permute-done((bf16[256,2048]{1,0:T(8,128)(2,1)S(1)}, bf16[256,2048]{1,0:T(8,128)(2,1)S(1)}, u32[]{:S(2)}, u32[]{:S(2)}) %collective-permute-start.76) | collective-permute-done | bytes 1048608 | tf_op jit(solution)/shard_map/ppermute | solution.py:62
  698.2 5.3 project_back.6
  703.6 5.4 project_back.7
  709.0 39.9 %attn_backward.2 = (bf16[4096,128]{1,0:T(8,128)(2,1)S(1)}, bf16[4096,128]{1,0:T(8,128)(2,1)S(1)}, bf16[4096,128]{1,0:T(8,128)(2,1)S(1)}, bf16[160,128]{1,0:T(8,1...) custom-call(s32[40]{0:T(128)S(1)} %copy-done.22, bf16[4096,256]{1,0:T(8,128)(2,1)} %get-tuple-element.346.q_ref, ...), custom_call_target="tpu_custom_call" | custom-call | flops 12884901888 | bytes 10485760 | tf_op jit(solution)/shard_map/attn_backward/pallas_call | solution.py:655
  749.1 3.5 add_convert_fusion.8
  757.6 3.6 all-to-all-start.4
  761.2 40.3 %attn_backward.3 = (bf16[4096,128]{1,0:T(8,128)(2,1)S(1)}, bf16[4096,128]{1,0:T(8,128)(2,1)S(1)}, bf16[4096,128]{1,0:T(8,128)(2,1)S(1)}, bf16[160,128]{1,0:T(8,1...) custom-call(s32[40]{0:T(128)S(1)} %copy-done.22, bf16[4096,256]{1,0:T(8,128)(2,1)} %get-tuple-element.346.q_ref, ...), custom_call_target="tpu_custom_call" | custom-call | flops 12884901888 | bytes 10485760 | tf_op jit(solution)/shard_map/attn_backward/pallas_call | solution.py:655
  805.5 7.1 project.12
  828.6 21.2 %fusion.7 = bf16[2048,768]{1,0:T(8,128)(2,1)} fusion(bf16[4352,2048]{1,0:T(8,128)(2,1)} %pad_dynamic-update-slice_fusion, bf16[160,512]{1,0:T(8,128)(2,1)S(1)} %constant_dynamic-update-slice_fusion, bf16[4096,768]{1,0:T(8,128)(2,1)} %constant_dynamic-update-slice_fusion.4), kind=kOutput, calls=%fused_computation.12 | convolution fusion | flops 13711835136 | bytes 27426816 | tf_op jit(solution)/shard_map/dot_general | solution.py:27
  855.4 7.1 project.13
  872.5 3.6 all-to-all-start.6
  876.2 9.4 convolution_convert_fusion.2
  885.6 7.1 project.14
  893.2 7.1 project.15
  900.4 5.9 all-to-all-done.6
  909.5 3.6 all-to-all-start.7
  913.2 3.7 add_convert_fusion.2
  923.9 4.6 add_convert_fusion.1
  938.9 4.2 all-to-all-start.5
  943.1 3.4 convert_add_fusion.4
  946.6 5.8 reduce-scatter.11.cloned.1.call-done
  954.2 3.5 convert_add_fusion.5
  957.9 4.0 fusion.22
  963.0 16.5 %all-to-all-start.8 = ((f32[32,1,768]{2,1,0:T(1,128)}), f32[32,1,768]{2,1,0:T(1,128)S(1)}, u32[]{:S(2)}, u32[]{:S(2)}) async-start(f32[32,1,768]{2,1,0:T(1,128)} %copy.112), calls=%async_computation.11 | async-start | bytes 196608 | tf_op jit(solution)/shard_map/all_to_all | solution.py:1189
  979.7 4.9 fusion.54
  987.0 4.8 add_add_fusion.5
  (808 shorter events, 242.2 us)
Async XLA Ops:
  7.2 143.0 %all-gather.5.cloned.1.call-start = ((), (), s32[]{:S(2)}) async-start(), calls=%async_computation.13 | async-start | bytes 3932160 | tf_op jit(solution)/shard_map/all_gather | solution.py:816
  34.3 226.3 %all-gather.9.cloned.1.call-start = ((), (), s32[]{:S(2)}) async-start(), calls=%async_computation.19 | async-start | bytes 6553600 | tf_op jit(solution)/shard_map/all_gather | solution.py:869
  42.1 25.4 %collective-permute-start.2 = (bf16[256,2048]{1,0:T(8,128)(2,1)S(1)}, bf16[256,2048]{1,0:T(8,128)(2,1)}, u32[]{:S(2)}, u32[]{:S(2)}) collective-permute-start(bf16[256,2048]{1,0:T(8,128)(2,1)S(1)} %get-tuple-element.324.refs_0_), channel_id=1, source_target_pairs={{0,2},{1,3},{2,0},{3,1},{4,6},{5,7},{6,4},{7,5},{8,10},{9,11},{10,... | collective-permute-start | bytes 3145736 | tf_op jit(solution)/shard_map/ppermute | solution.py:62
  42.5 29.7 %collective-permute-start.4 = (bf16[256,2048]{1,0:T(8,128)(2,1)S(1)}, bf16[256,2048]{1,0:T(8,128)(2,1)}, u32[]{:S(2)}, u32[]{:S(2)}) collective-permute-start(bf16[256,2048]{1,0:T(8,128)(2,1)S(1)} %get-tuple-element.324.refs_0_), channel_id=1, source_target_pairs={{0,1},{1,0},{2,3},{3,2},{4,5},{5,4},{6,7},{7,6},{8,9},{9,8},{10,11... | collective-permute-start | bytes 3145736 | tf_op jit(solution)/shard_map/ppermute | solution.py:62
  42.6 29.7 %collective-permute-start.5 = (bf16[256,2048]{1,0:T(8,128)(2,1)}, bf16[256,2048]{1,0:T(8,128)(2,1)}, u32[]{:S(2)}, u32[]{:S(2)}) collective-permute-start(bf16[256,2048]{1,0:T(8,128)(2,1)} %get-tuple-element.323.refs_1_), channel_id=1, source_target_pairs={{0,1},{1,0},{2,3},{3,2},{4,5},{5,4},{6,7},{7,6},{8,9},{9,8},{10,11... | collective-permute-start | bytes 3145736 | tf_op jit(solution)/shard_map/ppermute | solution.py:62
  43.1 35.0 %collective-permute-start.3 = (bf16[256,2048]{1,0:T(8,128)(2,1)}, bf16[256,2048]{1,0:T(8,128)(2,1)}, u32[]{:S(2)}, u32[]{:S(2)}) collective-permute-start(bf16[256,2048]{1,0:T(8,128)(2,1)} %get-tuple-element.323.refs_1_), channel_id=1, source_target_pairs={{0,4},{1,5},{2,6},{3,7},{4,0},{5,1},{6,2},{7,3},{8,12},{9,13},{10,... | collective-permute-start | bytes 3145736 | tf_op jit(solution)/shard_map/ppermute | solution.py:62
  78.6 26.2 %collective-permute-start = (bf16[256,2048]{1,0:T(8,128)(2,1)}, bf16[256,2048]{1,0:T(8,128)(2,1)S(1)}, u32[]{:S(2)}, u32[]{:S(2)}) collective-permute-start(bf16[256,2048]{1,0:T(8,128)(2,1)} %get-tuple-element.323.refs_1_), channel_id=1, source_target_pairs={{0,2},{1,3},{2,0},{3,1},{4,6},{5,7},{6,4},{7,5},{8,10},{9,11},{10,... | collective-permute-start | bytes 3145736 | tf_op jit(solution)/shard_map/ppermute | solution.py:62
  78.9 26.2 %collective-permute-start.1 = (bf16[256,2048]{1,0:T(8,128)(2,1)S(1)}, bf16[256,2048]{1,0:T(8,128)(2,1)}, u32[]{:S(2)}, u32[]{:S(2)}) collective-permute-start(bf16[256,2048]{1,0:T(8,128)(2,1)S(1)} %get-tuple-element.324.refs_0_), channel_id=1, source_target_pairs={{0,4},{1,5},{2,6},{3,7},{4,0},{5,1},{6,2},{7,3},{8,12},{9,13},{10,... | collective-permute-start | bytes 3145736 | tf_op jit(solution)/shard_map/ppermute | solution.py:62
  79.7 46.6 %collective-permute-start.6 = (bf16[256,2048]{1,0:T(8,128)(2,1)}, bf16[256,2048]{1,0:T(8,128)(2,1)S(1)}, u32[]{:S(2)}, u32[]{:S(2)}) collective-permute-start(bf16[256,2048]{1,0:T(8,128)(2,1)} %collective-permute-done.2.refs_0_), channel_id=1, source_target_pairs={{0,4},{1,5},{2,6},{3,7},{4,0},{5,1},{6,2},{7,3},{8,12},{9,13},{10,... | collective-permute-start | bytes 3145736 | tf_op jit(solution)/shard_map/ppermute | solution.py:62
  81.1 45.4 %collective-permute-start.7 = (bf16[256,2048]{1,0:T(8,128)(2,1)}, bf16[256,2048]{1,0:T(8,128)(2,1)}, u32[]{:S(2)}, u32[]{:S(2)}) collective-permute-start(bf16[256,2048]{1,0:T(8,128)(2,1)} %collective-permute-done.3.refs_2_), channel_id=1, source_target_pairs={{0,2},{1,3},{2,0},{3,1},{4,6},{5,7},{6,4},{7,5},{8,10},{9,11},{10,... | collective-permute-start | bytes 3145736 | tf_op jit(solution)/shard_map/ppermute | solution.py:62
  135.9 95.4 %collective-permute-start.15 = (bf16[256,2048]{1,0:T(8,128)(2,1)}, bf16[256,2048]{1,0:T(8,128)(2,1)}, u32[]{:S(2)}, u32[]{:S(2)}) collective-permute-start(bf16[256,2048]{1,0:T(8,128)(2,1)} %get-tuple-element.353.refs_5_), channel_id=1, source_target_pairs={{0,4},{1,5},{2,6},{3,7},{4,0},{5,1},{6,2},{7,3},{8,12},{9,13},{10,... | collective-permute-start | bytes 3145736 | tf_op jit(solution)/shard_map/ppermute | solution.py:62
  137.9 93.4 %collective-permute-start.16 = (bf16[256,2048]{1,0:T(8,128)(2,1)}, bf16[256,2048]{1,0:T(8,128)(2,1)}, u32[]{:S(2)}, u32[]{:S(2)}) collective-permute-start(bf16[256,2048]{1,0:T(8,128)(2,1)} %get-tuple-element.353.refs_5_), channel_id=1, source_target_pairs={{0,2},{1,3},{2,0},{3,1},{4,6},{5,7},{6,4},{7,5},{8,10},{9,11},{10,... | collective-permute-start | bytes 3145736 | tf_op jit(solution)/shard_map/ppermute | solution.py:62
  139.4 91.9 %collective-permute-start.14 = (bf16[256,2048]{1,0:T(8,128)(2,1)}, bf16[256,2048]{1,0:T(8,128)(2,1)}, u32[]{:S(2)}, u32[]{:S(2)}) collective-permute-start(bf16[256,2048]{1,0:T(8,128)(2,1)} %get-tuple-element.352.refs_4_), channel_id=1, source_target_pairs={{0,2},{1,3},{2,0},{3,1},{4,6},{5,7},{6,4},{7,5},{8,10},{9,11},{10,... | collective-permute-start | bytes 3145736 | tf_op jit(solution)/shard_map/ppermute | solution.py:62
  139.9 91.4 %collective-permute-start.17 = (bf16[256,2048]{1,0:T(8,128)(2,1)}, bf16[256,2048]{1,0:T(8,128)(2,1)}, u32[]{:S(2)}, u32[]{:S(2)}) collective-permute-start(bf16[256,2048]{1,0:T(8,128)(2,1)} %get-tuple-element.352.refs_4_), channel_id=1, source_target_pairs={{0,4},{1,5},{2,6},{3,7},{4,0},{5,1},{6,2},{7,3},{8,12},{9,13},{10,... | collective-permute-start | bytes 3145736 | tf_op jit(solution)/shard_map/ppermute | solution.py:62
  145.8 55.0 %all-to-all-start.3 = ((bf16[8,64,1024]{2,1,0:T(8,128)(2,1)}), bf16[8,64,1024]{2,1,0:T(8,128)(2,1)S(1)}, u32[]{:S(2)}, u32[]{:S(2)}) async-start(bf16[8,64,1024]{2,1,0:T(8,128)(2,1)} %reshape.683), calls=%async_computation.3 | async-start | bytes 2097152 | tf_op jit(solution)/shard_map/all_to_all | solution.py:878
  149.9 250.9 %all-gather.7.cloned.1.call-start = ((), (), s32[]{:S(2)}) async-start(), calls=%async_computation.14 | async-start | bytes 5242880 | tf_op jit(solution)/shard_map/all_gather | solution.py:895
  231.4 27.2 %collective-permute-start.18 = (bf16[256,2048]{1,0:T(8,128)(2,1)}, bf16[256,2048]{1,0:T(8,128)(2,1)S(1)}, u32[]{:S(2)}, u32[]{:S(2)}) collective-permute-start(bf16[256,2048]{1,0:T(8,128)(2,1)} %collective-permute-done.14.refs_4_), channel_id=1, source_target_pairs={{0,4},{1,5},{2,6},{3,7},{4,0},{5,1},{6,2},{7,3},{8,12},{9,13},{10,... | collective-permute-start | bytes 3145736 | tf_op jit(solution)/shard_map/ppermute | solution.py:62
  232.0 27.6 %collective-permute-start.19 = (bf16[256,2048]{1,0:T(8,128)(2,1)}, bf16[256,2048]{1,0:T(8,128)(2,1)S(1)}, u32[]{:S(2)}, u32[]{:S(2)}) collective-permute-start(bf16[256,2048]{1,0:T(8,128)(2,1)} %collective-permute-done.15.refs_6_), channel_id=1, source_target_pairs={{0,2},{1,3},{2,0},{3,1},{4,6},{5,7},{6,4},{7,5},{8,10},{9,11},{10,... | collective-permute-start | bytes 3145736 | tf_op jit(solution)/shard_map/ppermute | solution.py:62
  303.6 25.5 %collective-permute-start.28 = (bf16[256,2048]{1,0:T(8,128)(2,1)}, bf16[256,2048]{1,0:T(8,128)(2,1)}, u32[]{:S(2)}, u32[]{:S(2)}) collective-permute-start(bf16[256,2048]{1,0:T(8,128)(2,1)} %add_convert_fusion.24), channel_id=1, source_target_pairs={{0,2},{1,3},{2,0},{3,1},{4,6},{5,7},{6,4},{7,5},{8,10},{9,11},{10,... | collective-permute-start | bytes 3145736 | tf_op jit(solution)/shard_map/ppermute | solution.py:62
  312.2 396.7 %reduce-scatter.5.cloned.1.call-start = ((), (), s32[]{:S(2)}) async-start(), calls=%async_computation.15 | async-start | bytes 5242880 | tf_op jit(solution)/shard_map/reduce_scatter | solution.py:977
  369.5 26.4 %collective-permute-start.38 = (bf16[256,2048]{1,0:T(8,128)(2,1)}, bf16[256,2048]{1,0:T(8,128)(2,1)S(1)}, u32[]{:S(2)}, u32[]{:S(2)}) collective-permute-start(bf16[256,2048]{1,0:T(8,128)(2,1)} %collective-permute-done.14.refs_4_), channel_id=1, source_target_pairs={{0,1},{1,0},{2,3},{3,2},{4,5},{5,4},{6,7},{7,6},{8,9},{9,8},{10,11... | collective-permute-start | bytes 3145736 | tf_op jit(solution)/shard_map/ppermute | solution.py:62
  369.5 27.4 %collective-permute-start.39 = (bf16[256,2048]{1,0:T(8,128)(2,1)}, bf16[256,2048]{1,0:T(8,128)(2,1)S(1)}, u32[]{:S(2)}, u32[]{:S(2)}) collective-permute-start(bf16[256,2048]{1,0:T(8,128)(2,1)} %collective-permute-done.15.refs_6_), channel_id=1, source_target_pairs={{0,1},{1,0},{2,3},{3,2},{4,5},{5,4},{6,7},{7,6},{8,9},{9,8},{10,11... | collective-permute-start | bytes 3145736 | tf_op jit(solution)/shard_map/ppermute | solution.py:62
  393.1 38.6 %collective-permute-start.55 = (bf16[256,2048]{1,0:T(8,128)(2,1)}, bf16[256,2048]{1,0:T(8,128)(2,1)}, u32[]{:S(2)}, u32[]{:S(2)}) collective-permute-start(bf16[256,2048]{1,0:T(8,128)(2,1)} %collective-permute-done.16.refs_4_), channel_id=1, source_target_pairs={{0,1},{1,0},{2,3},{3,2},{4,5},{5,4},{6,7},{7,6},{8,9},{9,8},{10,11... | collective-permute-start | bytes 3145736 | tf_op jit(solution)/shard_map/ppermute | solution.py:62
  395.9 36.5 %collective-permute-start.56 = (bf16[256,2048]{1,0:T(8,128)(2,1)}, bf16[256,2048]{1,0:T(8,128)(2,1)}, u32[]{:S(2)}, u32[]{:S(2)}) collective-permute-start(bf16[256,2048]{1,0:T(8,128)(2,1)} %collective-permute-done.17.refs_6_), channel_id=1, source_target_pairs={{0,1},{1,0},{2,3},{3,2},{4,5},{5,4},{6,7},{7,6},{8,9},{9,8},{10,11... | collective-permute-start | bytes 3145736 | tf_op jit(solution)/shard_map/ppermute | solution.py:62
  397.9 32.7 %collective-permute-start.51 = (bf16[256,2048]{1,0:T(8,128)(2,1)S(1)}, bf16[256,2048]{1,0:T(8,128)(2,1)}, u32[]{:S(2)}, u32[]{:S(2)}) collective-permute-start(bf16[256,2048]{1,0:T(8,128)(2,1)S(1)} %get-tuple-element.705.refs_1_), channel_id=1, source_target_pairs={{0,2},{1,3},{2,0},{3,1},{4,6},{5,7},{6,4},{7,5},{8,10},{9,11},{10,... | collective-permute-start | bytes 3145736 | tf_op jit(solution)/shard_map/ppermute | solution.py:62
  399.3 31.4 %collective-permute-start.52 = (bf16[256,2048]{1,0:T(8,128)(2,1)}, bf16[256,2048]{1,0:T(8,128)(2,1)}, u32[]{:S(2)}, u32[]{:S(2)}) collective-permute-start(bf16[256,2048]{1,0:T(8,128)(2,1)} %get-tuple-element.706.refs_0_), channel_id=1, source_target_pairs={{0,4},{1,5},{2,6},{3,7},{4,0},{5,1},{6,2},{7,3},{8,12},{9,13},{10,... | collective-permute-start | bytes 3145736 | tf_op jit(solution)/shard_map/ppermute | solution.py:62
  431.2 35.5 %collective-permute-start.45 = (bf16[256,2048]{1,0:T(8,128)(2,1)}, bf16[256,2048]{1,0:T(8,128)(2,1)S(1)}, u32[]{:S(2)}, u32[]{:S(2)}) collective-permute-start(bf16[256,2048]{1,0:T(8,128)(2,1)} %collective-permute-done.34.refs_0_), channel_id=1, source_target_pairs={{0,4},{1,5},{2,6},{3,7},{4,0},{5,1},{6,2},{7,3},{8,12},{9,13},{10,... | collective-permute-start | bytes 3145736 | tf_op jit(solution)/shard_map/ppermute | solution.py:62
  431.8 35.4 %collective-permute-start.46 = (bf16[256,2048]{1,0:T(8,128)(2,1)}, bf16[256,2048]{1,0:T(8,128)(2,1)S(1)}, u32[]{:S(2)}, u32[]{:S(2)}) collective-permute-start(bf16[256,2048]{1,0:T(8,128)(2,1)} %collective-permute-done.36.refs_2_), channel_id=1, source_target_pairs={{0,2},{1,3},{2,0},{3,1},{4,6},{5,7},{6,4},{7,5},{8,10},{9,11},{10,... | collective-permute-start | bytes 3145736 | tf_op jit(solution)/shard_map/ppermute | solution.py:62
  471.9 35.6 %collective-permute-start.60 = (bf16[256,2048]{1,0:T(8,128)(2,1)}, bf16[256,2048]{1,0:T(8,128)(2,1)}, u32[]{:S(2)}, u32[]{:S(2)}) collective-permute-start(bf16[256,2048]{1,0:T(8,128)(2,1)} %add_convert_fusion.18), channel_id=1, source_target_pairs={{0,4},{1,5},{2,6},{3,7},{4,0},{5,1},{6,2},{7,3},{8,12},{9,13},{10,... | collective-permute-start | bytes 3145736 | tf_op jit(solution)/shard_map/ppermute | solution.py:62
  473.9 33.7 %collective-permute-start.59 = (bf16[256,2048]{1,0:T(8,128)(2,1)}, bf16[256,2048]{1,0:T(8,128)(2,1)S(1)}, u32[]{:S(2)}, u32[]{:S(2)}) collective-permute-start(bf16[256,2048]{1,0:T(8,128)(2,1)} %add_convert_fusion.19), channel_id=1, source_target_pairs={{0,2},{1,3},{2,0},{3,1},{4,6},{5,7},{6,4},{7,5},{8,10},{9,11},{10,... | collective-permute-start | bytes 3145736 | tf_op jit(solution)/shard_map/ppermute | solution.py:62
  513.5 38.3 %collective-permute-start.66 = (bf16[256,2048]{1,0:T(8,128)(2,1)}, bf16[256,2048]{1,0:T(8,128)(2,1)}, u32[]{:S(2)}, u32[]{:S(2)}) collective-permute-start(bf16[256,2048]{1,0:T(8,128)(2,1)} %get-tuple-element.439), channel_id=1, source_target_pairs={{0,1},{1,0},{2,3},{3,2},{4,5},{5,4},{6,7},{7,6},{8,9},{9,8},{10,11... | collective-permute-start | bytes 3145736 | tf_op jit(solution)/shard_map/ppermute | solution.py:62
  515.1 40.6 %collective-permute-start.40 = (bf16[256,2048]{1,0:T(8,128)(2,1)}, bf16[256,2048]{1,0:T(8,128)(2,1)S(1)}, u32[]{:S(2)}, u32[]{:S(2)}) collective-permute-start(bf16[256,2048]{1,0:T(8,128)(2,1)} %get-tuple-element.400), channel_id=1, source_target_pairs={{0,1},{1,0},{2,3},{3,2},{4,5},{5,4},{6,7},{7,6},{8,9},{9,8},{10,11... | collective-permute-start | bytes 3145736 | tf_op jit(solution)/shard_map/ppermute | solution.py:62
  516.3 35.5 %collective-permute-start.64 = (bf16[256,2048]{1,0:T(8,128)(2,1)}, bf16[256,2048]{1,0:T(8,128)(2,1)}, u32[]{:S(2)}, u32[]{:S(2)}) collective-permute-start(bf16[256,2048]{1,0:T(8,128)(2,1)} %add_convert_fusion.16), channel_id=1, source_target_pairs={{0,2},{1,3},{2,0},{3,1},{4,6},{5,7},{6,4},{7,5},{8,10},{9,11},{10,... | collective-permute-start | bytes 3145736 | tf_op jit(solution)/shard_map/ppermute | solution.py:62
  516.9 34.9 %collective-permute-start.63 = (bf16[256,2048]{1,0:T(8,128)(2,1)}, bf16[256,2048]{1,0:T(8,128)(2,1)S(1)}, u32[]{:S(2)}, u32[]{:S(2)}) collective-permute-start(bf16[256,2048]{1,0:T(8,128)(2,1)} %add_convert_fusion.17), channel_id=1, source_target_pairs={{0,4},{1,5},{2,6},{3,7},{4,0},{5,1},{6,2},{7,3},{8,12},{9,13},{10,... | collective-permute-start | bytes 3145736 | tf_op jit(solution)/shard_map/ppermute | solution.py:62
  555.1 32.5 %collective-permute-start.67 = (bf16[256,2048]{1,0:T(8,128)(2,1)}, bf16[256,2048]{1,0:T(8,128)(2,1)}, u32[]{:S(2)}, u32[]{:S(2)}) collective-permute-start(bf16[256,2048]{1,0:T(8,128)(2,1)} %add_convert_fusion.14), channel_id=1, source_target_pairs={{0,4},{1,5},{2,6},{3,7},{4,0},{5,1},{6,2},{7,3},{8,12},{9,13},{10,... | collective-permute-start | bytes 3145736 | tf_op jit(solution)/shard_map/ppermute | solution.py:62
  557.2 30.4 %collective-permute-start.65 = (bf16[256,2048]{1,0:T(8,128)(2,1)}, bf16[256,2048]{1,0:T(8,128)(2,1)}, u32[]{:S(2)}, u32[]{:S(2)}) collective-permute-start(bf16[256,2048]{1,0:T(8,128)(2,1)} %add_convert_fusion.15), channel_id=1, source_target_pairs={{0,2},{1,3},{2,0},{3,1},{4,6},{5,7},{6,4},{7,5},{8,10},{9,11},{10,... | collective-permute-start | bytes 3145736 | tf_op jit(solution)/shard_map/ppermute | solution.py:62
  558.6 25.5 %collective-permute-start.68 = (bf16[256,2048]{1,0:T(8,128)(2,1)}, bf16[256,2048]{1,0:T(8,128)(2,1)}, u32[]{:S(2)}, u32[]{:S(2)}) collective-permute-start(bf16[256,2048]{1,0:T(8,128)(2,1)} %get-tuple-element.442), channel_id=1, source_target_pairs={{0,1},{1,0},{2,3},{3,2},{4,5},{5,4},{6,7},{7,6},{8,9},{9,8},{10,11... | collective-permute-start | bytes 3145736 | tf_op jit(solution)/shard_map/ppermute | solution.py:62
  587.6 169.9 %reduce-scatter.7.cloned.1.call-start = ((), (), s32[]{:S(2)}) async-start(), calls=%async_computation.16 | async-start | bytes 5242880 | tf_op jit(solution)/shard_map/reduce_scatter | solution.py:1017
  600.2 31.7 %collective-permute-start.70 = (bf16[256,2048]{1,0:T(8,128)(2,1)S(1)}, bf16[256,2048]{1,0:T(8,128)(2,1)S(1)}, u32[]{:S(2)}, u32[]{:S(2)}) collective-permute-start(bf16[256,2048]{1,0:T(8,128)(2,1)S(1)} %get-tuple-element.690.refs_0_), channel_id=1, source_target_pairs={{0,2},{1,3},{2,0},{3,1},{4,6},{5,7},{6,4},{7,5},{8,10},{9,11},{10,... | collective-permute-start | bytes 3145736 | tf_op jit(solution)/shard_map/ppermute | solution.py:62
  600.8 31.1 %collective-permute-start.71 = (bf16[256,2048]{1,0:T(8,128)(2,1)}, bf16[256,2048]{1,0:T(8,128)(2,1)}, u32[]{:S(2)}, u32[]{:S(2)}) collective-permute-start(bf16[256,2048]{1,0:T(8,128)(2,1)} %get-tuple-element.660.refs_1_), channel_id=1, source_target_pairs={{0,4},{1,5},{2,6},{3,7},{4,0},{5,1},{6,2},{7,3},{8,12},{9,13},{10,... | collective-permute-start | bytes 3145736 | tf_op jit(solution)/shard_map/ppermute | solution.py:62
  602.3 45.5 %collective-permute-start.72 = (bf16[256,2048]{1,0:T(8,128)(2,1)}, bf16[256,2048]{1,0:T(8,128)(2,1)S(1)}, u32[]{:S(2)}, u32[]{:S(2)}) collective-permute-start(bf16[256,2048]{1,0:T(8,128)(2,1)} %get-tuple-element.660.refs_1_), channel_id=1, source_target_pairs={{0,2},{1,3},{2,0},{3,1},{4,6},{5,7},{6,4},{7,5},{8,10},{9,11},{10,... | collective-permute-start | bytes 3145736 | tf_op jit(solution)/shard_map/ppermute | solution.py:62
  604.0 44.4 %collective-permute-start.73 = (bf16[256,2048]{1,0:T(8,128)(2,1)S(1)}, bf16[256,2048]{1,0:T(8,128)(2,1)}, u32[]{:S(2)}, u32[]{:S(2)}) collective-permute-start(bf16[256,2048]{1,0:T(8,128)(2,1)S(1)} %get-tuple-element.690.refs_0_), channel_id=1, source_target_pairs={{0,4},{1,5},{2,6},{3,7},{4,0},{5,1},{6,2},{7,3},{8,12},{9,13},{10,... | collective-permute-start | bytes 3145736 | tf_op jit(solution)/shard_map/ppermute | solution.py:62
  651.7 26.2 %collective-permute-start.88 = (bf16[256,2048]{1,0:T(8,128)(2,1)}, bf16[256,2048]{1,0:T(8,128)(2,1)}, u32[]{:S(2)}, u32[]{:S(2)}) collective-permute-start(bf16[256,2048]{1,0:T(8,128)(2,1)} %get-tuple-element.496), channel_id=1, source_target_pairs={{0,1},{1,0},{2,3},{3,2},{4,5},{5,4},{6,7},{7,6},{8,9},{9,8},{10,11... | collective-permute-start | bytes 3145736 | tf_op jit(solution)/shard_map/ppermute | solution.py:62
  652.8 28.6 %collective-permute-start.87 = (bf16[256,2048]{1,0:T(8,128)(2,1)}, bf16[256,2048]{1,0:T(8,128)(2,1)}, u32[]{:S(2)}, u32[]{:S(2)}) collective-permute-start(bf16[256,2048]{1,0:T(8,128)(2,1)} %get-tuple-element.494), channel_id=1, source_target_pairs={{0,1},{1,0},{2,3},{3,2},{4,5},{5,4},{6,7},{7,6},{8,9},{9,8},{10,11... | collective-permute-start | bytes 3145736 | tf_op jit(solution)/shard_map/ppermute | solution.py:62
  693.1 55.9 %collective-permute-start.92 = (bf16[256,2048]{1,0:T(8,128)(2,1)}, bf16[256,2048]{1,0:T(8,128)(2,1)S(1)}, u32[]{:S(2)}, u32[]{:S(2)}) collective-permute-start(bf16[256,2048]{1,0:T(8,128)(2,1)} %add_convert_fusion.13), channel_id=1, source_target_pairs={{0,2},{1,3},{2,0},{3,1},{4,6},{5,7},{6,4},{7,5},{8,10},{9,11},{10,... | collective-permute-start | bytes 3145736 | tf_op jit(solution)/shard_map/ppermute | solution.py:62
  694.2 54.8 %collective-permute-start.93 = (bf16[256,2048]{1,0:T(8,128)(2,1)}, bf16[256,2048]{1,0:T(8,128)(2,1)}, u32[]{:S(2)}, u32[]{:S(2)}) collective-permute-start(bf16[256,2048]{1,0:T(8,128)(2,1)} %add_convert_fusion.12), channel_id=1, source_target_pairs={{0,4},{1,5},{2,6},{3,7},{4,0},{5,1},{6,2},{7,3},{8,12},{9,13},{10,... | collective-permute-start | bytes 3145736 | tf_op jit(solution)/shard_map/ppermute | solution.py:62
  695.6 53.4 %collective-permute-start.94 = (bf16[256,2048]{1,0:T(8,128)(2,1)}, bf16[256,2048]{1,0:T(8,128)(2,1)}, u32[]{:S(2)}, u32[]{:S(2)}) collective-permute-start(bf16[256,2048]{1,0:T(8,128)(2,1)} %add_convert_fusion.11), channel_id=1, source_target_pairs={{0,4},{1,5},{2,6},{3,7},{4,0},{5,1},{6,2},{7,3},{8,12},{9,13},{10,... | collective-permute-start | bytes 3145736 | tf_op jit(solution)/shard_map/ppermute | solution.py:62
  696.2 52.8 %collective-permute-start.95 = (bf16[256,2048]{1,0:T(8,128)(2,1)}, bf16[256,2048]{1,0:T(8,128)(2,1)}, u32[]{:S(2)}, u32[]{:S(2)}) collective-permute-start(bf16[256,2048]{1,0:T(8,128)(2,1)} %add_convert_fusion.10), channel_id=1, source_target_pairs={{0,2},{1,3},{2,0},{3,1},{4,6},{5,7},{6,4},{7,5},{8,10},{9,11},{10,... | collective-permute-start | bytes 3145736 | tf_op jit(solution)/shard_map/ppermute | solution.py:62
  752.5 51.9 %collective-permute-start.97 = (bf16[256,2048]{1,0:T(8,128)(2,1)}, bf16[256,2048]{1,0:T(8,128)(2,1)}, u32[]{:S(2)}, u32[]{:S(2)}) collective-permute-start(bf16[256,2048]{1,0:T(8,128)(2,1)} %add_convert_fusion.8), channel_id=1, source_target_pairs={{0,4},{1,5},{2,6},{3,7},{4,0},{5,1},{6,2},{7,3},{8,12},{9,13},{10,... | collective-permute-start | bytes 3145736 | tf_op jit(solution)/shard_map/ppermute | solution.py:62
  756.1 48.3 %collective-permute-start.96 = (bf16[256,2048]{1,0:T(8,128)(2,1)}, bf16[256,2048]{1,0:T(8,128)(2,1)}, u32[]{:S(2)}, u32[]{:S(2)}) collective-permute-start(bf16[256,2048]{1,0:T(8,128)(2,1)} %add_convert_fusion.9), channel_id=1, source_target_pairs={{0,2},{1,3},{2,0},{3,1},{4,6},{5,7},{6,4},{7,5},{8,10},{9,11},{10,... | collective-permute-start | bytes 3145736 | tf_op jit(solution)/shard_map/ppermute | solution.py:62
  757.6 46.9 %all-to-all-start.4 = ((bf16[8,64,1024]{2,1,0:T(8,128)(2,1)}), bf16[8,64,1024]{2,1,0:T(8,128)(2,1)S(1)}, u32[]{:S(2)}, u32[]{:S(2)}) async-start(bf16[8,64,1024]{2,1,0:T(8,128)(2,1)} %bitcast.223), calls=%async_computation.6 | async-start | bytes 2097152 | tf_op jit(solution)/shard_map/all_to_all | solution.py:1055
  761.1 177.8 %reduce-scatter.9.cloned.1.call-start = ((), (), s32[]{:S(2)}) async-start(), calls=%async_computation.17 | async-start | bytes 3932160 | tf_op jit(solution)/shard_map/reduce_scatter | solution.py:1081
  816.9 32.8 %collective-permute-start.101 = (bf16[256,2048]{1,0:T(8,128)(2,1)}, bf16[256,2048]{1,0:T(8,128)(2,1)}, u32[]{:S(2)}, u32[]{:S(2)}) collective-permute-start(bf16[256,2048]{1,0:T(8,128)(2,1)} %add_convert_fusion.6), channel_id=1, source_target_pairs={{0,4},{1,5},{2,6},{3,7},{4,0},{5,1},{6,2},{7,3},{8,12},{9,13},{10,... | collective-permute-start | bytes 3145736 | tf_op jit(solution)/shard_map/ppermute | solution.py:62
  820.2 29.6 %collective-permute-start.99 = (bf16[256,2048]{1,0:T(8,128)(2,1)}, bf16[256,2048]{1,0:T(8,128)(2,1)}, u32[]{:S(2)}, u32[]{:S(2)}) collective-permute-start(bf16[256,2048]{1,0:T(8,128)(2,1)} %add_convert_fusion.7), channel_id=1, source_target_pairs={{0,2},{1,3},{2,0},{3,1},{4,6},{5,7},{6,4},{7,5},{8,10},{9,11},{10,... | collective-permute-start | bytes 3145736 | tf_op jit(solution)/shard_map/ppermute | solution.py:62
  869.4 43.7 %collective-permute-start.106 = (bf16[256,2048]{1,0:T(8,128)(2,1)}, bf16[256,2048]{1,0:T(8,128)(2,1)}, u32[]{:S(2)}, u32[]{:S(2)}) collective-permute-start(bf16[256,2048]{1,0:T(8,128)(2,1)} %add_convert_fusion.4), channel_id=1, source_target_pairs={{0,2},{1,3},{2,0},{3,1},{4,6},{5,7},{6,4},{7,5},{8,10},{9,11},{10,... | collective-permute-start | bytes 3145736 | tf_op jit(solution)/shard_map/ppermute | solution.py:62
  870.0 43.2 %collective-permute-start.105 = (bf16[256,2048]{1,0:T(8,128)(2,1)}, bf16[256,2048]{1,0:T(8,128)(2,1)}, u32[]{:S(2)}, u32[]{:S(2)}) collective-permute-start(bf16[256,2048]{1,0:T(8,128)(2,1)} %add_convert_fusion.5), channel_id=1, source_target_pairs={{0,4},{1,5},{2,6},{3,7},{4,0},{5,1},{6,2},{7,3},{8,12},{9,13},{10,... | collective-permute-start | bytes 3145736 | tf_op jit(solution)/shard_map/ppermute | solution.py:62
  872.5 33.8 %all-to-all-start.6 = ((bf16[8,32,2048]{2,1,0:T(8,128)(2,1)}), bf16[8,32,2048]{2,1,0:T(8,128)(2,1)S(1)}, u32[]{:S(2)}, u32[]{:S(2)}) async-start(bf16[8,32,2048]{2,1,0:T(8,128)(2,1)} %bitcast.210), calls=%async_computation.9 | async-start | bytes 2097152 | tf_op jit(solution)/shard_map/all_to_all | solution.py:1133
  876.1 76.3 %reduce-scatter.11.cloned.1.call-start = ((), (), s32[]{:S(2)}) async-start(), calls=%async_computation.18 | async-start | bytes 1310720 | tf_op jit(solution)/shard_map/reduce_scatter | solution.py:1122
  893.1 25.7 %collective-permute-start.104 = (bf16[256,2048]{1,0:T(8,128)(2,1)}, bf16[256,2048]{1,0:T(8,128)(2,1)}, u32[]{:S(2)}, u32[]{:S(2)}) collective-permute-start(bf16[256,2048]{1,0:T(8,128)(2,1)} %get-tuple-element.575), channel_id=1, source_target_pairs={{0,1},{1,0},{2,3},{3,2},{4,5},{5,4},{6,7},{7,6},{8,9},{9,8},{10,11... | collective-permute-start | bytes 3145736 | tf_op jit(solution)/shard_map/ppermute | solution.py:62
  909.5 28.6 %all-to-all-start.7 = ((f32[8,32,256]{2,1,0:T(8,128)}), f32[8,32,256]{2,1,0:T(8,128)S(1)}, u32[]{:S(2)}, u32[]{:S(2)}) async-start(f32[8,32,256]{2,1,0:T(8,128)} %bitcast.224), calls=%async_computation.10 | async-start | bytes 524288 | tf_op jit(solution)/shard_map/all_to_all | solution.py:1157
  916.8 40.9 %collective-permute-start.109 = (bf16[256,2048]{1,0:T(8,128)(2,1)}, bf16[256,2048]{1,0:T(8,128)(2,1)}, u32[]{:S(2)}, u32[]{:S(2)}) collective-permute-start(bf16[256,2048]{1,0:T(8,128)(2,1)} %add_convert_fusion.2), channel_id=1, source_target_pairs={{0,4},{1,5},{2,6},{3,7},{4,0},{5,1},{6,2},{7,3},{8,12},{9,13},{10,... | collective-permute-start | bytes 3145736 | tf_op jit(solution)/shard_map/ppermute | solution.py:62
  921.9 35.8 %collective-permute-start.107 = (bf16[256,2048]{1,0:T(8,128)(2,1)}, bf16[256,2048]{1,0:T(8,128)(2,1)}, u32[]{:S(2)}, u32[]{:S(2)}) collective-permute-start(bf16[256,2048]{1,0:T(8,128)(2,1)} %add_convert_fusion.3), channel_id=1, source_target_pairs={{0,2},{1,3},{2,0},{3,1},{4,6},{5,7},{6,4},{7,5},{8,10},{9,11},{10,... | collective-permute-start | bytes 3145736 | tf_op jit(solution)/shard_map/ppermute | solution.py:62
  923.4 30.8 %collective-permute-start.110 = (bf16[256,2048]{1,0:T(8,128)(2,1)}, bf16[256,2048]{1,0:T(8,128)(2,1)}, u32[]{:S(2)}, u32[]{:S(2)}) collective-permute-start(bf16[256,2048]{1,0:T(8,128)(2,1)} %get-tuple-element.586), channel_id=1, source_target_pairs={{0,1},{1,0},{2,3},{3,2},{4,5},{5,4},{6,7},{7,6},{8,9},{9,8},{10,11... | collective-permute-start | bytes 3145736 | tf_op jit(solution)/shard_map/ppermute | solution.py:62
  963.0 31.3 %all-to-all-start.8 = ((f32[32,1,768]{2,1,0:T(1,128)}), f32[32,1,768]{2,1,0:T(1,128)S(1)}, u32[]{:S(2)}, u32[]{:S(2)}) async-start(f32[32,1,768]{2,1,0:T(1,128)} %copy.112), calls=%async_computation.11 | async-start | bytes 196608 | tf_op jit(solution)/shard_map/all_to_all | solution.py:1189
  (248 other events, 2977.3 us)
Sparse Core Ops, SparseCore 0:
  29.6 62.8 all-gather.4
  94.6 96.7 all-gather.8
  312.4 83.8 all-gather.6
  587.7 80.0 reduce-scatter.4
  670.6 77.2 reduce-scatter.6
  849.9 72.9 reduce-scatter.8
  925.2 27.1 reduce-scatter.10

commit v3 on v2

--- a/solution.py
+++ b/solution.py
@@ -113,7 +113,7 @@
             total(flat[n], swapped(flat[n + 2 * bit], bit)).astype(bf16) for n in range(2 * bit)
         ]
         bit //= 2
-    return [total(flat[h], swapped(flat[h + 2], 1)) for h in range(2)]
+    return [[flat[h], swapped(flat[h + 2], 1)] for h in range(2)]
 
 
 def scattered_sum(make, groups, first=None, second=None):
@@ -142,12 +142,12 @@
     own, a0, a1 = after((own, swapped(a0, 4), swapped(a1, 2)))
     x0 = total(near[0], swapped(near[1], 1), a0).astype(bf16)
     y1 = total(near[2], swapped(near[3], 1), a1).astype(bf16)
-    mine = [total(own[0], swapped(own[2], 1), y0), total(own[1], swapped(own[3], 1), x1)]
+    mine = [[own[0], swapped(own[2], 1), y0], [own[1], swapped(own[3], 1), x1]]
     done, use = second((x0, y1)) if second else ((), None)
     x0, y1, mine, done = after((swapped(x0, 2), swapped(y1, 4), mine, done))
     if use:
         use(done)
-    return [total(mine[0], x0), total(mine[1], y1)]
+    return [mine[0] + [x0], mine[1] + [y1]]
 
 
 def after(values, *earlier):
@@ -251,6 +251,63 @@
         6 * steps * size * wide * width,
         2 * steps * size * wide,
     )
+
+
+def norm_back_kernel(count, low, *refs):
+    values, terms, rest = refs[:2], refs[2 : 2 + 2 * count], refs[2 + 2 * count :]
+    extra_ref, gain_ref, grad_ref, sum_ref = rest[:4]
+
+    @pl.when(pl.program_id(0) == 0)
+    def _():
+        sum_ref[...] = jnp.zeros_like(sum_ref)
+
+    def average(one):
+        return jnp.mean(one, axis=-1, keepdims=True)
+
+    def add_rows(place, one):
+        sum_ref[place : place + 1, :] += jnp.sum(one, axis=0, keepdims=True)
+
+    for h in range(2):
+        value = values[h][...].astype(f32)
+        grad = total(*[ref[...] for ref in terms[h * count : (h + 1) * count]])
+        extra = extra_ref[h].astype(f32)
+        centred = value - average(value)
+        rate = lax.rsqrt(average(centred * centred) + epsilon)
+        unit = centred * rate
+        scaled = grad * gain_ref[...]
+        back = (scaled - average(scaled) - unit * average(scaled * unit)) * rate + extra
+        grad_ref[h] = back
+        add_rows(0, grad * unit)
+        add_rows(1, grad)
+        if low:
+            rounded = back.astype(bf16)
+            rest[4 + h][...] = rounded
+            add_rows(2, rounded.astype(f32))
+            add_rows(3, extra)
+
+
+def norm_back(values, sums, extra, gain, low):
+    half, wide = values[0].shape
+    chunk = min(half, 64)
+    rows = half_rows(chunk, wide)
+    both = pl.BlockSpec((2, chunk, wide), lambda s: (0, s, 0))
+    outs = [
+        jax.ShapeDtypeStruct((2, half, wide), f32), jax.ShapeDtypeStruct((8, wide), f32)
+    ] + [jax.ShapeDtypeStruct((half, wide), bf16)] * (2 * low)
+    return pl.pallas_call(
+        functools.partial(norm_back_kernel, len(sums[0]), low),
+        grid=(half // chunk,),
+        in_specs=[rows] * (2 + 2 * len(sums[0])) + [both, held(gain.shape)],
+        out_specs=[both, pl.BlockSpec((8, wide), lambda s: (0, 0))] + [rows] * (2 * low),
+        out_shape=outs,
+        compiler_params=pltpu.CompilerParams(
+            dimension_semantics=("arbitrary",), vmem_limit_bytes=40 * 2**20
+        ),
+        cost_estimate=pl.CostEstimate(
+            flops=80 * half * wide, bytes_accessed=36 * half * wide, transcendentals=0
+        ),
+        name="norm_back",
+    )(*values, *sums[0], *sums[1], extra, gain)
 
 
 def project_kernel(n_ins, n_earlier, *refs):
@@ -835,6 +892,10 @@
     up_parts = up_parts.reshape(shards, rows_held, own_units)
     more_slots = -(-padded_summ // half)
 
+    query_shift = own_columns(query_shift)
+    value_shift = own_columns(value_shift)
+    qkv_shift = jnp.concatenate([query_shift, jnp.zeros_like(query_shift), value_shift])[None]
+
     def normed_group(g, group, normed):
         return norm_rows(
             g, group, gain_one[None], shift_one[None], normed, 4 * groups + more_slots
@@ -844,36 +905,35 @@
         mine = [*token_halves, *[swapped(one, 1) for one in token_halves]]
         normed = normed_group(0, mine, [])
         x0, y1, x1, y0 = token_hops
-        x0, y1 = after((x0, y1), normed[0], up_parts, *grad_own)
+        x0, y1, x1, y0 = after((x0, y1, x1, y0), normed[0], up_parts, *grad_own)
         a0, a1 = swapped(x0, 4), swapped(y1, 2)
         normed = normed_group(1, [x0, swapped(x0, 1), y1, swapped(y1, 1)], normed)
-        x1, y0, a0, a1 = after((x1, y0, a0, a1), normed[0])
+        normed = normed_group(2, [x1, swapped(x1, 1), y0, swapped(y0, 1)], normed)
+        made = triple(0, groups - 1, slot_rows(normed[0]), qkv_own, qkv_shift, [], count)
+        a0, a1, made = after((a0, a1, made))
         last_tokens = [a0, a1, swapped(a0, 1), swapped(a1, 1)]
-        normed = normed_group(2, [x1, swapped(x1, 1), y0, swapped(y0, 1)], normed)
     else:
         normed = []
         token_groups = passed_on(token_halves, token_hops)
         last_tokens = token_groups[-1]
         for g in range(groups - 1):
             normed = normed_group(g, token_groups[g], normed)
+        made = triple(0, groups - 1, slot_rows(normed[0]), qkv_own, qkv_shift, [], count)
     up_shift = lax.dynamic_index_in_dim(
         vectors[:, 8 * rows_held :].reshape(items, shards, units_held), position, 1, keepdims=False
     ).reshape(1, own_units)
-    query_shift = own_columns(query_shift)
-    value_shift = own_columns(value_shift)
-    qkv_shift = jnp.concatenate([query_shift, jnp.zeros_like(query_shift), value_shift])[None]
-
-    early = token_hops[:1] if eight else ()
+
+    early = token_hops[:2] if eight else ()
     if spread:
         both = after(jnp.concatenate([out_weight, down_weight], axis=0), *early)
         both = lax.all_gather(both, "dp", axis=0)
         out_own = both[:, :rows_held].reshape(own_width, width)
-        down_own = both[:, rows_held:].reshape(own_units, width)
+        down_shares = both
     else:
         out_own = lax.dynamic_slice_in_dim(
             lax.all_gather(out_weight, BOTH, axis=0, tiled=True), position * own_width, own_width, 0
         )
-        down_own = lax.all_gather(down_weight, "dp", axis=0, tiled=True)
+        down_shares = lax.all_gather(down_weight, "dp", axis=0)
     up_parts = after(up_parts, last_tokens[0])
     up_parts = lax.all_to_all(up_parts, "fsdp", 0, 0, tiled=True)
     grad_own = after(grad_own, *last_tokens)
@@ -883,18 +943,11 @@
         jnp.broadcast_to(summaries, (shards,) + summaries.shape[1:]), last_tokens[0]
     )
     summ_full = lax.all_to_all(summ_full, "fsdp", 0, 0, tiled=True)
-    made = triple(0, groups - 1, slot_rows(normed[0]), qkv_own, qkv_shift, [], count)
-    last_tokens, made = after((last_tokens, made))
     normed = normed_group(groups - 1, last_tokens, normed)
     queries, keys, values = triple(
         groups - 1, 1, slot_rows(normed[0]), qkv_own, qkv_shift, made, count
     )
-    queries, keys, values, summ_full, up_parts = after(
-        (queries, keys, values, summ_full, up_parts)
-    )
-    up_own = lax.all_gather(
-        up_parts.reshape(shards * rows_held, own_units), "dp", axis=0, tiled=True
-    )
+    queries, keys, values, summ_full = after((queries, keys, values, summ_full))
     summ_full = summ_full.transpose(1, 0, 2).reshape(summary_rows, width)
     summ_inputs = jnp.pad(summ_full, ((0, padded_summ - summary_rows), (0, 0))).astype(f32)
     normed_summ = layer_norm(summ_inputs, gain_one, shift_one).astype(bf16)
@@ -920,7 +973,7 @@
             x0, y1, x1, y0 = grad_hops
             a0, a1 = swapped(x0, 4), swapped(y1, 2)
         elif eight:
-            one, log, a0, a1 = after((one, log, a0, a1))
+            one, log, a0, a1, up_parts, out_own = after((one, log, a0, a1, up_parts, out_own))
             grad_groups = [
                 [*grad_own, swapped(grad_own[0], 1), swapped(grad_own[1], 1)],
                 [x0, swapped(x0, 1), y1, swapped(y1, 1)],
@@ -931,15 +984,26 @@
         logs.append(log)
     if not eight:
         grad_groups = passed_on(grad_own, grad_hops)
+    up_own = lax.all_gather(
+        up_parts.reshape(shards * rows_held, own_units), "dp", axis=0, tiled=True
+    )
     attn_slots = [one.reshape(4 * groups, half, own_width // parts) for one in attn]
     inputs = [one.astype(f32) for one in halves(tokens[0])]
     proj_sums = scattered_sum(
         lambda g, earlier: project(g, attn_slots, after(out_own, *earlier), width), groups
     )
-    resid = [inputs[h] + proj_sums[h] + out_shift for h in range(2)]
+    resid = [
+        total(inputs[h], *proj_sums[h]) + out_shift for h in range(2)
+    ]
 
     normed_two_own = [layer_norm(one, gain_two, shift_two).astype(bf16) for one in resid]
     two_hops = sent(normed_two_own)
+    down_own = after(down_shares, *normed_two_own)[:, down_shares.shape[1] - units_held :]
+    down_own = down_own.reshape(own_units, width)
+    if eight:
+        x0, y1, x1, y0 = two_hops
+        x0, y1, down_own = after((x0, y1, down_own))
+        two_hops = (x0, y1, x1, y0)
     two_groups = passed_on(normed_two_own, two_hops)
     made = []
     back = {}
@@ -975,40 +1039,31 @@
     grad_normed_two = scattered_sum(feed, groups, None, down_grad_of)
     feed_made = made
     down_grad = lax.psum_scatter(kept["down"], "dp", scatter_dimension=0, tiled=True)
-    grad_floats = [one.astype(f32) for one in halves(output_grad[0])]
-    down_shift_grad = jnp.sum(output_grad[0].astype(f32), axis=0)
-
-    def norm_back(values, gains, shifts, grads):
-        pulled = [
-            jax.vjp(layer_norm, value, gains, shifts)[1](grad) for value, grad in zip(values, grads)
-        ]
-        return (
-            [one[0] for one in pulled],
-            sum(one[1] for one in pulled),
-            sum(one[2] for one in pulled),
-        )
-
-    grad_two, gain_two_grad, shift_two_grad = norm_back(resid, gain_two, shift_two, grad_normed_two)
-    grad_resid = [grad_two[h] + grad_floats[h] for h in range(2)]
-
-    grad_proj = [one.astype(bf16) for one in grad_resid]
-    out_shift_grad = sum(jnp.sum(one.astype(f32), axis=0) for one in grad_proj)
+    grad_resid, sums_two, *grad_proj = norm_back(
+        resid, grad_normed_two, output_grad.reshape(2, half, width), gain_two[None], True
+    )
+
     proj_hops = sent(grad_proj)
     if eight:
         mine = grad_proj + [swapped(one, 1) for one in grad_proj]
         made = project_back(0, mine, out_own, [], 4 * groups)
         up_grad = up_grad_of((made[0],))
-        x0, y1, x1, y0 = proj_hops
-        x0, y1, x1, y0, up_grad = after((x0, y1, x1, y0, up_grad))
-        up_grad_dot = up_grad
+        x0, y1, x1, y0, up_grad = after((*proj_hops, up_grad))
+        own, near, later, far = after([ahead[g] for g in range(groups)], up_grad)
+        sends = [
+            paired(later[0], later[1]), paired(later[2], later[3]),
+            paired(far[0], far[2]), paired(far[1], far[3]),
+        ]
+        near = [total(near[0], swapped(near[1], 1)), total(near[2], swapped(near[3], 1))]
+        own = [total(own[0], swapped(own[2], 1)), total(own[1], swapped(own[3], 1))]
         a0, a1 = swapped(x0, 4), swapped(y1, 2)
         made = project_back(
             1, [x0, swapped(x0, 1), y1, swapped(y1, 1)], out_own, made, 4 * groups
         )
-        x1, y0, a0, a1 = after((x1, y0, a0, a1), made[0])
         made = project_back(
             2, [x1, swapped(x1, 1), y0, swapped(y0, 1)], out_own, made, 4 * groups
         )
+        a0, a1, made, near, own, sends = after((a0, a1, made, near, own, sends))
         proj_groups = [None, None, None, [a0, a1, swapped(a0, 1), swapped(a1, 1)]]
     else:
         up_grad = up_grad_of(())
@@ -1019,23 +1074,13 @@
     if not eight:
         up_grad = lax.all_to_all(up_grad, "fsdp", 0, 0, tiled=True)
     ahead = [ahead[g] for g in range(groups)]
-    if eight:
-        own, near, later, far = after(ahead, up_grad_dot)
-        x1, y0 = paired(later[0], later[1]), paired(later[2], later[3])
-        a0, a1 = paired(far[0], far[2]), paired(far[1], far[3])
-        near = [total(near[0], swapped(near[1], 1)), total(near[2], swapped(near[3], 1))]
-        own = [total(own[0], swapped(own[2], 1)), total(own[1], swapped(own[3], 1))]
     for g in range(groups - 1 if eight else 0, groups):
         halves_now = proj_groups[g]
-        if eight:
-            halves_now, x1, y0, a0, a1, near, own = after(
-                (halves_now, x1, y0, a0, a1, near, own)
-            )
         made = project_back(g, halves_now, out_own, made, 4 * groups)
     grad_attn, proj_rows = (flat(one) for one in made)
     grad_attn, down_grad = after((grad_attn, down_grad))
     if eight:
-        x1, y0, a0, a1 = after((x1, y0, a0, a1), *proj_groups[-1])
+        x1, y0, a0, a1 = after(sends, *proj_groups[-1])
         travelling = [swapped(x1, 2), swapped(y0, 4), swapped(a0, 4), swapped(a1, 2)]
     else:
         result = plain_scattered_sum(ahead)
@@ -1078,6 +1123,7 @@
         return grad, functools.partial(kept.__setitem__, "qkv")
 
     def side_work(earlier):
+        kept["late"] = earlier
         grad = lax.psum_scatter(kept["qkv"], "dp", scatter_dimension=0, tiled=True)
         up_now, down_now, result_parts = after((up_grad, down_grad, result_terms), *earlier)
         grad = after(grad, *earlier).reshape(shards, rows_held, 3 * own_width)
@@ -1097,7 +1143,7 @@
         x0, y1 = travelling
         result_terms = [(resid[0], own[0], y0, x0), (resid[1], own[1], x1, y1)]
     else:
-        result_terms = [(resid[h], result[h]) for h in range(2)]
+        result_terms = [(resid[h], *result[h]) for h in range(2)]
 
     def grad_rows_back(g, earlier):
         if g == 1 or not eight:
@@ -1131,6 +1177,7 @@
         )
     out_grad = out_grad.astype(f32)
     grad_normed_summ = lax.all_to_all(kept["summ"], "fsdp", 0, 0, tiled=True)
+    grad_normed_summ = after(grad_normed_summ, *kept["late"])
     grad_normed_summ = jnp.sum(grad_normed_summ.astype(f32), axis=0)
     summ_own = lax.dynamic_slice_in_dim(
         jnp.pad(summ_inputs, more_rows),
@@ -1149,13 +1196,15 @@
     up_shift_grad = sum(unit_sums)
     query_shift_grad = jnp.concatenate([one[5][0] for one in pulled])
     value_shift_grad = jnp.concatenate([one[5][1] for one in pulled])
-    grad_one, gain_one_grad, shift_one_grad = norm_back(inputs, gain_one, shift_one, grad_normed)
-    grad_inputs = jnp.concatenate([grad_one[h] + grad_resid[h] for h in range(2)], axis=0)
+    grad_inputs, sums_one = norm_back(
+        halves(tokens[0]), grad_normed, grad_resid, gain_one[None], False
+    )
+    grad_inputs = grad_inputs.reshape(tok_rows, width)
     _, norm_summ_pull = jax.vjp(layer_norm, summ_own, gain_one, shift_one)
     grad_summ, gain_summ_grad, shift_summ_grad = norm_summ_pull(grad_normed_summ)
     summary_cols = summaries.shape[2]
     grad_summ = lax.all_to_all(
-        grad_summ.reshape(summ_share, shards, summary_cols).transpose(1, 0, 2),
+        after(grad_summ, sums_one).reshape(summ_share, shards, summary_cols).transpose(1, 0, 2),
         "fsdp",
         0,
         0,
@@ -1165,14 +1214,14 @@
 
     vector_grads = jnp.stack(
         [
-            gain_one_grad + gain_summ_grad,
-            shift_one_grad + shift_summ_grad,
+            sums_one[0] + gain_summ_grad,
+            sums_one[1] + shift_summ_grad,
             whole_columns(query_shift_grad),
             whole_columns(value_shift_grad),
-            out_shift_grad,
-            gain_two_grad,
-            shift_two_grad,
-            down_shift_grad,
+            sums_two[2],
+            sums_two[0],
+            sums_two[1],
+            sums_two[3],
         ]
     )
     vector_grads = vector_grads.reshape(8, devices, rows_held).transpose(1, 0, 2)

time: 1010 us -> 960 us (0.950)
  waiting for transfers between devices: 229 us -> 180 us
  other arithmetic: 124 us -> 87.4 us
  Pallas kernels: 364 us -> 398 us
    ppermute x112, waiting for transfers between devices: 188 us -> 157 us  [swapped(): return lax.ppermute(x, 'fsdp', [(i, i ^ bit) for i in range(devices)])]
    all_to_all x1, waiting for transfers between devices: 22.8 us -> 0.01 us  [per_device(): up_parts = lax.all_to_all(up_parts, 'fsdp', 0, 0, tiled=True)]
    pallas_call x0 -> x2, Pallas kernels: none -> 18.5 us  [norm_back(): pl.pallas_call(functools.partial(norm_back_kernel, len(sums[0]), low), gr...]
    add x10 -> x4, other arithmetic: 24.6 us -> 8.13 us  [total(): result = result + term.astype(f32)]
    all_to_all x1, starting transfers between devices: 16.5 us -> 2.57 us  [per_device(): lax.all_to_all(all_grads, BOTH, 0, 0, tiled=True)]
    unnamed x390 -> x297, local copies, waits for them, and re-layouts: 34.1 us -> 40.1 us
  transfers between devices with their start and end apart: 127 -> 127, of which waited for: 39 -> 40; matrix products, arithmetic and copies ran while one was open for 23% -> 22% of each run, Pallas kernels for 35% -> 40%
where the time goes in v3:
time: 960 us; the launch traced here: 955 us
  Pallas kernels  398 us (41%)
  waiting for transfers between devices  180 us (19%)
  starting transfers between devices  99.9 us (10%)
  other arithmetic  87.4 us (9%)
  matrix products  78.8 us (8%)
  local copies, waits for them, and re-layouts  77.1 us (8%)
  blocking collectives  17.6 us (2%)
  between operations  16.8 us (2%)
    pallas_call x22, Pallas kernels, group_call(): pl.pallas_call(functools.partial(kernel, len(ins), len(earlier)), grid=(s...  232 us
    ppermute x112, waiting for transfers between devices, swapped(): return lax.ppermute(x, 'fsdp', [(i, i ^ bit) for i in range(devices)])  157 us
    pallas_call x2, Pallas kernels, attn_backward(): pl.pallas_call(functools.partial(attn_backward_kernel, block, half, heads...  89.9 us
    dot_general x6, matrix products, dot(): return lax.dot_general(left, right, dims, preferred_element_type=f32)  78.8 us
    ppermute x112, starting transfers between devices, swapped(): return lax.ppermute(x, 'fsdp', [(i, i ^ bit) for i in range(devices)])  68.2 us
    pallas_call x2, Pallas kernels, attn_forward(): pl.pallas_call(functools.partial(attn_forward_kernel, block, half, heads)...  54.9 us
    unnamed x297, local copies, waits for them, and re-layouts  40.1 us
    convert_element_type x16, other arithmetic, paired(): return total(own, swapped(other, 1)).astype(bf16)  26.9 us
  transfers between devices with their start and end apart: 127, of which 40 were waited for; matrix products, arithmetic and copies ran while one was open for 22% of the time, Pallas kernels for 40%

profile of v3, /device:TPU:0, one launch (start us, length us, event | category | flops | bytes accessed | tf_op | source)
XLA Modules:
  0.0 954.8 jit_solution(345376751533401332)
XLA Ops:
  11.6 17.6 %all_to_all.53 = bf16[8,64,768]{2,1,0:T(8,128)(2,1)} all-to-all(bf16[8,64,768]{2,1,0:T(8,128)(2,1)S(1)} %pad_maximum_fusion.2), channel_id=1, replica_groups=mesh['dp'=4,'fsdp'=8] {'fsdp'}, dimensions={0} | all-to-all | bytes 1572864 | tf_op jit(solution)/shard_map/all_to_all | solution.py:872
  30.2 4.0 all-to-all-start.1
  36.2 5.7 all-to-all-done.1
  45.8 21.4 %collective-permute-done.refs_0_ = bf16[256,2048]{1,0:T(8,128)(2,1)S(1)} collective-permute-done((bf16[256,2048]{1,0:T(8,128)(2,1)S(1)}, bf16[256,2048]{1,0:T(8,128)(2,1)S(1)}, u32[]{:S(2)}, u32[]{:S(2)}) %collective-permute-start) | collective-permute-done | bytes 1048608 | tf_op jit(solution)/shard_map/ppermute | solution.py:62
  75.6 3.1 slice_bitcast_fusion
  79.6 5.7 norm_rows.4.refs_6_
  85.4 7.9 collective-permute-done.2.refs_0_
  100.2 5.9 norm_rows.5.refs_6_
  106.2 5.9 norm_rows.6.refs_6_
  112.1 14.5 %triple.2 = (bf16[4096,256]{1,0:T(8,128)(2,1)}, bf16[4096,256]{1,0:T(8,128)(2,1)}, bf16[4096,256]{1,0:T(8,128)(2,1)}) custom-call(bf16[4352,2048]{1,0:T(8,128)(2,1)} %bitcast.147, bf16[2048,768]{1,0:T(8,128)(2,1)} %all-gather.5.cloned.1.call-done.refs_1_.refs_6_, f32[1,768]{1,0:T(1,128)S(1)} %broadcast_in_dim.33.refs_2_), custom_call_target="tpu_custom_call" | custom-call | flops 9663676416 | bytes 12582912 | tf_op jit(solution)/shard_map/triple/pallas_call | solution.py:177
  128.2 3.8 all-to-all-start.2
  137.4 5.8 norm_rows.7
  143.2 7.6 triple.3
  155.4 27.4 %attn_forward.2 = (bf16[4096,128]{1,0:T(8,128)(2,1)S(1)}, f32[8,4096]{1,0:T(8,128)S(1)}) custom-call(s32[40]{0:T(128)S(1)} %pad_add_fusion.plan_ref, bf16[4096,256]{1,0:T(8,128)(2,1)S(1)} %copy-done.4, bf16[4096,256]{1,0:T(8,128)(2,1)S(1)} %copy-done.5, bf16[4096,256]{1,0:T(8,128)(2,1)S(1)} %copy-done.7, bf16[160,256]{1,0:T(8,128)(2,1)S(1)} %get-tuple-element.693.sk_ref, ...), custom_call_target="tpu_custom_call" | custom-call | flops 8589934592 | bytes 4194304 | tf_op jit(solution)/shard_map/attn_forward/pallas_call | solution.py:671
  183.8 3.0 collective-permute-done.14.refs_4_
  189.0 4.2 all-to-all-start.3
  196.9 27.4 %attn_forward.3 = (bf16[4096,128]{1,0:T(8,128)(2,1)S(1)}, f32[8,4096]{1,0:T(8,128)S(1)}) custom-call(s32[40]{0:T(128)S(1)} %pad_add_fusion.plan_ref, bf16[4096,256]{1,0:T(8,128)(2,1)S(1)} %copy-done.4, bf16[4096,256]{1,0:T(8,128)(2,1)S(1)} %copy-done.6, bf16[4096,256]{1,0:T(8,128)(2,1)S(1)} %copy-done.8, bf16[160,256]{1,0:T(8,128)(2,1)S(1)} %get-tuple-element.693.sk_ref, ...), custom_call_target="tpu_custom_call" | custom-call | flops 8589934592 | bytes 4194304 | tf_op jit(solution)/shard_map/attn_forward/pallas_call | solution.py:671
  227.7 4.0 project.8
  240.1 3.9 project.9
  244.0 17.7 %collective-permute-done.23 = bf16[256,2048]{1,0:T(8,128)(2,1)S(1)} collective-permute-done((bf16[256,2048]{1,0:T(8,128)(2,1)S(1)}, bf16[256,2048]{1,0:T(8,128)(2,1)S(1)}, u32[]{:S(2)}, u32[]{:S(2)}) %collective-permute-start.23) | collective-permute-done | bytes 1048608 | tf_op jit(solution)/shard_map/ppermute | solution.py:62
  271.5 3.9 project.10
  276.2 4.0 project.11
  280.2 13.2 %collective-permute-done.28 = bf16[256,2048]{1,0:T(8,128)(2,1)} collective-permute-done((bf16[256,2048]{1,0:T(8,128)(2,1)S(1)}, bf16[256,2048]{1,0:T(8,128)(2,1)}, u32[]{:S(2)}, u32[]{:S(2)}) %collective-permute-start.28) | collective-permute-done | bytes 1048608 | tf_op jit(solution)/shard_map/ppermute | solution.py:62
  296.2 3.1 add_convert_fusion.22
  299.9 3.1 add_convert_fusion.23
  304.1 19.5 %collective-permute-done.31 = bf16[256,2048]{1,0:T(8,128)(2,1)S(1)} collective-permute-done((bf16[256,2048]{1,0:T(8,128)(2,1)}, bf16[256,2048]{1,0:T(8,128)(2,1)S(1)}, u32[]{:S(2)}, u32[]{:S(2)}) %collective-permute-start.31) | collective-permute-done | bytes 1048608 | tf_op jit(solution)/shard_map/ppermute | solution.py:62
  323.6 3.4 collective-permute-done.29
  328.0 5.4 fusion.24
  339.1 4.8 slice.173
  343.9 15.8 %collective-permute-done.34.refs_0_ = bf16[256,2048]{1,0:T(8,128)(2,1)S(1)} collective-permute-done((bf16[256,2048]{1,0:T(8,128)(2,1)}, bf16[256,2048]{1,0:T(8,128)(2,1)S(1)}, u32[]{:S(2)}, u32[]{:S(2)}) %collective-permute-start.34) | collective-permute-done | bytes 1048608 | tf_op jit(solution)/shard_map/ppermute | solution.py:62
  366.4 29.8 %feed_forward.4 = (bf16[16,256,1024]{2,1,0:T(8,128)(2,1)}, bf16[16,256,1024]{2,1,0:T(8,128)(2,1)}, bf16[16,256,2048]{2,1,0:T(8,128)(2,1)}, bf16[16,256,2048]{2,1...) custom-call(bf16[256,2048]{1,0:T(8,128)(2,1)} %copy-done.136, ...), custom_call_target="tpu_custom_call" | custom-call | flops 17179869184 | bytes 33554432 | tf_op jit(solution)/shard_map/feed_forward/pallas_call | solution.py:177
  401.6 30.1 %feed_forward.5 = (bf16[16,256,1024]{2,1,0:T(8,128)(2,1)}, bf16[16,256,1024]{2,1,0:T(8,128)(2,1)}, bf16[16,256,2048]{2,1,0:T(8,128)(2,1)}, bf16[16,256,2048]{2,1...) custom-call(bf16[256,2048]{1,0:T(8,128)(2,1)} %collective-permute-do, ...), custom_call_target="tpu_custom_call", output_to_operand_aliasing={{0}: (11, {}), {1}: (12, {}), {2}: (13, {}), {3}: (14, {})} | custom-call | flops 17179869184 | bytes 33554432 | tf_op jit(solution)/shard_map/feed_forward/pallas_call | solution.py:177
  444.3 30.0 %feed_forward.6 = (bf16[16,256,1024]{2,1,0:T(8,128)(2,1)}, bf16[16,256,1024]{2,1,0:T(8,128)(2,1)}, bf16[16,256,2048]{2,1,0:T(8,128)(2,1)}, bf16[16,256,2048]{2,1...) custom-call(bf16[256,2048]{1,0:T(8,128)(2,1)} %copy-done.67, ...), custom_call_target="tpu_custom_call", output_to_operand_aliasing={{0}: (11, {}), {1}: (12, {}), {2}: (13, {}), {3}: (14, {})} | custom-call | flops 17179869184 | bytes 33554432 | tf_op jit(solution)/shard_map/feed_forward/pallas_call | solution.py:177
  488.5 30.2 %feed_forward.7 = (bf16[16,256,1024]{2,1,0:T(8,128)(2,1)}, bf16[16,256,1024]{2,1,0:T(8,128)(2,1)}, bf16[16,256,2048]{2,1,0:T(8,128)(2,1)}, bf16[16,256,2048]{2,1...) custom-call(bf16[256,2048]{1,0:T(8,128)(2,1)} %get-tuple-element.703, ...), custom_call_target="tpu_custom_call", output_to_operand_aliasing={{0}: (11, {}), {1}: (12, {}), {2}: (13, {}), {3}: (14, {})} | custom-call | flops 17179869184 | bytes 33554432 | tf_op jit(solution)/shard_map/feed_forward/pallas_call | solution.py:177
  518.8 3.4 add_convert_fusion.14
  526.3 21.3 %convolution_convert_fusion.1 = bf16[1024,2048]{1,0:T(8,128)(2,1)} fusion(bf16[4096,1024]{1,0:T(8,128)(2,1)S(1)} %bitcast.153, bf16[4096,2048]{1,0:T(8,128)(2,1)} %bitcast.152), kind=kOutput, calls=%fused_computation.9 | convolution fusion | flops 17181966336 | bytes 29360128 | tf_op jit(solution)/shard_map/dot_general | solution.py:27
  554.6 9.8 %norm_back.2 = (f32[2,256,2048]{2,1,0:T(8,128)}, f32[8,2048]{1,0:T(8,128)S(1)}, bf16[256,2048]{1,0:T(8,128)(2,1)}, bf16[256,2048]{1,0:T(8,128)(2,1)}) custom-call(f32[256,2048]{1,0:T(8,128)S(1)} %get-tuple-element.623.refs_0_, f32[256,2048]{1,0:T(8,128)} %copy-done.52, bf16[256,2048]{1,0:T(8,128)(2,1)S(1)} %copy-done.15, ...), custom_call_target="tpu_custom_call" | custom-call | flops 41943040 | bytes 18874368 | tf_op jit(solution)/shard_map/norm_back/pallas_call | solution.py:297
  570.0 5.4 project_back.4
  575.4 23.7 %convolution_convert_fusion = bf16[2048,1024]{1,0:T(8,128)(2,1)} fusion(bf16[4096,2048]{1,0:T(8,128)(2,1)} %bitcast.151, bf16[4096,1024]{1,0:T(8,128)(2,1)} %bitcast.154), kind=kOutput, calls=%fused_computation.8 | convolution fusion | flops 17181966336 | bytes 29360128 | tf_op jit(solution)/shard_map/dot_general | solution.py:27
  599.1 13.7 %collective-permute-done.72.refs_0_ = bf16[256,2048]{1,0:T(8,128)(2,1)} collective-permute-done((bf16[256,2048]{1,0:T(8,128)(2,1)}, bf16[256,2048]{1,0:T(8,128)(2,1)}, u32[]{:S(2)}, u32[]{:S(2)}) %collective-permute-start.72) | collective-permute-done | bytes 1048608 | tf_op jit(solution)/shard_map/ppermute | solution.py:62
  614.4 3.2 collective-permute-done.80.refs_1_
  618.8 5.2 project_back.5
  625.2 5.5 project_back.6
  657.6 5.5 project_back.7
  664.4 44.7 %attn_backward.2 = (bf16[4096,128]{1,0:T(8,128)(2,1)S(1)}, bf16[4096,128]{1,0:T(8,128)(2,1)S(1)}, bf16[4096,128]{1,0:T(8,128)(2,1)S(1)}, bf16[160,128]{1,0:T(8,1...) custom-call(s32[40]{0:T(128)S(1)} %copy-done.40, bf16[4096,256]{1,0:T(8,128)(2,1)} %get-tuple-element.358.q_ref, ...), custom_call_target="tpu_custom_call" | custom-call | flops 12884901888 | bytes 10485760 | tf_op jit(solution)/shard_map/attn_backward/pallas_call | solution.py:712
  709.2 3.5 add_convert_fusion.8
  717.7 4.2 all-to-all-start.4
  723.3 45.1 %attn_backward.3 = (bf16[4096,128]{1,0:T(8,128)(2,1)S(1)}, bf16[4096,128]{1,0:T(8,128)(2,1)S(1)}, bf16[4096,128]{1,0:T(8,128)(2,1)S(1)}, bf16[160,128]{1,0:T(8,1...) custom-call(s32[40]{0:T(128)S(1)} %copy-done.40, bf16[4096,256]{1,0:T(8,128)(2,1)} %get-tuple-element.358.q_ref, ...), custom_call_target="tpu_custom_call" | custom-call | flops 12884901888 | bytes 10485760 | tf_op jit(solution)/shard_map/attn_backward/pallas_call | solution.py:712
  771.3 7.1 project.12
  794.3 21.2 %fusion.7 = bf16[2048,768]{1,0:T(8,128)(2,1)} fusion(bf16[4352,2048]{1,0:T(8,128)(2,1)} %pad_dynamic-update-slice_fusion, bf16[160,512]{1,0:T(8,128)(2,1)S(1)} %constant_dynamic-update-slice_fusion, bf16[4096,768]{1,0:T(8,128)(2,1)} %constant_dynamic-update-slice_fusion.4), kind=kOutput, calls=%fused_computation.10 | convolution fusion | flops 13711835136 | bytes 27426816 | tf_op jit(solution)/shard_map/dot_general | solution.py:27
  818.3 7.5 project.13
  836.2 7.2 project.14
  844.4 9.4 convolution_convert_fusion.2
  858.4 4.2 all-to-all-start.6
  863.4 7.4 project.15
  870.9 3.5 add_convert_fusion.2
  876.4 3.1 add_convert_fusion.3
  881.0 5.0 add_convert_fusion.1
  896.2 4.2 all-to-all-start.5
  900.7 3.3 pad_maximum_fusion
  905.9 7.3 all-to-all-done.5.parts_ref
  915.6 8.6 norm_back.3
  929.6 7.0 all-to-all-done.8
  936.6 3.4 all-to-all-start.7
  (687 shorter events, 241.2 us)
Async XLA Ops:
  7.2 104.9 %all-gather.5.cloned.1.call-start = ((), (), s32[]{:S(2)}) async-start(), calls=%async_computation.13 | async-start | bytes 3932160 | tf_op jit(solution)/shard_map/all_gather | solution.py:873
  34.2 191.2 %all-gather.9.cloned.1.call-start = ((), (), s32[]{:S(2)}) async-start(), calls=%async_computation.19 | async-start | bytes 6553600 | tf_op jit(solution)/shard_map/all_gather | solution.py:929
  42.0 25.2 %collective-permute-start = (bf16[256,2048]{1,0:T(8,128)(2,1)S(1)}, bf16[256,2048]{1,0:T(8,128)(2,1)S(1)}, u32[]{:S(2)}, u32[]{:S(2)}) collective-permute-start(bf16[256,2048]{1,0:T(8,128)(2,1)S(1)} %get-tuple-element.340.refs_0_), channel_id=1, source_target_pairs={{0,2},{1,3},{2,0},{3,1},{4,6},{5,7},{6,4},{7,5},{8,10},{9,11},{10,... | collective-permute-start | bytes 3145736 | tf_op jit(solution)/shard_map/ppermute | solution.py:62
  42.4 25.1 %collective-permute-start.1 = (bf16[256,2048]{1,0:T(8,128)(2,1)S(1)}, bf16[256,2048]{1,0:T(8,128)(2,1)}, u32[]{:S(2)}, u32[]{:S(2)}) collective-permute-start(bf16[256,2048]{1,0:T(8,128)(2,1)S(1)} %get-tuple-element.341.refs_1_), channel_id=1, source_target_pairs={{0,4},{1,5},{2,6},{3,7},{4,0},{5,1},{6,2},{7,3},{8,12},{9,13},{10,... | collective-permute-start | bytes 3145736 | tf_op jit(solution)/shard_map/ppermute | solution.py:62
  68.0 25.2 %collective-permute-start.2 = (bf16[256,2048]{1,0:T(8,128)(2,1)S(1)}, bf16[256,2048]{1,0:T(8,128)(2,1)}, u32[]{:S(2)}, u32[]{:S(2)}) collective-permute-start(bf16[256,2048]{1,0:T(8,128)(2,1)S(1)} %get-tuple-element.341.refs_1_), channel_id=1, source_target_pairs={{0,2},{1,3},{2,0},{3,1},{4,6},{5,7},{6,4},{7,5},{8,10},{9,11},{10,... | collective-permute-start | bytes 3145736 | tf_op jit(solution)/shard_map/ppermute | solution.py:62
  69.7 25.0 %collective-permute-start.3 = (bf16[256,2048]{1,0:T(8,128)(2,1)S(1)}, bf16[256,2048]{1,0:T(8,128)(2,1)}, u32[]{:S(2)}, u32[]{:S(2)}) collective-permute-start(bf16[256,2048]{1,0:T(8,128)(2,1)S(1)} %get-tuple-element.340.refs_0_), channel_id=1, source_target_pairs={{0,4},{1,5},{2,6},{3,7},{4,0},{5,1},{6,2},{7,3},{8,12},{9,13},{10,... | collective-permute-start | bytes 3145736 | tf_op jit(solution)/shard_map/ppermute | solution.py:62
  96.0 30.6 %collective-permute-start.6 = (bf16[256,2048]{1,0:T(8,128)(2,1)S(1)}, bf16[256,2048]{1,0:T(8,128)(2,1)S(1)}, u32[]{:S(2)}, u32[]{:S(2)}) collective-permute-start(bf16[256,2048]{1,0:T(8,128)(2,1)S(1)} %collective-permute-done.refs_0_), channel_id=1, source_target_pairs={{0,4},{1,5},{2,6},{3,7},{4,0},{5,1},{6,2},{7,3},{8,12},{9,13},{10,... | collective-permute-start | bytes 3145736 | tf_op jit(solution)/shard_map/ppermute | solution.py:62
  98.8 27.8 %collective-permute-start.7 = (bf16[256,2048]{1,0:T(8,128)(2,1)}, bf16[256,2048]{1,0:T(8,128)(2,1)}, u32[]{:S(2)}, u32[]{:S(2)}) collective-permute-start(bf16[256,2048]{1,0:T(8,128)(2,1)} %collective-permute-done.1.refs_2_), channel_id=1, source_target_pairs={{0,2},{1,3},{2,0},{3,1},{4,6},{5,7},{6,4},{7,5},{8,10},{9,11},{10,... | collective-permute-start | bytes 3145736 | tf_op jit(solution)/shard_map/ppermute | solution.py:62
  133.3 53.6 %collective-permute-start.15 = (bf16[256,2048]{1,0:T(8,128)(2,1)}, bf16[256,2048]{1,0:T(8,128)(2,1)}, u32[]{:S(2)}, u32[]{:S(2)}) collective-permute-start(bf16[256,2048]{1,0:T(8,128)(2,1)} %get-tuple-element.365.refs_5_), channel_id=1, source_target_pairs={{0,4},{1,5},{2,6},{3,7},{4,0},{5,1},{6,2},{7,3},{8,12},{9,13},{10,... | collective-permute-start | bytes 3145736 | tf_op jit(solution)/shard_map/ppermute | solution.py:62
  135.3 51.5 %collective-permute-start.16 = (bf16[256,2048]{1,0:T(8,128)(2,1)}, bf16[256,2048]{1,0:T(8,128)(2,1)}, u32[]{:S(2)}, u32[]{:S(2)}) collective-permute-start(bf16[256,2048]{1,0:T(8,128)(2,1)} %get-tuple-element.365.refs_5_), channel_id=1, source_target_pairs={{0,2},{1,3},{2,0},{3,1},{4,6},{5,7},{6,4},{7,5},{8,10},{9,11},{10,... | collective-permute-start | bytes 3145736 | tf_op jit(solution)/shard_map/ppermute | solution.py:62
  136.8 50.0 %collective-permute-start.14 = (bf16[256,2048]{1,0:T(8,128)(2,1)}, bf16[256,2048]{1,0:T(8,128)(2,1)}, u32[]{:S(2)}, u32[]{:S(2)}) collective-permute-start(bf16[256,2048]{1,0:T(8,128)(2,1)} %get-tuple-element.364.refs_4_), channel_id=1, source_target_pairs={{0,2},{1,3},{2,0},{3,1},{4,6},{5,7},{6,4},{7,5},{8,10},{9,11},{10,... | collective-permute-start | bytes 3145736 | tf_op jit(solution)/shard_map/ppermute | solution.py:62
  137.3 49.5 %collective-permute-start.17 = (bf16[256,2048]{1,0:T(8,128)(2,1)}, bf16[256,2048]{1,0:T(8,128)(2,1)}, u32[]{:S(2)}, u32[]{:S(2)}) collective-permute-start(bf16[256,2048]{1,0:T(8,128)(2,1)} %get-tuple-element.364.refs_4_), channel_id=1, source_target_pairs={{0,4},{1,5},{2,6},{3,7},{4,0},{5,1},{6,2},{7,3},{8,12},{9,13},{10,... | collective-permute-start | bytes 3145736 | tf_op jit(solution)/shard_map/ppermute | solution.py:62
  186.9 40.9 %collective-permute-start.18 = (bf16[256,2048]{1,0:T(8,128)(2,1)}, bf16[256,2048]{1,0:T(8,128)(2,1)}, u32[]{:S(2)}, u32[]{:S(2)}) collective-permute-start(bf16[256,2048]{1,0:T(8,128)(2,1)} %collective-permute-done.14.refs_4_), channel_id=1, source_target_pairs={{0,4},{1,5},{2,6},{3,7},{4,0},{5,1},{6,2},{7,3},{8,12},{9,13},{10,... | collective-permute-start | bytes 3145736 | tf_op jit(solution)/shard_map/ppermute | solution.py:62
  188.4 39.3 %collective-permute-start.19 = (bf16[256,2048]{1,0:T(8,128)(2,1)}, bf16[256,2048]{1,0:T(8,128)(2,1)}, u32[]{:S(2)}, u32[]{:S(2)}) collective-permute-start(bf16[256,2048]{1,0:T(8,128)(2,1)} %collective-permute-done.15.refs_6_), channel_id=1, source_target_pairs={{0,2},{1,3},{2,0},{3,1},{4,6},{5,7},{6,4},{7,5},{8,10},{9,11},{10,... | collective-permute-start | bytes 3145736 | tf_op jit(solution)/shard_map/ppermute | solution.py:62
  189.0 38.7 %all-to-all-start.3 = ((bf16[8,64,1024]{2,1,0:T(8,128)(2,1)}), bf16[8,64,1024]{2,1,0:T(8,128)(2,1)}, u32[]{:S(2)}, u32[]{:S(2)}) async-start(bf16[8,64,1024]{2,1,0:T(8,128)(2,1)} %reshape.485), calls=%async_computation.3 | async-start | bytes 2097152 | tf_op jit(solution)/shard_map/all_to_all | solution.py:938
  193.2 173.2 %all-gather.7.cloned.1.call-start = ((), (), s32[]{:S(2)}) async-start(), calls=%async_computation.14 | async-start | bytes 5242880 | tf_op jit(solution)/shard_map/all_gather | solution.py:987
  236.2 25.5 %collective-permute-start.23 = (bf16[256,2048]{1,0:T(8,128)(2,1)S(1)}, bf16[256,2048]{1,0:T(8,128)(2,1)S(1)}, u32[]{:S(2)}, u32[]{:S(2)}) collective-permute-start(bf16[256,2048]{1,0:T(8,128)(2,1)S(1)} %add_convert_fusion.26), channel_id=1, source_target_pairs={{0,4},{1,5},{2,6},{3,7},{4,0},{5,1},{6,2},{7,3},{8,12},{9,13},{10,... | collective-permute-start | bytes 3145736 | tf_op jit(solution)/shard_map/ppermute | solution.py:62
  238.5 25.0 %collective-permute-start.22 = (bf16[256,2048]{1,0:T(8,128)(2,1)S(1)}, bf16[256,2048]{1,0:T(8,128)(2,1)S(1)}, u32[]{:S(2)}, u32[]{:S(2)}) collective-permute-start(bf16[256,2048]{1,0:T(8,128)(2,1)S(1)} %add_convert_fusion.27), channel_id=1, source_target_pairs={{0,2},{1,3},{2,0},{3,1},{4,6},{5,7},{6,4},{7,5},{8,10},{9,11},{10,... | collective-permute-start | bytes 3145736 | tf_op jit(solution)/shard_map/ppermute | solution.py:62
  268.0 25.4 %collective-permute-start.28 = (bf16[256,2048]{1,0:T(8,128)(2,1)S(1)}, bf16[256,2048]{1,0:T(8,128)(2,1)}, u32[]{:S(2)}, u32[]{:S(2)}) collective-permute-start(bf16[256,2048]{1,0:T(8,128)(2,1)S(1)} %add_convert_fusion.24), channel_id=1, source_target_pairs={{0,2},{1,3},{2,0},{3,1},{4,6},{5,7},{6,4},{7,5},{8,10},{9,11},{10,... | collective-permute-start | bytes 3145736 | tf_op jit(solution)/shard_map/ppermute | solution.py:62
  271.0 25.2 %collective-permute-start.27 = (bf16[256,2048]{1,0:T(8,128)(2,1)}, bf16[256,2048]{1,0:T(8,128)(2,1)}, u32[]{:S(2)}, u32[]{:S(2)}) collective-permute-start(bf16[256,2048]{1,0:T(8,128)(2,1)} %add_convert_fusion.25), channel_id=1, source_target_pairs={{0,4},{1,5},{2,6},{3,7},{4,0},{5,1},{6,2},{7,3},{8,12},{9,13},{10,... | collective-permute-start | bytes 3145736 | tf_op jit(solution)/shard_map/ppermute | solution.py:62
  275.4 24.5 %collective-permute-start.26 = (bf16[256,2048]{1,0:T(8,128)(2,1)}, bf16[256,2048]{1,0:T(8,128)(2,1)}, u32[]{:S(2)}, u32[]{:S(2)}) collective-permute-start(bf16[256,2048]{1,0:T(8,128)(2,1)} %get-tuple-element.392), channel_id=1, source_target_pairs={{0,1},{1,0},{2,3},{3,2},{4,5},{5,4},{6,7},{7,6},{8,9},{9,8},{10,11... | collective-permute-start | bytes 3145736 | tf_op jit(solution)/shard_map/ppermute | solution.py:62
  275.9 387.1 %reduce-scatter.5.cloned.1.call-start = ((), (), s32[]{:S(2)}) async-start(), calls=%async_computation.15 | async-start | bytes 5242880 | tf_op jit(solution)/shard_map/reduce_scatter | solution.py:1041
  299.3 24.3 %collective-permute-start.31 = (bf16[256,2048]{1,0:T(8,128)(2,1)}, bf16[256,2048]{1,0:T(8,128)(2,1)S(1)}, u32[]{:S(2)}, u32[]{:S(2)}) collective-permute-start(bf16[256,2048]{1,0:T(8,128)(2,1)} %add_convert_fusion.22), channel_id=1, source_target_pairs={{0,4},{1,5},{2,6},{3,7},{4,0},{5,1},{6,2},{7,3},{8,12},{9,13},{10,... | collective-permute-start | bytes 3145736 | tf_op jit(solution)/shard_map/ppermute | solution.py:62
  303.0 24.0 %collective-permute-start.29 = (bf16[256,2048]{1,0:T(8,128)(2,1)}, bf16[256,2048]{1,0:T(8,128)(2,1)S(1)}, u32[]{:S(2)}, u32[]{:S(2)}) collective-permute-start(bf16[256,2048]{1,0:T(8,128)(2,1)} %add_convert_fusion.23), channel_id=1, source_target_pairs={{0,2},{1,3},{2,0},{3,1},{4,6},{5,7},{6,4},{7,5},{8,10},{9,11},{10,... | collective-permute-start | bytes 3145736 | tf_op jit(solution)/shard_map/ppermute | solution.py:62
  303.4 24.6 %collective-permute-start.33 = (bf16[256,2048]{1,0:T(8,128)(2,1)}, bf16[256,2048]{1,0:T(8,128)(2,1)}, u32[]{:S(2)}, u32[]{:S(2)}) collective-permute-start(bf16[256,2048]{1,0:T(8,128)(2,1)} %get-tuple-element.406), channel_id=1, source_target_pairs={{0,1},{1,0},{2,3},{3,2},{4,5},{5,4},{6,7},{7,6},{8,9},{9,8},{10,11... | collective-permute-start | bytes 3145736 | tf_op jit(solution)/shard_map/ppermute | solution.py:62
  360.2 36.6 %collective-permute-start.55 = (bf16[256,2048]{1,0:T(8,128)(2,1)}, bf16[256,2048]{1,0:T(8,128)(2,1)}, u32[]{:S(2)}, u32[]{:S(2)}) collective-permute-start(bf16[256,2048]{1,0:T(8,128)(2,1)} %collective-permute-done.16.refs_4_), channel_id=1, source_target_pairs={{0,1},{1,0},{2,3},{3,2},{4,5},{5,4},{6,7},{7,6},{8,9},{9,8},{10,11... | collective-permute-start | bytes 3145736 | tf_op jit(solution)/shard_map/ppermute | solution.py:62
  360.4 38.5 %collective-permute-start.56 = (bf16[256,2048]{1,0:T(8,128)(2,1)}, bf16[256,2048]{1,0:T(8,128)(2,1)}, u32[]{:S(2)}, u32[]{:S(2)}) collective-permute-start(bf16[256,2048]{1,0:T(8,128)(2,1)} %collective-permute-done.17.refs_6_), channel_id=1, source_target_pairs={{0,1},{1,0},{2,3},{3,2},{4,5},{5,4},{6,7},{7,6},{8,9},{9,8},{10,11... | collective-permute-start | bytes 3145736 | tf_op jit(solution)/shard_map/ppermute | solution.py:62
  360.8 35.4 %collective-permute-start.51 = (bf16[256,2048]{1,0:T(8,128)(2,1)S(1)}, bf16[256,2048]{1,0:T(8,128)(2,1)}, u32[]{:S(2)}, u32[]{:S(2)}) collective-permute-start(bf16[256,2048]{1,0:T(8,128)(2,1)S(1)} %get-tuple-element.702.refs_1_), channel_id=1, source_target_pairs={{0,2},{1,3},{2,0},{3,1},{4,6},{5,7},{6,4},{7,5},{8,10},{9,11},{10,... | collective-permute-start | bytes 3145736 | tf_op jit(solution)/shard_map/ppermute | solution.py:62
  364.1 32.1 %collective-permute-start.52 = (bf16[256,2048]{1,0:T(8,128)(2,1)}, bf16[256,2048]{1,0:T(8,128)(2,1)}, u32[]{:S(2)}, u32[]{:S(2)}) collective-permute-start(bf16[256,2048]{1,0:T(8,128)(2,1)} %get-tuple-element.703.refs_0_), channel_id=1, source_target_pairs={{0,4},{1,5},{2,6},{3,7},{4,0},{5,1},{6,2},{7,3},{8,12},{9,13},{10,... | collective-permute-start | bytes 3145736 | tf_op jit(solution)/shard_map/ppermute | solution.py:62
  396.8 35.6 %collective-permute-start.45 = (bf16[256,2048]{1,0:T(8,128)(2,1)S(1)}, bf16[256,2048]{1,0:T(8,128)(2,1)S(1)}, u32[]{:S(2)}, u32[]{:S(2)}) collective-permute-start(bf16[256,2048]{1,0:T(8,128)(2,1)S(1)} %copy-done.137), channel_id=1, source_target_pairs={{0,4},{1,5},{2,6},{3,7},{4,0},{5,1},{6,2},{7,3},{8,12},{9,13},{10,... | collective-permute-start | bytes 3145736 | tf_op jit(solution)/shard_map/ppermute | solution.py:62
  396.8 35.9 %collective-permute-start.46 = (bf16[256,2048]{1,0:T(8,128)(2,1)}, bf16[256,2048]{1,0:T(8,128)(2,1)S(1)}, u32[]{:S(2)}, u32[]{:S(2)}) collective-permute-start(bf16[256,2048]{1,0:T(8,128)(2,1)} %collective-permute-done.35.refs_2_), channel_id=1, source_target_pairs={{0,2},{1,3},{2,0},{3,1},{4,6},{5,7},{6,4},{7,5},{8,10},{9,11},{10,... | collective-permute-start | bytes 3145736 | tf_op jit(solution)/shard_map/ppermute | solution.py:62
  439.1 35.2 %collective-permute-start.60 = (bf16[256,2048]{1,0:T(8,128)(2,1)}, bf16[256,2048]{1,0:T(8,128)(2,1)S(1)}, u32[]{:S(2)}, u32[]{:S(2)}) collective-permute-start(bf16[256,2048]{1,0:T(8,128)(2,1)} %add_convert_fusion.18), channel_id=1, source_target_pairs={{0,4},{1,5},{2,6},{3,7},{4,0},{5,1},{6,2},{7,3},{8,12},{9,13},{10,... | collective-permute-start | bytes 3145736 | tf_op jit(solution)/shard_map/ppermute | solution.py:62
  440.5 33.7 %collective-permute-start.59 = (bf16[256,2048]{1,0:T(8,128)(2,1)}, bf16[256,2048]{1,0:T(8,128)(2,1)S(1)}, u32[]{:S(2)}, u32[]{:S(2)}) collective-permute-start(bf16[256,2048]{1,0:T(8,128)(2,1)} %add_convert_fusion.19), channel_id=1, source_target_pairs={{0,2},{1,3},{2,0},{3,1},{4,6},{5,7},{6,4},{7,5},{8,10},{9,11},{10,... | collective-permute-start | bytes 3145736 | tf_op jit(solution)/shard_map/ppermute | solution.py:62
  480.2 38.5 %collective-permute-start.66 = (bf16[256,2048]{1,0:T(8,128)(2,1)}, bf16[256,2048]{1,0:T(8,128)(2,1)}, u32[]{:S(2)}, u32[]{:S(2)}) collective-permute-start(bf16[256,2048]{1,0:T(8,128)(2,1)} %get-tuple-element.461), channel_id=1, source_target_pairs={{0,1},{1,0},{2,3},{3,2},{4,5},{5,4},{6,7},{7,6},{8,9},{9,8},{10,11... | collective-permute-start | bytes 3145736 | tf_op jit(solution)/shard_map/ppermute | solution.py:62
  481.8 41.9 %collective-permute-start.40 = (bf16[256,2048]{1,0:T(8,128)(2,1)}, bf16[256,2048]{1,0:T(8,128)(2,1)S(1)}, u32[]{:S(2)}, u32[]{:S(2)}) collective-permute-start(bf16[256,2048]{1,0:T(8,128)(2,1)} %get-tuple-element.422), channel_id=1, source_target_pairs={{0,1},{1,0},{2,3},{3,2},{4,5},{5,4},{6,7},{7,6},{8,9},{9,8},{10,11... | collective-permute-start | bytes 3145736 | tf_op jit(solution)/shard_map/ppermute | solution.py:62
  483.0 35.7 %collective-permute-start.64 = (bf16[256,2048]{1,0:T(8,128)(2,1)}, bf16[256,2048]{1,0:T(8,128)(2,1)}, u32[]{:S(2)}, u32[]{:S(2)}) collective-permute-start(bf16[256,2048]{1,0:T(8,128)(2,1)} %add_convert_fusion.16), channel_id=1, source_target_pairs={{0,2},{1,3},{2,0},{3,1},{4,6},{5,7},{6,4},{7,5},{8,10},{9,11},{10,... | collective-permute-start | bytes 3145736 | tf_op jit(solution)/shard_map/ppermute | solution.py:62
  484.0 34.7 %collective-permute-start.63 = (bf16[256,2048]{1,0:T(8,128)(2,1)}, bf16[256,2048]{1,0:T(8,128)(2,1)S(1)}, u32[]{:S(2)}, u32[]{:S(2)}) collective-permute-start(bf16[256,2048]{1,0:T(8,128)(2,1)} %add_convert_fusion.17), channel_id=1, source_target_pairs={{0,4},{1,5},{2,6},{3,7},{4,0},{5,1},{6,2},{7,3},{8,12},{9,13},{10,... | collective-permute-start | bytes 3145736 | tf_op jit(solution)/shard_map/ppermute | solution.py:62
  522.3 25.5 %collective-permute-start.67 = (bf16[256,2048]{1,0:T(8,128)(2,1)}, bf16[256,2048]{1,0:T(8,128)(2,1)}, u32[]{:S(2)}, u32[]{:S(2)}) collective-permute-start(bf16[256,2048]{1,0:T(8,128)(2,1)} %add_convert_fusion.14), channel_id=1, source_target_pairs={{0,4},{1,5},{2,6},{3,7},{4,0},{5,1},{6,2},{7,3},{8,12},{9,13},{10,... | collective-permute-start | bytes 3145736 | tf_op jit(solution)/shard_map/ppermute | solution.py:62
  525.2 25.2 %collective-permute-start.65 = (bf16[256,2048]{1,0:T(8,128)(2,1)}, bf16[256,2048]{1,0:T(8,128)(2,1)}, u32[]{:S(2)}, u32[]{:S(2)}) collective-permute-start(bf16[256,2048]{1,0:T(8,128)(2,1)} %add_convert_fusion.15), channel_id=1, source_target_pairs={{0,2},{1,3},{2,0},{3,1},{4,6},{5,7},{6,4},{7,5},{8,10},{9,11},{10,... | collective-permute-start | bytes 3145736 | tf_op jit(solution)/shard_map/ppermute | solution.py:62
  525.8 24.7 %collective-permute-start.68 = (bf16[256,2048]{1,0:T(8,128)(2,1)}, bf16[256,2048]{1,0:T(8,128)(2,1)}, u32[]{:S(2)}, u32[]{:S(2)}) collective-permute-start(bf16[256,2048]{1,0:T(8,128)(2,1)} %get-tuple-element.464), channel_id=1, source_target_pairs={{0,1},{1,0},{2,3},{3,2},{4,5},{5,4},{6,7},{7,6},{8,9},{9,8},{10,11... | collective-permute-start | bytes 3145736 | tf_op jit(solution)/shard_map/ppermute | solution.py:62
  525.8 24.7 %collective-permute-start.69 = (bf16[256,2048]{1,0:T(8,128)(2,1)}, bf16[256,2048]{1,0:T(8,128)(2,1)}, u32[]{:S(2)}, u32[]{:S(2)}) collective-permute-start(bf16[256,2048]{1,0:T(8,128)(2,1)} %get-tuple-element.467), channel_id=1, source_target_pairs={{0,1},{1,0},{2,3},{3,2},{4,5},{5,4},{6,7},{7,6},{8,9},{9,8},{10,11... | collective-permute-start | bytes 3145736 | tf_op jit(solution)/shard_map/ppermute | solution.py:62
  550.5 167.2 %reduce-scatter.7.cloned.1.call-start = ((), (), s32[]{:S(2)}) async-start(), calls=%async_computation.16 | async-start | bytes 5242880 | tf_op jit(solution)/shard_map/reduce_scatter | solution.py:1072
  564.9 34.2 %collective-permute-start.70 = (bf16[256,2048]{1,0:T(8,128)(2,1)}, bf16[256,2048]{1,0:T(8,128)(2,1)S(1)}, u32[]{:S(2)}, u32[]{:S(2)}) collective-permute-start(bf16[256,2048]{1,0:T(8,128)(2,1)} %get-tuple-element.480.refs_0_), channel_id=1, source_target_pairs={{0,2},{1,3},{2,0},{3,1},{4,6},{5,7},{6,4},{7,5},{8,10},{9,11},{10,... | collective-permute-start | bytes 3145736 | tf_op jit(solution)/shard_map/ppermute | solution.py:62
  565.7 33.4 %collective-permute-start.71 = (bf16[256,2048]{1,0:T(8,128)(2,1)}, bf16[256,2048]{1,0:T(8,128)(2,1)}, u32[]{:S(2)}, u32[]{:S(2)}) collective-permute-start(bf16[256,2048]{1,0:T(8,128)(2,1)} %get-tuple-element.481.refs_1_), channel_id=1, source_target_pairs={{0,4},{1,5},{2,6},{3,7},{4,0},{5,1},{6,2},{7,3},{8,12},{9,13},{10,... | collective-permute-start | bytes 3145736 | tf_op jit(solution)/shard_map/ppermute | solution.py:62
  566.7 46.2 %collective-permute-start.72 = (bf16[256,2048]{1,0:T(8,128)(2,1)}, bf16[256,2048]{1,0:T(8,128)(2,1)}, u32[]{:S(2)}, u32[]{:S(2)}) collective-permute-start(bf16[256,2048]{1,0:T(8,128)(2,1)} %get-tuple-element.481.refs_1_), channel_id=1, source_target_pairs={{0,2},{1,3},{2,0},{3,1},{4,6},{5,7},{6,4},{7,5},{8,10},{9,11},{10,... | collective-permute-start | bytes 3145736 | tf_op jit(solution)/shard_map/ppermute | solution.py:62
  567.8 45.6 %collective-permute-start.73 = (bf16[256,2048]{1,0:T(8,128)(2,1)}, bf16[256,2048]{1,0:T(8,128)(2,1)}, u32[]{:S(2)}, u32[]{:S(2)}) collective-permute-start(bf16[256,2048]{1,0:T(8,128)(2,1)} %get-tuple-element.480.refs_0_), channel_id=1, source_target_pairs={{0,4},{1,5},{2,6},{3,7},{4,0},{5,1},{6,2},{7,3},{8,12},{9,13},{10,... | collective-permute-start | bytes 3145736 | tf_op jit(solution)/shard_map/ppermute | solution.py:62
  617.9 28.5 %collective-permute-start.76 = (bf16[256,2048]{1,0:T(8,128)(2,1)S(1)}, bf16[256,2048]{1,0:T(8,128)(2,1)S(1)}, u32[]{:S(2)}, u32[]{:S(2)}) collective-permute-start(bf16[256,2048]{1,0:T(8,128)(2,1)S(1)} %collective-permute-done.70.refs_0_), channel_id=1, source_target_pairs={{0,4},{1,5},{2,6},{3,7},{4,0},{5,1},{6,2},{7,3},{8,12},{9,13},{10,... | collective-permute-start | bytes 3145736 | tf_op jit(solution)/shard_map/ppermute | solution.py:62
  624.0 25.2 %collective-permute-start.77 = (bf16[256,2048]{1,0:T(8,128)(2,1)}, bf16[256,2048]{1,0:T(8,128)(2,1)S(1)}, u32[]{:S(2)}, u32[]{:S(2)}) collective-permute-start(bf16[256,2048]{1,0:T(8,128)(2,1)} %collective-permute-done.71.refs_2_), channel_id=1, source_target_pairs={{0,2},{1,3},{2,0},{3,1},{4,6},{5,7},{6,4},{7,5},{8,10},{9,11},{10,... | collective-permute-start | bytes 3145736 | tf_op jit(solution)/shard_map/ppermute | solution.py:62
  653.5 55.6 %collective-permute-start.92 = (bf16[256,2048]{1,0:T(8,128)(2,1)}, bf16[256,2048]{1,0:T(8,128)(2,1)}, u32[]{:S(2)}, u32[]{:S(2)}) collective-permute-start(bf16[256,2048]{1,0:T(8,128)(2,1)} %add_convert_fusion.13), channel_id=1, source_target_pairs={{0,2},{1,3},{2,0},{3,1},{4,6},{5,7},{6,4},{7,5},{8,10},{9,11},{10,... | collective-permute-start | bytes 3145736 | tf_op jit(solution)/shard_map/ppermute | solution.py:62
  654.7 54.5 %collective-permute-start.93 = (bf16[256,2048]{1,0:T(8,128)(2,1)}, bf16[256,2048]{1,0:T(8,128)(2,1)}, u32[]{:S(2)}, u32[]{:S(2)}) collective-permute-start(bf16[256,2048]{1,0:T(8,128)(2,1)} %add_convert_fusion.12), channel_id=1, source_target_pairs={{0,4},{1,5},{2,6},{3,7},{4,0},{5,1},{6,2},{7,3},{8,12},{9,13},{10,... | collective-permute-start | bytes 3145736 | tf_op jit(solution)/shard_map/ppermute | solution.py:62
  655.9 53.2 %collective-permute-start.94 = (bf16[256,2048]{1,0:T(8,128)(2,1)}, bf16[256,2048]{1,0:T(8,128)(2,1)}, u32[]{:S(2)}, u32[]{:S(2)}) collective-permute-start(bf16[256,2048]{1,0:T(8,128)(2,1)} %add_convert_fusion.11), channel_id=1, source_target_pairs={{0,4},{1,5},{2,6},{3,7},{4,0},{5,1},{6,2},{7,3},{8,12},{9,13},{10,... | collective-permute-start | bytes 3145736 | tf_op jit(solution)/shard_map/ppermute | solution.py:62
  656.7 52.5 %collective-permute-start.95 = (bf16[256,2048]{1,0:T(8,128)(2,1)}, bf16[256,2048]{1,0:T(8,128)(2,1)}, u32[]{:S(2)}, u32[]{:S(2)}) collective-permute-start(bf16[256,2048]{1,0:T(8,128)(2,1)} %add_convert_fusion.10), channel_id=1, source_target_pairs={{0,2},{1,3},{2,0},{3,1},{4,6},{5,7},{6,4},{7,5},{8,10},{9,11},{10,... | collective-permute-start | bytes 3145736 | tf_op jit(solution)/shard_map/ppermute | solution.py:62
  712.7 58.6 %collective-permute-start.97 = (bf16[256,2048]{1,0:T(8,128)(2,1)}, bf16[256,2048]{1,0:T(8,128)(2,1)}, u32[]{:S(2)}, u32[]{:S(2)}) collective-permute-start(bf16[256,2048]{1,0:T(8,128)(2,1)} %add_convert_fusion.8), channel_id=1, source_target_pairs={{0,4},{1,5},{2,6},{3,7},{4,0},{5,1},{6,2},{7,3},{8,12},{9,13},{10,... | collective-permute-start | bytes 3145736 | tf_op jit(solution)/shard_map/ppermute | solution.py:62
  716.5 54.8 %collective-permute-start.96 = (bf16[256,2048]{1,0:T(8,128)(2,1)}, bf16[256,2048]{1,0:T(8,128)(2,1)}, u32[]{:S(2)}, u32[]{:S(2)}) collective-permute-start(bf16[256,2048]{1,0:T(8,128)(2,1)} %add_convert_fusion.9), channel_id=1, source_target_pairs={{0,2},{1,3},{2,0},{3,1},{4,6},{5,7},{6,4},{7,5},{8,10},{9,11},{10,... | collective-permute-start | bytes 3145736 | tf_op jit(solution)/shard_map/ppermute | solution.py:62
  717.7 53.6 %all-to-all-start.4 = ((bf16[8,64,1024]{2,1,0:T(8,128)(2,1)}), bf16[8,64,1024]{2,1,0:T(8,128)(2,1)}, u32[]{:S(2)}, u32[]{:S(2)}) async-start(bf16[8,64,1024]{2,1,0:T(8,128)(2,1)} %bitcast.190), calls=%async_computation.6 | async-start | bytes 2097152 | tf_op jit(solution)/shard_map/all_to_all | solution.py:1100
  722.0 174.2 %reduce-scatter.9.cloned.1.call-start = ((), (), s32[]{:S(2)}) async-start(), calls=%async_computation.17 | async-start | bytes 3932160 | tf_op jit(solution)/shard_map/reduce_scatter | solution.py:1127
  782.8 32.8 %collective-permute-start.101 = (bf16[256,2048]{1,0:T(8,128)(2,1)}, bf16[256,2048]{1,0:T(8,128)(2,1)S(1)}, u32[]{:S(2)}, u32[]{:S(2)}) collective-permute-start(bf16[256,2048]{1,0:T(8,128)(2,1)} %add_convert_fusion.6), channel_id=1, source_target_pairs={{0,4},{1,5},{2,6},{3,7},{4,0},{5,1},{6,2},{7,3},{8,12},{9,13},{10,... | collective-permute-start | bytes 3145736 | tf_op jit(solution)/shard_map/ppermute | solution.py:62
  786.0 29.5 %collective-permute-start.99 = (bf16[256,2048]{1,0:T(8,128)(2,1)}, bf16[256,2048]{1,0:T(8,128)(2,1)}, u32[]{:S(2)}, u32[]{:S(2)}) collective-permute-start(bf16[256,2048]{1,0:T(8,128)(2,1)} %add_convert_fusion.7), channel_id=1, source_target_pairs={{0,2},{1,3},{2,0},{3,1},{4,6},{5,7},{6,4},{7,5},{8,10},{9,11},{10,... | collective-permute-start | bytes 3145736 | tf_op jit(solution)/shard_map/ppermute | solution.py:62
  832.7 38.1 %collective-permute-start.106 = (bf16[256,2048]{1,0:T(8,128)(2,1)}, bf16[256,2048]{1,0:T(8,128)(2,1)}, u32[]{:S(2)}, u32[]{:S(2)}) collective-permute-start(bf16[256,2048]{1,0:T(8,128)(2,1)} %add_convert_fusion.4), channel_id=1, source_target_pairs={{0,2},{1,3},{2,0},{3,1},{4,6},{5,7},{6,4},{7,5},{8,10},{9,11},{10,... | collective-permute-start | bytes 3145736 | tf_op jit(solution)/shard_map/ppermute | solution.py:62
  836.2 34.6 %collective-permute-start.105 = (bf16[256,2048]{1,0:T(8,128)(2,1)}, bf16[256,2048]{1,0:T(8,128)(2,1)}, u32[]{:S(2)}, u32[]{:S(2)}) collective-permute-start(bf16[256,2048]{1,0:T(8,128)(2,1)} %add_convert_fusion.5), channel_id=1, source_target_pairs={{0,4},{1,5},{2,6},{3,7},{4,0},{5,1},{6,2},{7,3},{8,12},{9,13},{10,... | collective-permute-start | bytes 3145736 | tf_op jit(solution)/shard_map/ppermute | solution.py:62
  858.4 27.6 %all-to-all-start.6 = ((bf16[8,32,2048]{2,1,0:T(8,128)(2,1)}), bf16[8,32,2048]{2,1,0:T(8,128)(2,1)}, u32[]{:S(2)}, u32[]{:S(2)}) async-start(bf16[8,32,2048]{2,1,0:T(8,128)(2,1)} %bitcast.178), calls=%async_computation.9 | async-start | bytes 2097152 | tf_op jit(solution)/shard_map/all_to_all | solution.py:1179
  862.7 77.4 %reduce-scatter.11.cloned.1.call-start = ((), (), s32[]{:S(2)}) async-start(), calls=%async_computation.18 | async-start | bytes 1310720 | tf_op jit(solution)/shard_map/reduce_scatter | solution.py:1168
  874.4 29.5 %collective-permute-start.109 = (bf16[256,2048]{1,0:T(8,128)(2,1)}, bf16[256,2048]{1,0:T(8,128)(2,1)}, u32[]{:S(2)}, u32[]{:S(2)}) collective-permute-start(bf16[256,2048]{1,0:T(8,128)(2,1)} %add_convert_fusion.2), channel_id=1, source_target_pairs={{0,4},{1,5},{2,6},{3,7},{4,0},{5,1},{6,2},{7,3},{8,12},{9,13},{10,... | collective-permute-start | bytes 3145736 | tf_op jit(solution)/shard_map/ppermute | solution.py:62
  879.5 26.4 %collective-permute-start.107 = (bf16[256,2048]{1,0:T(8,128)(2,1)}, bf16[256,2048]{1,0:T(8,128)(2,1)}, u32[]{:S(2)}, u32[]{:S(2)}) collective-permute-start(bf16[256,2048]{1,0:T(8,128)(2,1)} %add_convert_fusion.3), channel_id=1, source_target_pairs={{0,2},{1,3},{2,0},{3,1},{4,6},{5,7},{6,4},{7,5},{8,10},{9,11},{10,... | collective-permute-start | bytes 3145736 | tf_op jit(solution)/shard_map/ppermute | solution.py:62
  (205 other events, 1880.4 us)
Sparse Core Ops, SparseCore 0:
  29.4 62.8 all-gather.4
  94.5 96.6 all-gather.8
  276.1 78.4 all-gather.6
  550.6 73.9 reduce-scatter.4
  627.4 77.2 reduce-scatter.6
  815.7 57.2 reduce-scatter.8
  875.2 27.1 reduce-scatter.10

commit v4 on v3

--- a/solution.py
+++ b/solution.py
@@ -101,8 +101,41 @@
     return result
 
 
-def paired(own, other):
-    return total(own, swapped(other, 1)).astype(bf16)
+def low_sums_kernel(counts, *refs):
+    place = 0
+    for count, out in zip(counts, refs[sum(counts) :]):
+        terms = [ref[...].reshape(out.shape) for ref in refs[place : place + count]]
+        out[...] = total(*terms).astype(bf16)
+        place += count
+
+
+def low_sums(*lists):
+    half, wide = lists[0][0].shape
+    chunk = half // 2
+    rows = pl.BlockSpec((chunk, wide), lambda s: (s, 0))
+    terms = [term for one in lists for term in one]
+
+    def place_of(term):
+        if not isinstance(term, tuple):
+            return rows
+        return pl.BlockSpec((1, chunk, wide), lambda s, slot=term[1]: (slot, s, 0))
+
+    return pl.pallas_call(
+        functools.partial(low_sums_kernel, [len(one) for one in lists]),
+        grid=(2,),
+        in_specs=[place_of(term) for term in terms],
+        out_specs=[rows] * len(lists),
+        out_shape=[jax.ShapeDtypeStruct((half, wide), bf16)] * len(lists),
+        compiler_params=pltpu.CompilerParams(
+            dimension_semantics=("arbitrary",), vmem_limit_bytes=32 * 2**20
+        ),
+        cost_estimate=pl.CostEstimate(
+            flops=half * wide * len(terms),
+            bytes_accessed=2 * half * wide * (len(terms) + len(lists)),
+            transcendentals=0,
+        ),
+        name="low_sums",
+    )(*[term[0] if isinstance(term, tuple) else term for term in terms])
 
 
 def plain_scattered_sum(groups):
@@ -125,8 +158,7 @@
                 use(done)
         return plain_scattered_sum(made)
     later = make(2, ())
-    x1 = paired(later[0], later[1])
-    y0 = paired(later[2], later[3])
+    x1, y0 = low_sums([later[0], swapped(later[1], 1)], [later[2], swapped(later[3], 1)])
     if first:
         done, use = first((x1, y0))
         x1, y0, done = after((swapped(x1, 2), swapped(y0, 4), done))
@@ -135,13 +167,11 @@
     else:
         far = make(3, (x1, y0))
         far, x1, y0 = after((far, swapped(x1, 2), swapped(y0, 4)))
-    a0 = paired(far[0], far[2])
-    a1 = paired(far[1], far[3])
+    a0, a1 = low_sums([far[0], swapped(far[2], 1)], [far[1], swapped(far[3], 1)])
     near = make(1, (a0, a1))
     own = make(0, (a0, a1, near[0]))
     own, a0, a1 = after((own, swapped(a0, 4), swapped(a1, 2)))
-    x0 = total(near[0], swapped(near[1], 1), a0).astype(bf16)
-    y1 = total(near[2], swapped(near[3], 1), a1).astype(bf16)
+    x0, y1 = low_sums([near[0], swapped(near[1], 1), a0], [near[2], swapped(near[3], 1), a1])
     mine = [[own[0], swapped(own[2], 1), y0], [own[1], swapped(own[3], 1), x1]]
     done, use = second((x0, y1)) if second else ((), None)
     x0, y1, mine, done = after((swapped(x0, 2), swapped(y1, 4), mine, done))
@@ -383,13 +413,16 @@
 gelu_cube = 0.044715
 
 
-def feed_forward_kernel(n_ins, n_earlier, *refs):
+def feed_forward_kernel(keep, n_ins, n_earlier, *refs):
     ins, rest = split_refs(n_ins, n_earlier, refs)
     up_ref, shift_ref, down_ref = ins[8:]
-    active_ref, grad_ref, rows_ref, grad_rows_ref = rest[:4]
-    back = rest[4:8]
-    ahead = rest[8:12]
-    shift_grad_ref, rows, grad_rows, active, grad_upper = rest[12:]
+    active_ref, grad_ref, rows_ref, grad_rows_ref, other_ref = rest[:5]
+    back = rest[5:9]
+    gone = [n for n in range(4) if n not in keep]
+    ahead = [
+        rest[9 + keep.index(n)] if n in keep else other_ref.at[gone.index(n)] for n in range(4)
+    ]
+    shift_grad_ref, rows, grad_rows, active, grad_upper = rest[11:]
     chunk, wide = ins[0].shape
     units = up_ref.shape[1]
     for n in range(4):
@@ -437,30 +470,32 @@
     lax.fori_loop(0, wide // step, outer, 0)
 
 
-def feed_forward(group, halves, grad_halves, up, shift, down, earlier, slots):
+def feed_forward(group, keep, halves, grad_halves, up, shift, down, earlier, slots):
     half, wide = halves[0].shape
     chunk = half // 2
     units = up.shape[1]
     sizes = (units, units, wide, wide)
     outs = [jax.ShapeDtypeStruct((slots, half, n), bf16) for n in sizes]
-    outs += [jax.ShapeDtypeStruct((half, wide), bf16)] * 8
+    outs += [jax.ShapeDtypeStruct((slots // 2, half, wide), bf16)]
+    outs += [jax.ShapeDtypeStruct((half, wide), bf16)] * 6
     outs += [jax.ShapeDtypeStruct((2, 8, units), f32)]
     made = group_call(
-        feed_forward_kernel,
+        functools.partial(feed_forward_kernel, keep),
         "feed_forward",
         2,
         list(halves) + list(grad_halves) + [up, shift, down],
         [half_rows(chunk, wide)] * 8 + [held(up.shape), held(shift.shape), held(down.shape)],
         outs,
         [group_rows(group, chunk, n) for n in sizes]
-        + [half_rows(chunk, wide)] * 8
+        + [pl.BlockSpec((2, chunk, wide), lambda s: (group, s, 0))]
+        + [half_rows(chunk, wide)] * 6
         + [pl.BlockSpec((1, 8, units), lambda s: (s, 0, 0))],
         earlier,
         [pltpu.VMEM((4 * chunk, n), bf16) for n in (wide, wide, units, units)],
         32 * half * wide * units,
         48 * half * wide + 4 * wide * units,
     )
-    return made[:4], made[4:8], made[8:12], jnp.sum(made[12][:, 0], axis=0)
+    return made[:5], made[5:9], made[9:11], jnp.sum(made[11][:, 0], axis=0)
 
 
 def only_head(values, head):
@@ -1018,8 +1053,9 @@
                 if n == 2 and eight:
                     x1, y0 = after((mine[0], mine[2]), back[1][0])
                     mine = [x1, swapped(x1, 1), y0, swapped(y0, 1)]
+                keep = (0, 2) if eight and n in (1, 2) else (0, 1)
                 made, back[n], ahead[n], unit_sum = feed_forward(
-                    n, mine, grad_groups[n], up_own, up_shift, after(down_own, *earlier),
+                    n, keep, mine, grad_groups[n], up_own, up_shift, after(down_own, *earlier),
                     made, 4 * groups,
                 )
                 unit_sums.append(unit_sum)
@@ -1028,12 +1064,17 @@
     kept = {}
 
     def down_grad_of(earlier):
-        active, _, _, grad_rows = (flat(one) for one in made)
+        active, grad_rows = flat(made[0]), flat(made[3])
         grad = dot(after(active, *earlier), grad_rows, COLS_BY_ROWS).astype(bf16)
-        return grad, functools.partial(kept.__setitem__, "down")
+        others = swapped(after(made[4], *earlier), 1) if eight else made[4]
+
+        def use(done):
+            kept["down"], kept["others"] = done
+
+        return (grad, others), use
 
     def up_grad_of(earlier):
-        _, grad_upper, normed_two, _ = (flat(one) for one in feed_made)
+        grad_upper, normed_two = flat(feed_made[1]), flat(feed_made[2])
         return dot(after(normed_two, *earlier), grad_upper, COLS_BY_ROWS).astype(bf16)
 
     grad_normed_two = scattered_sum(feed, groups, None, down_grad_of)
@@ -1049,13 +1090,15 @@
         made = project_back(0, mine, out_own, [], 4 * groups)
         up_grad = up_grad_of((made[0],))
         x0, y1, x1, y0, up_grad = after((*proj_hops, up_grad))
+        others = kept["others"]
         own, near, later, far = after([ahead[g] for g in range(groups)], up_grad)
-        sends = [
-            paired(later[0], later[1]), paired(later[2], later[3]),
-            paired(far[0], far[2]), paired(far[1], far[3]),
-        ]
-        near = [total(near[0], swapped(near[1], 1)), total(near[2], swapped(near[3], 1))]
-        own = [total(own[0], swapped(own[2], 1)), total(own[1], swapped(own[3], 1))]
+        sends = low_sums(
+            [later[0], (others, 4)],
+            [later[1], (others, 5)],
+            [far[0], (others, 6)],
+            [far[1], (others, 7)],
+        )
+        near = [[near[0], (others, 2)], [near[1], (others, 3)]]
         a0, a1 = swapped(x0, 4), swapped(y1, 2)
         made = project_back(
             1, [x0, swapped(x0, 1), y1, swapped(y1, 1)], out_own, made, 4 * groups
@@ -1063,7 +1106,7 @@
         made = project_back(
             2, [x1, swapped(x1, 1), y0, swapped(y0, 1)], out_own, made, 4 * groups
         )
-        a0, a1, made, near, own, sends = after((a0, a1, made, near, own, sends))
+        a0, a1, made, sends = after((a0, a1, made, sends))
         proj_groups = [None, None, None, [a0, a1, swapped(a0, 1), swapped(a1, 1)]]
     else:
         up_grad = up_grad_of(())
@@ -1073,7 +1116,9 @@
     up_grad = up_grad.reshape(shards, rows_held, own_units)
     if not eight:
         up_grad = lax.all_to_all(up_grad, "fsdp", 0, 0, tiled=True)
-    ahead = [ahead[g] for g in range(groups)]
+    ahead = [
+        [*ahead[g], kept["others"][2 * g], kept["others"][2 * g + 1]] for g in range(groups)
+    ]
     for g in range(groups - 1 if eight else 0, groups):
         halves_now = proj_groups[g]
         made = project_back(g, halves_now, out_own, made, 4 * groups)
@@ -1094,7 +1139,7 @@
         if eight and part == 0:
             one, again, *travelling = after((one, again, *travelling))
             x1, y0, a0, a1 = travelling
-            x0, y1 = total(near[0], a0).astype(bf16), total(near[1], a1).astype(bf16)
+            x0, y1 = low_sums(near[0] + [a0], near[1] + [a1])
             travelling = [swapped(x0, 2), swapped(y1, 4)]
             up_grad = after(up_grad, x0, y1)
             up_grad = lax.all_to_all(up_grad, "fsdp", 0, 0, tiled=True)
@@ -1125,19 +1170,16 @@
     def side_work(earlier):
         kept["late"] = earlier
         grad = lax.psum_scatter(kept["qkv"], "dp", scatter_dimension=0, tiled=True)
-        up_now, down_now, result_parts = after((up_grad, down_grad, result_terms), *earlier)
+        up_now, down_now = after((up_grad, down_grad), *earlier)
         grad = after(grad, *earlier).reshape(shards, rows_held, 3 * own_width)
         kept["qkv_parts"] = lax.all_to_all(grad, "fsdp", 0, 0, tiled=True)
-        made = jnp.concatenate(
-            [(total(*result_parts[h]) + down_shift).astype(bf16) for h in range(2)], axis=0
-        )
         up_now = up_now.reshape(shards, rows_held, items, units_held).transpose(1, 2, 0, 3)
         up_now = up_now.reshape(rows_held, hidden).astype(f32)
 
         def use(done):
-            kept.update(zip(("qkv_parts", "result", "up", "down"), done))
-
-        return (kept["qkv_parts"], made, up_now, down_now.astype(f32)), use
+            kept.update(zip(("qkv_parts", "up", "down"), done))
+
+        return (kept["qkv_parts"], up_now, down_now.astype(f32)), use
 
     if eight:
         x0, y1 = travelling
@@ -1163,7 +1205,7 @@
         side_work,
     )
     out_grad = kept["out"]
-    result, up_grad, down_grad = kept["result"], kept["up"], kept["down"]
+    up_grad, down_grad = kept["up"], kept["down"]
     if spread:
         out_grad = lax.psum_scatter(out_grad, "dp", scatter_dimension=0, tiled=True)
     else:
@@ -1175,7 +1217,7 @@
             scatter_dimension=0,
             tiled=True,
         )
-    out_grad = out_grad.astype(f32)
+    out_grad_low = out_grad
     grad_normed_summ = lax.all_to_all(kept["summ"], "fsdp", 0, 0, tiled=True)
     grad_normed_summ = after(grad_normed_summ, *kept["late"])
     grad_normed_summ = jnp.sum(grad_normed_summ.astype(f32), axis=0)
@@ -1200,6 +1242,13 @@
         halves(tokens[0]), grad_normed, grad_resid, gain_one[None], False
     )
     grad_inputs = grad_inputs.reshape(tok_rows, width)
+    result_terms, out_grad, others = after((result_terms, out_grad_low, kept["others"]), sums_one)
+    if eight:
+        result_terms = [(*result_terms[h], others[h]) for h in range(2)]
+    out_grad = out_grad.astype(f32)
+    result = jnp.concatenate(
+        [(total(*result_terms[h]) + down_shift).astype(bf16) for h in range(2)], axis=0
+    )
     _, norm_summ_pull = jax.vjp(layer_norm, summ_own, gain_one, shift_one)
     grad_summ, gain_summ_grad, shift_summ_grad = norm_summ_pull(grad_normed_summ)
     summary_cols = summaries.shape[2]

time: 960 us -> 942 us (0.981)
  other arithmetic: 87.4 us -> 35.1 us
  Pallas kernels: 398 us -> 423 us
  local copies, waits for them, and re-layouts: 77.1 us -> 93 us
    convert_element_type x26 -> x2, other arithmetic: 57.3 us -> 8.12 us  [the longest x1 6.57 us: per_device(): (total(*result_terms[h]) + down_shift).astype(bf16)]
    pallas_call x0 -> x11, Pallas kernels: none -> 23.1 us  [low_sums(): pl.pallas_call(functools.partial(low_sums_kernel, [len(one) for one in li...]
    unnamed x297, local copies, waits for them, and re-layouts: 40.1 us -> 53.9 us
    ppermute x112 -> x105, starting transfers between devices: 68.2 us -> 63 us  [swapped(): return lax.ppermute(x, 'fsdp', [(i, i ^ bit) for i in range(devices)])]
    ppermute x112 -> x105, waiting for transfers between devices: 157 us -> 162 us  [swapped(): return lax.ppermute(x, 'fsdp', [(i, i ^ bit) for i in range(devices)])]
  transfers between devices with their start and end apart: 127 -> 120, of which waited for: 40 -> 43; matrix products, arithmetic and copies ran while one was open for 22% -> 17% of each run, Pallas kernels for 40% -> 43%
where the time goes in v4:
time: 942 us; the launch traced here: 936 us
  Pallas kernels  423 us (45%)
  waiting for transfers between devices  175 us (19%)
  starting transfers between devices  95 us (10%)
  local copies, waits for them, and re-layouts  93 us (10%)
  matrix products  80.1 us (9%)
  other arithmetic  35.1 us (4%)
  blocking collectives  17.6 us (2%)
  between operations  16.9 us (2%)
    pallas_call x22, Pallas kernels, group_call(): pl.pallas_call(functools.partial(kernel, len(ins), len(earlier)), grid=(s...  233 us
    ppermute x105, waiting for transfers between devices, swapped(): return lax.ppermute(x, 'fsdp', [(i, i ^ bit) for i in range(devices)])  162 us
    pallas_call x2, Pallas kernels, attn_backward(): pl.pallas_call(functools.partial(attn_backward_kernel, block, half, heads...  90.6 us
    dot_general x6, matrix products, dot(): return lax.dot_general(left, right, dims, preferred_element_type=f32)  80.1 us
    ppermute x105, starting transfers between devices, swapped(): return lax.ppermute(x, 'fsdp', [(i, i ^ bit) for i in range(devices)])  63 us
    pallas_call x2, Pallas kernels, attn_forward(): pl.pallas_call(functools.partial(attn_forward_kernel, block, half, heads)...  55 us
    unnamed x297, local copies, waits for them, and re-layouts  53.9 us
    pallas_call x11, Pallas kernels, low_sums(): pl.pallas_call(functools.partial(low_sums_kernel, [len(one) for one in li...  23.1 us
  transfers between devices with their start and end apart: 120, of which 43 were waited for; matrix products, arithmetic and copies ran while one was open for 17% of the time, Pallas kernels for 43%

profile of v4, /device:TPU:0, one launch (start us, length us, event | category | flops | bytes accessed | tf_op | source)
XLA Modules:
  0.0 936.1 jit_solution(13563510476503061998)
XLA Ops:
  11.7 17.6 %all_to_all.53 = bf16[8,64,768]{2,1,0:T(8,128)(2,1)} all-to-all(bf16[8,64,768]{2,1,0:T(8,128)(2,1)S(1)} %pad_maximum_fusion.1), channel_id=1, replica_groups=mesh['dp'=4,'fsdp'=8] {'fsdp'}, dimensions={0} | all-to-all | bytes 1572864 | tf_op jit(solution)/shard_map/all_to_all | solution.py:907
  30.2 4.0 all-to-all-start.1
  36.3 5.7 all-to-all-done.1
  45.9 21.3 %collective-permute-done.refs_0_ = bf16[256,2048]{1,0:T(8,128)(2,1)S(1)} collective-permute-done((bf16[256,2048]{1,0:T(8,128)(2,1)S(1)}, bf16[256,2048]{1,0:T(8,128)(2,1)S(1)}, u32[]{:S(2)}, u32[]{:S(2)}) %collective-permute-start) | collective-permute-done | bytes 1048608 | tf_op jit(solution)/shard_map/ppermute | solution.py:62
  75.7 3.2 slice_bitcast_fusion
  79.7 5.8 norm_rows.4.refs_6_
  85.5 7.8 collective-permute-done.2.refs_0_
  100.4 5.9 norm_rows.5.refs_6_
  106.3 5.9 norm_rows.6.refs_6_
  112.2 14.5 %triple.2 = (bf16[4096,256]{1,0:T(8,128)(2,1)}, bf16[4096,256]{1,0:T(8,128)(2,1)}, bf16[4096,256]{1,0:T(8,128)(2,1)}) custom-call(bf16[4352,2048]{1,0:T(8,128)(2,1)} %bitcast.154, bf16[2048,768]{1,0:T(8,128)(2,1)} %all-gather.5.cloned.1.call-done.refs_1_.refs_6_, f32[1,768]{1,0:T(1,128)S(1)} %broadcast_in_dim.33.refs_2_), custom_call_target="tpu_custom_call" | custom-call | flops 9663676416 | bytes 12582912 | tf_op jit(solution)/shard_map/triple/pallas_call | solution.py:207
  128.4 3.8 all-to-all-start.2
  137.6 5.7 norm_rows.7
  143.4 7.6 triple.3
  155.6 27.5 %attn_forward.2 = (bf16[4096,128]{1,0:T(8,128)(2,1)S(1)}, f32[8,4096]{1,0:T(8,128)S(1)}) custom-call(s32[40]{0:T(128)S(1)} %pad_add_fusion.plan_ref, bf16[4096,256]{1,0:T(8,128)(2,1)S(1)} %copy-done.4, bf16[4096,256]{1,0:T(8,128)(2,1)S(1)} %copy-done.5, bf16[4096,256]{1,0:T(8,128)(2,1)S(1)} %copy-done.7, bf16[160,256]{1,0:T(8,128)(2,1)S(1)} %get-tuple-element.717.sk_ref, ...), custom_call_target="tpu_custom_call" | custom-call | flops 8589934592 | bytes 4194304 | tf_op jit(solution)/shard_map/attn_forward/pallas_call | solution.py:706
  184.1 2.9 collective-permute-done.14.refs_4_
  189.2 4.2 all-to-all-start.3
  197.2 27.5 %attn_forward.3 = (bf16[4096,128]{1,0:T(8,128)(2,1)S(1)}, f32[8,4096]{1,0:T(8,128)S(1)}) custom-call(s32[40]{0:T(128)S(1)} %pad_add_fusion.plan_ref, bf16[4096,256]{1,0:T(8,128)(2,1)S(1)} %copy-done.4, bf16[4096,256]{1,0:T(8,128)(2,1)S(1)} %copy-done.6, bf16[4096,256]{1,0:T(8,128)(2,1)S(1)} %copy-done.8, bf16[160,256]{1,0:T(8,128)(2,1)S(1)} %get-tuple-element.717.sk_ref, ...), custom_call_target="tpu_custom_call" | custom-call | flops 8589934592 | bytes 4194304 | tf_op jit(solution)/shard_map/attn_forward/pallas_call | solution.py:706
  228.1 4.0 project.8
  241.6 3.9 project.9
  245.5 18.1 %collective-permute-done.22 = bf16[256,2048]{1,0:T(8,128)(2,1)S(1)} collective-permute-done((bf16[256,2048]{1,0:T(8,128)(2,1)S(1)}, bf16[256,2048]{1,0:T(8,128)(2,1)S(1)}, u32[]{:S(2)}, u32[]{:S(2)}) %collective-permute-start.22) | collective-permute-done | bytes 1048608 | tf_op jit(solution)/shard_map/ppermute | solution.py:62
  274.2 3.9 project.10
  279.8 4.1 project.11
  283.9 13.7 %collective-permute-done.27.refs_2_ = bf16[256,2048]{1,0:T(8,128)(2,1)S(1)} collective-permute-done((bf16[256,2048]{1,0:T(8,128)(2,1)}, bf16[256,2048]{1,0:T(8,128)(2,1)S(1)}, u32[]{:S(2)}, u32[]{:S(2)}) %collective-permute-start.27) | collective-permute-done | bytes 1048608 | tf_op jit(solution)/shard_map/ppermute | solution.py:62
  298.8 3.0 low_sums.13
  303.4 22.8 %collective-permute-done.30 = bf16[256,2048]{1,0:T(8,128)(2,1)S(1)} collective-permute-done((bf16[256,2048]{1,0:T(8,128)(2,1)}, bf16[256,2048]{1,0:T(8,128)(2,1)S(1)}, u32[]{:S(2)}, u32[]{:S(2)}) %collective-permute-start.30) | collective-permute-done | bytes 1048608 | tf_op jit(solution)/shard_map/ppermute | solution.py:62
  327.5 5.3 fusion.28
  338.5 4.8 slice.180
  343.2 16.2 %collective-permute-done.38.refs_0_ = bf16[256,2048]{1,0:T(8,128)(2,1)S(1)} collective-permute-done((bf16[256,2048]{1,0:T(8,128)(2,1)}, bf16[256,2048]{1,0:T(8,128)(2,1)S(1)}, u32[]{:S(2)}, u32[]{:S(2)}) %collective-permute-start.38) | collective-permute-done | bytes 1048608 | tf_op jit(solution)/shard_map/ppermute | solution.py:62
  366.1 30.0 %feed_forward.4 = (bf16[16,256,1024]{2,1,0:T(8,128)(2,1)}, bf16[16,256,1024]{2,1,0:T(8,128)(2,1)}, bf16[16,256,2048]{2,1,0:T(8,128)(2,1)}, bf16[16,256,2048]{2,1...) custom-call(bf16[256,2048]{1,0:T(8,128)(2,1)} %copy-done.136, ...), custom_call_target="tpu_custom_call" | custom-call | flops 17179869184 | bytes 33554432 | tf_op jit(solution)/shard_map/feed_forward/pallas_call | solution.py:207
  401.5 30.3 %feed_forward.5 = (bf16[16,256,1024]{2,1,0:T(8,128)(2,1)}, bf16[16,256,1024]{2,1,0:T(8,128)(2,1)}, bf16[16,256,2048]{2,1,0:T(8,128)(2,1)}, bf16[16,256,2048]{2,1...) custom-call(bf16[256,2048]{1,0:T(8,128)(2,1)} %collective-permute-do, ...), custom_call_target="tpu_custom_call", output_to_operand_aliasing={{0}: (11, {}), {1}: (12, {}), {2}: (13, {}), {3}: (14, {}),... | custom-call | flops 17179869184 | bytes 33554432 | tf_op jit(solution)/shard_map/feed_forward/pallas_call | solution.py:207
  443.3 30.0 %feed_forward.6 = (bf16[16,256,1024]{2,1,0:T(8,128)(2,1)}, bf16[16,256,1024]{2,1,0:T(8,128)(2,1)}, bf16[16,256,2048]{2,1,0:T(8,128)(2,1)}, bf16[16,256,2048]{2,1...) custom-call(bf16[256,2048]{1,0:T(8,128)(2,1)} %collective-permute-do, ...), custom_call_target="tpu_custom_call", output_to_operand_aliasing={{0}: (11, {}), {1}: (12, {}), {2}: (13, {}), {3}: (14, {}),... | custom-call | flops 17179869184 | bytes 33554432 | tf_op jit(solution)/shard_map/feed_forward/pallas_call | solution.py:207
  484.7 30.4 %feed_forward.7 = (bf16[16,256,1024]{2,1,0:T(8,128)(2,1)}, bf16[16,256,1024]{2,1,0:T(8,128)(2,1)}, bf16[16,256,2048]{2,1,0:T(8,128)(2,1)}, bf16[16,256,2048]{2,1...) custom-call(bf16[256,2048]{1,0:T(8,128)(2,1)} %get-tuple-element.727, ...), custom_call_target="tpu_custom_call", output_to_operand_aliasing={{0}: (11, {}), {1}: (12, {}), {2}: (13, {}), {3}: (14, {}),... | custom-call | flops 17179869184 | bytes 33554432 | tf_op jit(solution)/shard_map/feed_forward/pallas_call | solution.py:207
  519.7 23.9 %convolution_convert_fusion.1 = bf16[1024,2048]{1,0:T(8,128)(2,1)} fusion(bf16[4096,1024]{1,0:T(8,128)(2,1)} %bitcast.160, bf16[4096,2048]{1,0:T(8,128)(2,1)} %bitcast.158), kind=kOutput, calls=%fused_computation.9 | convolution fusion | flops 17181966336 | bytes 29360128 | tf_op jit(solution)/shard_map/dot_general | solution.py:27
  547.5 10.1 %norm_back.2 = (f32[2,256,2048]{2,1,0:T(8,128)}, f32[8,2048]{1,0:T(8,128)S(1)}, bf16[256,2048]{1,0:T(8,128)(2,1)}, bf16[256,2048]{1,0:T(8,128)(2,1)}) custom-call(f32[256,2048]{1,0:T(8,128)S(1)} %get-tuple-element.657.refs_0_, f32[256,2048]{1,0:T(8,128)} %copy-done.74, bf16[256,2048]{1,0:T(8,128)(2,1)S(1)} %copy-done.23, ...), custom_call_target="tpu_custom_call" | custom-call | flops 41943040 | bytes 18874368 | tf_op jit(solution)/shard_map/norm_back/pallas_call | solution.py:327
  564.0 5.4 project_back.4
  569.5 23.7 %convolution_convert_fusion = bf16[2048,1024]{1,0:T(8,128)(2,1)} fusion(bf16[4096,2048]{1,0:T(8,128)(2,1)} %bitcast.157, bf16[4096,1024]{1,0:T(8,128)(2,1)} %bitcast.161), kind=kOutput, calls=%fused_computation.8 | convolution fusion | flops 17181966336 | bytes 29360128 | tf_op jit(solution)/shard_map/dot_general | solution.py:27
  593.2 13.5 %collective-permute-done.73.refs_0_ = bf16[256,2048]{1,0:T(8,128)(2,1)} collective-permute-done((bf16[256,2048]{1,0:T(8,128)(2,1)}, bf16[256,2048]{1,0:T(8,128)(2,1)}, u32[]{:S(2)}, u32[]{:S(2)}) %collective-permute-start.73) | collective-permute-done | bytes 1048608 | tf_op jit(solution)/shard_map/ppermute | solution.py:62
  616.0 4.1 low_sums.17
  620.1 5.4 project_back.5
  625.5 5.5 project_back.6
  631.0 3.1 collective-permute-done.77.refs_0_
  637.5 2.9 collective-permute-done.83.refs_2_
  645.4 5.2 project_back.7
  652.8 45.3 %attn_backward.2 = (bf16[4096,128]{1,0:T(8,128)(2,1)S(1)}, bf16[4096,128]{1,0:T(8,128)(2,1)S(1)}, bf16[4096,128]{1,0:T(8,128)(2,1)S(1)}, bf16[160,128]{1,0:T(8,1...) custom-call(s32[40]{0:T(128)S(1)} %copy-done.63, bf16[4096,256]{1,0:T(8,128)(2,1)} %get-tuple-element.369.q_ref, ...), custom_call_target="tpu_custom_call" | custom-call | flops 12884901888 | bytes 10485760 | tf_op jit(solution)/shard_map/attn_backward/pallas_call | solution.py:747
  698.2 4.2 low_sums.18
  704.5 4.2 all-to-all-start.4
  710.0 45.3 %attn_backward.3 = (bf16[4096,128]{1,0:T(8,128)(2,1)S(1)}, bf16[4096,128]{1,0:T(8,128)(2,1)S(1)}, bf16[4096,128]{1,0:T(8,128)(2,1)S(1)}, bf16[160,128]{1,0:T(8,1...) custom-call(s32[40]{0:T(128)S(1)} %copy-done.63, bf16[4096,256]{1,0:T(8,128)(2,1)} %get-tuple-element.369.q_ref, ...), custom_call_target="tpu_custom_call" | custom-call | flops 12884901888 | bytes 10485760 | tf_op jit(solution)/shard_map/attn_backward/pallas_call | solution.py:747
  758.3 7.1 project.12
  781.6 21.5 %fusion.7 = bf16[2048,768]{1,0:T(8,128)(2,1)} fusion(bf16[4352,2048]{1,0:T(8,128)(2,1)} %pad_dynamic-update-slice_fusion, bf16[160,512]{1,0:T(8,128)(2,1)S(1)} %constant_dynamic-update-slice_fusion, bf16[4096,768]{1,0:T(8,128)(2,1)} %constant_dynamic-update-slice_fusion.4), kind=kOutput, calls=%fused_computation.10 | convolution fusion | flops 13711835136 | bytes 27426816 | tf_op jit(solution)/shard_map/dot_general | solution.py:27
  804.4 7.7 project.13
  821.9 4.2 all-to-all-start.6
  826.2 7.6 project.14
  834.8 9.4 %convolution_convert_fusion.2 = bf16[256,2048]{1,0:T(8,128)(2,1)} fusion(bf16[4096,2048]{1,0:T(8,128)(2,1)} %bitcast.159, bf16[4096,128]{1,0:T(8,128)(2,1)S(1)} %copy-done.69, bf16[4096,128]{1,0:T(8,128)(2,1)S(1)} %copy-done.66), kind=kOutput, calls=%fused_computation.14 | convolution fusion | flops 4299685888 | bytes 19922944 | tf_op jit(solution)/shard_map/dot_general | solution.py:27
  845.7 7.3 project.15
  853.0 3.4 low_sums.21
  865.1 4.2 all-to-all-start.5
  871.8 2.9 reshape.535
  874.8 2.8 copy.125
  885.2 6.7 all-to-all-done.5.parts_ref
  896.8 8.7 norm_back.3
  906.7 2.8 all-to-all-start.8
  909.6 6.6 fusion.18
  917.3 3.4 all-to-all-start.7
  920.8 3.0 maximum_bitcast_fusion
  (656 shorter events, 216.7 us)
Async XLA Ops:
  7.2 105.0 %all-gather.5.cloned.1.call-start = ((), (), s32[]{:S(2)}) async-start(), calls=%async_computation.13 | async-start | bytes 3932160 | tf_op jit(solution)/shard_map/all_gather | solution.py:908
  34.2 191.5 %all-gather.9.cloned.1.call-start = ((), (), s32[]{:S(2)}) async-start(), calls=%async_computation.19 | async-start | bytes 6553600 | tf_op jit(solution)/shard_map/all_gather | solution.py:964
  42.0 25.2 %collective-permute-start = (bf16[256,2048]{1,0:T(8,128)(2,1)S(1)}, bf16[256,2048]{1,0:T(8,128)(2,1)S(1)}, u32[]{:S(2)}, u32[]{:S(2)}) collective-permute-start(bf16[256,2048]{1,0:T(8,128)(2,1)S(1)} %get-tuple-element.351.refs_0_), channel_id=1, source_target_pairs={{0,2},{1,3},{2,0},{3,1},{4,6},{5,7},{6,4},{7,5},{8,10},{9,11},{10,... | collective-permute-start | bytes 3145736 | tf_op jit(solution)/shard_map/ppermute | solution.py:62
  42.4 25.1 %collective-permute-start.1 = (bf16[256,2048]{1,0:T(8,128)(2,1)S(1)}, bf16[256,2048]{1,0:T(8,128)(2,1)}, u32[]{:S(2)}, u32[]{:S(2)}) collective-permute-start(bf16[256,2048]{1,0:T(8,128)(2,1)S(1)} %get-tuple-element.352.refs_1_), channel_id=1, source_target_pairs={{0,4},{1,5},{2,6},{3,7},{4,0},{5,1},{6,2},{7,3},{8,12},{9,13},{10,... | collective-permute-start | bytes 3145736 | tf_op jit(solution)/shard_map/ppermute | solution.py:62
  68.1 25.2 %collective-permute-start.2 = (bf16[256,2048]{1,0:T(8,128)(2,1)S(1)}, bf16[256,2048]{1,0:T(8,128)(2,1)}, u32[]{:S(2)}, u32[]{:S(2)}) collective-permute-start(bf16[256,2048]{1,0:T(8,128)(2,1)S(1)} %get-tuple-element.352.refs_1_), channel_id=1, source_target_pairs={{0,2},{1,3},{2,0},{3,1},{4,6},{5,7},{6,4},{7,5},{8,10},{9,11},{10,... | collective-permute-start | bytes 3145736 | tf_op jit(solution)/shard_map/ppermute | solution.py:62
  69.7 25.0 %collective-permute-start.3 = (bf16[256,2048]{1,0:T(8,128)(2,1)S(1)}, bf16[256,2048]{1,0:T(8,128)(2,1)}, u32[]{:S(2)}, u32[]{:S(2)}) collective-permute-start(bf16[256,2048]{1,0:T(8,128)(2,1)S(1)} %get-tuple-element.351.refs_0_), channel_id=1, source_target_pairs={{0,4},{1,5},{2,6},{3,7},{4,0},{5,1},{6,2},{7,3},{8,12},{9,13},{10,... | collective-permute-start | bytes 3145736 | tf_op jit(solution)/shard_map/ppermute | solution.py:62
  96.1 30.7 %collective-permute-start.6 = (bf16[256,2048]{1,0:T(8,128)(2,1)S(1)}, bf16[256,2048]{1,0:T(8,128)(2,1)S(1)}, u32[]{:S(2)}, u32[]{:S(2)}) collective-permute-start(bf16[256,2048]{1,0:T(8,128)(2,1)S(1)} %collective-permute-done.refs_0_), channel_id=1, source_target_pairs={{0,4},{1,5},{2,6},{3,7},{4,0},{5,1},{6,2},{7,3},{8,12},{9,13},{10,... | collective-permute-start | bytes 3145736 | tf_op jit(solution)/shard_map/ppermute | solution.py:62
  98.9 27.8 %collective-permute-start.7 = (bf16[256,2048]{1,0:T(8,128)(2,1)}, bf16[256,2048]{1,0:T(8,128)(2,1)S(1)}, u32[]{:S(2)}, u32[]{:S(2)}) collective-permute-start(bf16[256,2048]{1,0:T(8,128)(2,1)} %collective-permute-done.1.refs_2_), channel_id=1, source_target_pairs={{0,2},{1,3},{2,0},{3,1},{4,6},{5,7},{6,4},{7,5},{8,10},{9,11},{10,... | collective-permute-start | bytes 3145736 | tf_op jit(solution)/shard_map/ppermute | solution.py:62
  133.5 53.6 %collective-permute-start.15 = (bf16[256,2048]{1,0:T(8,128)(2,1)}, bf16[256,2048]{1,0:T(8,128)(2,1)}, u32[]{:S(2)}, u32[]{:S(2)}) collective-permute-start(bf16[256,2048]{1,0:T(8,128)(2,1)} %get-tuple-element.376.refs_5_), channel_id=1, source_target_pairs={{0,4},{1,5},{2,6},{3,7},{4,0},{5,1},{6,2},{7,3},{8,12},{9,13},{10,... | collective-permute-start | bytes 3145736 | tf_op jit(solution)/shard_map/ppermute | solution.py:62
  135.5 51.5 %collective-permute-start.16 = (bf16[256,2048]{1,0:T(8,128)(2,1)}, bf16[256,2048]{1,0:T(8,128)(2,1)}, u32[]{:S(2)}, u32[]{:S(2)}) collective-permute-start(bf16[256,2048]{1,0:T(8,128)(2,1)} %get-tuple-element.376.refs_5_), channel_id=1, source_target_pairs={{0,2},{1,3},{2,0},{3,1},{4,6},{5,7},{6,4},{7,5},{8,10},{9,11},{10,... | collective-permute-start | bytes 3145736 | tf_op jit(solution)/shard_map/ppermute | solution.py:62
  137.0 50.0 %collective-permute-start.14 = (bf16[256,2048]{1,0:T(8,128)(2,1)}, bf16[256,2048]{1,0:T(8,128)(2,1)}, u32[]{:S(2)}, u32[]{:S(2)}) collective-permute-start(bf16[256,2048]{1,0:T(8,128)(2,1)} %get-tuple-element.375.refs_4_), channel_id=1, source_target_pairs={{0,2},{1,3},{2,0},{3,1},{4,6},{5,7},{6,4},{7,5},{8,10},{9,11},{10,... | collective-permute-start | bytes 3145736 | tf_op jit(solution)/shard_map/ppermute | solution.py:62
  137.6 49.5 %collective-permute-start.17 = (bf16[256,2048]{1,0:T(8,128)(2,1)}, bf16[256,2048]{1,0:T(8,128)(2,1)}, u32[]{:S(2)}, u32[]{:S(2)}) collective-permute-start(bf16[256,2048]{1,0:T(8,128)(2,1)} %get-tuple-element.375.refs_4_), channel_id=1, source_target_pairs={{0,4},{1,5},{2,6},{3,7},{4,0},{5,1},{6,2},{7,3},{8,12},{9,13},{10,... | collective-permute-start | bytes 3145736 | tf_op jit(solution)/shard_map/ppermute | solution.py:62
  187.1 41.0 %collective-permute-start.18 = (bf16[256,2048]{1,0:T(8,128)(2,1)}, bf16[256,2048]{1,0:T(8,128)(2,1)}, u32[]{:S(2)}, u32[]{:S(2)}) collective-permute-start(bf16[256,2048]{1,0:T(8,128)(2,1)} %collective-permute-done.14.refs_4_), channel_id=1, source_target_pairs={{0,4},{1,5},{2,6},{3,7},{4,0},{5,1},{6,2},{7,3},{8,12},{9,13},{10,... | collective-permute-start | bytes 3145736 | tf_op jit(solution)/shard_map/ppermute | solution.py:62
  188.6 39.4 %collective-permute-start.19 = (bf16[256,2048]{1,0:T(8,128)(2,1)}, bf16[256,2048]{1,0:T(8,128)(2,1)}, u32[]{:S(2)}, u32[]{:S(2)}) collective-permute-start(bf16[256,2048]{1,0:T(8,128)(2,1)} %collective-permute-done.15.refs_6_), channel_id=1, source_target_pairs={{0,2},{1,3},{2,0},{3,1},{4,6},{5,7},{6,4},{7,5},{8,10},{9,11},{10,... | collective-permute-start | bytes 3145736 | tf_op jit(solution)/shard_map/ppermute | solution.py:62
  189.2 38.9 %all-to-all-start.3 = ((bf16[8,64,1024]{2,1,0:T(8,128)(2,1)}), bf16[8,64,1024]{2,1,0:T(8,128)(2,1)}, u32[]{:S(2)}, u32[]{:S(2)}) async-start(bf16[8,64,1024]{2,1,0:T(8,128)(2,1)} %reshape.489), calls=%async_computation.3 | async-start | bytes 2097152 | tf_op jit(solution)/shard_map/all_to_all | solution.py:973
  193.4 172.7 %all-gather.7.cloned.1.call-start = ((), (), s32[]{:S(2)}) async-start(), calls=%async_computation.14 | async-start | bytes 5242880 | tf_op jit(solution)/shard_map/all_gather | solution.py:1022
  238.2 25.5 %collective-permute-start.22 = (bf16[256,2048]{1,0:T(8,128)(2,1)S(1)}, bf16[256,2048]{1,0:T(8,128)(2,1)S(1)}, u32[]{:S(2)}, u32[]{:S(2)}) collective-permute-start(bf16[256,2048]{1,0:T(8,128)(2,1)S(1)} %get-tuple-element.391), channel_id=1, source_target_pairs={{0,2},{1,3},{2,0},{3,1},{4,6},{5,7},{6,4},{7,5},{8,10},{9,11},{10,... | collective-permute-start | bytes 3145736 | tf_op jit(solution)/shard_map/ppermute | solution.py:62
  240.1 24.9 %collective-permute-start.23 = (bf16[256,2048]{1,0:T(8,128)(2,1)S(1)}, bf16[256,2048]{1,0:T(8,128)(2,1)S(1)}, u32[]{:S(2)}, u32[]{:S(2)}) collective-permute-start(bf16[256,2048]{1,0:T(8,128)(2,1)S(1)} %get-tuple-element.392), channel_id=1, source_target_pairs={{0,4},{1,5},{2,6},{3,7},{4,0},{5,1},{6,2},{7,3},{8,12},{9,13},{10,... | collective-permute-start | bytes 3145736 | tf_op jit(solution)/shard_map/ppermute | solution.py:62
  272.1 25.4 %collective-permute-start.27 = (bf16[256,2048]{1,0:T(8,128)(2,1)}, bf16[256,2048]{1,0:T(8,128)(2,1)S(1)}, u32[]{:S(2)}, u32[]{:S(2)}) collective-permute-start(bf16[256,2048]{1,0:T(8,128)(2,1)} %get-tuple-element.402), channel_id=1, source_target_pairs={{0,4},{1,5},{2,6},{3,7},{4,0},{5,1},{6,2},{7,3},{8,12},{9,13},{10,... | collective-permute-start | bytes 3145736 | tf_op jit(solution)/shard_map/ppermute | solution.py:62
  273.7 25.1 %collective-permute-start.28 = (bf16[256,2048]{1,0:T(8,128)(2,1)}, bf16[256,2048]{1,0:T(8,128)(2,1)S(1)}, u32[]{:S(2)}, u32[]{:S(2)}) collective-permute-start(bf16[256,2048]{1,0:T(8,128)(2,1)} %get-tuple-element.403), channel_id=1, source_target_pairs={{0,2},{1,3},{2,0},{3,1},{4,6},{5,7},{6,4},{7,5},{8,10},{9,11},{10,... | collective-permute-start | bytes 3145736 | tf_op jit(solution)/shard_map/ppermute | solution.py:62
  279.6 371.0 %reduce-scatter.5.cloned.1.call-start = ((), (), s32[]{:S(2)}) async-start(), calls=%async_computation.15 | async-start | bytes 5242880 | tf_op jit(solution)/shard_map/reduce_scatter | solution.py:1082
  302.7 24.8 %collective-permute-start.33 = (bf16[256,2048]{1,0:T(8,128)(2,1)}, bf16[256,2048]{1,0:T(8,128)(2,1)}, u32[]{:S(2)}, u32[]{:S(2)}) collective-permute-start(bf16[256,2048]{1,0:T(8,128)(2,1)} %get-tuple-element.422), channel_id=1, source_target_pairs={{0,1},{1,0},{2,3},{3,2},{4,5},{5,4},{6,7},{7,6},{8,9},{9,8},{10,11... | collective-permute-start | bytes 3145736 | tf_op jit(solution)/shard_map/ppermute | solution.py:62
  360.8 37.2 %collective-permute-start.54 = (bf16[256,2048]{1,0:T(8,128)(2,1)}, bf16[256,2048]{1,0:T(8,128)(2,1)}, u32[]{:S(2)}, u32[]{:S(2)}) collective-permute-start(bf16[256,2048]{1,0:T(8,128)(2,1)} %collective-permute-done.16.refs_4_), channel_id=1, source_target_pairs={{0,1},{1,0},{2,3},{3,2},{4,5},{5,4},{6,7},{7,6},{8,9},{9,8},{10,11... | collective-permute-start | bytes 3145736 | tf_op jit(solution)/shard_map/ppermute | solution.py:62
  360.9 38.0 %collective-permute-start.55 = (bf16[256,2048]{1,0:T(8,128)(2,1)}, bf16[256,2048]{1,0:T(8,128)(2,1)}, u32[]{:S(2)}, u32[]{:S(2)}) collective-permute-start(bf16[256,2048]{1,0:T(8,128)(2,1)} %collective-permute-done.17.refs_6_), channel_id=1, source_target_pairs={{0,1},{1,0},{2,3},{3,2},{4,5},{5,4},{6,7},{7,6},{8,9},{9,8},{10,11... | collective-permute-start | bytes 3145736 | tf_op jit(solution)/shard_map/ppermute | solution.py:62
  361.4 34.7 %collective-permute-start.46 = (bf16[256,2048]{1,0:T(8,128)(2,1)S(1)}, bf16[256,2048]{1,0:T(8,128)(2,1)}, u32[]{:S(2)}, u32[]{:S(2)}) collective-permute-start(bf16[256,2048]{1,0:T(8,128)(2,1)S(1)} %get-tuple-element.726.refs_1_), channel_id=1, source_target_pairs={{0,2},{1,3},{2,0},{3,1},{4,6},{5,7},{6,4},{7,5},{8,10},{9,11},{10,... | collective-permute-start | bytes 3145736 | tf_op jit(solution)/shard_map/ppermute | solution.py:62
  365.3 30.8 %collective-permute-start.47 = (bf16[256,2048]{1,0:T(8,128)(2,1)}, bf16[256,2048]{1,0:T(8,128)(2,1)}, u32[]{:S(2)}, u32[]{:S(2)}) collective-permute-start(bf16[256,2048]{1,0:T(8,128)(2,1)} %get-tuple-element.727.refs_0_), channel_id=1, source_target_pairs={{0,4},{1,5},{2,6},{3,7},{4,0},{5,1},{6,2},{7,3},{8,12},{9,13},{10,... | collective-permute-start | bytes 3145736 | tf_op jit(solution)/shard_map/ppermute | solution.py:62
  396.7 35.9 %collective-permute-start.40 = (bf16[256,2048]{1,0:T(8,128)(2,1)S(1)}, bf16[256,2048]{1,0:T(8,128)(2,1)}, u32[]{:S(2)}, u32[]{:S(2)}) collective-permute-start(bf16[256,2048]{1,0:T(8,128)(2,1)S(1)} %copy-done.137), channel_id=1, source_target_pairs={{0,4},{1,5},{2,6},{3,7},{4,0},{5,1},{6,2},{7,3},{8,12},{9,13},{10,... | collective-permute-start | bytes 3145736 | tf_op jit(solution)/shard_map/ppermute | solution.py:62
  398.0 34.9 %collective-permute-start.41 = (bf16[256,2048]{1,0:T(8,128)(2,1)}, bf16[256,2048]{1,0:T(8,128)(2,1)}, u32[]{:S(2)}, u32[]{:S(2)}) collective-permute-start(bf16[256,2048]{1,0:T(8,128)(2,1)} %collective-permute-done.39.refs_2_), channel_id=1, source_target_pairs={{0,2},{1,3},{2,0},{3,1},{4,6},{5,7},{6,4},{7,5},{8,10},{9,11},{10,... | collective-permute-start | bytes 3145736 | tf_op jit(solution)/shard_map/ppermute | solution.py:62
  438.0 35.2 %collective-permute-start.58 = (bf16[256,2048]{1,0:T(8,128)(2,1)S(1)}, bf16[256,2048]{1,0:T(8,128)(2,1)S(1)}, u32[]{:S(2)}, u32[]{:S(2)}) collective-permute-start(bf16[256,2048]{1,0:T(8,128)(2,1)S(1)} %get-tuple-element.453), channel_id=1, source_target_pairs={{0,2},{1,3},{2,0},{3,1},{4,6},{5,7},{6,4},{7,5},{8,10},{9,11},{10,... | collective-permute-start | bytes 3145736 | tf_op jit(solution)/shard_map/ppermute | solution.py:62
  438.9 34.3 %collective-permute-start.59 = (bf16[256,2048]{1,0:T(8,128)(2,1)S(1)}, bf16[256,2048]{1,0:T(8,128)(2,1)S(1)}, u32[]{:S(2)}, u32[]{:S(2)}) collective-permute-start(bf16[256,2048]{1,0:T(8,128)(2,1)S(1)} %get-tuple-element.454), channel_id=1, source_target_pairs={{0,4},{1,5},{2,6},{3,7},{4,0},{5,1},{6,2},{7,3},{8,12},{9,13},{10,... | collective-permute-start | bytes 3145736 | tf_op jit(solution)/shard_map/ppermute | solution.py:62
  477.7 37.4 %collective-permute-start.62 = (bf16[256,2048]{1,0:T(8,128)(2,1)}, bf16[256,2048]{1,0:T(8,128)(2,1)S(1)}, u32[]{:S(2)}, u32[]{:S(2)}) collective-permute-start(bf16[256,2048]{1,0:T(8,128)(2,1)} %get-tuple-element.485), channel_id=1, source_target_pairs={{0,1},{1,0},{2,3},{3,2},{4,5},{5,4},{6,7},{7,6},{8,9},{9,8},{10,11... | collective-permute-start | bytes 3145736 | tf_op jit(solution)/shard_map/ppermute | solution.py:62
  480.3 34.8 %collective-permute-start.65 = (bf16[256,2048]{1,0:T(8,128)(2,1)}, bf16[256,2048]{1,0:T(8,128)(2,1)S(1)}, u32[]{:S(2)}, u32[]{:S(2)}) collective-permute-start(bf16[256,2048]{1,0:T(8,128)(2,1)} %get-tuple-element.492), channel_id=1, source_target_pairs={{0,1},{1,0},{2,3},{3,2},{4,5},{5,4},{6,7},{7,6},{8,9},{9,8},{10,11... | collective-permute-start | bytes 3145736 | tf_op jit(solution)/shard_map/ppermute | solution.py:62
  480.7 34.3 %collective-permute-start.63 = (bf16[256,2048]{1,0:T(8,128)(2,1)}, bf16[256,2048]{1,0:T(8,128)(2,1)S(1)}, u32[]{:S(2)}, u32[]{:S(2)}) collective-permute-start(bf16[256,2048]{1,0:T(8,128)(2,1)} %get-tuple-element.469), channel_id=1, source_target_pairs={{0,4},{1,5},{2,6},{3,7},{4,0},{5,1},{6,2},{7,3},{8,12},{9,13},{10,... | collective-permute-start | bytes 3145736 | tf_op jit(solution)/shard_map/ppermute | solution.py:62
  482.2 32.9 %collective-permute-start.64 = (bf16[256,2048]{1,0:T(8,128)(2,1)S(1)}, bf16[256,2048]{1,0:T(8,128)(2,1)S(1)}, u32[]{:S(2)}, u32[]{:S(2)}) collective-permute-start(bf16[256,2048]{1,0:T(8,128)(2,1)S(1)} %get-tuple-element.470), channel_id=1, source_target_pairs={{0,2},{1,3},{2,0},{3,1},{4,6},{5,7},{6,4},{7,5},{8,10},{9,11},{10,... | collective-permute-start | bytes 3145736 | tf_op jit(solution)/shard_map/ppermute | solution.py:62
  516.8 26.8 %collective-permute-start.70 = (bf16[8,256,2048]{2,1,0:T(8,128)(2,1)}, bf16[8,256,2048]{2,1,0:T(8,128)(2,1)}, u32[]{:S(2)}, u32[]{:S(2)}) collective-permute-start(bf16[8,256,2048]{2,1,0:T(8,128)(2,1)} %get-tuple-element.506), channel_id=1, source_target_pairs={{0,1},{1,0},{2,3},{3,2},{4,5},{5,4},{6,7},{7,6},{8,9},{9,8},{10,11... | collective-permute-start | bytes 25165832 | tf_op jit(solution)/shard_map/ppermute | solution.py:62
  517.0 26.6 %collective-permute-start.66 = (bf16[256,2048]{1,0:T(8,128)(2,1)}, bf16[256,2048]{1,0:T(8,128)(2,1)}, u32[]{:S(2)}, u32[]{:S(2)}) collective-permute-start(bf16[256,2048]{1,0:T(8,128)(2,1)} %get-tuple-element.494), channel_id=1, source_target_pairs={{0,2},{1,3},{2,0},{3,1},{4,6},{5,7},{6,4},{7,5},{8,10},{9,11},{10,... | collective-permute-start | bytes 3145736 | tf_op jit(solution)/shard_map/ppermute | solution.py:62
  517.9 25.7 %collective-permute-start.67 = (bf16[256,2048]{1,0:T(8,128)(2,1)}, bf16[256,2048]{1,0:T(8,128)(2,1)}, u32[]{:S(2)}, u32[]{:S(2)}) collective-permute-start(bf16[256,2048]{1,0:T(8,128)(2,1)} %get-tuple-element.495), channel_id=1, source_target_pairs={{0,4},{1,5},{2,6},{3,7},{4,0},{5,1},{6,2},{7,3},{8,12},{9,13},{10,... | collective-permute-start | bytes 3145736 | tf_op jit(solution)/shard_map/ppermute | solution.py:62
  519.2 24.4 %collective-permute-start.69 = (bf16[256,2048]{1,0:T(8,128)(2,1)}, bf16[256,2048]{1,0:T(8,128)(2,1)}, u32[]{:S(2)}, u32[]{:S(2)}) collective-permute-start(bf16[256,2048]{1,0:T(8,128)(2,1)} %get-tuple-element.500), channel_id=1, source_target_pairs={{0,1},{1,0},{2,3},{3,2},{4,5},{5,4},{6,7},{7,6},{8,9},{9,8},{10,11... | collective-permute-start | bytes 3145736 | tf_op jit(solution)/shard_map/ppermute | solution.py:62
  543.6 160.8 %reduce-scatter.7.cloned.1.call-start = ((), (), s32[]{:S(2)}) async-start(), calls=%async_computation.16 | async-start | bytes 5242880 | tf_op jit(solution)/shard_map/reduce_scatter | solution.py:1115
  558.7 34.5 %collective-permute-start.71 = (bf16[256,2048]{1,0:T(8,128)(2,1)}, bf16[256,2048]{1,0:T(8,128)(2,1)}, u32[]{:S(2)}, u32[]{:S(2)}) collective-permute-start(bf16[256,2048]{1,0:T(8,128)(2,1)} %get-tuple-element.515.refs_0_), channel_id=1, source_target_pairs={{0,2},{1,3},{2,0},{3,1},{4,6},{5,7},{6,4},{7,5},{8,10},{9,11},{10,... | collective-permute-start | bytes 3145736 | tf_op jit(solution)/shard_map/ppermute | solution.py:62
  560.1 33.1 %collective-permute-start.72 = (bf16[256,2048]{1,0:T(8,128)(2,1)}, bf16[256,2048]{1,0:T(8,128)(2,1)}, u32[]{:S(2)}, u32[]{:S(2)}) collective-permute-start(bf16[256,2048]{1,0:T(8,128)(2,1)} %get-tuple-element.516.refs_1_), channel_id=1, source_target_pairs={{0,4},{1,5},{2,6},{3,7},{4,0},{5,1},{6,2},{7,3},{8,12},{9,13},{10,... | collective-permute-start | bytes 3145736 | tf_op jit(solution)/shard_map/ppermute | solution.py:62
  561.1 45.6 %collective-permute-start.73 = (bf16[256,2048]{1,0:T(8,128)(2,1)}, bf16[256,2048]{1,0:T(8,128)(2,1)}, u32[]{:S(2)}, u32[]{:S(2)}) collective-permute-start(bf16[256,2048]{1,0:T(8,128)(2,1)} %get-tuple-element.516.refs_1_), channel_id=1, source_target_pairs={{0,2},{1,3},{2,0},{3,1},{4,6},{5,7},{6,4},{7,5},{8,10},{9,11},{10,... | collective-permute-start | bytes 3145736 | tf_op jit(solution)/shard_map/ppermute | solution.py:62
  562.1 45.6 %collective-permute-start.74 = (bf16[256,2048]{1,0:T(8,128)(2,1)}, bf16[256,2048]{1,0:T(8,128)(2,1)}, u32[]{:S(2)}, u32[]{:S(2)}) collective-permute-start(bf16[256,2048]{1,0:T(8,128)(2,1)} %get-tuple-element.515.refs_0_), channel_id=1, source_target_pairs={{0,4},{1,5},{2,6},{3,7},{4,0},{5,1},{6,2},{7,3},{8,12},{9,13},{10,... | collective-permute-start | bytes 3145736 | tf_op jit(solution)/shard_map/ppermute | solution.py:62
  608.8 25.4 %collective-permute-start.77 = (bf16[256,2048]{1,0:T(8,128)(2,1)}, bf16[256,2048]{1,0:T(8,128)(2,1)S(1)}, u32[]{:S(2)}, u32[]{:S(2)}) collective-permute-start(bf16[256,2048]{1,0:T(8,128)(2,1)} %collective-permute-done.71.refs_0_), channel_id=1, source_target_pairs={{0,4},{1,5},{2,6},{3,7},{4,0},{5,1},{6,2},{7,3},{8,12},{9,13},{10,... | collective-permute-start | bytes 3145736 | tf_op jit(solution)/shard_map/ppermute | solution.py:62
  611.4 25.5 %collective-permute-start.78 = (bf16[256,2048]{1,0:T(8,128)(2,1)}, bf16[256,2048]{1,0:T(8,128)(2,1)}, u32[]{:S(2)}, u32[]{:S(2)}) collective-permute-start(bf16[256,2048]{1,0:T(8,128)(2,1)} %collective-permute-done.72.refs_2_), channel_id=1, source_target_pairs={{0,2},{1,3},{2,0},{3,1},{4,6},{5,7},{6,4},{7,5},{8,10},{9,11},{10,... | collective-permute-start | bytes 3145736 | tf_op jit(solution)/shard_map/ppermute | solution.py:62
  641.3 56.8 %collective-permute-start.85 = (bf16[256,2048]{1,0:T(8,128)(2,1)}, bf16[256,2048]{1,0:T(8,128)(2,1)}, u32[]{:S(2)}, u32[]{:S(2)}) collective-permute-start(bf16[256,2048]{1,0:T(8,128)(2,1)} %get-tuple-element.559), channel_id=1, source_target_pairs={{0,2},{1,3},{2,0},{3,1},{4,6},{5,7},{6,4},{7,5},{8,10},{9,11},{10,... | collective-permute-start | bytes 3145736 | tf_op jit(solution)/shard_map/ppermute | solution.py:62
  642.1 56.1 %collective-permute-start.86 = (bf16[256,2048]{1,0:T(8,128)(2,1)}, bf16[256,2048]{1,0:T(8,128)(2,1)}, u32[]{:S(2)}, u32[]{:S(2)}) collective-permute-start(bf16[256,2048]{1,0:T(8,128)(2,1)} %get-tuple-element.560), channel_id=1, source_target_pairs={{0,4},{1,5},{2,6},{3,7},{4,0},{5,1},{6,2},{7,3},{8,12},{9,13},{10,... | collective-permute-start | bytes 3145736 | tf_op jit(solution)/shard_map/ppermute | solution.py:62
  643.3 54.8 %collective-permute-start.87 = (bf16[256,2048]{1,0:T(8,128)(2,1)}, bf16[256,2048]{1,0:T(8,128)(2,1)S(1)}, u32[]{:S(2)}, u32[]{:S(2)}) collective-permute-start(bf16[256,2048]{1,0:T(8,128)(2,1)} %get-tuple-element.561), channel_id=1, source_target_pairs={{0,4},{1,5},{2,6},{3,7},{4,0},{5,1},{6,2},{7,3},{8,12},{9,13},{10,... | collective-permute-start | bytes 3145736 | tf_op jit(solution)/shard_map/ppermute | solution.py:62
  644.1 54.0 %collective-permute-start.88 = (bf16[256,2048]{1,0:T(8,128)(2,1)}, bf16[256,2048]{1,0:T(8,128)(2,1)}, u32[]{:S(2)}, u32[]{:S(2)}) collective-permute-start(bf16[256,2048]{1,0:T(8,128)(2,1)} %get-tuple-element.562), channel_id=1, source_target_pairs={{0,2},{1,3},{2,0},{3,1},{4,6},{5,7},{6,4},{7,5},{8,10},{9,11},{10,... | collective-permute-start | bytes 3145736 | tf_op jit(solution)/shard_map/ppermute | solution.py:62
  702.4 55.9 %collective-permute-start.89 = (bf16[256,2048]{1,0:T(8,128)(2,1)}, bf16[256,2048]{1,0:T(8,128)(2,1)}, u32[]{:S(2)}, u32[]{:S(2)}) collective-permute-start(bf16[256,2048]{1,0:T(8,128)(2,1)} %get-tuple-element.576), channel_id=1, source_target_pairs={{0,2},{1,3},{2,0},{3,1},{4,6},{5,7},{6,4},{7,5},{8,10},{9,11},{10,... | collective-permute-start | bytes 3145736 | tf_op jit(solution)/shard_map/ppermute | solution.py:62
  703.2 55.1 %collective-permute-start.90 = (bf16[256,2048]{1,0:T(8,128)(2,1)}, bf16[256,2048]{1,0:T(8,128)(2,1)}, u32[]{:S(2)}, u32[]{:S(2)}) collective-permute-start(bf16[256,2048]{1,0:T(8,128)(2,1)} %get-tuple-element.577), channel_id=1, source_target_pairs={{0,4},{1,5},{2,6},{3,7},{4,0},{5,1},{6,2},{7,3},{8,12},{9,13},{10,... | collective-permute-start | bytes 3145736 | tf_op jit(solution)/shard_map/ppermute | solution.py:62
  704.5 53.8 %all-to-all-start.4 = ((bf16[8,64,1024]{2,1,0:T(8,128)(2,1)}), bf16[8,64,1024]{2,1,0:T(8,128)(2,1)}, u32[]{:S(2)}, u32[]{:S(2)}) async-start(bf16[8,64,1024]{2,1,0:T(8,128)(2,1)} %bitcast.196), calls=%async_computation.6 | async-start | bytes 2097152 | tf_op jit(solution)/shard_map/all_to_all | solution.py:1145
  708.7 156.4 %reduce-scatter.11.cloned.1.call-start = ((), (), s32[]{:S(2)}) async-start(), calls=%async_computation.18 | async-start | bytes 3932160 | tf_op jit(solution)/shard_map/reduce_scatter | solution.py:1172
  771.3 31.7 %collective-permute-start.93 = (bf16[256,2048]{1,0:T(8,128)(2,1)}, bf16[256,2048]{1,0:T(8,128)(2,1)S(1)}, u32[]{:S(2)}, u32[]{:S(2)}) collective-permute-start(bf16[256,2048]{1,0:T(8,128)(2,1)} %get-tuple-element.593), channel_id=1, source_target_pairs={{0,2},{1,3},{2,0},{3,1},{4,6},{5,7},{6,4},{7,5},{8,10},{9,11},{10,... | collective-permute-start | bytes 3145736 | tf_op jit(solution)/shard_map/ppermute | solution.py:62
  773.2 29.9 %collective-permute-start.94 = (bf16[256,2048]{1,0:T(8,128)(2,1)}, bf16[256,2048]{1,0:T(8,128)(2,1)}, u32[]{:S(2)}, u32[]{:S(2)}) collective-permute-start(bf16[256,2048]{1,0:T(8,128)(2,1)} %get-tuple-element.594), channel_id=1, source_target_pairs={{0,4},{1,5},{2,6},{3,7},{4,0},{5,1},{6,2},{7,3},{8,12},{9,13},{10,... | collective-permute-start | bytes 3145736 | tf_op jit(solution)/shard_map/ppermute | solution.py:62
  818.8 34.2 %collective-permute-start.98 = (bf16[256,2048]{1,0:T(8,128)(2,1)}, bf16[256,2048]{1,0:T(8,128)(2,1)S(1)}, u32[]{:S(2)}, u32[]{:S(2)}) collective-permute-start(bf16[256,2048]{1,0:T(8,128)(2,1)} %get-tuple-element.613), channel_id=1, source_target_pairs={{0,4},{1,5},{2,6},{3,7},{4,0},{5,1},{6,2},{7,3},{8,12},{9,13},{10,... | collective-permute-start | bytes 3145736 | tf_op jit(solution)/shard_map/ppermute | solution.py:62
  818.8 34.2 %collective-permute-start.99 = (bf16[256,2048]{1,0:T(8,128)(2,1)}, bf16[256,2048]{1,0:T(8,128)(2,1)}, u32[]{:S(2)}, u32[]{:S(2)}) collective-permute-start(bf16[256,2048]{1,0:T(8,128)(2,1)} %get-tuple-element.614), channel_id=1, source_target_pairs={{0,2},{1,3},{2,0},{3,1},{4,6},{5,7},{6,4},{7,5},{8,10},{9,11},{10,... | collective-permute-start | bytes 3145736 | tf_op jit(solution)/shard_map/ppermute | solution.py:62
  821.9 38.0 %all-to-all-start.6 = ((bf16[8,32,2048]{2,1,0:T(8,128)(2,1)}), bf16[8,32,2048]{2,1,0:T(8,128)(2,1)}, u32[]{:S(2)}, u32[]{:S(2)}) async-start(bf16[8,32,2048]{2,1,0:T(8,128)(2,1)} %bitcast.185), calls=%async_computation.10 | async-start | bytes 2097152 | tf_op jit(solution)/shard_map/all_to_all | solution.py:1221
  826.1 83.4 %reduce-scatter.9.cloned.1.call-start = ((), (), s32[]{:S(2)}) async-start(), calls=%async_computation.17 | async-start | bytes 1310720 | tf_op jit(solution)/shard_map/reduce_scatter | solution.py:1210
  856.4 26.4 %collective-permute-start.101 = (bf16[256,2048]{1,0:T(8,128)(2,1)}, bf16[256,2048]{1,0:T(8,128)(2,1)}, u32[]{:S(2)}, u32[]{:S(2)}) collective-permute-start(bf16[256,2048]{1,0:T(8,128)(2,1)} %get-tuple-element.635), channel_id=1, source_target_pairs={{0,2},{1,3},{2,0},{3,1},{4,6},{5,7},{6,4},{7,5},{8,10},{9,11},{10,... | collective-permute-start | bytes 3145736 | tf_op jit(solution)/shard_map/ppermute | solution.py:62
  858.4 26.8 %collective-permute-start.102 = (bf16[256,2048]{1,0:T(8,128)(2,1)}, bf16[256,2048]{1,0:T(8,128)(2,1)}, u32[]{:S(2)}, u32[]{:S(2)}) collective-permute-start(bf16[256,2048]{1,0:T(8,128)(2,1)} %get-tuple-element.636), channel_id=1, source_target_pairs={{0,4},{1,5},{2,6},{3,7},{4,0},{5,1},{6,2},{7,3},{8,12},{9,13},{10,... | collective-permute-start | bytes 3145736 | tf_op jit(solution)/shard_map/ppermute | solution.py:62
  859.9 25.3 %collective-permute-start.103 = (bf16[256,2048]{1,0:T(8,128)(2,1)}, bf16[256,2048]{1,0:T(8,128)(2,1)}, u32[]{:S(2)}, u32[]{:S(2)}) collective-permute-start(bf16[256,2048]{1,0:T(8,128)(2,1)} %get-tuple-element.638), channel_id=1, source_target_pairs={{0,1},{1,0},{2,3},{3,2},{4,5},{5,4},{6,7},{7,6},{8,9},{9,8},{10,11... | collective-permute-start | bytes 3145736 | tf_op jit(solution)/shard_map/ppermute | solution.py:62
  859.9 25.3 %collective-permute-start.104 = (bf16[256,2048]{1,0:T(8,128)(2,1)}, bf16[256,2048]{1,0:T(8,128)(2,1)}, u32[]{:S(2)}, u32[]{:S(2)}) collective-permute-start(bf16[256,2048]{1,0:T(8,128)(2,1)} %get-tuple-element.640), channel_id=1, source_target_pairs={{0,1},{1,0},{2,3},{3,2},{4,5},{5,4},{6,7},{7,6},{8,9},{9,8},{10,11... | collective-permute-start | bytes 3145736 | tf_op jit(solution)/shard_map/ppermute | solution.py:62
  865.1 26.8 %all-to-all-start.5 = ((bf16[8,64,768]{2,1,0:T(8,128)(2,1)}), bf16[8,64,768]{2,1,0:T(8,128)(2,1)}, u32[]{:S(2)}, u32[]{:S(2)}) async-start(bf16[8,64,768]{2,1,0:T(8,128)(2,1)} %bitcast.197), calls=%async_computation.9 | async-start | bytes 1572864 | tf_op jit(solution)/shard_map/all_to_all | solution.py:1175
  (198 other events, 1801.3 us)
Sparse Core Ops, SparseCore 0:
  29.4 62.8 all-gather.4
  94.5 96.6 all-gather.8
  279.7 78.5 all-gather.6
  543.8 74.5 reduce-scatter.4
  621.2 77.2 reduce-scatter.6
  803.2 56.5 reduce-scatter.10
  862.1 27.1 reduce-scatter.8

commit v5 on v4

--- a/solution.py
+++ b/solution.py
@@ -136,6 +136,35 @@
         ),
         name="low_sums",
     )(*[term[0] if isinstance(term, tuple) else term for term in terms])
+
+
+def finish_kernel(count, *refs):
+    other_ref, shift_ref, out_ref = refs[2 * count :]
+    for h in range(2):
+        terms = [ref[...] for ref in refs[h * count : (h + 1) * count]]
+        out_ref[h] = (total(*terms, other_ref[h]) + shift_ref[...]).astype(bf16)
+
+
+def finish(lists, others, shift):
+    half, wide = lists[0][0].shape
+    chunk = half // 2
+    rows = pl.BlockSpec((chunk, wide), lambda s: (s, 0))
+    both = pl.BlockSpec((2, chunk, wide), lambda s: (0, s, 0))
+    terms = [term for one in lists for term in one]
+    return pl.pallas_call(
+        functools.partial(finish_kernel, len(lists[0])),
+        grid=(2,),
+        in_specs=[rows] * len(terms) + [both, held(shift.shape)],
+        out_specs=both,
+        out_shape=jax.ShapeDtypeStruct((2, half, wide), bf16),
+        compiler_params=pltpu.CompilerParams(
+            dimension_semantics=("arbitrary",), vmem_limit_bytes=40 * 2**20
+        ),
+        cost_estimate=pl.CostEstimate(
+            flops=10 * half * wide, bytes_accessed=24 * half * wide, transcendentals=0
+        ),
+        name="finish",
+    )(*terms, others, shift)
 
 
 def plain_scattered_sum(groups):
@@ -1243,12 +1272,13 @@
     )
     grad_inputs = grad_inputs.reshape(tok_rows, width)
     result_terms, out_grad, others = after((result_terms, out_grad_low, kept["others"]), sums_one)
+    out_grad = out_grad.astype(f32)
     if eight:
-        result_terms = [(*result_terms[h], others[h]) for h in range(2)]
-    out_grad = out_grad.astype(f32)
-    result = jnp.concatenate(
-        [(total(*result_terms[h]) + down_shift).astype(bf16) for h in range(2)], axis=0
-    )
+        result = finish(result_terms, others, down_shift[None]).reshape(tok_rows, width)
+    else:
+        result = jnp.concatenate(
+            [(total(*result_terms[h]) + down_shift).astype(bf16) for h in range(2)], axis=0
+        )
     _, norm_summ_pull = jax.vjp(layer_norm, summ_own, gain_one, shift_one)
     grad_summ, gain_summ_grad, shift_summ_grad = norm_summ_pull(grad_normed_summ)
     summary_cols = summaries.shape[2]

time: 942 us -> 950 us (level)
  waiting for transfers between devices: 175 us -> 191 us
  other arithmetic: 35.1 us -> 23.1 us
    unnamed x297 -> x333, local copies, waits for them, and re-layouts: 53.9 us -> 59.2 us
  transfers between devices with their start and end apart: 120 -> 120, of which waited for: 43 -> 44; matrix products, arithmetic and copies ran while one was open for 17% -> 15% of each run, Pallas kernels for 43% -> 43%
where the time goes in v5:
time: 950 us
  Pallas kernels  425 us (45%)
  waiting for transfers between devices  191 us (20%)
  local copies, waits for them, and re-layouts  99.5 us (10%)
  starting transfers between devices  96.7 us (10%)
  matrix products  80 us (8%)
  other arithmetic  23.1 us (2%)
  blocking collectives  17.6 us (2%)
  between operations  17.1 us (2%)
    pallas_call x22, Pallas kernels, group_call(): pl.pallas_call(functools.partial(kernel, len(ins), len(earlier)), grid=(s...  233 us
    ppermute x105, waiting for transfers between devices, swapped(): return lax.ppermute(x, 'fsdp', [(i, i ^ bit) for i in range(devices)])  171 us
    pallas_call x2, Pallas kernels, attn_backward(): pl.pallas_call(functools.partial(attn_backward_kernel, block, half, heads...  90 us
    dot_general x6, matrix products, dot(): return lax.dot_general(left, right, dims, preferred_element_type=f32)  80 us
    ppermute x105, starting transfers between devices, swapped(): return lax.ppermute(x, 'fsdp', [(i, i ^ bit) for i in range(devices)])  65 us
    unnamed x333, local copies, waits for them, and re-layouts  59.2 us
    pallas_call x2, Pallas kernels, attn_forward(): pl.pallas_call(functools.partial(attn_forward_kernel, block, half, heads)...  54.9 us
    pallas_call x11, Pallas kernels, low_sums(): pl.pallas_call(functools.partial(low_sums_kernel, [len(one) for one in li...  22.8 us
  transfers between devices with their start and end apart: 120, of which 44 were waited for; matrix products, arithmetic and copies ran while one was open for 15% of the time, Pallas kernels for 43%

profile of v5, /device:TPU:0, one launch (start us, length us, event | category | flops | bytes accessed | tf_op | source)
XLA Modules:
  0.0 950.4 jit_solution(333888798958289464)
XLA Ops:
  11.6 17.6 %all_to_all.53 = bf16[8,64,768]{2,1,0:T(8,128)(2,1)} all-to-all(bf16[8,64,768]{2,1,0:T(8,128)(2,1)S(1)} %pad_maximum_fusion.1), channel_id=1, replica_groups=mesh['dp'=4,'fsdp'=8] {'fsdp'}, dimensions={0} | all-to-all | bytes 1572864 | tf_op jit(solution)/shard_map/all_to_all | solution.py:936
  30.2 4.0 all-to-all-start.1
  36.2 5.7 all-to-all-done.1
  45.8 21.4 %collective-permute-done.refs_0_ = bf16[256,2048]{1,0:T(8,128)(2,1)S(1)} collective-permute-done((bf16[256,2048]{1,0:T(8,128)(2,1)S(1)}, bf16[256,2048]{1,0:T(8,128)(2,1)S(1)}, u32[]{:S(2)}, u32[]{:S(2)}) %collective-permute-start) | collective-permute-done | bytes 1048608 | tf_op jit(solution)/shard_map/ppermute | solution.py:62
  73.0 2.6 reshape.484
  75.7 3.2 slice_bitcast_fusion
  79.7 5.7 norm_rows.4.refs_6_
  85.5 7.8 collective-permute-done.2.refs_0_
  100.2 6.0 norm_rows.5.refs_6_
  106.2 5.9 norm_rows.6.refs_6_
  112.2 14.5 %triple.2 = (bf16[4096,256]{1,0:T(8,128)(2,1)}, bf16[4096,256]{1,0:T(8,128)(2,1)}, bf16[4096,256]{1,0:T(8,128)(2,1)}) custom-call(bf16[4352,2048]{1,0:T(8,128)(2,1)} %bitcast.147, bf16[2048,768]{1,0:T(8,128)(2,1)} %all-gather.5.cloned.1.call-done.refs_1_.refs_6_, f32[1,768]{1,0:T(1,128)S(1)} %broadcast_in_dim.31.refs_2_), custom_call_target="tpu_custom_call" | custom-call | flops 9663676416 | bytes 12582912 | tf_op jit(solution)/shard_map/triple/pallas_call | solution.py:236
  128.3 3.8 all-to-all-start.2
  137.5 5.7 norm_rows.7
  143.2 7.6 triple.3
  155.4 27.4 %attn_forward.2 = (bf16[4096,128]{1,0:T(8,128)(2,1)S(1)}, f32[8,4096]{1,0:T(8,128)S(1)}) custom-call(s32[40]{0:T(128)S(1)} %pad_add_fusion.plan_ref, bf16[4096,256]{1,0:T(8,128)(2,1)S(1)} %copy-done.9, bf16[4096,256]{1,0:T(8,128)(2,1)S(1)} %copy-done.10, bf16[4096,256]{1,0:T(8,128)(2,1)S(1)} %copy-done.12, bf16[160,256]{1,0:T(8,128)(2,1)S(1)} %get-tuple-element.715.sk_ref, ...), custom_call_target="tpu_custom_call" | custom-call | flops 8589934592 | bytes 4194304 | tf_op jit(solution)/shard_map/attn_forward/pallas_call | solution.py:735
  183.8 3.0 collective-permute-done.14.refs_4_
  189.0 4.2 all-to-all-start.3
  197.0 27.4 %attn_forward.3 = (bf16[4096,128]{1,0:T(8,128)(2,1)S(1)}, f32[8,4096]{1,0:T(8,128)S(1)}) custom-call(s32[40]{0:T(128)S(1)} %pad_add_fusion.plan_ref, bf16[4096,256]{1,0:T(8,128)(2,1)S(1)} %copy-done.9, bf16[4096,256]{1,0:T(8,128)(2,1)S(1)} %copy-done.11, bf16[4096,256]{1,0:T(8,128)(2,1)S(1)} %copy-done.13, bf16[160,256]{1,0:T(8,128)(2,1)S(1)} %get-tuple-element.715.sk_ref, ...), custom_call_target="tpu_custom_call" | custom-call | flops 8589934592 | bytes 4194304 | tf_op jit(solution)/shard_map/attn_forward/pallas_call | solution.py:735
  227.7 4.0 project.8
  241.2 3.9 project.9
  245.1 18.1 %collective-permute-done.22 = bf16[256,2048]{1,0:T(8,128)(2,1)S(1)} collective-permute-done((bf16[256,2048]{1,0:T(8,128)(2,1)S(1)}, bf16[256,2048]{1,0:T(8,128)(2,1)S(1)}, u32[]{:S(2)}, u32[]{:S(2)}) %collective-permute-start.22) | collective-permute-done | bytes 1048608 | tf_op jit(solution)/shard_map/ppermute | solution.py:62
  273.8 3.9 project.10
  279.5 4.1 project.11
  283.6 13.6 %collective-permute-done.27.refs_2_ = bf16[256,2048]{1,0:T(8,128)(2,1)S(1)} collective-permute-done((bf16[256,2048]{1,0:T(8,128)(2,1)}, bf16[256,2048]{1,0:T(8,128)(2,1)S(1)}, u32[]{:S(2)}, u32[]{:S(2)}) %collective-permute-start.27) | collective-permute-done | bytes 1048608 | tf_op jit(solution)/shard_map/ppermute | solution.py:62
  298.4 2.9 low_sums.13
  303.0 22.7 %collective-permute-done.30 = bf16[256,2048]{1,0:T(8,128)(2,1)S(1)} collective-permute-done((bf16[256,2048]{1,0:T(8,128)(2,1)}, bf16[256,2048]{1,0:T(8,128)(2,1)S(1)}, u32[]{:S(2)}, u32[]{:S(2)}) %collective-permute-start.30) | collective-permute-done | bytes 1048608 | tf_op jit(solution)/shard_map/ppermute | solution.py:62
  327.0 5.3 fusion.24
  338.6 4.8 slice.174
  343.4 16.1 %collective-permute-done.38.refs_0_ = bf16[256,2048]{1,0:T(8,128)(2,1)S(1)} collective-permute-done((bf16[256,2048]{1,0:T(8,128)(2,1)S(1)}, bf16[256,2048]{1,0:T(8,128)(2,1)S(1)}, u32[]{:S(2)}, u32[]{:S(2)}) %collective-permute-start.38) | collective-permute-done | bytes 1048608 | tf_op jit(solution)/shard_map/ppermute | solution.py:62
  366.4 29.8 %feed_forward.4 = (bf16[16,256,1024]{2,1,0:T(8,128)(2,1)}, bf16[16,256,1024]{2,1,0:T(8,128)(2,1)}, bf16[16,256,2048]{2,1,0:T(8,128)(2,1)}, bf16[16,256,2048]{2,1...) custom-call(bf16[256,2048]{1,0:T(8,128)(2,1)} %copy-done.154, ...), custom_call_target="tpu_custom_call" | custom-call | flops 17179869184 | bytes 33554432 | tf_op jit(solution)/shard_map/feed_forward/pallas_call | solution.py:236
  402.2 30.0 %feed_forward.5 = (bf16[16,256,1024]{2,1,0:T(8,128)(2,1)}, bf16[16,256,1024]{2,1,0:T(8,128)(2,1)}, bf16[16,256,2048]{2,1,0:T(8,128)(2,1)}, bf16[16,256,2048]{2,1...) custom-call(bf16[256,2048]{1,0:T(8,128)(2,1)} %collective-permute-do, ...), custom_call_target="tpu_custom_call", output_to_operand_aliasing={{0}: (11, {}), {1}: (12, {}), {2}: (13, {}), {3}: (14, {}),... | custom-call | flops 17179869184 | bytes 33554432 | tf_op jit(solution)/shard_map/feed_forward/pallas_call | solution.py:236
  435.9 2.8 collective-permute-done.57.refs_3_
  444.9 30.1 %feed_forward.6 = (bf16[16,256,1024]{2,1,0:T(8,128)(2,1)}, bf16[16,256,1024]{2,1,0:T(8,128)(2,1)}, bf16[16,256,2048]{2,1,0:T(8,128)(2,1)}, bf16[16,256,2048]{2,1...) custom-call(bf16[256,2048]{1,0:T(8,128)(2,1)} %copy-done.100, ...), custom_call_target="tpu_custom_call", output_to_operand_aliasing={{0}: (11, {}), {1}: (12, {}), {2}: (13, {}), {3}: (14, {}),... | custom-call | flops 17179869184 | bytes 33554432 | tf_op jit(solution)/shard_map/feed_forward/pallas_call | solution.py:236
  478.2 2.8 collective-permute-done.61.refs_3_
  488.7 30.3 %feed_forward.7 = (bf16[16,256,1024]{2,1,0:T(8,128)(2,1)}, bf16[16,256,1024]{2,1,0:T(8,128)(2,1)}, bf16[16,256,2048]{2,1,0:T(8,128)(2,1)}, bf16[16,256,2048]{2,1...) custom-call(bf16[256,2048]{1,0:T(8,128)(2,1)} %copy-done.97, ...), custom_call_target="tpu_custom_call", output_to_operand_aliasing={{0}: (11, {}), {1}: (12, {}), {2}: (13, {}), {3}: (14, {}),... | custom-call | flops 17179869184 | bytes 33554432 | tf_op jit(solution)/shard_map/feed_forward/pallas_call | solution.py:236
  523.9 23.9 %convolution_convert_fusion.1 = bf16[1024,2048]{1,0:T(8,128)(2,1)} fusion(bf16[4096,1024]{1,0:T(8,128)(2,1)} %bitcast.153, bf16[4096,2048]{1,0:T(8,128)(2,1)} %bitcast.151), kind=kOutput, calls=%fused_computation.9 | convolution fusion | flops 17181966336 | bytes 29360128 | tf_op jit(solution)/shard_map/dot_general | solution.py:27
  553.3 9.8 %norm_back.2 = (f32[2,256,2048]{2,1,0:T(8,128)}, f32[8,2048]{1,0:T(8,128)S(1)}, bf16[256,2048]{1,0:T(8,128)(2,1)}, bf16[256,2048]{1,0:T(8,128)(2,1)}) custom-call(f32[256,2048]{1,0:T(8,128)S(1)} %copy-done.3, f32[256,2048]{1,0:T(8,128)} %copy-done, bf16[256,2048]{1,0:T(8,128)(2,1)S(1)} %copy-done.38, bf16[256,2048]{1,0:T(8,128)(2,1)} %collective-permute-done.68.refs_3_, ...), custom_call_target="tpu_custom_call" | custom-call | flops 41943040 | bytes 18874368 | tf_op jit(solution)/shard_map/norm_back/pallas_call | solution.py:356
  569.3 5.4 project_back.4
  574.7 23.7 %convolution_convert_fusion = bf16[2048,1024]{1,0:T(8,128)(2,1)} fusion(bf16[4096,2048]{1,0:T(8,128)(2,1)} %bitcast.150, bf16[4096,1024]{1,0:T(8,128)(2,1)} %bitcast.154), kind=kOutput, calls=%fused_computation.8 | convolution fusion | flops 17181966336 | bytes 29360128 | tf_op jit(solution)/shard_map/dot_general | solution.py:27
  598.4 13.7 %collective-permute-done.73.refs_0_ = bf16[256,2048]{1,0:T(8,128)(2,1)} collective-permute-done((bf16[256,2048]{1,0:T(8,128)(2,1)}, bf16[256,2048]{1,0:T(8,128)(2,1)}, u32[]{:S(2)}, u32[]{:S(2)}) %collective-permute-start.73) | collective-permute-done | bytes 1048608 | tf_op jit(solution)/shard_map/ppermute | solution.py:62
  618.1 4.0 low_sums.17
  623.1 5.4 project_back.5
  629.8 6.2 project_back.6
  636.0 3.2 collective-permute-done.77.refs_0_
  649.4 5.3 project_back.7
  657.0 44.9 %attn_backward.2 = (bf16[4096,128]{1,0:T(8,128)(2,1)S(1)}, bf16[4096,128]{1,0:T(8,128)(2,1)S(1)}, bf16[4096,128]{1,0:T(8,128)(2,1)S(1)}, bf16[160,128]{1,0:T(8,1...) custom-call(s32[40]{0:T(128)S(1)} %copy-done.78, bf16[4096,256]{1,0:T(8,128)(2,1)} %get-tuple-element.369.q_ref, ...), custom_call_target="tpu_custom_call" | custom-call | flops 12884901888 | bytes 10485760 | tf_op jit(solution)/shard_map/attn_backward/pallas_call | solution.py:776
  702.0 4.9 low_sums.18
  708.8 4.2 all-to-all-start.4
  714.3 45.1 %attn_backward.3 = (bf16[4096,128]{1,0:T(8,128)(2,1)S(1)}, bf16[4096,128]{1,0:T(8,128)(2,1)S(1)}, bf16[4096,128]{1,0:T(8,128)(2,1)S(1)}, bf16[160,128]{1,0:T(8,1...) custom-call(s32[40]{0:T(128)S(1)} %copy-done.78, bf16[4096,256]{1,0:T(8,128)(2,1)} %get-tuple-element.369.q_ref, ...), custom_call_target="tpu_custom_call" | custom-call | flops 12884901888 | bytes 10485760 | tf_op jit(solution)/shard_map/attn_backward/pallas_call | solution.py:776
  762.5 7.8 project.12
  782.7 19.7 %fusion.7 = bf16[2048,768]{1,0:T(8,128)(2,1)} fusion(bf16[4352,2048]{1,0:T(8,128)(2,1)} %pad_dynamic-update-slice_fusion, bf16[160,512]{1,0:T(8,128)(2,1)S(1)} %constant_dynamic-update-slice_fusion, bf16[4096,768]{1,0:T(8,128)(2,1)S(1)} %constant_dynamic-update-slice_fusion.4), kind=kOutput, calls=%fused_computation.10 | convolution fusion | flops 13711835136 | bytes 27426816 | tf_op jit(solution)/shard_map/dot_general | solution.py:27
  803.2 7.4 project.13
  818.9 7.1 project.14
  827.0 9.5 %convolution_convert_fusion.2 = bf16[256,2048]{1,0:T(8,128)(2,1)} fusion(bf16[4096,2048]{1,0:T(8,128)(2,1)} %bitcast.152, bf16[4096,128]{1,0:T(8,128)(2,1)S(1)} %copy-done.84, bf16[4096,128]{1,0:T(8,128)(2,1)S(1)} %copy-done.81), kind=kOutput, calls=%fused_computation.14 | convolution fusion | flops 4299685888 | bytes 19922944 | tf_op jit(solution)/shard_map/dot_general | solution.py:27
  840.5 4.2 all-to-all-start.6
  848.1 7.2 project.15
  855.3 3.2 low_sums.21
  864.2 4.2 all-to-all-start.5
  877.0 7.9 collective-permute-done.101.refs_5_
  886.9 7.2 all-to-all-done.5.parts_ref
  897.8 8.5 norm_back.3
  914.6 7.0 all-to-all-done.8
  921.6 3.4 all-to-all-start.7
  937.7 3.5 finish.1
  (691 shorter events, 226.6 us)
Async XLA Ops:
  7.2 105.0 %all-gather.5.cloned.1.call-start = ((), (), s32[]{:S(2)}) async-start(), calls=%async_computation.13 | async-start | bytes 3932160 | tf_op jit(solution)/shard_map/all_gather | solution.py:937
  34.2 191.2 %all-gather.9.cloned.1.call-start = ((), (), s32[]{:S(2)}) async-start(), calls=%async_computation.19 | async-start | bytes 6553600 | tf_op jit(solution)/shard_map/all_gather | solution.py:993
  42.0 25.2 %collective-permute-start = (bf16[256,2048]{1,0:T(8,128)(2,1)S(1)}, bf16[256,2048]{1,0:T(8,128)(2,1)S(1)}, u32[]{:S(2)}, u32[]{:S(2)}) collective-permute-start(bf16[256,2048]{1,0:T(8,128)(2,1)S(1)} %get-tuple-element.351.refs_0_), channel_id=1, source_target_pairs={{0,2},{1,3},{2,0},{3,1},{4,6},{5,7},{6,4},{7,5},{8,10},{9,11},{10,... | collective-permute-start | bytes 3145736 | tf_op jit(solution)/shard_map/ppermute | solution.py:62
  42.4 25.1 %collective-permute-start.1 = (bf16[256,2048]{1,0:T(8,128)(2,1)S(1)}, bf16[256,2048]{1,0:T(8,128)(2,1)}, u32[]{:S(2)}, u32[]{:S(2)}) collective-permute-start(bf16[256,2048]{1,0:T(8,128)(2,1)S(1)} %get-tuple-element.352.refs_1_), channel_id=1, source_target_pairs={{0,4},{1,5},{2,6},{3,7},{4,0},{5,1},{6,2},{7,3},{8,12},{9,13},{10,... | collective-permute-start | bytes 3145736 | tf_op jit(solution)/shard_map/ppermute | solution.py:62
  68.0 25.2 %collective-permute-start.2 = (bf16[256,2048]{1,0:T(8,128)(2,1)S(1)}, bf16[256,2048]{1,0:T(8,128)(2,1)}, u32[]{:S(2)}, u32[]{:S(2)}) collective-permute-start(bf16[256,2048]{1,0:T(8,128)(2,1)S(1)} %get-tuple-element.352.refs_1_), channel_id=1, source_target_pairs={{0,2},{1,3},{2,0},{3,1},{4,6},{5,7},{6,4},{7,5},{8,10},{9,11},{10,... | collective-permute-start | bytes 3145736 | tf_op jit(solution)/shard_map/ppermute | solution.py:62
  69.7 25.0 %collective-permute-start.3 = (bf16[256,2048]{1,0:T(8,128)(2,1)S(1)}, bf16[256,2048]{1,0:T(8,128)(2,1)}, u32[]{:S(2)}, u32[]{:S(2)}) collective-permute-start(bf16[256,2048]{1,0:T(8,128)(2,1)S(1)} %get-tuple-element.351.refs_0_), channel_id=1, source_target_pairs={{0,4},{1,5},{2,6},{3,7},{4,0},{5,1},{6,2},{7,3},{8,12},{9,13},{10,... | collective-permute-start | bytes 3145736 | tf_op jit(solution)/shard_map/ppermute | solution.py:62
  96.0 30.6 %collective-permute-start.6 = (bf16[256,2048]{1,0:T(8,128)(2,1)S(1)}, bf16[256,2048]{1,0:T(8,128)(2,1)S(1)}, u32[]{:S(2)}, u32[]{:S(2)}) collective-permute-start(bf16[256,2048]{1,0:T(8,128)(2,1)S(1)} %collective-permute-done.refs_0_), channel_id=1, source_target_pairs={{0,4},{1,5},{2,6},{3,7},{4,0},{5,1},{6,2},{7,3},{8,12},{9,13},{10,... | collective-permute-start | bytes 3145736 | tf_op jit(solution)/shard_map/ppermute | solution.py:62
  98.8 27.9 %collective-permute-start.7 = (bf16[256,2048]{1,0:T(8,128)(2,1)}, bf16[256,2048]{1,0:T(8,128)(2,1)}, u32[]{:S(2)}, u32[]{:S(2)}) collective-permute-start(bf16[256,2048]{1,0:T(8,128)(2,1)} %collective-permute-done.1.refs_2_), channel_id=1, source_target_pairs={{0,2},{1,3},{2,0},{3,1},{4,6},{5,7},{6,4},{7,5},{8,10},{9,11},{10,... | collective-permute-start | bytes 3145736 | tf_op jit(solution)/shard_map/ppermute | solution.py:62
  133.3 53.6 %collective-permute-start.15 = (bf16[256,2048]{1,0:T(8,128)(2,1)}, bf16[256,2048]{1,0:T(8,128)(2,1)}, u32[]{:S(2)}, u32[]{:S(2)}) collective-permute-start(bf16[256,2048]{1,0:T(8,128)(2,1)} %get-tuple-element.376.refs_5_), channel_id=1, source_target_pairs={{0,4},{1,5},{2,6},{3,7},{4,0},{5,1},{6,2},{7,3},{8,12},{9,13},{10,... | collective-permute-start | bytes 3145736 | tf_op jit(solution)/shard_map/ppermute | solution.py:62
  135.4 51.5 %collective-permute-start.16 = (bf16[256,2048]{1,0:T(8,128)(2,1)}, bf16[256,2048]{1,0:T(8,128)(2,1)}, u32[]{:S(2)}, u32[]{:S(2)}) collective-permute-start(bf16[256,2048]{1,0:T(8,128)(2,1)} %get-tuple-element.376.refs_5_), channel_id=1, source_target_pairs={{0,2},{1,3},{2,0},{3,1},{4,6},{5,7},{6,4},{7,5},{8,10},{9,11},{10,... | collective-permute-start | bytes 3145736 | tf_op jit(solution)/shard_map/ppermute | solution.py:62
  136.8 50.0 %collective-permute-start.14 = (bf16[256,2048]{1,0:T(8,128)(2,1)}, bf16[256,2048]{1,0:T(8,128)(2,1)}, u32[]{:S(2)}, u32[]{:S(2)}) collective-permute-start(bf16[256,2048]{1,0:T(8,128)(2,1)} %get-tuple-element.375.refs_4_), channel_id=1, source_target_pairs={{0,2},{1,3},{2,0},{3,1},{4,6},{5,7},{6,4},{7,5},{8,10},{9,11},{10,... | collective-permute-start | bytes 3145736 | tf_op jit(solution)/shard_map/ppermute | solution.py:62
  137.4 49.5 %collective-permute-start.17 = (bf16[256,2048]{1,0:T(8,128)(2,1)}, bf16[256,2048]{1,0:T(8,128)(2,1)}, u32[]{:S(2)}, u32[]{:S(2)}) collective-permute-start(bf16[256,2048]{1,0:T(8,128)(2,1)} %get-tuple-element.375.refs_4_), channel_id=1, source_target_pairs={{0,4},{1,5},{2,6},{3,7},{4,0},{5,1},{6,2},{7,3},{8,12},{9,13},{10,... | collective-permute-start | bytes 3145736 | tf_op jit(solution)/shard_map/ppermute | solution.py:62
  186.9 40.8 %collective-permute-start.18 = (bf16[256,2048]{1,0:T(8,128)(2,1)}, bf16[256,2048]{1,0:T(8,128)(2,1)}, u32[]{:S(2)}, u32[]{:S(2)}) collective-permute-start(bf16[256,2048]{1,0:T(8,128)(2,1)} %collective-permute-done.14.refs_4_), channel_id=1, source_target_pairs={{0,4},{1,5},{2,6},{3,7},{4,0},{5,1},{6,2},{7,3},{8,12},{9,13},{10,... | collective-permute-start | bytes 3145736 | tf_op jit(solution)/shard_map/ppermute | solution.py:62
  188.5 39.3 %collective-permute-start.19 = (bf16[256,2048]{1,0:T(8,128)(2,1)}, bf16[256,2048]{1,0:T(8,128)(2,1)}, u32[]{:S(2)}, u32[]{:S(2)}) collective-permute-start(bf16[256,2048]{1,0:T(8,128)(2,1)} %collective-permute-done.15.refs_6_), channel_id=1, source_target_pairs={{0,2},{1,3},{2,0},{3,1},{4,6},{5,7},{6,4},{7,5},{8,10},{9,11},{10,... | collective-permute-start | bytes 3145736 | tf_op jit(solution)/shard_map/ppermute | solution.py:62
  189.0 38.7 %all-to-all-start.3 = ((bf16[8,64,1024]{2,1,0:T(8,128)(2,1)}), bf16[8,64,1024]{2,1,0:T(8,128)(2,1)}, u32[]{:S(2)}, u32[]{:S(2)}) async-start(bf16[8,64,1024]{2,1,0:T(8,128)(2,1)} %reshape.484), calls=%async_computation.3 | async-start | bytes 2097152 | tf_op jit(solution)/shard_map/all_to_all | solution.py:1002
  193.3 173.2 %all-gather.7.cloned.1.call-start = ((), (), s32[]{:S(2)}) async-start(), calls=%async_computation.14 | async-start | bytes 5242880 | tf_op jit(solution)/shard_map/all_gather | solution.py:1051
  237.8 25.5 %collective-permute-start.22 = (bf16[256,2048]{1,0:T(8,128)(2,1)S(1)}, bf16[256,2048]{1,0:T(8,128)(2,1)S(1)}, u32[]{:S(2)}, u32[]{:S(2)}) collective-permute-start(bf16[256,2048]{1,0:T(8,128)(2,1)S(1)} %get-tuple-element.391), channel_id=1, source_target_pairs={{0,2},{1,3},{2,0},{3,1},{4,6},{5,7},{6,4},{7,5},{8,10},{9,11},{10,... | collective-permute-start | bytes 3145736 | tf_op jit(solution)/shard_map/ppermute | solution.py:62
  239.7 24.9 %collective-permute-start.23 = (bf16[256,2048]{1,0:T(8,128)(2,1)S(1)}, bf16[256,2048]{1,0:T(8,128)(2,1)S(1)}, u32[]{:S(2)}, u32[]{:S(2)}) collective-permute-start(bf16[256,2048]{1,0:T(8,128)(2,1)S(1)} %get-tuple-element.392), channel_id=1, source_target_pairs={{0,4},{1,5},{2,6},{3,7},{4,0},{5,1},{6,2},{7,3},{8,12},{9,13},{10,... | collective-permute-start | bytes 3145736 | tf_op jit(solution)/shard_map/ppermute | solution.py:62
  271.8 25.4 %collective-permute-start.27 = (bf16[256,2048]{1,0:T(8,128)(2,1)}, bf16[256,2048]{1,0:T(8,128)(2,1)S(1)}, u32[]{:S(2)}, u32[]{:S(2)}) collective-permute-start(bf16[256,2048]{1,0:T(8,128)(2,1)} %get-tuple-element.402), channel_id=1, source_target_pairs={{0,4},{1,5},{2,6},{3,7},{4,0},{5,1},{6,2},{7,3},{8,12},{9,13},{10,... | collective-permute-start | bytes 3145736 | tf_op jit(solution)/shard_map/ppermute | solution.py:62
  273.3 25.1 %collective-permute-start.28 = (bf16[256,2048]{1,0:T(8,128)(2,1)}, bf16[256,2048]{1,0:T(8,128)(2,1)S(1)}, u32[]{:S(2)}, u32[]{:S(2)}) collective-permute-start(bf16[256,2048]{1,0:T(8,128)(2,1)} %get-tuple-element.403), channel_id=1, source_target_pairs={{0,2},{1,3},{2,0},{3,1},{4,6},{5,7},{6,4},{7,5},{8,10},{9,11},{10,... | collective-permute-start | bytes 3145736 | tf_op jit(solution)/shard_map/ppermute | solution.py:62
  279.3 375.5 %reduce-scatter.5.cloned.1.call-start = ((), (), s32[]{:S(2)}) async-start(), calls=%async_computation.15 | async-start | bytes 5242880 | tf_op jit(solution)/shard_map/reduce_scatter | solution.py:1111
  302.2 24.8 %collective-permute-start.33 = (bf16[256,2048]{1,0:T(8,128)(2,1)}, bf16[256,2048]{1,0:T(8,128)(2,1)}, u32[]{:S(2)}, u32[]{:S(2)}) collective-permute-start(bf16[256,2048]{1,0:T(8,128)(2,1)} %get-tuple-element.422), channel_id=1, source_target_pairs={{0,1},{1,0},{2,3},{3,2},{4,5},{5,4},{6,7},{7,6},{8,9},{9,8},{10,11... | collective-permute-start | bytes 3145736 | tf_op jit(solution)/shard_map/ppermute | solution.py:62
  361.1 37.5 %collective-permute-start.54 = (bf16[256,2048]{1,0:T(8,128)(2,1)}, bf16[256,2048]{1,0:T(8,128)(2,1)S(1)}, u32[]{:S(2)}, u32[]{:S(2)}) collective-permute-start(bf16[256,2048]{1,0:T(8,128)(2,1)} %collective-permute-done.16.refs_4_), channel_id=1, source_target_pairs={{0,1},{1,0},{2,3},{3,2},{4,5},{5,4},{6,7},{7,6},{8,9},{9,8},{10,11... | collective-permute-start | bytes 3145736 | tf_op jit(solution)/shard_map/ppermute | solution.py:62
  361.2 38.3 %collective-permute-start.55 = (bf16[256,2048]{1,0:T(8,128)(2,1)}, bf16[256,2048]{1,0:T(8,128)(2,1)}, u32[]{:S(2)}, u32[]{:S(2)}) collective-permute-start(bf16[256,2048]{1,0:T(8,128)(2,1)} %collective-permute-done.17.refs_6_), channel_id=1, source_target_pairs={{0,1},{1,0},{2,3},{3,2},{4,5},{5,4},{6,7},{7,6},{8,9},{9,8},{10,11... | collective-permute-start | bytes 3145736 | tf_op jit(solution)/shard_map/ppermute | solution.py:62
  361.7 35.1 %collective-permute-start.46 = (bf16[256,2048]{1,0:T(8,128)(2,1)}, bf16[256,2048]{1,0:T(8,128)(2,1)}, u32[]{:S(2)}, u32[]{:S(2)}) collective-permute-start(bf16[256,2048]{1,0:T(8,128)(2,1)} %get-tuple-element.724.refs_1_), channel_id=1, source_target_pairs={{0,2},{1,3},{2,0},{3,1},{4,6},{5,7},{6,4},{7,5},{8,10},{9,11},{10,... | collective-permute-start | bytes 3145736 | tf_op jit(solution)/shard_map/ppermute | solution.py:62
  365.7 31.1 %collective-permute-start.47 = (bf16[256,2048]{1,0:T(8,128)(2,1)S(1)}, bf16[256,2048]{1,0:T(8,128)(2,1)}, u32[]{:S(2)}, u32[]{:S(2)}) collective-permute-start(bf16[256,2048]{1,0:T(8,128)(2,1)S(1)} %get-tuple-element.725.refs_0_), channel_id=1, source_target_pairs={{0,4},{1,5},{2,6},{3,7},{4,0},{5,1},{6,2},{7,3},{8,12},{9,13},{10,... | collective-permute-start | bytes 3145736 | tf_op jit(solution)/shard_map/ppermute | solution.py:62
  397.4 36.2 %collective-permute-start.40 = (bf16[256,2048]{1,0:T(8,128)(2,1)S(1)}, bf16[256,2048]{1,0:T(8,128)(2,1)S(1)}, u32[]{:S(2)}, u32[]{:S(2)}) collective-permute-start(bf16[256,2048]{1,0:T(8,128)(2,1)S(1)} %copy-done.155), channel_id=1, source_target_pairs={{0,4},{1,5},{2,6},{3,7},{4,0},{5,1},{6,2},{7,3},{8,12},{9,13},{10,... | collective-permute-start | bytes 3145736 | tf_op jit(solution)/shard_map/ppermute | solution.py:62
  398.7 35.2 %collective-permute-start.41 = (bf16[256,2048]{1,0:T(8,128)(2,1)}, bf16[256,2048]{1,0:T(8,128)(2,1)S(1)}, u32[]{:S(2)}, u32[]{:S(2)}) collective-permute-start(bf16[256,2048]{1,0:T(8,128)(2,1)} %collective-permute-done.39.refs_2_), channel_id=1, source_target_pairs={{0,2},{1,3},{2,0},{3,1},{4,6},{5,7},{6,4},{7,5},{8,10},{9,11},{10,... | collective-permute-start | bytes 3145736 | tf_op jit(solution)/shard_map/ppermute | solution.py:62
  440.5 34.6 %collective-permute-start.58 = (bf16[256,2048]{1,0:T(8,128)(2,1)S(1)}, bf16[256,2048]{1,0:T(8,128)(2,1)S(1)}, u32[]{:S(2)}, u32[]{:S(2)}) collective-permute-start(bf16[256,2048]{1,0:T(8,128)(2,1)S(1)} %get-tuple-element.453), channel_id=1, source_target_pairs={{0,2},{1,3},{2,0},{3,1},{4,6},{5,7},{6,4},{7,5},{8,10},{9,11},{10,... | collective-permute-start | bytes 3145736 | tf_op jit(solution)/shard_map/ppermute | solution.py:62
  441.7 33.3 %collective-permute-start.59 = (bf16[256,2048]{1,0:T(8,128)(2,1)S(1)}, bf16[256,2048]{1,0:T(8,128)(2,1)S(1)}, u32[]{:S(2)}, u32[]{:S(2)}) collective-permute-start(bf16[256,2048]{1,0:T(8,128)(2,1)S(1)} %get-tuple-element.454), channel_id=1, source_target_pairs={{0,4},{1,5},{2,6},{3,7},{4,0},{5,1},{6,2},{7,3},{8,12},{9,13},{10,... | collective-permute-start | bytes 3145736 | tf_op jit(solution)/shard_map/ppermute | solution.py:62
  481.0 38.0 %collective-permute-start.62 = (bf16[256,2048]{1,0:T(8,128)(2,1)}, bf16[256,2048]{1,0:T(8,128)(2,1)S(1)}, u32[]{:S(2)}, u32[]{:S(2)}) collective-permute-start(bf16[256,2048]{1,0:T(8,128)(2,1)} %get-tuple-element.485), channel_id=1, source_target_pairs={{0,1},{1,0},{2,3},{3,2},{4,5},{5,4},{6,7},{7,6},{8,9},{9,8},{10,11... | collective-permute-start | bytes 3145736 | tf_op jit(solution)/shard_map/ppermute | solution.py:62
  483.0 36.1 %collective-permute-start.65 = (bf16[256,2048]{1,0:T(8,128)(2,1)}, bf16[256,2048]{1,0:T(8,128)(2,1)S(1)}, u32[]{:S(2)}, u32[]{:S(2)}) collective-permute-start(bf16[256,2048]{1,0:T(8,128)(2,1)} %get-tuple-element.492), channel_id=1, source_target_pairs={{0,1},{1,0},{2,3},{3,2},{4,5},{5,4},{6,7},{7,6},{8,9},{9,8},{10,11... | collective-permute-start | bytes 3145736 | tf_op jit(solution)/shard_map/ppermute | solution.py:62
  483.8 35.2 %collective-permute-start.63 = (bf16[256,2048]{1,0:T(8,128)(2,1)S(1)}, bf16[256,2048]{1,0:T(8,128)(2,1)S(1)}, u32[]{:S(2)}, u32[]{:S(2)}) collective-permute-start(bf16[256,2048]{1,0:T(8,128)(2,1)S(1)} %get-tuple-element.469), channel_id=1, source_target_pairs={{0,4},{1,5},{2,6},{3,7},{4,0},{5,1},{6,2},{7,3},{8,12},{9,13},{10,... | collective-permute-start | bytes 3145736 | tf_op jit(solution)/shard_map/ppermute | solution.py:62
  486.8 32.2 %collective-permute-start.64 = (bf16[256,2048]{1,0:T(8,128)(2,1)S(1)}, bf16[256,2048]{1,0:T(8,128)(2,1)S(1)}, u32[]{:S(2)}, u32[]{:S(2)}) collective-permute-start(bf16[256,2048]{1,0:T(8,128)(2,1)S(1)} %get-tuple-element.470), channel_id=1, source_target_pairs={{0,2},{1,3},{2,0},{3,1},{4,6},{5,7},{6,4},{7,5},{8,10},{9,11},{10,... | collective-permute-start | bytes 3145736 | tf_op jit(solution)/shard_map/ppermute | solution.py:62
  520.8 26.9 %collective-permute-start.70 = (bf16[8,256,2048]{2,1,0:T(8,128)(2,1)}, bf16[8,256,2048]{2,1,0:T(8,128)(2,1)}, u32[]{:S(2)}, u32[]{:S(2)}) collective-permute-start(bf16[8,256,2048]{2,1,0:T(8,128)(2,1)} %get-tuple-element.506), channel_id=1, source_target_pairs={{0,1},{1,0},{2,3},{3,2},{4,5},{5,4},{6,7},{7,6},{8,9},{9,8},{10,11... | collective-permute-start | bytes 25165832 | tf_op jit(solution)/shard_map/ppermute | solution.py:62
  520.9 26.9 %collective-permute-start.66 = (bf16[256,2048]{1,0:T(8,128)(2,1)}, bf16[256,2048]{1,0:T(8,128)(2,1)}, u32[]{:S(2)}, u32[]{:S(2)}) collective-permute-start(bf16[256,2048]{1,0:T(8,128)(2,1)} %get-tuple-element.494), channel_id=1, source_target_pairs={{0,2},{1,3},{2,0},{3,1},{4,6},{5,7},{6,4},{7,5},{8,10},{9,11},{10,... | collective-permute-start | bytes 3145736 | tf_op jit(solution)/shard_map/ppermute | solution.py:62
  522.0 25.7 %collective-permute-start.67 = (bf16[256,2048]{1,0:T(8,128)(2,1)}, bf16[256,2048]{1,0:T(8,128)(2,1)}, u32[]{:S(2)}, u32[]{:S(2)}) collective-permute-start(bf16[256,2048]{1,0:T(8,128)(2,1)} %get-tuple-element.495), channel_id=1, source_target_pairs={{0,4},{1,5},{2,6},{3,7},{4,0},{5,1},{6,2},{7,3},{8,12},{9,13},{10,... | collective-permute-start | bytes 3145736 | tf_op jit(solution)/shard_map/ppermute | solution.py:62
  523.4 24.4 %collective-permute-start.68 = (bf16[256,2048]{1,0:T(8,128)(2,1)}, bf16[256,2048]{1,0:T(8,128)(2,1)}, u32[]{:S(2)}, u32[]{:S(2)}) collective-permute-start(bf16[256,2048]{1,0:T(8,128)(2,1)} %get-tuple-element.497), channel_id=1, source_target_pairs={{0,1},{1,0},{2,3},{3,2},{4,5},{5,4},{6,7},{7,6},{8,9},{9,8},{10,11... | collective-permute-start | bytes 3145736 | tf_op jit(solution)/shard_map/ppermute | solution.py:62
  523.4 24.4 %collective-permute-start.69 = (bf16[256,2048]{1,0:T(8,128)(2,1)}, bf16[256,2048]{1,0:T(8,128)(2,1)}, u32[]{:S(2)}, u32[]{:S(2)}) collective-permute-start(bf16[256,2048]{1,0:T(8,128)(2,1)} %get-tuple-element.500), channel_id=1, source_target_pairs={{0,1},{1,0},{2,3},{3,2},{4,5},{5,4},{6,7},{7,6},{8,9},{9,8},{10,11... | collective-permute-start | bytes 3145736 | tf_op jit(solution)/shard_map/ppermute | solution.py:62
  547.8 161.0 %reduce-scatter.7.cloned.1.call-start = ((), (), s32[]{:S(2)}) async-start(), calls=%async_computation.16 | async-start | bytes 5242880 | tf_op jit(solution)/shard_map/reduce_scatter | solution.py:1144
  564.3 34.1 %collective-permute-start.71 = (bf16[256,2048]{1,0:T(8,128)(2,1)}, bf16[256,2048]{1,0:T(8,128)(2,1)}, u32[]{:S(2)}, u32[]{:S(2)}) collective-permute-start(bf16[256,2048]{1,0:T(8,128)(2,1)} %get-tuple-element.515.refs_0_), channel_id=1, source_target_pairs={{0,2},{1,3},{2,0},{3,1},{4,6},{5,7},{6,4},{7,5},{8,10},{9,11},{10,... | collective-permute-start | bytes 3145736 | tf_op jit(solution)/shard_map/ppermute | solution.py:62
  565.1 33.3 %collective-permute-start.72 = (bf16[256,2048]{1,0:T(8,128)(2,1)}, bf16[256,2048]{1,0:T(8,128)(2,1)}, u32[]{:S(2)}, u32[]{:S(2)}) collective-permute-start(bf16[256,2048]{1,0:T(8,128)(2,1)} %get-tuple-element.516.refs_1_), channel_id=1, source_target_pairs={{0,4},{1,5},{2,6},{3,7},{4,0},{5,1},{6,2},{7,3},{8,12},{9,13},{10,... | collective-permute-start | bytes 3145736 | tf_op jit(solution)/shard_map/ppermute | solution.py:62
  565.8 46.3 %collective-permute-start.73 = (bf16[256,2048]{1,0:T(8,128)(2,1)}, bf16[256,2048]{1,0:T(8,128)(2,1)}, u32[]{:S(2)}, u32[]{:S(2)}) collective-permute-start(bf16[256,2048]{1,0:T(8,128)(2,1)} %get-tuple-element.516.refs_1_), channel_id=1, source_target_pairs={{0,2},{1,3},{2,0},{3,1},{4,6},{5,7},{6,4},{7,5},{8,10},{9,11},{10,... | collective-permute-start | bytes 3145736 | tf_op jit(solution)/shard_map/ppermute | solution.py:62
  567.0 45.7 %collective-permute-start.74 = (bf16[256,2048]{1,0:T(8,128)(2,1)}, bf16[256,2048]{1,0:T(8,128)(2,1)}, u32[]{:S(2)}, u32[]{:S(2)}) collective-permute-start(bf16[256,2048]{1,0:T(8,128)(2,1)} %get-tuple-element.515.refs_0_), channel_id=1, source_target_pairs={{0,4},{1,5},{2,6},{3,7},{4,0},{5,1},{6,2},{7,3},{8,12},{9,13},{10,... | collective-permute-start | bytes 3145736 | tf_op jit(solution)/shard_map/ppermute | solution.py:62
  613.9 25.4 %collective-permute-start.77 = (bf16[256,2048]{1,0:T(8,128)(2,1)}, bf16[256,2048]{1,0:T(8,128)(2,1)S(1)}, u32[]{:S(2)}, u32[]{:S(2)}) collective-permute-start(bf16[256,2048]{1,0:T(8,128)(2,1)} %collective-permute-done.71.refs_0_), channel_id=1, source_target_pairs={{0,4},{1,5},{2,6},{3,7},{4,0},{5,1},{6,2},{7,3},{8,12},{9,13},{10,... | collective-permute-start | bytes 3145736 | tf_op jit(solution)/shard_map/ppermute | solution.py:62
  615.7 25.4 %collective-permute-start.78 = (bf16[256,2048]{1,0:T(8,128)(2,1)}, bf16[256,2048]{1,0:T(8,128)(2,1)S(1)}, u32[]{:S(2)}, u32[]{:S(2)}) collective-permute-start(bf16[256,2048]{1,0:T(8,128)(2,1)} %collective-permute-done.72.refs_2_), channel_id=1, source_target_pairs={{0,2},{1,3},{2,0},{3,1},{4,6},{5,7},{6,4},{7,5},{8,10},{9,11},{10,... | collective-permute-start | bytes 3145736 | tf_op jit(solution)/shard_map/ppermute | solution.py:62
  645.4 56.5 %collective-permute-start.85 = (bf16[256,2048]{1,0:T(8,128)(2,1)}, bf16[256,2048]{1,0:T(8,128)(2,1)S(1)}, u32[]{:S(2)}, u32[]{:S(2)}) collective-permute-start(bf16[256,2048]{1,0:T(8,128)(2,1)} %get-tuple-element.559), channel_id=1, source_target_pairs={{0,2},{1,3},{2,0},{3,1},{4,6},{5,7},{6,4},{7,5},{8,10},{9,11},{10,... | collective-permute-start | bytes 3145736 | tf_op jit(solution)/shard_map/ppermute | solution.py:62
  646.5 55.4 %collective-permute-start.86 = (bf16[256,2048]{1,0:T(8,128)(2,1)}, bf16[256,2048]{1,0:T(8,128)(2,1)S(1)}, u32[]{:S(2)}, u32[]{:S(2)}) collective-permute-start(bf16[256,2048]{1,0:T(8,128)(2,1)} %get-tuple-element.560), channel_id=1, source_target_pairs={{0,4},{1,5},{2,6},{3,7},{4,0},{5,1},{6,2},{7,3},{8,12},{9,13},{10,... | collective-permute-start | bytes 3145736 | tf_op jit(solution)/shard_map/ppermute | solution.py:62
  647.2 54.7 %collective-permute-start.87 = (bf16[256,2048]{1,0:T(8,128)(2,1)}, bf16[256,2048]{1,0:T(8,128)(2,1)S(1)}, u32[]{:S(2)}, u32[]{:S(2)}) collective-permute-start(bf16[256,2048]{1,0:T(8,128)(2,1)} %get-tuple-element.561), channel_id=1, source_target_pairs={{0,4},{1,5},{2,6},{3,7},{4,0},{5,1},{6,2},{7,3},{8,12},{9,13},{10,... | collective-permute-start | bytes 3145736 | tf_op jit(solution)/shard_map/ppermute | solution.py:62
  648.5 53.4 %collective-permute-start.88 = (bf16[256,2048]{1,0:T(8,128)(2,1)}, bf16[256,2048]{1,0:T(8,128)(2,1)}, u32[]{:S(2)}, u32[]{:S(2)}) collective-permute-start(bf16[256,2048]{1,0:T(8,128)(2,1)} %get-tuple-element.562), channel_id=1, source_target_pairs={{0,2},{1,3},{2,0},{3,1},{4,6},{5,7},{6,4},{7,5},{8,10},{9,11},{10,... | collective-permute-start | bytes 3145736 | tf_op jit(solution)/shard_map/ppermute | solution.py:62
  706.9 55.5 %collective-permute-start.89 = (bf16[256,2048]{1,0:T(8,128)(2,1)}, bf16[256,2048]{1,0:T(8,128)(2,1)S(1)}, u32[]{:S(2)}, u32[]{:S(2)}) collective-permute-start(bf16[256,2048]{1,0:T(8,128)(2,1)} %get-tuple-element.576), channel_id=1, source_target_pairs={{0,2},{1,3},{2,0},{3,1},{4,6},{5,7},{6,4},{7,5},{8,10},{9,11},{10,... | collective-permute-start | bytes 3145736 | tf_op jit(solution)/shard_map/ppermute | solution.py:62
  708.1 54.2 %collective-permute-start.90 = (bf16[256,2048]{1,0:T(8,128)(2,1)}, bf16[256,2048]{1,0:T(8,128)(2,1)S(1)}, u32[]{:S(2)}, u32[]{:S(2)}) collective-permute-start(bf16[256,2048]{1,0:T(8,128)(2,1)} %get-tuple-element.577), channel_id=1, source_target_pairs={{0,4},{1,5},{2,6},{3,7},{4,0},{5,1},{6,2},{7,3},{8,12},{9,13},{10,... | collective-permute-start | bytes 3145736 | tf_op jit(solution)/shard_map/ppermute | solution.py:62
  708.8 53.6 %all-to-all-start.4 = ((bf16[8,64,1024]{2,1,0:T(8,128)(2,1)}), bf16[8,64,1024]{2,1,0:T(8,128)(2,1)}, u32[]{:S(2)}, u32[]{:S(2)}) async-start(bf16[8,64,1024]{2,1,0:T(8,128)(2,1)} %bitcast.190), calls=%async_computation.6 | async-start | bytes 2097152 | tf_op jit(solution)/shard_map/all_to_all | solution.py:1174
  713.1 151.1 %reduce-scatter.11.cloned.1.call-start = ((), (), s32[]{:S(2)}) async-start(), calls=%async_computation.18 | async-start | bytes 3932160 | tf_op jit(solution)/shard_map/reduce_scatter | solution.py:1201
  776.2 26.2 %collective-permute-start.93 = (bf16[256,2048]{1,0:T(8,128)(2,1)}, bf16[256,2048]{1,0:T(8,128)(2,1)S(1)}, u32[]{:S(2)}, u32[]{:S(2)}) collective-permute-start(bf16[256,2048]{1,0:T(8,128)(2,1)} %get-tuple-element.593), channel_id=1, source_target_pairs={{0,2},{1,3},{2,0},{3,1},{4,6},{5,7},{6,4},{7,5},{8,10},{9,11},{10,... | collective-permute-start | bytes 3145736 | tf_op jit(solution)/shard_map/ppermute | solution.py:62
  778.0 25.2 %collective-permute-start.94 = (bf16[256,2048]{1,0:T(8,128)(2,1)}, bf16[256,2048]{1,0:T(8,128)(2,1)S(1)}, u32[]{:S(2)}, u32[]{:S(2)}) collective-permute-start(bf16[256,2048]{1,0:T(8,128)(2,1)} %get-tuple-element.594), channel_id=1, source_target_pairs={{0,4},{1,5},{2,6},{3,7},{4,0},{5,1},{6,2},{7,3},{8,12},{9,13},{10,... | collective-permute-start | bytes 3145736 | tf_op jit(solution)/shard_map/ppermute | solution.py:62
  816.9 38.4 %collective-permute-start.98 = (bf16[256,2048]{1,0:T(8,128)(2,1)}, bf16[256,2048]{1,0:T(8,128)(2,1)S(1)}, u32[]{:S(2)}, u32[]{:S(2)}) collective-permute-start(bf16[256,2048]{1,0:T(8,128)(2,1)} %get-tuple-element.613), channel_id=1, source_target_pairs={{0,4},{1,5},{2,6},{3,7},{4,0},{5,1},{6,2},{7,3},{8,12},{9,13},{10,... | collective-permute-start | bytes 3145736 | tf_op jit(solution)/shard_map/ppermute | solution.py:62
  818.3 36.9 %collective-permute-start.99 = (bf16[256,2048]{1,0:T(8,128)(2,1)}, bf16[256,2048]{1,0:T(8,128)(2,1)S(1)}, u32[]{:S(2)}, u32[]{:S(2)}) collective-permute-start(bf16[256,2048]{1,0:T(8,128)(2,1)} %get-tuple-element.614), channel_id=1, source_target_pairs={{0,2},{1,3},{2,0},{3,1},{4,6},{5,7},{6,4},{7,5},{8,10},{9,11},{10,... | collective-permute-start | bytes 3145736 | tf_op jit(solution)/shard_map/ppermute | solution.py:62
  844.8 81.0 %reduce-scatter.9.cloned.1.call-start = ((), (), s32[]{:S(2)}) async-start(), calls=%async_computation.17 | async-start | bytes 1310720 | tf_op jit(solution)/shard_map/reduce_scatter | solution.py:1239
  858.6 26.4 %collective-permute-start.101 = (bf16[256,2048]{1,0:T(8,128)(2,1)}, bf16[256,2048]{1,0:T(8,128)(2,1)}, u32[]{:S(2)}, u32[]{:S(2)}) collective-permute-start(bf16[256,2048]{1,0:T(8,128)(2,1)} %get-tuple-element.635), channel_id=1, source_target_pairs={{0,2},{1,3},{2,0},{3,1},{4,6},{5,7},{6,4},{7,5},{8,10},{9,11},{10,... | collective-permute-start | bytes 3145736 | tf_op jit(solution)/shard_map/ppermute | solution.py:62
  860.5 26.5 %collective-permute-start.102 = (bf16[256,2048]{1,0:T(8,128)(2,1)}, bf16[256,2048]{1,0:T(8,128)(2,1)}, u32[]{:S(2)}, u32[]{:S(2)}) collective-permute-start(bf16[256,2048]{1,0:T(8,128)(2,1)} %get-tuple-element.636), channel_id=1, source_target_pairs={{0,4},{1,5},{2,6},{3,7},{4,0},{5,1},{6,2},{7,3},{8,12},{9,13},{10,... | collective-permute-start | bytes 3145736 | tf_op jit(solution)/shard_map/ppermute | solution.py:62
  862.0 25.0 %collective-permute-start.103 = (bf16[256,2048]{1,0:T(8,128)(2,1)}, bf16[256,2048]{1,0:T(8,128)(2,1)}, u32[]{:S(2)}, u32[]{:S(2)}) collective-permute-start(bf16[256,2048]{1,0:T(8,128)(2,1)} %get-tuple-element.638), channel_id=1, source_target_pairs={{0,1},{1,0},{2,3},{3,2},{4,5},{5,4},{6,7},{7,6},{8,9},{9,8},{10,11... | collective-permute-start | bytes 3145736 | tf_op jit(solution)/shard_map/ppermute | solution.py:62
  862.0 25.0 %collective-permute-start.104 = (bf16[256,2048]{1,0:T(8,128)(2,1)}, bf16[256,2048]{1,0:T(8,128)(2,1)}, u32[]{:S(2)}, u32[]{:S(2)}) collective-permute-start(bf16[256,2048]{1,0:T(8,128)(2,1)} %get-tuple-element.640), channel_id=1, source_target_pairs={{0,1},{1,0},{2,3},{3,2},{4,5},{5,4},{6,7},{7,6},{8,9},{9,8},{10,11... | collective-permute-start | bytes 3145736 | tf_op jit(solution)/shard_map/ppermute | solution.py:62
  864.2 30.0 %all-to-all-start.5 = ((bf16[8,64,768]{2,1,0:T(8,128)(2,1)}), bf16[8,64,768]{2,1,0:T(8,128)(2,1)}, u32[]{:S(2)}, u32[]{:S(2)}) async-start(bf16[8,64,768]{2,1,0:T(8,128)(2,1)} %bitcast.191), calls=%async_computation.9 | async-start | bytes 1572864 | tf_op jit(solution)/shard_map/all_to_all | solution.py:1204
  (216 other events, 2044.4 us)
Sparse Core Ops, SparseCore 0:
  29.4 62.8 all-gather.4
  94.5 96.6 all-gather.8
  279.4 78.0 all-gather.6
  547.9 74.0 reduce-scatter.4
  624.8 77.1 reduce-scatter.6
  803.3 57.4 reduce-scatter.10
  863.2 27.1 reduce-scatter.8

commit v6 on v4

--- a/solution.py
+++ b/solution.py
@@ -318,7 +318,7 @@
 
 def norm_back(values, sums, extra, gain, low):
     half, wide = values[0].shape
-    chunk = min(half, 64)
+    chunk = min(half, 128)
     rows = half_rows(chunk, wide)
     both = pl.BlockSpec((2, chunk, wide), lambda s: (0, s, 0))
     outs = [

time: 942 us -> 940 us (level)
  Pallas kernels: 423 us -> 407 us
  starting transfers between devices: 95 us -> 107 us
    all_to_all x1, starting transfers between devices: 2.78 us -> 13.3 us  [per_device(): lax.all_to_all(all_grads, BOTH, 0, 0, tiled=True)]
    pallas_call x2, Pallas kernels: 90.6 us -> 80.8 us  [attn_backward(): pl.pallas_call(functools.partial(attn_backward_kernel, block, half, heads...]
  transfers between devices with their start and end apart: 120 -> 120, of which waited for: 43 -> 43; matrix products, arithmetic and copies ran while one was open for 17% -> 17% of each run, Pallas kernels for 43% -> 42%
where the time goes in v6:
time: 940 us; the launch traced here: 934 us
  Pallas kernels  407 us (43%)
  waiting for transfers between devices  179 us (19%)
  starting transfers between devices  107 us (11%)
  local copies, waits for them, and re-layouts  92.1 us (10%)
  matrix products  79.9 us (9%)
  other arithmetic  35.2 us (4%)
  blocking collectives  17.6 us (2%)
  between operations  17 us (2%)
    pallas_call x22, Pallas kernels, group_call(): pl.pallas_call(functools.partial(kernel, len(ins), len(earlier)), grid=(s...  232 us
    ppermute x105, waiting for transfers between devices, swapped(): return lax.ppermute(x, 'fsdp', [(i, i ^ bit) for i in range(devices)])  161 us
    pallas_call x2, Pallas kernels, attn_backward(): pl.pallas_call(functools.partial(attn_backward_kernel, block, half, heads...  80.8 us
    dot_general x6, matrix products, dot(): return lax.dot_general(left, right, dims, preferred_element_type=f32)  79.9 us
    ppermute x105, starting transfers between devices, swapped(): return lax.ppermute(x, 'fsdp', [(i, i ^ bit) for i in range(devices)])  64.1 us
    unnamed x297, local copies, waits for them, and re-layouts  53 us
    pallas_call x2, Pallas kernels, attn_forward(): pl.pallas_call(functools.partial(attn_forward_kernel, block, half, heads)...  49.3 us
    pallas_call x11, Pallas kernels, low_sums(): pl.pallas_call(functools.partial(low_sums_kernel, [len(one) for one in li...  23.1 us
  transfers between devices with their start and end apart: 120, of which 43 were waited for; matrix products, arithmetic and copies ran while one was open for 17% of the time, Pallas kernels for 42%

profile of v6, /device:TPU:0, one launch (start us, length us, event | category | flops | bytes accessed | tf_op | source)
XLA Modules:
  0.0 934.3 jit_solution(10859304976526196225)
XLA Ops:
  11.7 17.6 %all_to_all.53 = bf16[8,64,768]{2,1,0:T(8,128)(2,1)} all-to-all(bf16[8,64,768]{2,1,0:T(8,128)(2,1)S(1)} %pad_maximum_fusion.1), channel_id=1, replica_groups=mesh['dp'=4,'fsdp'=8] {'fsdp'}, dimensions={0} | all-to-all | bytes 1572864 | tf_op jit(solution)/shard_map/all_to_all | solution.py:907
  30.2 4.0 all-to-all-start.1
  36.3 5.7 all-to-all-done.1
  45.9 21.3 %collective-permute-done.refs_0_ = bf16[256,2048]{1,0:T(8,128)(2,1)S(1)} collective-permute-done((bf16[256,2048]{1,0:T(8,128)(2,1)S(1)}, bf16[256,2048]{1,0:T(8,128)(2,1)S(1)}, u32[]{:S(2)}, u32[]{:S(2)}) %collective-permute-start) | collective-permute-done | bytes 1048608 | tf_op jit(solution)/shard_map/ppermute | solution.py:62
  75.7 3.2 slice_bitcast_fusion
  79.7 5.8 norm_rows.4.refs_6_
  85.5 7.8 collective-permute-done.2.refs_0_
  100.4 5.9 norm_rows.5.refs_6_
  106.4 5.9 norm_rows.6.refs_6_
  112.2 14.5 %triple.2 = (bf16[4096,256]{1,0:T(8,128)(2,1)}, bf16[4096,256]{1,0:T(8,128)(2,1)}, bf16[4096,256]{1,0:T(8,128)(2,1)}) custom-call(bf16[4352,2048]{1,0:T(8,128)(2,1)} %bitcast.154, bf16[2048,768]{1,0:T(8,128)(2,1)} %all-gather.5.cloned.1.call-done.refs_1_.refs_6_, f32[1,768]{1,0:T(1,128)S(1)} %broadcast_in_dim.33.refs_2_), custom_call_target="tpu_custom_call" | custom-call | flops 9663676416 | bytes 12582912 | tf_op jit(solution)/shard_map/triple/pallas_call | solution.py:207
  128.4 3.8 all-to-all-start.2
  137.6 5.7 norm_rows.7
  143.4 7.6 triple.3
  155.6 24.7 %attn_forward.2 = (bf16[4096,128]{1,0:T(8,128)(2,1)S(1)}, f32[8,4096]{1,0:T(8,128)S(1)}) custom-call(s32[40]{0:T(128)S(1)} %pad_add_fusion.plan_ref, bf16[4096,256]{1,0:T(8,128)(2,1)S(1)} %copy-done.4, bf16[4096,256]{1,0:T(8,128)(2,1)S(1)} %copy-done.5, bf16[4096,256]{1,0:T(8,128)(2,1)S(1)} %copy-done.7, bf16[160,256]{1,0:T(8,128)(2,1)S(1)} %get-tuple-element.717.sk_ref, ...), custom_call_target="tpu_custom_call" | custom-call | flops 8589934592 | bytes 4194304 | tf_op jit(solution)/shard_map/attn_forward/pallas_call | solution.py:706
  181.2 5.8 collective-permute-done.14.refs_4_
  189.1 4.2 all-to-all-start.3
  197.1 24.7 %attn_forward.3 = (bf16[4096,128]{1,0:T(8,128)(2,1)S(1)}, f32[8,4096]{1,0:T(8,128)S(1)}) custom-call(s32[40]{0:T(128)S(1)} %pad_add_fusion.plan_ref, bf16[4096,256]{1,0:T(8,128)(2,1)S(1)} %copy-done.4, bf16[4096,256]{1,0:T(8,128)(2,1)S(1)} %copy-done.6, bf16[4096,256]{1,0:T(8,128)(2,1)S(1)} %copy-done.8, bf16[160,256]{1,0:T(8,128)(2,1)S(1)} %get-tuple-element.717.sk_ref, ...), custom_call_target="tpu_custom_call" | custom-call | flops 8589934592 | bytes 4194304 | tf_op jit(solution)/shard_map/attn_forward/pallas_call | solution.py:706
  225.1 4.0 project.8
  238.6 3.9 project.9
  242.5 18.1 %collective-permute-done.22 = bf16[256,2048]{1,0:T(8,128)(2,1)S(1)} collective-permute-done((bf16[256,2048]{1,0:T(8,128)(2,1)S(1)}, bf16[256,2048]{1,0:T(8,128)(2,1)S(1)}, u32[]{:S(2)}, u32[]{:S(2)}) %collective-permute-start.22) | collective-permute-done | bytes 1048608 | tf_op jit(solution)/shard_map/ppermute | solution.py:62
  271.2 3.9 project.10
  276.9 4.0 project.11
  280.9 13.7 %collective-permute-done.27.refs_2_ = bf16[256,2048]{1,0:T(8,128)(2,1)S(1)} collective-permute-done((bf16[256,2048]{1,0:T(8,128)(2,1)}, bf16[256,2048]{1,0:T(8,128)(2,1)S(1)}, u32[]{:S(2)}, u32[]{:S(2)}) %collective-permute-start.27) | collective-permute-done | bytes 1048608 | tf_op jit(solution)/shard_map/ppermute | solution.py:62
  295.8 3.0 low_sums.13
  300.4 22.8 %collective-permute-done.30 = bf16[256,2048]{1,0:T(8,128)(2,1)S(1)} collective-permute-done((bf16[256,2048]{1,0:T(8,128)(2,1)}, bf16[256,2048]{1,0:T(8,128)(2,1)S(1)}, u32[]{:S(2)}, u32[]{:S(2)}) %collective-permute-start.30) | collective-permute-done | bytes 1048608 | tf_op jit(solution)/shard_map/ppermute | solution.py:62
  324.5 5.4 fusion.28
  335.5 4.8 slice.180
  340.3 16.2 %collective-permute-done.38.refs_0_ = bf16[256,2048]{1,0:T(8,128)(2,1)S(1)} collective-permute-done((bf16[256,2048]{1,0:T(8,128)(2,1)}, bf16[256,2048]{1,0:T(8,128)(2,1)S(1)}, u32[]{:S(2)}, u32[]{:S(2)}) %collective-permute-start.38) | collective-permute-done | bytes 1048608 | tf_op jit(solution)/shard_map/ppermute | solution.py:62
  363.0 30.0 %feed_forward.4 = (bf16[16,256,1024]{2,1,0:T(8,128)(2,1)}, bf16[16,256,1024]{2,1,0:T(8,128)(2,1)}, bf16[16,256,2048]{2,1,0:T(8,128)(2,1)}, bf16[16,256,2048]{2,1...) custom-call(bf16[256,2048]{1,0:T(8,128)(2,1)} %copy-done.136, ...), custom_call_target="tpu_custom_call" | custom-call | flops 17179869184 | bytes 33554432 | tf_op jit(solution)/shard_map/feed_forward/pallas_call | solution.py:207
  398.5 30.2 %feed_forward.5 = (bf16[16,256,1024]{2,1,0:T(8,128)(2,1)}, bf16[16,256,1024]{2,1,0:T(8,128)(2,1)}, bf16[16,256,2048]{2,1,0:T(8,128)(2,1)}, bf16[16,256,2048]{2,1...) custom-call(bf16[256,2048]{1,0:T(8,128)(2,1)} %collective-permute-do, ...), custom_call_target="tpu_custom_call", output_to_operand_aliasing={{0}: (11, {}), {1}: (12, {}), {2}: (13, {}), {3}: (14, {}),... | custom-call | flops 17179869184 | bytes 33554432 | tf_op jit(solution)/shard_map/feed_forward/pallas_call | solution.py:207
  440.2 30.0 %feed_forward.6 = (bf16[16,256,1024]{2,1,0:T(8,128)(2,1)}, bf16[16,256,1024]{2,1,0:T(8,128)(2,1)}, bf16[16,256,2048]{2,1,0:T(8,128)(2,1)}, bf16[16,256,2048]{2,1...) custom-call(bf16[256,2048]{1,0:T(8,128)(2,1)} %collective-permute-do, ...), custom_call_target="tpu_custom_call", output_to_operand_aliasing={{0}: (11, {}), {1}: (12, {}), {2}: (13, {}), {3}: (14, {}),... | custom-call | flops 17179869184 | bytes 33554432 | tf_op jit(solution)/shard_map/feed_forward/pallas_call | solution.py:207
  481.6 30.4 %feed_forward.7 = (bf16[16,256,1024]{2,1,0:T(8,128)(2,1)}, bf16[16,256,1024]{2,1,0:T(8,128)(2,1)}, bf16[16,256,2048]{2,1,0:T(8,128)(2,1)}, bf16[16,256,2048]{2,1...) custom-call(bf16[256,2048]{1,0:T(8,128)(2,1)} %get-tuple-element.727, ...), custom_call_target="tpu_custom_call", output_to_operand_aliasing={{0}: (11, {}), {1}: (12, {}), {2}: (13, {}), {3}: (14, {}),... | custom-call | flops 17179869184 | bytes 33554432 | tf_op jit(solution)/shard_map/feed_forward/pallas_call | solution.py:207
  516.7 23.9 %convolution_convert_fusion.1 = bf16[1024,2048]{1,0:T(8,128)(2,1)} fusion(bf16[4096,1024]{1,0:T(8,128)(2,1)} %bitcast.160, bf16[4096,2048]{1,0:T(8,128)(2,1)} %bitcast.158), kind=kOutput, calls=%fused_computation.9 | convolution fusion | flops 17181966336 | bytes 29360128 | tf_op jit(solution)/shard_map/dot_general | solution.py:27
  544.5 10.2 %norm_back.2 = (f32[2,256,2048]{2,1,0:T(8,128)}, f32[8,2048]{1,0:T(8,128)S(1)}, bf16[256,2048]{1,0:T(8,128)(2,1)}, bf16[256,2048]{1,0:T(8,128)(2,1)}) custom-call(f32[256,2048]{1,0:T(8,128)S(1)} %get-tuple-element.657.refs_0_, f32[256,2048]{1,0:T(8,128)} %copy-done.74, bf16[256,2048]{1,0:T(8,128)(2,1)S(1)} %copy-done.23, ...), custom_call_target="tpu_custom_call" | custom-call | flops 41943040 | bytes 18874368 | tf_op jit(solution)/shard_map/norm_back/pallas_call | solution.py:327
  560.9 5.5 project_back.4
  566.4 23.8 %convolution_convert_fusion = bf16[2048,1024]{1,0:T(8,128)(2,1)} fusion(bf16[4096,2048]{1,0:T(8,128)(2,1)} %bitcast.157, bf16[4096,1024]{1,0:T(8,128)(2,1)} %bitcast.161), kind=kOutput, calls=%fused_computation.8 | convolution fusion | flops 17181966336 | bytes 29360128 | tf_op jit(solution)/shard_map/dot_general | solution.py:27
  590.2 13.5 %collective-permute-done.73.refs_0_ = bf16[256,2048]{1,0:T(8,128)(2,1)} collective-permute-done((bf16[256,2048]{1,0:T(8,128)(2,1)}, bf16[256,2048]{1,0:T(8,128)(2,1)}, u32[]{:S(2)}, u32[]{:S(2)}) %collective-permute-start.73) | collective-permute-done | bytes 1048608 | tf_op jit(solution)/shard_map/ppermute | solution.py:62
  612.9 4.1 low_sums.17
  616.9 5.5 project_back.5
  622.5 5.5 project_back.6
  627.9 3.1 collective-permute-done.77.refs_0_
  634.3 2.9 collective-permute-done.83.refs_2_
  642.2 5.3 project_back.7
  649.7 40.3 %attn_backward.2 = (bf16[4096,128]{1,0:T(8,128)(2,1)S(1)}, bf16[4096,128]{1,0:T(8,128)(2,1)S(1)}, bf16[4096,128]{1,0:T(8,128)(2,1)S(1)}, bf16[160,128]{1,0:T(8,1...) custom-call(s32[40]{0:T(128)S(1)} %copy-done.63, bf16[4096,256]{1,0:T(8,128)(2,1)} %get-tuple-element.369.q_ref, ...), custom_call_target="tpu_custom_call" | custom-call | flops 12884901888 | bytes 10485760 | tf_op jit(solution)/shard_map/attn_backward/pallas_call | solution.py:747
  690.1 4.2 low_sums.18
  698.2 4.2 all-to-all-start.4
  703.8 40.5 %attn_backward.3 = (bf16[4096,128]{1,0:T(8,128)(2,1)S(1)}, bf16[4096,128]{1,0:T(8,128)(2,1)S(1)}, bf16[4096,128]{1,0:T(8,128)(2,1)S(1)}, bf16[160,128]{1,0:T(8,1...) custom-call(s32[40]{0:T(128)S(1)} %copy-done.63, bf16[4096,256]{1,0:T(8,128)(2,1)} %get-tuple-element.369.q_ref, ...), custom_call_target="tpu_custom_call" | custom-call | flops 12884901888 | bytes 10485760 | tf_op jit(solution)/shard_map/attn_backward/pallas_call | solution.py:747
  747.3 7.1 project.12
  770.5 21.2 %fusion.7 = bf16[2048,768]{1,0:T(8,128)(2,1)} fusion(bf16[4352,2048]{1,0:T(8,128)(2,1)} %pad_dynamic-update-slice_fusion, bf16[160,512]{1,0:T(8,128)(2,1)S(1)} %constant_dynamic-update-slice_fusion, bf16[4096,768]{1,0:T(8,128)(2,1)} %constant_dynamic-update-slice_fusion.4), kind=kOutput, calls=%fused_computation.10 | convolution fusion | flops 13711835136 | bytes 27426816 | tf_op jit(solution)/shard_map/dot_general | solution.py:27
  793.1 7.1 project.13
  810.1 4.2 all-to-all-start.6
  814.4 7.5 project.14
  822.9 9.4 %convolution_convert_fusion.2 = bf16[256,2048]{1,0:T(8,128)(2,1)} fusion(bf16[4096,2048]{1,0:T(8,128)(2,1)} %bitcast.159, bf16[4096,128]{1,0:T(8,128)(2,1)S(1)} %copy-done.69, bf16[4096,128]{1,0:T(8,128)(2,1)S(1)} %copy-done.66), kind=kOutput, calls=%fused_computation.14 | convolution fusion | flops 4299685888 | bytes 19922944 | tf_op jit(solution)/shard_map/dot_general | solution.py:27
  833.8 7.2 project.15
  841.0 3.4 low_sums.21
  853.2 6.8 reduce-scatter.11.cloned.1.call-done
  859.9 4.5 all-to-all-start.5
  866.9 2.9 reshape.535
  876.8 3.3 all-to-all-done.5.parts_ref
  885.0 8.1 norm_back.3
  894.4 13.3 %all-to-all-start.8 = ((f32[32,1,768]{2,1,0:T(1,128)}), f32[32,1,768]{2,1,0:T(1,128)S(1)}, u32[]{:S(2)}, u32[]{:S(2)}) async-start(f32[32,1,768]{2,1,0:T(1,128)} %copy.134), calls=%async_computation.12 | async-start | bytes 196608 | tf_op jit(solution)/shard_map/all_to_all | solution.py:1287
  907.7 6.6 fusion.18
  915.5 3.5 all-to-all-start.7
  919.0 3.0 maximum_bitcast_fusion
  (656 shorter events, 217.5 us)
Async XLA Ops:
  7.2 105.0 %all-gather.5.cloned.1.call-start = ((), (), s32[]{:S(2)}) async-start(), calls=%async_computation.13 | async-start | bytes 3932160 | tf_op jit(solution)/shard_map/all_gather | solution.py:908
  34.2 188.5 %all-gather.9.cloned.1.call-start = ((), (), s32[]{:S(2)}) async-start(), calls=%async_computation.19 | async-start | bytes 6553600 | tf_op jit(solution)/shard_map/all_gather | solution.py:964
  42.0 25.2 %collective-permute-start = (bf16[256,2048]{1,0:T(8,128)(2,1)S(1)}, bf16[256,2048]{1,0:T(8,128)(2,1)S(1)}, u32[]{:S(2)}, u32[]{:S(2)}) collective-permute-start(bf16[256,2048]{1,0:T(8,128)(2,1)S(1)} %get-tuple-element.351.refs_0_), channel_id=1, source_target_pairs={{0,2},{1,3},{2,0},{3,1},{4,6},{5,7},{6,4},{7,5},{8,10},{9,11},{10,... | collective-permute-start | bytes 3145736 | tf_op jit(solution)/shard_map/ppermute | solution.py:62
  42.4 25.1 %collective-permute-start.1 = (bf16[256,2048]{1,0:T(8,128)(2,1)S(1)}, bf16[256,2048]{1,0:T(8,128)(2,1)}, u32[]{:S(2)}, u32[]{:S(2)}) collective-permute-start(bf16[256,2048]{1,0:T(8,128)(2,1)S(1)} %get-tuple-element.352.refs_1_), channel_id=1, source_target_pairs={{0,4},{1,5},{2,6},{3,7},{4,0},{5,1},{6,2},{7,3},{8,12},{9,13},{10,... | collective-permute-start | bytes 3145736 | tf_op jit(solution)/shard_map/ppermute | solution.py:62
  68.1 25.2 %collective-permute-start.2 = (bf16[256,2048]{1,0:T(8,128)(2,1)S(1)}, bf16[256,2048]{1,0:T(8,128)(2,1)}, u32[]{:S(2)}, u32[]{:S(2)}) collective-permute-start(bf16[256,2048]{1,0:T(8,128)(2,1)S(1)} %get-tuple-element.352.refs_1_), channel_id=1, source_target_pairs={{0,2},{1,3},{2,0},{3,1},{4,6},{5,7},{6,4},{7,5},{8,10},{9,11},{10,... | collective-permute-start | bytes 3145736 | tf_op jit(solution)/shard_map/ppermute | solution.py:62
  69.7 25.0 %collective-permute-start.3 = (bf16[256,2048]{1,0:T(8,128)(2,1)S(1)}, bf16[256,2048]{1,0:T(8,128)(2,1)}, u32[]{:S(2)}, u32[]{:S(2)}) collective-permute-start(bf16[256,2048]{1,0:T(8,128)(2,1)S(1)} %get-tuple-element.351.refs_0_), channel_id=1, source_target_pairs={{0,4},{1,5},{2,6},{3,7},{4,0},{5,1},{6,2},{7,3},{8,12},{9,13},{10,... | collective-permute-start | bytes 3145736 | tf_op jit(solution)/shard_map/ppermute | solution.py:62
  96.1 30.7 %collective-permute-start.6 = (bf16[256,2048]{1,0:T(8,128)(2,1)S(1)}, bf16[256,2048]{1,0:T(8,128)(2,1)S(1)}, u32[]{:S(2)}, u32[]{:S(2)}) collective-permute-start(bf16[256,2048]{1,0:T(8,128)(2,1)S(1)} %collective-permute-done.refs_0_), channel_id=1, source_target_pairs={{0,4},{1,5},{2,6},{3,7},{4,0},{5,1},{6,2},{7,3},{8,12},{9,13},{10,... | collective-permute-start | bytes 3145736 | tf_op jit(solution)/shard_map/ppermute | solution.py:62
  98.9 27.8 %collective-permute-start.7 = (bf16[256,2048]{1,0:T(8,128)(2,1)}, bf16[256,2048]{1,0:T(8,128)(2,1)S(1)}, u32[]{:S(2)}, u32[]{:S(2)}) collective-permute-start(bf16[256,2048]{1,0:T(8,128)(2,1)} %collective-permute-done.1.refs_2_), channel_id=1, source_target_pairs={{0,2},{1,3},{2,0},{3,1},{4,6},{5,7},{6,4},{7,5},{8,10},{9,11},{10,... | collective-permute-start | bytes 3145736 | tf_op jit(solution)/shard_map/ppermute | solution.py:62
  133.5 53.6 %collective-permute-start.15 = (bf16[256,2048]{1,0:T(8,128)(2,1)}, bf16[256,2048]{1,0:T(8,128)(2,1)}, u32[]{:S(2)}, u32[]{:S(2)}) collective-permute-start(bf16[256,2048]{1,0:T(8,128)(2,1)} %get-tuple-element.376.refs_5_), channel_id=1, source_target_pairs={{0,4},{1,5},{2,6},{3,7},{4,0},{5,1},{6,2},{7,3},{8,12},{9,13},{10,... | collective-permute-start | bytes 3145736 | tf_op jit(solution)/shard_map/ppermute | solution.py:62
  135.5 51.5 %collective-permute-start.16 = (bf16[256,2048]{1,0:T(8,128)(2,1)}, bf16[256,2048]{1,0:T(8,128)(2,1)}, u32[]{:S(2)}, u32[]{:S(2)}) collective-permute-start(bf16[256,2048]{1,0:T(8,128)(2,1)} %get-tuple-element.376.refs_5_), channel_id=1, source_target_pairs={{0,2},{1,3},{2,0},{3,1},{4,6},{5,7},{6,4},{7,5},{8,10},{9,11},{10,... | collective-permute-start | bytes 3145736 | tf_op jit(solution)/shard_map/ppermute | solution.py:62
  137.0 50.0 %collective-permute-start.14 = (bf16[256,2048]{1,0:T(8,128)(2,1)}, bf16[256,2048]{1,0:T(8,128)(2,1)}, u32[]{:S(2)}, u32[]{:S(2)}) collective-permute-start(bf16[256,2048]{1,0:T(8,128)(2,1)} %get-tuple-element.375.refs_4_), channel_id=1, source_target_pairs={{0,2},{1,3},{2,0},{3,1},{4,6},{5,7},{6,4},{7,5},{8,10},{9,11},{10,... | collective-permute-start | bytes 3145736 | tf_op jit(solution)/shard_map/ppermute | solution.py:62
  137.5 49.5 %collective-permute-start.17 = (bf16[256,2048]{1,0:T(8,128)(2,1)}, bf16[256,2048]{1,0:T(8,128)(2,1)}, u32[]{:S(2)}, u32[]{:S(2)}) collective-permute-start(bf16[256,2048]{1,0:T(8,128)(2,1)} %get-tuple-element.375.refs_4_), channel_id=1, source_target_pairs={{0,4},{1,5},{2,6},{3,7},{4,0},{5,1},{6,2},{7,3},{8,12},{9,13},{10,... | collective-permute-start | bytes 3145736 | tf_op jit(solution)/shard_map/ppermute | solution.py:62
  187.0 38.1 %collective-permute-start.18 = (bf16[256,2048]{1,0:T(8,128)(2,1)}, bf16[256,2048]{1,0:T(8,128)(2,1)}, u32[]{:S(2)}, u32[]{:S(2)}) collective-permute-start(bf16[256,2048]{1,0:T(8,128)(2,1)} %collective-permute-done.14.refs_4_), channel_id=1, source_target_pairs={{0,4},{1,5},{2,6},{3,7},{4,0},{5,1},{6,2},{7,3},{8,12},{9,13},{10,... | collective-permute-start | bytes 3145736 | tf_op jit(solution)/shard_map/ppermute | solution.py:62
  188.6 36.5 %collective-permute-start.19 = (bf16[256,2048]{1,0:T(8,128)(2,1)}, bf16[256,2048]{1,0:T(8,128)(2,1)}, u32[]{:S(2)}, u32[]{:S(2)}) collective-permute-start(bf16[256,2048]{1,0:T(8,128)(2,1)} %collective-permute-done.15.refs_6_), channel_id=1, source_target_pairs={{0,2},{1,3},{2,0},{3,1},{4,6},{5,7},{6,4},{7,5},{8,10},{9,11},{10,... | collective-permute-start | bytes 3145736 | tf_op jit(solution)/shard_map/ppermute | solution.py:62
  189.1 36.0 %all-to-all-start.3 = ((bf16[8,64,1024]{2,1,0:T(8,128)(2,1)}), bf16[8,64,1024]{2,1,0:T(8,128)(2,1)}, u32[]{:S(2)}, u32[]{:S(2)}) async-start(bf16[8,64,1024]{2,1,0:T(8,128)(2,1)} %reshape.489), calls=%async_computation.3 | async-start | bytes 2097152 | tf_op jit(solution)/shard_map/all_to_all | solution.py:973
  193.4 169.6 %all-gather.7.cloned.1.call-start = ((), (), s32[]{:S(2)}) async-start(), calls=%async_computation.14 | async-start | bytes 5242880 | tf_op jit(solution)/shard_map/all_gather | solution.py:1022
  235.2 25.5 %collective-permute-start.22 = (bf16[256,2048]{1,0:T(8,128)(2,1)S(1)}, bf16[256,2048]{1,0:T(8,128)(2,1)S(1)}, u32[]{:S(2)}, u32[]{:S(2)}) collective-permute-start(bf16[256,2048]{1,0:T(8,128)(2,1)S(1)} %get-tuple-element.391), channel_id=1, source_target_pairs={{0,2},{1,3},{2,0},{3,1},{4,6},{5,7},{6,4},{7,5},{8,10},{9,11},{10,... | collective-permute-start | bytes 3145736 | tf_op jit(solution)/shard_map/ppermute | solution.py:62
  237.1 24.9 %collective-permute-start.23 = (bf16[256,2048]{1,0:T(8,128)(2,1)S(1)}, bf16[256,2048]{1,0:T(8,128)(2,1)S(1)}, u32[]{:S(2)}, u32[]{:S(2)}) collective-permute-start(bf16[256,2048]{1,0:T(8,128)(2,1)S(1)} %get-tuple-element.392), channel_id=1, source_target_pairs={{0,4},{1,5},{2,6},{3,7},{4,0},{5,1},{6,2},{7,3},{8,12},{9,13},{10,... | collective-permute-start | bytes 3145736 | tf_op jit(solution)/shard_map/ppermute | solution.py:62
  269.2 25.4 %collective-permute-start.27 = (bf16[256,2048]{1,0:T(8,128)(2,1)}, bf16[256,2048]{1,0:T(8,128)(2,1)S(1)}, u32[]{:S(2)}, u32[]{:S(2)}) collective-permute-start(bf16[256,2048]{1,0:T(8,128)(2,1)} %get-tuple-element.402), channel_id=1, source_target_pairs={{0,4},{1,5},{2,6},{3,7},{4,0},{5,1},{6,2},{7,3},{8,12},{9,13},{10,... | collective-permute-start | bytes 3145736 | tf_op jit(solution)/shard_map/ppermute | solution.py:62
  270.7 25.1 %collective-permute-start.28 = (bf16[256,2048]{1,0:T(8,128)(2,1)}, bf16[256,2048]{1,0:T(8,128)(2,1)S(1)}, u32[]{:S(2)}, u32[]{:S(2)}) collective-permute-start(bf16[256,2048]{1,0:T(8,128)(2,1)} %get-tuple-element.403), channel_id=1, source_target_pairs={{0,2},{1,3},{2,0},{3,1},{4,6},{5,7},{6,4},{7,5},{8,10},{9,11},{10,... | collective-permute-start | bytes 3145736 | tf_op jit(solution)/shard_map/ppermute | solution.py:62
  276.6 370.9 %reduce-scatter.5.cloned.1.call-start = ((), (), s32[]{:S(2)}) async-start(), calls=%async_computation.15 | async-start | bytes 5242880 | tf_op jit(solution)/shard_map/reduce_scatter | solution.py:1082
  299.7 24.8 %collective-permute-start.33 = (bf16[256,2048]{1,0:T(8,128)(2,1)}, bf16[256,2048]{1,0:T(8,128)(2,1)}, u32[]{:S(2)}, u32[]{:S(2)}) collective-permute-start(bf16[256,2048]{1,0:T(8,128)(2,1)} %get-tuple-element.422), channel_id=1, source_target_pairs={{0,1},{1,0},{2,3},{3,2},{4,5},{5,4},{6,7},{7,6},{8,9},{9,8},{10,11... | collective-permute-start | bytes 3145736 | tf_op jit(solution)/shard_map/ppermute | solution.py:62
  357.8 37.2 %collective-permute-start.54 = (bf16[256,2048]{1,0:T(8,128)(2,1)}, bf16[256,2048]{1,0:T(8,128)(2,1)}, u32[]{:S(2)}, u32[]{:S(2)}) collective-permute-start(bf16[256,2048]{1,0:T(8,128)(2,1)} %collective-permute-done.16.refs_4_), channel_id=1, source_target_pairs={{0,1},{1,0},{2,3},{3,2},{4,5},{5,4},{6,7},{7,6},{8,9},{9,8},{10,11... | collective-permute-start | bytes 3145736 | tf_op jit(solution)/shard_map/ppermute | solution.py:62
  357.9 38.0 %collective-permute-start.55 = (bf16[256,2048]{1,0:T(8,128)(2,1)}, bf16[256,2048]{1,0:T(8,128)(2,1)}, u32[]{:S(2)}, u32[]{:S(2)}) collective-permute-start(bf16[256,2048]{1,0:T(8,128)(2,1)} %collective-permute-done.17.refs_6_), channel_id=1, source_target_pairs={{0,1},{1,0},{2,3},{3,2},{4,5},{5,4},{6,7},{7,6},{8,9},{9,8},{10,11... | collective-permute-start | bytes 3145736 | tf_op jit(solution)/shard_map/ppermute | solution.py:62
  358.4 34.7 %collective-permute-start.46 = (bf16[256,2048]{1,0:T(8,128)(2,1)S(1)}, bf16[256,2048]{1,0:T(8,128)(2,1)}, u32[]{:S(2)}, u32[]{:S(2)}) collective-permute-start(bf16[256,2048]{1,0:T(8,128)(2,1)S(1)} %get-tuple-element.726.refs_1_), channel_id=1, source_target_pairs={{0,2},{1,3},{2,0},{3,1},{4,6},{5,7},{6,4},{7,5},{8,10},{9,11},{10,... | collective-permute-start | bytes 3145736 | tf_op jit(solution)/shard_map/ppermute | solution.py:62
  362.3 30.7 %collective-permute-start.47 = (bf16[256,2048]{1,0:T(8,128)(2,1)}, bf16[256,2048]{1,0:T(8,128)(2,1)}, u32[]{:S(2)}, u32[]{:S(2)}) collective-permute-start(bf16[256,2048]{1,0:T(8,128)(2,1)} %get-tuple-element.727.refs_0_), channel_id=1, source_target_pairs={{0,4},{1,5},{2,6},{3,7},{4,0},{5,1},{6,2},{7,3},{8,12},{9,13},{10,... | collective-permute-start | bytes 3145736 | tf_op jit(solution)/shard_map/ppermute | solution.py:62
  393.7 35.9 %collective-permute-start.40 = (bf16[256,2048]{1,0:T(8,128)(2,1)S(1)}, bf16[256,2048]{1,0:T(8,128)(2,1)}, u32[]{:S(2)}, u32[]{:S(2)}) collective-permute-start(bf16[256,2048]{1,0:T(8,128)(2,1)S(1)} %copy-done.137), channel_id=1, source_target_pairs={{0,4},{1,5},{2,6},{3,7},{4,0},{5,1},{6,2},{7,3},{8,12},{9,13},{10,... | collective-permute-start | bytes 3145736 | tf_op jit(solution)/shard_map/ppermute | solution.py:62
  395.0 34.9 %collective-permute-start.41 = (bf16[256,2048]{1,0:T(8,128)(2,1)}, bf16[256,2048]{1,0:T(8,128)(2,1)}, u32[]{:S(2)}, u32[]{:S(2)}) collective-permute-start(bf16[256,2048]{1,0:T(8,128)(2,1)} %collective-permute-done.39.refs_2_), channel_id=1, source_target_pairs={{0,2},{1,3},{2,0},{3,1},{4,6},{5,7},{6,4},{7,5},{8,10},{9,11},{10,... | collective-permute-start | bytes 3145736 | tf_op jit(solution)/shard_map/ppermute | solution.py:62
  434.9 35.2 %collective-permute-start.58 = (bf16[256,2048]{1,0:T(8,128)(2,1)S(1)}, bf16[256,2048]{1,0:T(8,128)(2,1)S(1)}, u32[]{:S(2)}, u32[]{:S(2)}) collective-permute-start(bf16[256,2048]{1,0:T(8,128)(2,1)S(1)} %get-tuple-element.453), channel_id=1, source_target_pairs={{0,2},{1,3},{2,0},{3,1},{4,6},{5,7},{6,4},{7,5},{8,10},{9,11},{10,... | collective-permute-start | bytes 3145736 | tf_op jit(solution)/shard_map/ppermute | solution.py:62
  435.9 34.3 %collective-permute-start.59 = (bf16[256,2048]{1,0:T(8,128)(2,1)S(1)}, bf16[256,2048]{1,0:T(8,128)(2,1)S(1)}, u32[]{:S(2)}, u32[]{:S(2)}) collective-permute-start(bf16[256,2048]{1,0:T(8,128)(2,1)S(1)} %get-tuple-element.454), channel_id=1, source_target_pairs={{0,4},{1,5},{2,6},{3,7},{4,0},{5,1},{6,2},{7,3},{8,12},{9,13},{10,... | collective-permute-start | bytes 3145736 | tf_op jit(solution)/shard_map/ppermute | solution.py:62
  474.6 37.4 %collective-permute-start.62 = (bf16[256,2048]{1,0:T(8,128)(2,1)}, bf16[256,2048]{1,0:T(8,128)(2,1)S(1)}, u32[]{:S(2)}, u32[]{:S(2)}) collective-permute-start(bf16[256,2048]{1,0:T(8,128)(2,1)} %get-tuple-element.485), channel_id=1, source_target_pairs={{0,1},{1,0},{2,3},{3,2},{4,5},{5,4},{6,7},{7,6},{8,9},{9,8},{10,11... | collective-permute-start | bytes 3145736 | tf_op jit(solution)/shard_map/ppermute | solution.py:62
  477.3 34.8 %collective-permute-start.65 = (bf16[256,2048]{1,0:T(8,128)(2,1)}, bf16[256,2048]{1,0:T(8,128)(2,1)S(1)}, u32[]{:S(2)}, u32[]{:S(2)}) collective-permute-start(bf16[256,2048]{1,0:T(8,128)(2,1)} %get-tuple-element.492), channel_id=1, source_target_pairs={{0,1},{1,0},{2,3},{3,2},{4,5},{5,4},{6,7},{7,6},{8,9},{9,8},{10,11... | collective-permute-start | bytes 3145736 | tf_op jit(solution)/shard_map/ppermute | solution.py:62
  477.7 34.3 %collective-permute-start.63 = (bf16[256,2048]{1,0:T(8,128)(2,1)}, bf16[256,2048]{1,0:T(8,128)(2,1)S(1)}, u32[]{:S(2)}, u32[]{:S(2)}) collective-permute-start(bf16[256,2048]{1,0:T(8,128)(2,1)} %get-tuple-element.469), channel_id=1, source_target_pairs={{0,4},{1,5},{2,6},{3,7},{4,0},{5,1},{6,2},{7,3},{8,12},{9,13},{10,... | collective-permute-start | bytes 3145736 | tf_op jit(solution)/shard_map/ppermute | solution.py:62
  479.1 32.9 %collective-permute-start.64 = (bf16[256,2048]{1,0:T(8,128)(2,1)S(1)}, bf16[256,2048]{1,0:T(8,128)(2,1)S(1)}, u32[]{:S(2)}, u32[]{:S(2)}) collective-permute-start(bf16[256,2048]{1,0:T(8,128)(2,1)S(1)} %get-tuple-element.470), channel_id=1, source_target_pairs={{0,2},{1,3},{2,0},{3,1},{4,6},{5,7},{6,4},{7,5},{8,10},{9,11},{10,... | collective-permute-start | bytes 3145736 | tf_op jit(solution)/shard_map/ppermute | solution.py:62
  513.8 26.8 %collective-permute-start.70 = (bf16[8,256,2048]{2,1,0:T(8,128)(2,1)}, bf16[8,256,2048]{2,1,0:T(8,128)(2,1)}, u32[]{:S(2)}, u32[]{:S(2)}) collective-permute-start(bf16[8,256,2048]{2,1,0:T(8,128)(2,1)} %get-tuple-element.506), channel_id=1, source_target_pairs={{0,1},{1,0},{2,3},{3,2},{4,5},{5,4},{6,7},{7,6},{8,9},{9,8},{10,11... | collective-permute-start | bytes 25165832 | tf_op jit(solution)/shard_map/ppermute | solution.py:62
  514.0 26.6 %collective-permute-start.66 = (bf16[256,2048]{1,0:T(8,128)(2,1)}, bf16[256,2048]{1,0:T(8,128)(2,1)}, u32[]{:S(2)}, u32[]{:S(2)}) collective-permute-start(bf16[256,2048]{1,0:T(8,128)(2,1)} %get-tuple-element.494), channel_id=1, source_target_pairs={{0,2},{1,3},{2,0},{3,1},{4,6},{5,7},{6,4},{7,5},{8,10},{9,11},{10,... | collective-permute-start | bytes 3145736 | tf_op jit(solution)/shard_map/ppermute | solution.py:62
  514.9 25.7 %collective-permute-start.67 = (bf16[256,2048]{1,0:T(8,128)(2,1)}, bf16[256,2048]{1,0:T(8,128)(2,1)}, u32[]{:S(2)}, u32[]{:S(2)}) collective-permute-start(bf16[256,2048]{1,0:T(8,128)(2,1)} %get-tuple-element.495), channel_id=1, source_target_pairs={{0,4},{1,5},{2,6},{3,7},{4,0},{5,1},{6,2},{7,3},{8,12},{9,13},{10,... | collective-permute-start | bytes 3145736 | tf_op jit(solution)/shard_map/ppermute | solution.py:62
  516.2 24.4 %collective-permute-start.68 = (bf16[256,2048]{1,0:T(8,128)(2,1)}, bf16[256,2048]{1,0:T(8,128)(2,1)}, u32[]{:S(2)}, u32[]{:S(2)}) collective-permute-start(bf16[256,2048]{1,0:T(8,128)(2,1)} %get-tuple-element.497), channel_id=1, source_target_pairs={{0,1},{1,0},{2,3},{3,2},{4,5},{5,4},{6,7},{7,6},{8,9},{9,8},{10,11... | collective-permute-start | bytes 3145736 | tf_op jit(solution)/shard_map/ppermute | solution.py:62
  516.2 24.4 %collective-permute-start.69 = (bf16[256,2048]{1,0:T(8,128)(2,1)}, bf16[256,2048]{1,0:T(8,128)(2,1)}, u32[]{:S(2)}, u32[]{:S(2)}) collective-permute-start(bf16[256,2048]{1,0:T(8,128)(2,1)} %get-tuple-element.500), channel_id=1, source_target_pairs={{0,1},{1,0},{2,3},{3,2},{4,5},{5,4},{6,7},{7,6},{8,9},{9,8},{10,11... | collective-permute-start | bytes 3145736 | tf_op jit(solution)/shard_map/ppermute | solution.py:62
  540.7 157.6 %reduce-scatter.7.cloned.1.call-start = ((), (), s32[]{:S(2)}) async-start(), calls=%async_computation.16 | async-start | bytes 5242880 | tf_op jit(solution)/shard_map/reduce_scatter | solution.py:1115
  555.9 34.4 %collective-permute-start.71 = (bf16[256,2048]{1,0:T(8,128)(2,1)}, bf16[256,2048]{1,0:T(8,128)(2,1)}, u32[]{:S(2)}, u32[]{:S(2)}) collective-permute-start(bf16[256,2048]{1,0:T(8,128)(2,1)} %get-tuple-element.515.refs_0_), channel_id=1, source_target_pairs={{0,2},{1,3},{2,0},{3,1},{4,6},{5,7},{6,4},{7,5},{8,10},{9,11},{10,... | collective-permute-start | bytes 3145736 | tf_op jit(solution)/shard_map/ppermute | solution.py:62
  557.0 33.3 %collective-permute-start.72 = (bf16[256,2048]{1,0:T(8,128)(2,1)}, bf16[256,2048]{1,0:T(8,128)(2,1)}, u32[]{:S(2)}, u32[]{:S(2)}) collective-permute-start(bf16[256,2048]{1,0:T(8,128)(2,1)} %get-tuple-element.516.refs_1_), channel_id=1, source_target_pairs={{0,4},{1,5},{2,6},{3,7},{4,0},{5,1},{6,2},{7,3},{8,12},{9,13},{10,... | collective-permute-start | bytes 3145736 | tf_op jit(solution)/shard_map/ppermute | solution.py:62
  558.0 45.7 %collective-permute-start.73 = (bf16[256,2048]{1,0:T(8,128)(2,1)}, bf16[256,2048]{1,0:T(8,128)(2,1)}, u32[]{:S(2)}, u32[]{:S(2)}) collective-permute-start(bf16[256,2048]{1,0:T(8,128)(2,1)} %get-tuple-element.516.refs_1_), channel_id=1, source_target_pairs={{0,2},{1,3},{2,0},{3,1},{4,6},{5,7},{6,4},{7,5},{8,10},{9,11},{10,... | collective-permute-start | bytes 3145736 | tf_op jit(solution)/shard_map/ppermute | solution.py:62
  558.9 45.6 %collective-permute-start.74 = (bf16[256,2048]{1,0:T(8,128)(2,1)}, bf16[256,2048]{1,0:T(8,128)(2,1)}, u32[]{:S(2)}, u32[]{:S(2)}) collective-permute-start(bf16[256,2048]{1,0:T(8,128)(2,1)} %get-tuple-element.515.refs_0_), channel_id=1, source_target_pairs={{0,4},{1,5},{2,6},{3,7},{4,0},{5,1},{6,2},{7,3},{8,12},{9,13},{10,... | collective-permute-start | bytes 3145736 | tf_op jit(solution)/shard_map/ppermute | solution.py:62
  605.7 25.4 %collective-permute-start.77 = (bf16[256,2048]{1,0:T(8,128)(2,1)}, bf16[256,2048]{1,0:T(8,128)(2,1)S(1)}, u32[]{:S(2)}, u32[]{:S(2)}) collective-permute-start(bf16[256,2048]{1,0:T(8,128)(2,1)} %collective-permute-done.71.refs_0_), channel_id=1, source_target_pairs={{0,4},{1,5},{2,6},{3,7},{4,0},{5,1},{6,2},{7,3},{8,12},{9,13},{10,... | collective-permute-start | bytes 3145736 | tf_op jit(solution)/shard_map/ppermute | solution.py:62
  608.2 25.5 %collective-permute-start.78 = (bf16[256,2048]{1,0:T(8,128)(2,1)}, bf16[256,2048]{1,0:T(8,128)(2,1)}, u32[]{:S(2)}, u32[]{:S(2)}) collective-permute-start(bf16[256,2048]{1,0:T(8,128)(2,1)} %collective-permute-done.72.refs_2_), channel_id=1, source_target_pairs={{0,2},{1,3},{2,0},{3,1},{4,6},{5,7},{6,4},{7,5},{8,10},{9,11},{10,... | collective-permute-start | bytes 3145736 | tf_op jit(solution)/shard_map/ppermute | solution.py:62
  638.2 51.8 %collective-permute-start.85 = (bf16[256,2048]{1,0:T(8,128)(2,1)}, bf16[256,2048]{1,0:T(8,128)(2,1)}, u32[]{:S(2)}, u32[]{:S(2)}) collective-permute-start(bf16[256,2048]{1,0:T(8,128)(2,1)} %get-tuple-element.559), channel_id=1, source_target_pairs={{0,2},{1,3},{2,0},{3,1},{4,6},{5,7},{6,4},{7,5},{8,10},{9,11},{10,... | collective-permute-start | bytes 3145736 | tf_op jit(solution)/shard_map/ppermute | solution.py:62
  639.1 51.0 %collective-permute-start.86 = (bf16[256,2048]{1,0:T(8,128)(2,1)}, bf16[256,2048]{1,0:T(8,128)(2,1)}, u32[]{:S(2)}, u32[]{:S(2)}) collective-permute-start(bf16[256,2048]{1,0:T(8,128)(2,1)} %get-tuple-element.560), channel_id=1, source_target_pairs={{0,4},{1,5},{2,6},{3,7},{4,0},{5,1},{6,2},{7,3},{8,12},{9,13},{10,... | collective-permute-start | bytes 3145736 | tf_op jit(solution)/shard_map/ppermute | solution.py:62
  640.1 49.9 %collective-permute-start.87 = (bf16[256,2048]{1,0:T(8,128)(2,1)}, bf16[256,2048]{1,0:T(8,128)(2,1)S(1)}, u32[]{:S(2)}, u32[]{:S(2)}) collective-permute-start(bf16[256,2048]{1,0:T(8,128)(2,1)} %get-tuple-element.561), channel_id=1, source_target_pairs={{0,4},{1,5},{2,6},{3,7},{4,0},{5,1},{6,2},{7,3},{8,12},{9,13},{10,... | collective-permute-start | bytes 3145736 | tf_op jit(solution)/shard_map/ppermute | solution.py:62
  641.1 48.9 %collective-permute-start.88 = (bf16[256,2048]{1,0:T(8,128)(2,1)}, bf16[256,2048]{1,0:T(8,128)(2,1)}, u32[]{:S(2)}, u32[]{:S(2)}) collective-permute-start(bf16[256,2048]{1,0:T(8,128)(2,1)} %get-tuple-element.562), channel_id=1, source_target_pairs={{0,2},{1,3},{2,0},{3,1},{4,6},{5,7},{6,4},{7,5},{8,10},{9,11},{10,... | collective-permute-start | bytes 3145736 | tf_op jit(solution)/shard_map/ppermute | solution.py:62
  694.4 52.9 %collective-permute-start.89 = (bf16[256,2048]{1,0:T(8,128)(2,1)}, bf16[256,2048]{1,0:T(8,128)(2,1)}, u32[]{:S(2)}, u32[]{:S(2)}) collective-permute-start(bf16[256,2048]{1,0:T(8,128)(2,1)} %get-tuple-element.576), channel_id=1, source_target_pairs={{0,2},{1,3},{2,0},{3,1},{4,6},{5,7},{6,4},{7,5},{8,10},{9,11},{10,... | collective-permute-start | bytes 3145736 | tf_op jit(solution)/shard_map/ppermute | solution.py:62
  695.4 51.9 %collective-permute-start.90 = (bf16[256,2048]{1,0:T(8,128)(2,1)}, bf16[256,2048]{1,0:T(8,128)(2,1)}, u32[]{:S(2)}, u32[]{:S(2)}) collective-permute-start(bf16[256,2048]{1,0:T(8,128)(2,1)} %get-tuple-element.577), channel_id=1, source_target_pairs={{0,4},{1,5},{2,6},{3,7},{4,0},{5,1},{6,2},{7,3},{8,12},{9,13},{10,... | collective-permute-start | bytes 3145736 | tf_op jit(solution)/shard_map/ppermute | solution.py:62
  698.2 49.0 %all-to-all-start.4 = ((bf16[8,64,1024]{2,1,0:T(8,128)(2,1)}), bf16[8,64,1024]{2,1,0:T(8,128)(2,1)}, u32[]{:S(2)}, u32[]{:S(2)}) async-start(bf16[8,64,1024]{2,1,0:T(8,128)(2,1)} %bitcast.196), calls=%async_computation.6 | async-start | bytes 2097152 | tf_op jit(solution)/shard_map/all_to_all | solution.py:1145
  702.5 157.4 %reduce-scatter.11.cloned.1.call-start = ((), (), s32[]{:S(2)}) async-start(), calls=%async_computation.18 | async-start | bytes 3932160 | tf_op jit(solution)/shard_map/reduce_scatter | solution.py:1172
  760.3 31.4 %collective-permute-start.93 = (bf16[256,2048]{1,0:T(8,128)(2,1)}, bf16[256,2048]{1,0:T(8,128)(2,1)S(1)}, u32[]{:S(2)}, u32[]{:S(2)}) collective-permute-start(bf16[256,2048]{1,0:T(8,128)(2,1)} %get-tuple-element.593), channel_id=1, source_target_pairs={{0,2},{1,3},{2,0},{3,1},{4,6},{5,7},{6,4},{7,5},{8,10},{9,11},{10,... | collective-permute-start | bytes 3145736 | tf_op jit(solution)/shard_map/ppermute | solution.py:62
  762.1 29.6 %collective-permute-start.94 = (bf16[256,2048]{1,0:T(8,128)(2,1)}, bf16[256,2048]{1,0:T(8,128)(2,1)}, u32[]{:S(2)}, u32[]{:S(2)}) collective-permute-start(bf16[256,2048]{1,0:T(8,128)(2,1)} %get-tuple-element.594), channel_id=1, source_target_pairs={{0,4},{1,5},{2,6},{3,7},{4,0},{5,1},{6,2},{7,3},{8,12},{9,13},{10,... | collective-permute-start | bytes 3145736 | tf_op jit(solution)/shard_map/ppermute | solution.py:62
  806.9 34.1 %collective-permute-start.98 = (bf16[256,2048]{1,0:T(8,128)(2,1)}, bf16[256,2048]{1,0:T(8,128)(2,1)S(1)}, u32[]{:S(2)}, u32[]{:S(2)}) collective-permute-start(bf16[256,2048]{1,0:T(8,128)(2,1)} %get-tuple-element.613), channel_id=1, source_target_pairs={{0,4},{1,5},{2,6},{3,7},{4,0},{5,1},{6,2},{7,3},{8,12},{9,13},{10,... | collective-permute-start | bytes 3145736 | tf_op jit(solution)/shard_map/ppermute | solution.py:62
  807.4 33.6 %collective-permute-start.99 = (bf16[256,2048]{1,0:T(8,128)(2,1)}, bf16[256,2048]{1,0:T(8,128)(2,1)}, u32[]{:S(2)}, u32[]{:S(2)}) collective-permute-start(bf16[256,2048]{1,0:T(8,128)(2,1)} %get-tuple-element.614), channel_id=1, source_target_pairs={{0,2},{1,3},{2,0},{3,1},{4,6},{5,7},{6,4},{7,5},{8,10},{9,11},{10,... | collective-permute-start | bytes 3145736 | tf_op jit(solution)/shard_map/ppermute | solution.py:62
  810.1 37.8 %all-to-all-start.6 = ((bf16[8,32,2048]{2,1,0:T(8,128)(2,1)}), bf16[8,32,2048]{2,1,0:T(8,128)(2,1)}, u32[]{:S(2)}, u32[]{:S(2)}) async-start(bf16[8,32,2048]{2,1,0:T(8,128)(2,1)} %bitcast.185), calls=%async_computation.10 | async-start | bytes 2097152 | tf_op jit(solution)/shard_map/all_to_all | solution.py:1221
  814.3 93.4 %reduce-scatter.9.cloned.1.call-start = ((), (), s32[]{:S(2)}) async-start(), calls=%async_computation.17 | async-start | bytes 1310720 | tf_op jit(solution)/shard_map/reduce_scatter | solution.py:1210
  844.5 32.3 %collective-permute-start.101 = (bf16[256,2048]{1,0:T(8,128)(2,1)}, bf16[256,2048]{1,0:T(8,128)(2,1)}, u32[]{:S(2)}, u32[]{:S(2)}) collective-permute-start(bf16[256,2048]{1,0:T(8,128)(2,1)} %get-tuple-element.635), channel_id=1, source_target_pairs={{0,2},{1,3},{2,0},{3,1},{4,6},{5,7},{6,4},{7,5},{8,10},{9,11},{10,... | collective-permute-start | bytes 3145736 | tf_op jit(solution)/shard_map/ppermute | solution.py:62
  846.4 30.4 %collective-permute-start.102 = (bf16[256,2048]{1,0:T(8,128)(2,1)}, bf16[256,2048]{1,0:T(8,128)(2,1)}, u32[]{:S(2)}, u32[]{:S(2)}) collective-permute-start(bf16[256,2048]{1,0:T(8,128)(2,1)} %get-tuple-element.636), channel_id=1, source_target_pairs={{0,4},{1,5},{2,6},{3,7},{4,0},{5,1},{6,2},{7,3},{8,12},{9,13},{10,... | collective-permute-start | bytes 3145736 | tf_op jit(solution)/shard_map/ppermute | solution.py:62
  847.9 29.0 %collective-permute-start.103 = (bf16[256,2048]{1,0:T(8,128)(2,1)}, bf16[256,2048]{1,0:T(8,128)(2,1)}, u32[]{:S(2)}, u32[]{:S(2)}) collective-permute-start(bf16[256,2048]{1,0:T(8,128)(2,1)} %get-tuple-element.638), channel_id=1, source_target_pairs={{0,1},{1,0},{2,3},{3,2},{4,5},{5,4},{6,7},{7,6},{8,9},{9,8},{10,11... | collective-permute-start | bytes 3145736 | tf_op jit(solution)/shard_map/ppermute | solution.py:62
  847.9 29.0 %collective-permute-start.104 = (bf16[256,2048]{1,0:T(8,128)(2,1)}, bf16[256,2048]{1,0:T(8,128)(2,1)}, u32[]{:S(2)}, u32[]{:S(2)}) collective-permute-start(bf16[256,2048]{1,0:T(8,128)(2,1)} %get-tuple-element.640), channel_id=1, source_target_pairs={{0,1},{1,0},{2,3},{3,2},{4,5},{5,4},{6,7},{7,6},{8,9},{9,8},{10,11... | collective-permute-start | bytes 3145736 | tf_op jit(solution)/shard_map/ppermute | solution.py:62
  (198 other events, 1791.8 us)
Sparse Core Ops, SparseCore 0:
  29.4 62.8 all-gather.4
  94.5 96.6 all-gather.8
  276.8 81.3 all-gather.6
  540.8 77.2 reduce-scatter.4
  620.9 77.2 reduce-scatter.6
  791.9 67.9 reduce-scatter.10
  862.2 27.1 reduce-scatter.8
